TPU v7x, 32 devices: a whole 2x2x4 slice. The times are simulated.
32 devices in a mesh: wide: 8 (over z, y), narrow: 4 (over x, core).
Axes of the slice: x: 2, y: 2, z: 4, core: 2. Of those that a mesh axis runs over, the one named last changes fastest.
Arguments:
- hidden_in: bfloat16 [3072, 2048], P('wide', 'narrow'), may hold values from -6 to 6
- gain_attn: bfloat16 [2048], P('wide'), may hold values from 0.25 to 1.75
- w_query: bfloat16 [2048, 2048], P('wide', 'narrow'), may hold values from -0.37565048 to 0.37565048
- w_key: bfloat16 [2048, 2048], P('wide', 'narrow'), may hold values from -0.125 to 0.125
- w_value: bfloat16 [2048, 2048], P('wide', 'narrow'), may hold values from -0.125 to 0.125
- w_out: bfloat16 [2048, 2048], P('narrow', 'wide'), may hold values from -1 to 1
- gain_ffn: bfloat16 [2048], P('wide'), may hold values from 0.25 to 1.75
- w_gate: bfloat16 [2048, 8192], P('wide', 'narrow'), may hold values from -0.125 to 0.125
- w_up: bfloat16 [2048, 8192], P('wide', 'narrow'), may hold values from -0.125 to 0.125
- w_down: bfloat16 [8192, 2048], P('narrow', 'wide'), may hold values from -0.0625 to 0.0625
- cotangent: bfloat16 [3072, 2048], P('wide', 'narrow'), may hold values from -6 to 6
- segment_ids: int32 [3072], replicated, may hold values from 0 to 12, as said below
- parents: int32 [13], replicated, may hold values from 0 to 11, as said below
Outputs:
- hidden_out: bfloat16 [3072, 2048], P('wide', 'narrow')
- grad_in: bfloat16 [3072, 2048], P('wide', 'narrow')
- grad_query: float32 [2048, 2048], P('wide', 'narrow')
- grad_key: float32 [2048, 2048], P('wide', 'narrow')
- grad_value: float32 [2048, 2048], P('wide', 'narrow')
- grad_wout: float32 [2048, 2048], P('narrow', 'wide')
- grad_gate: float32 [2048, 8192], P('wide', 'narrow')
- grad_up: float32 [2048, 8192], P('wide', 'narrow')
- grad_down: float32 [8192, 2048], P('narrow', 'wide')
- grad_gainattn: float32 [2048], P('wide')
- grad_gainffn: float32 [2048], P('wide')
- clipped_query: float32 [2048, 2048], P('wide', 'narrow')
- clipped_key: float32 [2048, 2048], P('wide', 'narrow')
- logit_peaks: float32 [32], P('narrow')
Inputs may be any that keep to these rules, and one draw needn't show every extreme that they name: `segment_ids`: segment numbers never fall along the tokens; segment 0 starts at token 0 and every segment holds at least one token. parents[0] = 0; for s >= 1, parents[s] < s and parents[parents[parents[s]]] = 0, so all segments form one tree of depth two at most.
All inputs are finite; a program needn't handle non-finite values.
Results may differ from a plain program's by a relative error of at most 0.03.
Values may be sent and summed in bfloat16 or wider, within the bound.
No kernel may reach another device: no remote copies, remote signals or barrier semaphores. Data moves between devices by JAX's collectives and lax.ppermute only.
A program may use at most 320 MiB of HBM per device.

v0:
```python
import jax
import jax.numpy as jnp
from jax import lax
from jax.sharding import PartitionSpec as P

HDIM = 64
NSEG = 13


eps_norm = 1e-05
rope_base = 130000.0
clip_limit = 5.0
masked_fill = -1e30


def lookup(lookup_table, indices):
    labels = jnp.arange(lookup_table.shape[0], dtype=jnp.int32)
    return jnp.sum(
        jnp.where(indices[:, None] == labels[None, :], lookup_table[None, :], 0),
        axis=1,
        dtype=jnp.int32,
    )


def segment_tables(segment_ids, parents):
    labels = jnp.arange(NSEG, dtype=jnp.int32)
    counts = jnp.sum(
        (segment_ids[:, None] == labels[None, :]).astype(jnp.int32), axis=0, dtype=jnp.int32
    )
    starts = jnp.cumsum(counts, dtype=jnp.int32) - counts
    ancestor = lookup(parents, parents)
    parent_len = jnp.where(parents != labels, lookup(counts, parents), 0)
    ancestor_len = jnp.where(ancestor != parents, lookup(counts, ancestor), 0)
    return (ancestor, starts, parent_len, ancestor_len)


def token_tables(seg_rows, first_row, parents, tables):
    ancestor, starts, parent_len, ancestor_len = tables
    row_index = first_row + jnp.arange(seg_rows.shape[0], dtype=jnp.int32)
    parent_tok = lookup(parents, seg_rows)
    ancestor_tok = lookup(ancestor, seg_rows)
    places = (
        row_index
        - lookup(starts, seg_rows)
        + lookup(parent_len, seg_rows)
        + lookup(ancestor_len, seg_rows)
    )
    return (row_index, parent_tok, ancestor_tok, places)


def allowed_pairs(query_index, query_seg, parent_tok, ancestor_tok, key_index, key_seg):
    same_tree = (
        (key_seg[None, :] == query_seg[:, None])
        | (key_seg[None, :] == parent_tok[:, None])
        | (key_seg[None, :] == ancestor_tok[:, None])
    )
    return same_tree & (key_index[None, :] <= query_index[:, None])


def rotary_tables(places):
    frequency = rope_base ** (-2.0 * jnp.arange(HDIM // 2, dtype=jnp.float32) / HDIM)
    angles = places.astype(jnp.float32)[:, None] * frequency[None, :]
    return (jnp.cos(angles), jnp.sin(angles))


def rotate(values, cos_table, sin_table):
    halfway = values.shape[-1] // 2
    leading = values[..., :halfway]
    trailing = values[..., halfway:]
    cosine = cos_table[:, None, :]
    sine_part = sin_table[:, None, :]
    return jnp.concatenate(
        [leading * cosine - trailing * sine_part, trailing * cosine + leading * sine_part], axis=-1
    )


def unrotate(values, cos_table, sin_table):
    halfway = values.shape[-1] // 2
    leading = values[..., :halfway]
    trailing = values[..., halfway:]
    cosine = cos_table[:, None, :]
    sine_part = sin_table[:, None, :]
    return jnp.concatenate(
        [leading * cosine + trailing * sine_part, trailing * cosine - leading * sine_part], axis=-1
    )


def normalize(values):
    factor = lax.rsqrt(jnp.mean(values * values, axis=-1, keepdims=True) + eps_norm)
    return (factor, values * factor)


def norm_back(grad_normed, norm_gain, factor, unit_rows):
    grad_unit = grad_normed * norm_gain.astype(jnp.float32)
    return factor * (
        grad_unit - unit_rows * jnp.mean(grad_unit * unit_rows, axis=-1, keepdims=True)
    )


def contract_rows(left, right):
    return lax.dot_general(
        left, right, (((0,), (0,)), ((), ())), preferred_element_type=jnp.float32
    )


def contract_cols(left, right):
    return lax.dot_general(
        left, right, (((1,), (1,)), ((), ())), preferred_element_type=jnp.float32
    )


def on_device(
    hidden_in,
    gain_attn,
    w_query,
    w_key,
    w_value,
    w_out,
    gain_ffn,
    w_gate,
    w_up,
    w_down,
    cotangent,
    segment_ids,
    parents,
):
    local_rows = hidden_in.shape[0]
    width_local = hidden_in.shape[1]
    heads_local = w_query.shape[1] // HDIM
    head_width = heads_local * HDIM
    score_scale = HDIM ** (-0.5)
    first_row = lax.axis_index("wide") * local_rows
    tables = segment_tables(segment_ids, parents)
    seg_rows = lax.dynamic_slice_in_dim(segment_ids, first_row, local_rows)
    row_index, parent_tok, ancestor_tok, places = token_tables(seg_rows, first_row, parents, tables)
    cos_table, sin_table = rotary_tables(places)
    inputs_full, cotangent_full = (
        lax.all_gather(hidden_in, "narrow", axis=1, tiled=True),
        lax.all_gather(cotangent, "narrow", axis=1, tiled=True),
    )
    wq_full, wk_full, wv_full, gattn_full, wo_full, wg_full, wu_full, gffn_full, wd_full = (
        lax.all_gather(w_query, "wide", axis=0, tiled=True),
        lax.all_gather(w_key, "wide", axis=0, tiled=True),
        lax.all_gather(w_value, "wide", axis=0, tiled=True),
        lax.all_gather(gain_attn, "wide", axis=0, tiled=True),
        lax.all_gather(w_out, "wide", axis=1, tiled=True),
        lax.all_gather(w_gate, "wide", axis=0, tiled=True),
        lax.all_gather(w_up, "wide", axis=0, tiled=True),
        lax.all_gather(gain_ffn, "wide", axis=0, tiled=True),
        lax.all_gather(w_down, "wide", axis=1, tiled=True),
    )
    rstd_attn, unit_attn = normalize(inputs_full.astype(jnp.float32))
    normed_attn = (unit_attn * gattn_full.astype(jnp.float32)).astype(jnp.bfloat16)
    query_lin = jnp.dot(normed_attn, wq_full, preferred_element_type=jnp.float32)
    key_lin = jnp.dot(normed_attn, wk_full, preferred_element_type=jnp.float32)
    value_lin = jnp.dot(normed_attn, wv_full, preferred_element_type=jnp.float32)
    queries = rotate(query_lin.reshape(local_rows, heads_local, HDIM), cos_table, sin_table).astype(
        jnp.bfloat16
    )
    keys_local = (
        rotate(key_lin.reshape(local_rows, heads_local, HDIM), cos_table, sin_table)
        .reshape(local_rows, head_width)
        .astype(jnp.bfloat16)
    )
    values_local = value_lin.astype(jnp.bfloat16)
    key_piece = lax.all_gather(keys_local, "wide", axis=0, tiled=True)
    value_piece = lax.all_gather(values_local, "wide", axis=0, tiled=True)
    count_keys = key_piece.shape[0]
    key_index = jnp.arange(count_keys, dtype=jnp.int32)
    key_seg = segment_ids
    allowed = allowed_pairs(row_index, seg_rows, parent_tok, ancestor_tok, key_index, key_seg)
    highest = jnp.full((heads_local, local_rows), masked_fill, jnp.float32)
    largest = jnp.full((heads_local,), masked_fill, jnp.float32)
    scores = (
        jnp.einsum(
            "qhd,khd->hqk",
            queries,
            key_piece.reshape(count_keys, heads_local, HDIM),
            preferred_element_type=jnp.float32,
        )
        * score_scale
    )
    masked = jnp.where(allowed[None], scores, masked_fill)
    new_high = jnp.maximum(highest, jnp.max(masked, axis=-1))
    weights = jnp.where(allowed[None], jnp.exp(masked - new_high[..., None]), 0.0)
    normalizer = jnp.sum(weights, axis=-1)
    added = jnp.einsum(
        "hqk,khd->qhd",
        weights.astype(jnp.bfloat16),
        value_piece.reshape(count_keys, heads_local, HDIM),
        preferred_element_type=jnp.float32,
    )
    weighted = added
    largest = jnp.maximum(largest, jnp.max(masked, axis=(1, 2)))
    highest, normalizer, weighted, largest = (new_high, normalizer, weighted, largest)
    head_peaks = lax.pmax(largest, "wide")
    attended = weighted / jnp.transpose(normalizer)[..., None]
    log_norm = highest + jnp.log(normalizer)
    attended_low = attended.reshape(local_rows, head_width).astype(jnp.bfloat16)
    branch_attn = lax.psum_scatter(
        jnp.dot(attended_low, wo_full, preferred_element_type=jnp.float32).astype(jnp.bfloat16),
        "narrow",
        scatter_dimension=1,
        tiled=True,
    ).astype(jnp.float32)
    residual_mid = hidden_in.astype(jnp.float32) + branch_attn
    mid_full = lax.all_gather(residual_mid.astype(jnp.bfloat16), "narrow", axis=1, tiled=True)
    rstd_ffn, unit_ffn = normalize(mid_full.astype(jnp.float32))
    normed_ffn = (unit_ffn * gffn_full.astype(jnp.float32)).astype(jnp.bfloat16)
    gate_lin = jnp.dot(normed_ffn, wg_full, preferred_element_type=jnp.float32)
    up_lin = jnp.dot(normed_ffn, wu_full, preferred_element_type=jnp.float32)
    gate_sigmoid = jax.nn.sigmoid(gate_lin)
    activated = gate_lin * gate_sigmoid
    hidden_low = (activated * up_lin).astype(jnp.bfloat16)
    branch_ffn = lax.psum_scatter(
        jnp.dot(hidden_low, wd_full, preferred_element_type=jnp.float32).astype(jnp.bfloat16),
        "narrow",
        scatter_dimension=1,
        tiled=True,
    ).astype(jnp.float32)
    hidden_out = (residual_mid + branch_ffn).astype(jnp.bfloat16)
    grad_down_t = contract_rows(cotangent_full, hidden_low)
    grad_hidden = contract_cols(cotangent_full, wd_full)
    grad_gate_lin = (
        grad_hidden * up_lin * gate_sigmoid * (1.0 + gate_lin * (1.0 - gate_sigmoid))
    ).astype(jnp.bfloat16)
    grad_up_lin = (grad_hidden * activated).astype(jnp.bfloat16)
    grad_gate_t = contract_rows(normed_ffn, grad_gate_lin)
    grad_up_t = contract_rows(normed_ffn, grad_up_lin)
    partial_ffn = contract_cols(grad_gate_lin, wg_full) + contract_cols(grad_up_lin, wu_full)
    grad_normed_ffn = lax.psum(partial_ffn.astype(jnp.bfloat16), "narrow").astype(jnp.float32)
    gain_ffn_term = jnp.sum(grad_normed_ffn * unit_ffn, axis=0)
    grad_mid = cotangent_full.astype(jnp.float32) + norm_back(
        grad_normed_ffn, gffn_full, rstd_ffn, unit_ffn
    )
    grad_branch = grad_mid.astype(jnp.bfloat16)
    grad_wout_t = contract_rows(grad_branch, attended_low)
    grad_att_low = contract_cols(grad_branch, wo_full).astype(jnp.bfloat16)
    grad_heads = grad_att_low.reshape(local_rows, heads_local, HDIM)
    row_delta = jnp.transpose(jnp.sum(grad_heads.astype(jnp.float32) * attended, axis=-1))
    keys_whole, values_whole = (
        lax.all_gather(keys_local, "wide", axis=0, tiled=True),
        lax.all_gather(values_local, "wide", axis=0, tiled=True),
    )
    total_keys = keys_whole.shape[0]
    block_keys = min(512, total_keys)

    def key_block(grad_query, block_number):
        offset = block_number * block_keys
        key_rows = lax.dynamic_slice_in_dim(keys_whole, offset, block_keys).reshape(
            block_keys, heads_local, HDIM
        )
        value_rows = lax.dynamic_slice_in_dim(values_whole, offset, block_keys).reshape(
            block_keys, heads_local, HDIM
        )
        key_index = offset + jnp.arange(block_keys, dtype=jnp.int32)
        key_seg = lax.dynamic_slice_in_dim(segment_ids, offset, block_keys)
        allowed = allowed_pairs(row_index, seg_rows, parent_tok, ancestor_tok, key_index, key_seg)
        grad_running = grad_query
        scores = (
            jnp.einsum("qhd,khd->hqk", queries, key_rows, preferred_element_type=jnp.float32)
            * score_scale
        )
        probabilities = jnp.where(allowed[None], jnp.exp(scores - log_norm[..., None]), 0.0)
        prob_low = probabilities.astype(jnp.bfloat16)
        grad_value_rows = jnp.einsum(
            "hqk,qhd->khd", prob_low, grad_heads, preferred_element_type=jnp.float32
        )
        grad_probs = jnp.einsum(
            "qhd,khd->hqk", grad_heads, value_rows, preferred_element_type=jnp.float32
        )
        grad_scores = (probabilities * (grad_probs - row_delta[..., None])).astype(jnp.bfloat16)
        grad_running = (
            grad_running
            + jnp.einsum("hqk,khd->qhd", grad_scores, key_rows, preferred_element_type=jnp.float32)
            * score_scale
        )
        grad_key_rows = (
            jnp.einsum("hqk,qhd->khd", grad_scores, queries, preferred_element_type=jnp.float32)
            * score_scale
        )
        return (
            grad_running,
            (
                grad_key_rows.reshape(block_keys, head_width),
                grad_value_rows.reshape(block_keys, head_width),
            ),
        )

    grad_query_rot, (grad_key_blocks, grad_value_blocks) = lax.scan(
        key_block,
        jnp.zeros((local_rows, heads_local, HDIM), jnp.float32),
        jnp.arange(total_keys // block_keys, dtype=jnp.int32),
    )
    grad_keys, grad_values = (
        lax.psum_scatter(
            grad_key_blocks.reshape(total_keys, head_width).astype(jnp.bfloat16),
            "wide",
            scatter_dimension=0,
            tiled=True,
        ).astype(jnp.float32),
        lax.psum_scatter(
            grad_value_blocks.reshape(total_keys, head_width).astype(jnp.bfloat16),
            "wide",
            scatter_dimension=0,
            tiled=True,
        ).astype(jnp.float32),
    )
    grad_query_lin = (
        unrotate(grad_query_rot, cos_table, sin_table)
        .reshape(local_rows, head_width)
        .astype(jnp.bfloat16)
    )
    grad_key_lin = (
        unrotate(grad_keys.reshape(local_rows, heads_local, HDIM), cos_table, sin_table)
        .reshape(local_rows, head_width)
        .astype(jnp.bfloat16)
    )
    grad_value_lin = grad_values.astype(jnp.bfloat16)
    grad_wq_t = contract_rows(normed_attn, grad_query_lin)
    grad_wk_t = contract_rows(normed_attn, grad_key_lin)
    grad_wv_t = contract_rows(normed_attn, grad_value_lin)
    partial_attn = (
        contract_cols(grad_query_lin, wq_full)
        + contract_cols(grad_key_lin, wk_full)
        + contract_cols(grad_value_lin, wv_full)
    )
    grad_normed_attn = lax.psum(partial_attn.astype(jnp.bfloat16), "narrow").astype(jnp.float32)
    gain_attn_term = jnp.sum(grad_normed_attn * unit_attn, axis=0)
    grad_full = grad_mid + norm_back(grad_normed_attn, gattn_full, rstd_attn, unit_attn)
    grad_in = lax.dynamic_slice_in_dim(
        grad_full, lax.axis_index("narrow") * width_local, width_local, 1
    ).astype(jnp.bfloat16)
    reduced = (
        lax.psum_scatter(
            grad_wq_t.astype(jnp.bfloat16), "wide", scatter_dimension=0, tiled=True
        ).astype(jnp.float32),
        lax.psum_scatter(
            grad_wk_t.astype(jnp.bfloat16), "wide", scatter_dimension=0, tiled=True
        ).astype(jnp.float32),
        lax.psum_scatter(
            grad_wv_t.astype(jnp.bfloat16), "wide", scatter_dimension=0, tiled=True
        ).astype(jnp.float32),
        lax.psum_scatter(
            grad_wout_t.astype(jnp.bfloat16), "wide", scatter_dimension=0, tiled=True
        ).astype(jnp.float32),
        lax.psum_scatter(
            gain_attn_term.astype(jnp.bfloat16), "wide", scatter_dimension=0, tiled=True
        ).astype(jnp.float32),
        lax.psum_scatter(
            grad_gate_t.astype(jnp.bfloat16), "wide", scatter_dimension=0, tiled=True
        ).astype(jnp.float32),
        lax.psum_scatter(
            grad_up_t.astype(jnp.bfloat16), "wide", scatter_dimension=0, tiled=True
        ).astype(jnp.float32),
        lax.psum_scatter(
            grad_down_t.astype(jnp.bfloat16), "wide", scatter_dimension=0, tiled=True
        ).astype(jnp.float32),
        lax.psum_scatter(
            gain_ffn_term.astype(jnp.bfloat16), "wide", scatter_dimension=0, tiled=True
        ).astype(jnp.float32),
    )
    (
        grad_wq,
        grad_wk,
        grad_wv,
        grad_wo_local,
        grad_gattn,
        grad_wg,
        grad_wu,
        grad_wd_local,
        grad_gffn,
    ) = reduced
    factor = jnp.sqrt(clip_limit / jnp.maximum(head_peaks, clip_limit))
    column_factor = jnp.repeat(factor, HDIM)
    clipped_query = w_query.astype(jnp.float32) * column_factor[None, :]
    clipped_key = w_key.astype(jnp.float32) * column_factor[None, :]
    return (
        hidden_out,
        grad_in,
        grad_wq,
        grad_wk,
        grad_wv,
        jnp.transpose(grad_wo_local),
        grad_wg,
        grad_wu,
        jnp.transpose(grad_wd_local),
        grad_gattn,
        grad_gffn,
        clipped_query,
        clipped_key,
        head_peaks,
    )


def solution(mesh):
    placed = (
        P("wide", "narrow"),
        P("wide"),
        P("wide", "narrow"),
        P("wide", "narrow"),
        P("wide", "narrow"),
        P("narrow", "wide"),
        P("wide"),
        P("wide", "narrow"),
        P("wide", "narrow"),
        P("narrow", "wide"),
        P("wide", "narrow"),
        P(),
        P(),
    )
    return jax.shard_map(
        on_device,
        mesh=mesh,
        in_specs=placed,
        out_specs=(
            P("wide", "narrow"),
            P("wide", "narrow"),
            P("wide", "narrow"),
            P("wide", "narrow"),
            P("wide", "narrow"),
            P("narrow", "wide"),
            P("wide", "narrow"),
            P("wide", "narrow"),
            P("narrow", "wide"),
            P("wide"),
            P("wide"),
            P("wide", "narrow"),
            P("wide", "narrow"),
            P("narrow"),
        ),
        check_vma=False,
    )
```

profile of v0, /device:TPU:0, one launch (start us, length us, event | category | flops | bytes accessed | tf_op | source)
XLA Modules:
  0.0 2024.7 jit_solution(7449612320400286630)
XLA Ops:
  12.5 22.2 %all-gather = bf16[8,1,256]{2,1,0:T(2,128)(2,1)S(1)} all-gather(bf16[1,1,256]{2,1,0:T(2,128)(2,1)S(1)} %reshape.431), channel_id=1, replica_groups=mesh['wide'=8,'narrow'=4] {'wide'}, dimensions={0}, use_global_device_ids=true | all-gather | bytes 4608 | tf_op jit(solution)/shard_map/all_gather | solution.py:145
  40.0 43.4 %all-gather.21.cloned.1.call-done = bf16[2048,512]{1,0:T(8,128)(2,1)} async-done(((bf16[256,512]{1,0:T(8,128)(2,1)}), bf16[2048,512]{1,0:T(8,128)(2,1)}) %all-gather.21.cloned.1.call-update) | async-done | bytes 2097168 | tf_op jit(solution)/shard_map/all_gather | solution.py:142
  86.9 46.5 %all-gather.23.cloned.1.call-done = bf16[2048,512]{1,0:T(8,128)(2,1)} async-done(((bf16[256,512]{1,0:T(8,128)(2,1)}), bf16[2048,512]{1,0:T(8,128)(2,1)}) %all-gather.23.cloned.1.call-update) | async-done | bytes 2097168 | tf_op jit(solution)/shard_map/all_gather | solution.py:143
  137.5 45.7 %all-gather.17.cloned.1.call-done = bf16[2048,512]{1,0:T(8,128)(2,1)} async-done(((bf16[256,512]{1,0:T(8,128)(2,1)}), bf16[2048,512]{1,0:T(8,128)(2,1)}) %all-gather.17.cloned.1.call-update) | async-done | bytes 2097168 | tf_op jit(solution)/shard_map/all_gather | solution.py:144
  190.2 57.0 %all-gather.25.cloned.1.call-done = bf16[3072,512]{0,1:T(8,128)(2,1)} async-done(((bf16[384,512]{0,1:T(8,128)(2,1)}), bf16[3072,512]{0,1:T(8,128)(2,1)}) %all-gather.25.cloned.1.call-update) | async-done | bytes 3145744 | tf_op jit(solution)/shard_map/all_gather | solution.py:166
  247.2 16.7 fusion.14
  264.0 19.6 fusion.13
  283.5 25.0 %all-gather.19.cloned.1.call-done = bf16[3072,512]{1,0:T(8,128)(2,1)} async-done(((bf16[384,512]{1,0:T(8,128)(2,1)}), bf16[3072,512]{1,0:T(8,128)(2,1)}) %all-gather.19.cloned.1.call-update) | async-done | bytes 3145744 | tf_op jit(solution)/shard_map/all_gather | solution.py:167
  308.5 4.7 copy.65
  313.2 18.0 fusion.55
  331.3 29.0 %all-gather.27.cloned.1.call-done = bf16[512,2048]{1,0:T(8,128)(2,1)} async-done(((bf16[512,256]{1,0:T(8,128)(2,1)}), bf16[512,2048]{1,0:T(8,128)(2,1)}) %all-gather.27.cloned.1.call-update) | async-done | bytes 2097168 | tf_op jit(solution)/shard_map/all_gather | solution.py:146
  364.1 26.5 %reduce-scatter.12.cloned.1.call-done = bf16[384,512]{1,0:T(8,128)(2,1)} async-done(((bf16[384,2048]{1,0:T(8,128)(2,1)}), bf16[384,512]{1,0:T(8,128)(2,1)}) %reduce-scatter.12.cloned.1.call-update) | async-done | bytes 393232 | tf_op jit(solution)/shard_map/reduce_scatter | solution.py:200
  395.2 21.0 %all-gather.1 = bf16[8,1,256]{2,1,0:T(2,128)(2,1)S(1)} all-gather(bf16[1,1,256]{2,1,0:T(2,128)(2,1)S(1)} %reshape.433), channel_id=1, replica_groups=mesh['wide'=8,'narrow'=4] {'wide'}, dimensions={0}, use_global_device_ids=true | all-gather | bytes 4608 | tf_op jit(solution)/shard_map/all_gather | solution.py:149
  418.1 121.6 %all-gather.33.cloned.1.call-done = bf16[2048,2048]{1,0:T(8,128)(2,1)} async-done(((bf16[256,2048]{1,0:T(8,128)(2,1)}), bf16[2048,2048]{1,0:T(8,128)(2,1)}) %all-gather.33.cloned.1.call-update) | async-done | bytes 8388624 | tf_op jit(solution)/shard_map/all_gather | solution.py:148
  539.7 9.2 fusion.49
  548.8 116.3 %all-gather.31.cloned.1.call-done = bf16[2048,2048]{1,0:T(8,128)(2,1)} async-done(((bf16[256,2048]{1,0:T(8,128)(2,1)}), bf16[2048,2048]{1,0:T(8,128)(2,1)}) %all-gather.31.cloned.1.call-update) | async-done | bytes 8388624 | tf_op jit(solution)/shard_map/all_gather | solution.py:147
  665.2 8.5 fusion.51
  673.7 10.8 all-gather.37.cloned.1.call-done
  684.5 127.7 %all-gather.35.cloned.1.call-done = bf16[2048,2048]{1,0:T(8,128)(2,1)} async-done(((bf16[2048,256]{1,0:T(8,128)(2,1)}), bf16[2048,2048]{1,0:T(8,128)(2,1)}) %all-gather.35.cloned.1.call-update) | async-done | bytes 8388624 | tf_op jit(solution)/shard_map/all_gather | solution.py:150
  812.2 11.9 multiply_convert_fusion
  827.6 10.3 add_convert_fusion.1
  838.7 40.4 %all-reduce.6.cloned.1.call-done = bf16[384,2048]{1,0:T(8,128)(2,1)} async-done(((bf16[384,2048]{1,0:T(8,128)(2,1)}), bf16[384,2048]{1,0:T(8,128)(2,1)}) %all-reduce.6.cloned.1.call-update) | async-done | bytes 1572880 | tf_op jit(solution)/shard_map/psum | solution.py:231
  890.8 158.0 %while.15 = (s32[]{:T(128)}, f32[384,8,64]{0,2,1:T(8,128)}, bf16[6,512,512]{2,1,0:T(8,128)(2,1)}, bf16[6,512,512]{2,1,0:T(8,128)(2,1)}, s32[6]{0:T(128)}, /*inde...) while((s32[]{:T(128)}, f32[384,8,64]{0,2,1:T(8,128)}, ...), condition=%wide.region_20.21_spmd.clone, body=%wide.region_19.20_spmd.clone.sunk | while | flops 1024852864 | bytes 69163416 | solution.py:290
  905.0 5.1 fusion.128
  931.1 5.1 fusion.128
  957.5 5.1 fusion.128
  983.8 5.1 fusion.128
  1010.2 5.1 fusion.128
  1036.5 5.1 fusion.128
  1049.6 8.6 convolution_convert_fusion.6
  1061.1 62.2 %reduce-scatter.16.cloned.1.call-done = bf16[384,512]{1,0:T(8,128)(2,1)} async-done(((bf16[3072,512]{1,0:T(8,128)(2,1)}), bf16[384,512]{1,0:T(8,128)(2,1)}) %reduce-scatter.16.cloned.1.call-update) | async-done | bytes 393232 | tf_op jit(solution)/shard_map/reduce_scatter | solution.py:296
  1132.8 67.8 %reduce-scatter.18.cloned.1.call-done = bf16[384,512]{1,0:T(8,128)(2,1)} async-done(((bf16[3072,512]{1,0:T(8,128)(2,1)}), bf16[384,512]{1,0:T(8,128)(2,1)}) %reduce-scatter.18.cloned.1.call-update) | async-done | bytes 393232 | tf_op jit(solution)/shard_map/reduce_scatter | solution.py:302
  1200.6 5.7 add_convert_fusion
  1206.4 4.5 convolution_convert_fusion.4
  1220.0 9.8 convolution_convert_fusion
  1229.9 9.8 convolution_convert_fusion.1
  1239.9 9.9 convert_bitcast_fusion
  1252.3 19.8 pmax.7
  1277.6 24.1 %reduce-scatter.26.cloned.1.call-done = bf16[256,512]{1,0:T(8,128)(2,1)} async-done(((bf16[2048,512]{1,0:T(8,128)(2,1)}), bf16[256,512]{1,0:T(8,128)(2,1)}) %reduce-scatter.26.cloned.1.call-update) | async-done | bytes 262160 | tf_op jit(solution)/shard_map/reduce_scatter | solution.py:344
  1305.5 40.4 %all-reduce.8.cloned.1.call-done = bf16[384,2048]{1,0:T(8,128)(2,1)} async-done(((bf16[384,2048]{1,0:T(8,128)(2,1)}), bf16[384,2048]{1,0:T(8,128)(2,1)}) %all-reduce.8.cloned.1.call-update) | async-done | bytes 1572880 | tf_op jit(solution)/shard_map/psum | solution.py:328
  1345.9 5.5 fusion.30
  1351.4 22.2 %all-reduce.2 = (bf16[2048]{0:T(1024)(128)(2,1)S(1)}, bf16[2048]{0:T(1024)(128)(2,1)S(1)}) all-reduce(bf16[2048]{0:T(1024)(128)(2,1)S(1)} %get-tuple-element.279, bf16[2048]{0:T(1024)(128)(2,1)S(1)} %copy-done.30), channel_id=13, replica_groups=mesh['wide'=8,'narrow'=4] {'wide'}, use_global_device_ids=true, to_apply=%region_33.34.clone | all-reduce | flops 4096 | bytes 16384
  1377.3 40.3 %reduce-scatter.22.cloned.1.call-done = bf16[256,512]{1,0:T(8,128)(2,1)} async-done(((bf16[2048,512]{1,0:T(8,128)(2,1)}), bf16[256,512]{1,0:T(8,128)(2,1)}) %reduce-scatter.22.cloned.1.call-update) | async-done | bytes 262160 | tf_op jit(solution)/shard_map/reduce_scatter | solution.py:338
  1419.4 69.2 %reduce-scatter.20.cloned.1.call-done = bf16[256,512]{1,0:T(8,128)(2,1)} async-done(((bf16[2048,512]{1,0:T(8,128)(2,1)}), bf16[256,512]{1,0:T(8,128)(2,1)}) %reduce-scatter.20.cloned.1.call-update) | async-done | bytes 262160 | tf_op jit(solution)/shard_map/reduce_scatter | solution.py:335
  1490.4 69.2 %reduce-scatter.24.cloned.1.call-done = bf16[256,512]{1,0:T(8,128)(2,1)} async-done(((bf16[2048,512]{1,0:T(8,128)(2,1)}), bf16[256,512]{1,0:T(8,128)(2,1)}) %reduce-scatter.24.cloned.1.call-update) | async-done | bytes 262160 | tf_op jit(solution)/shard_map/reduce_scatter | solution.py:341
  1561.4 149.8 %reduce-scatter.30.cloned.1.call-done = bf16[256,2048]{1,0:T(8,128)(2,1)} async-done(((bf16[2048,2048]{1,0:T(8,128)(2,1)}), bf16[256,2048]{1,0:T(8,128)(2,1)}) %reduce-scatter.30.cloned.1.call-update) | async-done | bytes 1048592 | tf_op jit(solution)/shard_map/reduce_scatter | solution.py:353
  1714.0 149.2 %reduce-scatter.28.cloned.1.call-done = bf16[256,2048]{1,0:T(8,128)(2,1)} async-done(((bf16[2048,2048]{1,0:T(8,128)(2,1)}), bf16[256,2048]{1,0:T(8,128)(2,1)}) %reduce-scatter.28.cloned.1.call-update) | async-done | bytes 1048592 | tf_op jit(solution)/shard_map/reduce_scatter | solution.py:350
  1866.0 149.3 %reduce-scatter.32.cloned.1.call-done = bf16[256,2048]{0,1:T(8,128)(2,1)} async-done(((bf16[2048,2048]{0,1:T(8,128)(2,1)}), bf16[256,2048]{0,1:T(8,128)(2,1)}) %reduce-scatter.32.cloned.1.call-update) | async-done | bytes 1048592 | tf_op jit(solution)/shard_map/reduce_scatter | solution.py:356
  (334 shorter events, 224.6 us)
Async XLA Ops:
  7.2 31.0 %all-gather.15.cloned.1.call-start = ((), (), s32[]{:S(2)}) async-start(), calls=%async_computation.11 | async-start | bytes 1966080 | tf_op jit(solution)/shard_map/all_gather | solution.py:138
  7.9 75.5 %all-gather.21.cloned.1.call-start = ((), (), s32[]{:S(2)}) async-start(), calls=%async_computation.14 | async-start | bytes 2359296 | tf_op jit(solution)/shard_map/all_gather | solution.py:142
  8.7 124.7 %all-gather.23.cloned.1.call-start = ((), (), s32[]{:S(2)}) async-start(), calls=%async_computation.15 | async-start | bytes 2359296 | tf_op jit(solution)/shard_map/all_gather | solution.py:143
  9.4 173.8 %all-gather.17.cloned.1.call-start = ((), (), s32[]{:S(2)}) async-start(), calls=%async_computation.12 | async-start | bytes 2359296 | tf_op jit(solution)/shard_map/all_gather | solution.py:144
  10.0 237.3 %all-gather.25.cloned.1.call-start = ((), (), s32[]{:S(2)}) async-start(), calls=%async_computation.16 | async-start | bytes 3538944 | tf_op jit(solution)/shard_map/all_gather | solution.py:166
  34.7 148.4 %copy-start.24 = (f32[8,1,256]{2,1,0:T(1,128)}, f32[8,1,256]{2,1,0:T(1,128)S(1)}, u32[]{:S(2)}) copy-start(f32[8,1,256]{2,1,0:T(1,128)S(1)} %convert_element_type.249) | copy-start | bytes 24580
  38.2 98.2 %copy-start.17 = (f32[384,32]{0,1:T(8,128)}, f32[384,32]{0,1:T(8,128)S(1)}, u32[]{:S(2)}) copy-start(f32[384,32]{0,1:T(8,128)S(1)} %get-tuple-element.341) | copy-start | bytes 147460
  38.2 98.2 %copy-start.19 = (f32[384,32]{0,1:T(8,128)}, f32[384,32]{0,1:T(8,128)S(1)}, u32[]{:S(2)}) copy-start(f32[384,32]{0,1:T(8,128)S(1)} %get-tuple-element.342) | copy-start | bytes 147460
  40.0 93.4 %copy-start.6 = (bf16[384,2048]{1,0:T(8,128)(2,1)S(1)}, bf16[384,2048]{1,0:T(8,128)(2,1)}, u32[]{:S(2)}) copy-start(bf16[384,2048]{1,0:T(8,128)(2,1)} %all-gather.15.cloned.1.call-done) | copy-start | bytes 4718596
  40.0 143.2 %copy-start.26 = (f32[384]{0:T(512)}, f32[384]{0:T(512)S(1)}, u32[]{:S(2)}) copy-start(f32[384]{0:T(512)S(1)} %add_rsqrt_fusion.1) | copy-start | bytes 4612
  137.4 50.3 %copy-start.21 = (s32[3072]{0:T(1024)S(1)}, s32[3072]{0:T(1024)}, u32[]{:S(2)}) copy-start(s32[3072]{0:T(1024)} %param.26) | copy-start | bytes 36868
  137.4 171.1 %all-gather.19.cloned.1.call-start = ((), (), s32[]{:S(2)}) async-start(), calls=%async_computation.13 | async-start | bytes 3538944 | tf_op jit(solution)/shard_map/all_gather | solution.py:167
  186.6 173.7 %all-gather.27.cloned.1.call-start = ((), (), s32[]{:S(2)}) async-start(), calls=%async_computation.17 | async-start | bytes 2359296 | tf_op jit(solution)/shard_map/all_gather | solution.py:146
  187.3 203.2 %reduce-scatter.12.cloned.1.call-start = ((), (), s32[]{:S(2)}) async-start(), calls=%async_computation.18 | async-start | bytes 1966080 | tf_op jit(solution)/shard_map/reduce_scatter | solution.py:200
  331.3 61.1 %copy-start.14 = (bf16[384,8,64]{0,2,1:T(8,128)(2,1)}, bf16[384,8,64]{0,2,1:T(8,128)(2,1)S(1)}, u32[]{:S(2)}) copy-start(bf16[384,8,64]{0,2,1:T(8,128)(2,1)S(1)} %get-tuple-element.349) | copy-start | bytes 1179652
  331.3 59.3 %copy-start.9 = (bf16[384,512]{1,0:T(8,128)(2,1)S(1)}, bf16[384,512]{1,0:T(8,128)(2,1)}, u32[]{:S(2)}) copy-start(bf16[384,512]{1,0:T(8,128)(2,1)} %param.15) | copy-start | bytes 1179652
  364.0 31.1 %copy-start.35 = (bf16[256]{0:T(256)(128)(2,1)S(1)}, bf16[256]{0:T(256)(128)(2,1)}, u32[]{:S(2)}) copy-start(bf16[256]{0:T(256)(128)(2,1)} %param.21) | copy-start | bytes 1540
  364.1 52.2 %all-gather.29.cloned.1.call-start = ((), (), s32[]{:S(2)}) async-start(), calls=%async_computation.19 | async-start | bytes 1966080 | tf_op jit(solution)/shard_map/all_gather | solution.py:207
  392.4 147.2 %all-gather.33.cloned.1.call-start = ((), (), s32[]{:S(2)}) async-start(), calls=%async_computation.21 | async-start | bytes 9437184 | tf_op jit(solution)/shard_map/all_gather | solution.py:148
  393.0 272.1 %all-gather.31.cloned.1.call-start = ((), (), s32[]{:S(2)}) async-start(), calls=%async_computation.20 | async-start | bytes 9437184 | tf_op jit(solution)/shard_map/all_gather | solution.py:147
  393.8 290.8 %all-gather.37.cloned.1.call-start = ((), (), s32[]{:S(2)}) async-start(), calls=%async_computation.24 | async-start | bytes 1966080 | tf_op jit(solution)/shard_map/all_gather | solution.py:139
  394.4 417.9 %all-gather.35.cloned.1.call-start = ((), (), s32[]{:S(2)}) async-start(), calls=%async_computation.22 | async-start | bytes 9437184 | tf_op jit(solution)/shard_map/all_gather | solution.py:150
  395.1 484.0 %all-reduce.6.cloned.1.call-start = ((), (), s32[]{:S(2)}) async-start(), calls=%async_computation.25 | async-start | bytes 3145728 | tf_op jit(solution)/shard_map/psum | solution.py:231
  416.2 249.0 %copy-start.22 = (f32[8,1,256]{2,1,0:T(1,128)}, f32[8,1,256]{2,1,0:T(1,128)S(1)}, u32[]{:S(2)}) copy-start(f32[8,1,256]{2,1,0:T(1,128)S(1)} %convert_element_type.250) | copy-start | bytes 24580
  418.1 247.1 %copy-start.28 = (f32[384]{0:T(512)}, f32[384]{0:T(512)S(1)}, u32[]{:S(2)}) copy-start(f32[384]{0:T(512)S(1)} %add_rsqrt_fusion) | copy-start | bytes 4612
  539.7 125.5 %copy-start.4 = (bf16[384,2048]{1,0:T(8,128)(2,1)S(1)}, bf16[384,2048]{1,0:T(8,128)(2,1)}, u32[]{:S(2)}) copy-start(bf16[384,2048]{1,0:T(8,128)(2,1)} %all-gather.29.cloned.1.call-done) | copy-start | bytes 4718596
  812.2 11.9 copy-start.34
  837.9 285.4 %reduce-scatter.16.cloned.1.call-start = ((), (), s32[]{:S(2)}) async-start(), calls=%async_computation.26 | async-start | bytes 3538944 | tf_op jit(solution)/shard_map/reduce_scatter | solution.py:296
  922.1 5.1 copy-start
  1001.1 5.1 copy-start
  1048.7 151.9 %reduce-scatter.18.cloned.1.call-start = ((), (), s32[]{:S(2)}) async-start(), calls=%async_computation.27 | async-start | bytes 3538944 | tf_op jit(solution)/shard_map/reduce_scatter | solution.py:302
  1049.3 226.2 %reduce-scatter.14.cloned.1.call-start = ((), (), s32[]{:S(2)}) async-start(), calls=%async_computation.23 | async-start | bytes 1966080 | tf_op jit(solution)/shard_map/reduce_scatter | solution.py:215
  1049.6 8.7 copy-start.3
  1049.6 8.7 copy-start.15
  1058.2 243.4 %reduce-scatter.26.cloned.1.call-start = ((), (), s32[]{:S(2)}) async-start(), calls=%async_computation.32 | async-start | bytes 2359296 | tf_op jit(solution)/shard_map/reduce_scatter | solution.py:344
  1061.0 64.4 %copy-start.18 = (f32[384,32]{0,1:T(8,128)S(1)}, f32[384,32]{0,1:T(8,128)}, u32[]{:S(2)}) copy-start(f32[384,32]{0,1:T(8,128)} %copy-done.17) | copy-start | bytes 147460
  1061.0 64.4 %copy-start.20 = (f32[384,32]{0,1:T(8,128)S(1)}, f32[384,32]{0,1:T(8,128)}, u32[]{:S(2)}) copy-start(f32[384,32]{0,1:T(8,128)} %copy-done.19) | copy-start | bytes 147460
  1061.0 284.9 %all-reduce.8.cloned.1.call-start = ((), (), s32[]{:S(2)}) async-start(), calls=%async_computation.28 | async-start | bytes 3145728 | tf_op jit(solution)/shard_map/psum | solution.py:328
  1132.8 73.6 %copy-start.25 = (f32[8,1,256]{2,1,0:T(1,128)S(1)}, f32[8,1,256]{2,1,0:T(1,128)}, u32[]{:S(2)}) copy-start(f32[8,1,256]{2,1,0:T(1,128)} %copy-done.24) | copy-start | bytes 24580
  1132.8 73.6 %copy-start.27 = (f32[384]{0:T(512)S(1)}, f32[384]{0:T(512)}, u32[]{:S(2)}) copy-start(f32[384]{0:T(512)} %copy-done.26) | copy-start | bytes 4612
  1206.4 211.2 %reduce-scatter.22.cloned.1.call-start = ((), (), s32[]{:S(2)}) async-start(), calls=%async_computation.30 | async-start | bytes 2359296 | tf_op jit(solution)/shard_map/reduce_scatter | solution.py:338
  1210.9 277.6 %reduce-scatter.20.cloned.1.call-start = ((), (), s32[]{:S(2)}) async-start(), calls=%async_computation.29 | async-start | bytes 2359296 | tf_op jit(solution)/shard_map/reduce_scatter | solution.py:335
  1215.2 344.4 %reduce-scatter.24.cloned.1.call-start = ((), (), s32[]{:S(2)}) async-start(), calls=%async_computation.31 | async-start | bytes 2359296 | tf_op jit(solution)/shard_map/reduce_scatter | solution.py:341
  1219.5 491.7 %reduce-scatter.30.cloned.1.call-start = ((), (), s32[]{:S(2)}) async-start(), calls=%async_computation.34 | async-start | bytes 9437184 | tf_op jit(solution)/shard_map/reduce_scatter | solution.py:353
  1229.8 633.4 %reduce-scatter.28.cloned.1.call-start = ((), (), s32[]{:S(2)}) async-start(), calls=%async_computation.33 | async-start | bytes 9437184 | tf_op jit(solution)/shard_map/reduce_scatter | solution.py:350
  1239.7 775.6 %reduce-scatter.32.cloned.1.call-start = ((), (), s32[]{:S(2)}) async-start(), calls=%async_computation.35 | async-start | bytes 9437184 | tf_op jit(solution)/shard_map/reduce_scatter | solution.py:356
  1249.8 25.7 %copy-start.10 = (bf16[384,512]{1,0:T(8,128)(2,1)S(1)}, bf16[384,512]{1,0:T(8,128)(2,1)}, u32[]{:S(2)}) copy-start(bf16[384,512]{1,0:T(8,128)(2,1)} %param.15) | copy-start | bytes 1179652
  1305.5 45.9 %copy-start.30 = (bf16[2048]{0:T(1024)(128)(2,1)S(1)}, bf16[2048]{0:T(1024)(128)(2,1)}, u32[]{:S(2)}) copy-start(bf16[2048]{0:T(1024)(128)(2,1)} %get-tuple-element.277) | copy-start | bytes 12292
  (41 other events, 117.7 us)
Sparse Core Ops, SparseCore 0:
  9.6 22.3 all-gather.14
  34.1 49.3 all-gather.20
  85.6 47.7 all-gather.22
  135.4 47.7 all-gather.16
  185.7 61.5 all-gather.24
  249.9 58.6 all-gather.18
  310.6 49.6 all-gather.26
  364.2 26.3 reduce-scatter.11
  392.8 19.6 all-gather.28
  414.7 124.9 all-gather.32
  542.0 123.1 all-gather.30
  666.7 17.8 all-gather.36
  686.8 125.3 all-gather.34
  838.1 41.0 all-reduce.5
  1048.9 74.4 reduce-scatter.15
  1127.2 73.3 reduce-scatter.17
  1203.2 27.2 reduce-scatter.13
  1233.9 67.7 reduce-scatter.25
  1304.0 41.8 all-reduce.7
  1349.9 67.6 reduce-scatter.21
  1421.7 66.8 reduce-scatter.19
  1492.7 66.8 reduce-scatter.23
  1563.2 147.9 reduce-scatter.29
  1715.2 148.0 reduce-scatter.27
  1866.9 148.3 reduce-scatter.31
where the time goes:
time: 2030 us; the launch traced here: 2020 us
  waiting for transfers between devices  1520 us (75%)
  matrix products  243 us (12%)
  blocking collectives  85.3 us (4%)
  local copies, waits for them, and re-layouts  78.2 us (4%)
  other arithmetic  78 us (4%)
    reduce_scatter x1, waiting for transfers between devices, on_device(): lax.psum_scatter(grad_up_t.astype(jnp.bfloat16), 'wide', scatter_dimensio...  150 us
    reduce_scatter x1, waiting for transfers between devices, on_device(): lax.psum_scatter(grad_down_t.astype(jnp.bfloat16), 'wide', scatter_dimens...  149 us
    reduce_scatter x1, waiting for transfers between devices, on_device(): lax.psum_scatter(grad_gate_t.astype(jnp.bfloat16), 'wide', scatter_dimens...  149 us
    all_gather x1, waiting for transfers between devices, on_device(): lax.all_gather(w_down, 'wide', axis=1, tiled=True)  128 us
    all_gather x1, waiting for transfers between devices, on_device(): lax.all_gather(w_up, 'wide', axis=0, tiled=True)  122 us
    all_gather x1, waiting for transfers between devices, on_device(): lax.all_gather(w_gate, 'wide', axis=0, tiled=True)  116 us
    reduce_scatter x1, waiting for transfers between devices, on_device(): lax.psum_scatter(grad_wv_t.astype(jnp.bfloat16), 'wide', scatter_dimensio...  69.2 us
    reduce_scatter x1, waiting for transfers between devices, on_device(): lax.psum_scatter(grad_wq_t.astype(jnp.bfloat16), 'wide', scatter_dimensio...  69.2 us
  transfers between devices with their start and end apart: 25, of which 22 were waited for; matrix products, arithmetic and copies ran while one was open for 10% of the time, Pallas kernels for 0%

commit v1 on v0

v1 whole, which is shorter than its diff:
```python
import functools

import jax
import jax.numpy as jnp
from jax import lax
from jax.experimental import pallas as pl
from jax.experimental.pallas import tpu as pltpu
from jax.sharding import Mesh
from jax.sharding import PartitionSpec as P

HDIM = 64
HALF = HDIM // 2

eps_norm = 1e-05
rope_base = 130000.0
clip_limit = 5.0
masked_fill = -1e30

F32 = jnp.float32
BF16 = jnp.bfloat16
WIDE = ("z", "q", "y")
GROUP = ("q", "y")
NARROW = ("x", "c")
VMEM_BYTES = 48 * 2**20
EXTRA = 16


def lookup(lookup_table, indices):
    labels = jnp.arange(lookup_table.shape[0], dtype=jnp.int32)
    return jnp.sum(
        jnp.where(indices[:, None] == labels[None, :], lookup_table[None, :], 0),
        axis=1,
        dtype=jnp.int32,
    )


def segment_tables(segment_ids, parents):
    labels = jnp.arange(parents.shape[0], dtype=jnp.int32)
    counts = jnp.sum(
        (segment_ids[:, None] == labels[None, :]).astype(jnp.int32), axis=0, dtype=jnp.int32
    )
    starts = jnp.sum(
        jnp.where(labels[None, :] < labels[:, None], counts[None, :], 0), axis=1, dtype=jnp.int32
    )
    ancestor = lookup(parents, parents)
    parent_len = jnp.where(parents != labels, lookup(counts, parents), 0)
    ancestor_len = jnp.where(ancestor != parents, lookup(counts, ancestor), 0)
    return (ancestor, starts, parent_len, ancestor_len)


def dot(left, right, left_dim, right_dim):
    return lax.dot_general(
        left, right, (((left_dim,), (right_dim,)), ((), ())), preferred_element_type=F32
    )


def take(array, index, axis=0):
    return lax.dynamic_index_in_dim(array, index, axis, keepdims=False)


def swap(array, axis):
    return lax.ppermute(array, axis, [(0, 1), (1, 0)])


def ring(array, size):
    return lax.ppermute(array, "z", [(i, (i + 1) % size) for i in range(size)])


def pick(flag, first, second):
    return jnp.where(flag == 0, first, second)


def in_order(flag, own, theirs, axis=0):
    return jnp.stack([pick(flag, own, theirs), pick(flag, theirs, own)], axis=axis)


def params():
    return pltpu.CompilerParams(vmem_limit_bytes=VMEM_BYTES)


def shape(dims, dtype):
    return jax.ShapeDtypeStruct(dims, dtype)


def full(dims):
    return pl.BlockSpec(dims, lambda *_: (0,) * len(dims))


def columns_of(where, k, cols):
    return pl.ds(pl.multiple_of((where[0] ^ k) * cols, cols), cols)


def fill_keys(keys, mask, k_ext, values_t):
    for t in range(keys.shape[0]):
        tile = keys[t].astype(F32)
        spare = k_ext.shape[2] - HDIM - mask.shape[1]
        parts = [tile[HDIM : 2 * HDIM], mask[t].astype(F32)]
        parts.append(jnp.zeros((spare, tile.shape[1]), F32))
        k_ext[t] = jnp.concatenate(parts, axis=0).T.astype(BF16)
        if values_t is not None:
            values_t[t] = jnp.concatenate(
                [tile[2 * HDIM :], jnp.zeros((HDIM, tile.shape[1]), F32)], axis=0
            ).T.astype(BF16)


def query_ext(queries, mask, depth):
    q = queries[0, :HDIM]
    spare = depth - HDIM - mask.shape[1]
    return jnp.concatenate([q, mask[0], jnp.zeros((spare, q.shape[1]), BF16)], axis=0)


def attend_kernel(
    visible, counts, q_pos, k_pos, queries, q_mask, keys, k_mask, low, out, log_norm, peak, k_ext
):
    i = pl.program_id(0)
    tiles, _, width = keys.shape

    @pl.when(i == 0)
    def _():
        fill_keys(keys, k_mask, k_ext, None)

    q_tile = query_ext(queries, q_mask, k_ext.shape[2])
    relative = lax.broadcasted_iota(jnp.int32, (width, width), 0) - lax.broadcasted_iota(
        jnp.int32, (width, width), 1
    )

    def step(n, carry):
        high, total, acc = carry
        j = visible[i * tiles + n]
        scores = dot(k_ext[j], q_tile, 1, 0)
        scores = jnp.where(relative <= (q_pos[i] - k_pos[j]) * width, scores, masked_fill)
        new_high = jnp.maximum(high, jnp.max(scores, axis=0, keepdims=True))
        weights = jnp.exp(scores - new_high)
        shrink = jnp.exp(high - new_high)
        total = total * shrink + jnp.sum(weights, axis=0, keepdims=True)
        acc = acc * shrink + dot(keys[j, 2 * HDIM :], weights.astype(BF16), 1, 0)
        return new_high, total, acc

    high, total, acc = lax.fori_loop(
        0,
        counts[i],
        step,
        (
            jnp.full((1, width), masked_fill, F32),
            jnp.zeros((1, width), F32),
            jnp.zeros((HDIM, width), F32),
        ),
    )
    result = acc / total
    out[0] = result
    low[0] = result.astype(BF16)
    log_norm[0] = high + jnp.log(total)
    peak[0] = high


def attend(tables, queries, q_mask, keys, k_mask):
    q_tiles, features, width = queries.shape
    k_tiles, labels = keys.shape[0], q_mask.shape[1]
    part = lambda i, *_: (i, 0, 0)
    placed = lambda i, visible, counts, q_pos, k_pos: (q_pos[i + q_tiles], 0, 0)
    return pl.pallas_call(
        attend_kernel,
        grid_spec=pltpu.PrefetchScalarGridSpec(
            num_scalar_prefetch=4,
            grid=(q_tiles,),
            in_specs=[
                pl.BlockSpec((1, features, width), part),
                pl.BlockSpec((1, labels, width), part),
                full(keys.shape),
                full(k_mask.shape),
            ],
            out_specs=[
                pl.BlockSpec((1, HDIM, width), placed),
                pl.BlockSpec((1, HDIM, width), part),
                pl.BlockSpec((1, 1, width), part),
                pl.BlockSpec((1, 1, width), part),
            ],
            scratch_shapes=[pltpu.VMEM((k_tiles, width, 2 * HDIM), BF16)],
        ),
        out_shape=[
            shape((q_tiles, HDIM, width), BF16),
            shape((q_tiles, HDIM, width), F32),
            shape((q_tiles, 1, width), F32),
            shape((q_tiles, 1, width), F32),
        ],
        compiler_params=params(),
        cost_estimate=pl.CostEstimate(
            flops=q_tiles * k_tiles * width * width * 3 * HDIM,
            bytes_accessed=(q_tiles + k_tiles) * width * 8 * HDIM,
            transcendentals=q_tiles * k_tiles * width * width // 2,
        ),
        name="attend",
    )(*tables, queries, q_mask, keys, k_mask)


def attend_back_kernel(
    visible,
    counts,
    q_pos,
    k_pos,
    queries,
    q_mask,
    keys,
    k_mask,
    grads,
    out,
    log_norm,
    cosine,
    sine,
    grad_q,
    grad_kv,
    k_ext,
    values_t,
    acc_k,
    acc_v,
):
    i = pl.program_id(0)
    tiles, _, width = keys.shape

    @pl.when(i == 0)
    def _():
        fill_keys(keys, k_mask, k_ext, values_t)
        acc_k[...] = jnp.zeros_like(acc_k)
        acc_v[...] = jnp.zeros_like(acc_v)

    q_tile = query_ext(queries, q_mask, k_ext.shape[2])
    q_rows = q_tile[:HDIM]
    g_tile = grads[0]
    g_ext = jnp.concatenate([g_tile, jnp.zeros_like(g_tile)], axis=0)
    lse = log_norm[0]
    delta = jnp.sum(g_tile.astype(F32) * out[0], axis=0, keepdims=True)
    relative = lax.broadcasted_iota(jnp.int32, (width, width), 0) - lax.broadcasted_iota(
        jnp.int32, (width, width), 1
    )

    def step(n, acc):
        j = visible[i * tiles + n]
        scores = dot(k_ext[j], q_tile, 1, 0)
        scores = jnp.where(relative <= (q_pos[i] - k_pos[j]) * width, scores, masked_fill)
        probs = jnp.exp(scores - lse)
        grad_probs = dot(values_t[j], g_ext, 1, 0)
        grad_scores = (probs * (grad_probs - delta)).astype(BF16)
        acc_v[j] += dot(g_tile, probs.astype(BF16), 1, 1)
        acc_k[j] += dot(q_rows, grad_scores, 1, 1)
        return acc + dot(keys[j, HDIM : 2 * HDIM], grad_scores, 1, 0)

    acc = lax.fori_loop(0, counts[i], step, jnp.zeros((HDIM, width), F32))

    def unrotate(grad, t):
        first, second, c, s = grad[:HALF], grad[HALF:], cosine[t], sine[t]
        return first * c + second * s, second * c - first * s

    mine = q_pos[pl.num_programs(0) * 2]
    first, second = unrotate(acc * HDIM ** (-0.5), mine + i)
    grad_q[0, :HALF] = first.astype(BF16)
    grad_q[0, HALF:] = second.astype(BF16)

    @pl.when(i == pl.num_programs(0) - 1)
    def _():
        for t in range(tiles):
            first, second = unrotate(acc_k[t], t)
            grad_kv[t, :HALF] = first.astype(BF16)
            grad_kv[t, HALF:HDIM] = second.astype(BF16)
            grad_kv[t, HDIM:] = acc_v[t].astype(BF16)


def attend_back(tables, queries, q_mask, keys, k_mask, grads, out, log_norm, cosine, sine):
    q_tiles, features, width = queries.shape
    k_tiles, labels = keys.shape[0], q_mask.shape[1]
    part = lambda i, *_: (i, 0, 0)
    placed = lambda i, visible, counts, q_pos, k_pos: (q_pos[i + q_tiles], 0, 0)
    return pl.pallas_call(
        attend_back_kernel,
        grid_spec=pltpu.PrefetchScalarGridSpec(
            num_scalar_prefetch=4,
            grid=(q_tiles,),
            in_specs=[
                pl.BlockSpec((1, features, width), part),
                pl.BlockSpec((1, labels, width), part),
                full(keys.shape),
                full(k_mask.shape),
                pl.BlockSpec((1, HDIM, width), placed),
                pl.BlockSpec((1, HDIM, width), part),
                pl.BlockSpec((1, 1, width), part),
                full(cosine.shape),
                full(sine.shape),
            ],
            out_specs=[
                pl.BlockSpec((1, HDIM, width), part),
                full((k_tiles, 2 * HDIM, width)),
            ],
            scratch_shapes=[
                pltpu.VMEM((k_tiles, width, 2 * HDIM), BF16),
                pltpu.VMEM((k_tiles, width, 2 * HDIM), BF16),
                pltpu.VMEM((k_tiles, HDIM, width), F32),
                pltpu.VMEM((k_tiles, HDIM, width), F32),
            ],
        ),
        out_shape=[
            shape((q_tiles, HDIM, width), BF16),
            shape((k_tiles, 2 * HDIM, width), BF16),
        ],
        compiler_params=params(),
        cost_estimate=pl.CostEstimate(
            flops=q_tiles * k_tiles * width * width * 6 * HDIM,
            bytes_accessed=(q_tiles + k_tiles) * width * 16 * HDIM,
            transcendentals=q_tiles * k_tiles * width * width // 2,
        ),
        name="attend_back",
    )(*tables, queries, q_mask, keys, k_mask, grads, out, log_norm, cosine, sine)


def row_scale(pieces, width):
    squares = 0.0
    for piece in pieces:
        values = piece[...].astype(F32)
        squares = squares + jnp.sum(values * values, axis=1, keepdims=True)
    return lax.rsqrt(squares / width + eps_norm)


def qkv_kernel(where, *refs):
    pieces, (gain, weights, cosine, sine) = refs[:4], refs[4:8]
    normed, mine, other, scale = refs[-4:]
    rows, cols = pieces[0].shape
    rstd = row_scale(pieces, 4 * cols)
    scale[...] = rstd
    for k, piece in enumerate(pieces):
        span = columns_of(where, k, cols)
        normed[:, span] = (piece[...].astype(F32) * rstd * gain[:, span]).astype(BF16)
    c, s = cosine[...], sine[...]
    features = 3 * HDIM
    for head, out in enumerate((mine, other)):
        lin = dot(weights[head * features : (head + 1) * features, :], normed[...], 1, 1)
        for part, factor in ((0, HDIM ** (-0.5)), (1, 1.0)):
            base = part * HDIM
            first, second = lin[base : base + HALF], lin[base + HALF : base + HDIM]
            out[base : base + HALF] = ((first * c - second * s) * factor).astype(BF16)
            out[base + HALF : base + HDIM] = ((second * c + first * s) * factor).astype(BF16)
        out[2 * HDIM :] = lin[2 * HDIM :].astype(BF16)


def chunk_call(kernel, name, where, inputs, buffers, whole_shapes, out_shapes, cost):
    rows = whole_shapes[0][0] // 4
    in_specs = [full(a.shape) for a in inputs]
    aliases = {}
    extra = []
    if buffers is not None:
        for n, buffer in enumerate(buffers):
            aliases[1 + len(inputs) + n] = n
            in_specs.append(pl.BlockSpec(memory_space=pl.ANY))
            extra.append(buffer)
    chunk = lambda i, where: (where[1], 0)
    out_specs = [pl.BlockSpec((rows, dims[1]), chunk) for dims in whole_shapes]
    out_specs += [full(s.shape) for s in out_shapes]
    return pl.pallas_call(
        kernel,
        grid_spec=pltpu.PrefetchScalarGridSpec(
            num_scalar_prefetch=1, grid=(1,), in_specs=in_specs, out_specs=out_specs
        ),
        out_shape=[shape(dims, BF16) for dims in whole_shapes] + list(out_shapes),
        input_output_aliases=aliases,
        compiler_params=params(),
        cost_estimate=pl.CostEstimate(flops=cost, bytes_accessed=2**23, transcendentals=2**18),
        name=name,
    )(where, *inputs, *extra)


def ffn_kernel(where, *refs):
    mids, cots, (gain, w_gate, w_up, w_down) = refs[:4], refs[4:8], refs[8:12]
    (normed, cot_rows, hidden, grad_gate, grad_up) = refs[-11:-6]
    (keep_out, send_out, keep_back, send_back, gain_term, scale) = refs[-6:]
    rows, cols = mids[0].shape
    width, units = w_gate.shape
    rstd = row_scale(mids, width)
    scale[...] = rstd
    for k in range(4):
        span = columns_of(where, k, cols)
        normed[:, span] = (mids[k][...].astype(F32) * rstd * gain[:, span]).astype(BF16)
        cot_rows[:, span] = cots[k][...]
    step = 256
    for n in range(0, units, step):
        gate = dot(normed[...], w_gate[:, n : n + step], 1, 0)
        up = dot(normed[...], w_up[:, n : n + step], 1, 0)
        grad_hidden = dot(cot_rows[...], w_down[n : n + step, :], 1, 1)
        sigmoid = jax.nn.sigmoid(gate)
        activated = gate * sigmoid
        hidden[:, n : n + step] = (activated * up).astype(BF16)
        grad_gate[:, n : n + step] = (
            grad_hidden * up * sigmoid * (1.0 + gate * (1.0 - sigmoid))
        ).astype(BF16)
        grad_up[:, n : n + step] = (grad_hidden * activated).astype(BF16)
    row_term = 0.0
    for k in range(4):
        span = columns_of(where, k, cols)
        out, back = ((keep_out, keep_back), (send_out, send_back))[k % 2]
        out[k // 2] = dot(hidden[...], w_down[:, span], 1, 0).astype(BF16)
        partial = dot(grad_gate[...], w_gate[span, :], 1, 1)
        partial = partial + dot(grad_up[...], w_up[span, :], 1, 1)
        back[k // 2, :rows] = partial.astype(BF16)
        terms = partial * (mids[k][...].astype(F32) * rstd)
        gain_term[:, span] = jnp.sum(terms, axis=0, keepdims=True)
        row_term = row_term + jnp.sum(terms * gain[:, span], axis=1, keepdims=True)
    put_row_term(row_term, cols, keep_back, send_back)


def put_row_term(row_term, cols, keep, send):
    rows = row_term.shape[0]
    line = jnp.broadcast_to(row_term, (rows, 128)).T[:EXTRA]
    line = jnp.concatenate([line, jnp.zeros((EXTRA, cols - rows), F32)], axis=1).astype(BF16)
    for ref in (keep, send):
        ref[0, rows:] = line
        ref[1, rows:] = line


def qkv_back_kernel(where, *refs):
    pieces, (scale, gain, weights, mine, other) = refs[:4], refs[4:9]
    keep, send, gain_term = refs[-3:]
    rows, cols = pieces[0].shape
    rstd = scale[...]
    features = 3 * HDIM
    row_term = 0.0
    for k in range(4):
        span = columns_of(where, k, cols)
        back = (keep, send)[k % 2]
        partial = dot(mine[...], weights[:features, span], 0, 0)
        partial = partial + dot(other[...], weights[features:, span], 0, 0)
        back[k // 2, :rows] = partial.astype(BF16)
        terms = partial * (pieces[k][...].astype(F32) * rstd)
        gain_term[:, span] = jnp.sum(terms, axis=0, keepdims=True)
        row_term = row_term + jnp.sum(terms * gain[:, span], axis=1, keepdims=True)
    put_row_term(row_term, cols, keep, send)


def project_kernel(where, attended, weights, keep, send):
    cols = keep.shape[2]
    for k in range(4):
        span = columns_of(where, k, cols)
        (keep, send)[k % 2][k // 2] = dot(attended[...], weights[:, span], 0, 0).astype(BF16)


def project_back_kernel(where, p0, p1, p2, p3, attended, weights, grad_att, grad_weights):
    cols = p0.shape[1]
    total = 0.0
    for k, piece in enumerate((p0, p1, p2, p3)):
        span = columns_of(where, k, cols)
        total = total + dot(weights[:, span], piece[...], 1, 1)
        grad_weights[:, span] = dot(attended[...], piece[...], 1, 0).astype(BF16)
    grad_att[...] = total.astype(BF16)


def small_call(kernel, name, where, inputs, out_shapes, cost):
    return pl.pallas_call(
        kernel,
        grid_spec=pltpu.PrefetchScalarGridSpec(
            num_scalar_prefetch=1,
            grid=(1,),
            in_specs=[full(a.shape) for a in inputs],
            out_specs=[full(s.shape) for s in out_shapes],
        ),
        out_shape=list(out_shapes),
        compiler_params=params(),
        cost_estimate=pl.CostEstimate(flops=cost, bytes_accessed=2**22, transcendentals=0),
        name=name,
    )(where, *inputs)


def on_device(
    sizes,
    hidden_in,
    gain_attn,
    w_query,
    w_key,
    w_value,
    w_out,
    gain_ffn,
    w_gate,
    w_up,
    w_down,
    cotangent,
    segment_ids,
    parents,
):
    nz, nq, ny, nx, nc = sizes
    rows, cols = hidden_in.shape
    groups = nq * ny
    group_rows = nz * rows
    width = cols * nx * nc
    slab = gain_attn.shape[0]
    head = 3 * HDIM
    units = w_gate.shape[1] // nz

    zi, qi, yi, xi, ci = [lax.axis_index(a) for a in ("z", "q", "y", "x", "c")]
    group = qi * ny + yi
    own_columns = xi * nc + ci
    zs = [(zi - s) % nz for s in range(nz)]
    where = [jnp.stack([own_columns, z]).astype(jnp.int32) for z in zs]

    def gather_chunks(block):
        held = [block]
        for _ in range(nz - 1):
            held.append(ring(held[-1], nz))
        chunks = []
        for mine in held:
            other = swap(mine, "x")
            chunks.append([mine, swap(mine, "c"), other, swap(other, "c")])
        return chunks, held[-1]

    def scatter_narrow(keep, send):
        held = keep.astype(F32) + swap(send, "c").astype(F32)
        return held[0] + swap(held[1].astype(BF16), "x").astype(F32)

    def scatter_chunks(parts):
        carried = None
        for s in list(range(1, nz)) + [0]:
            own = scatter_narrow(*parts[s])
            if carried is not None:
                own = own + ring(carried, nz).astype(F32)
            carried = own.astype(BF16)
        return own

    def spread_z(parts):
        return lax.all_to_all(parts, "z", split_axis=0, concat_axis=0, tiled=True)

    def gather_group(parts):
        if nq > 1:
            return lax.all_gather(parts, GROUP, axis=0, tiled=False)
        return in_order(yi, parts, swap(parts, "y"))

    def scatter_groups(parts):
        if nq > 1:
            return lax.psum_scatter(parts, GROUP, scatter_dimension=0, tiled=False)
        return take(parts, yi).astype(F32) + swap(take(parts, 1 - yi), "y").astype(F32)

    def sum_small(values, axes):
        for axis in axes:
            if axis == "z":
                for bit in (1, 2):
                    values = values + lax.ppermute(values, "z", [(i, i ^ bit) for i in range(nz)])
            elif axis == "q":
                values = lax.psum(values, "q") if nq > 1 else values
            else:
                values = values + swap(values, axis)
        return values

    gain_slots = jnp.zeros((nz * groups, 2, slab), F32)
    both_gains = jnp.stack([gain_attn, gain_ffn]).astype(F32)
    gain_slots = lax.dynamic_update_slice(gain_slots, both_gains[None], (zi * groups + group, 0, 0))
    gains = sum_small(gain_slots, ("y", "z", "q")).transpose(1, 0, 2).reshape(2, width)
    gain1, gain2 = gains[:1], gains[1:]

    x_chunks, x_last = gather_chunks(hidden_in)
    stacked = jnp.stack([w_query, w_key, w_value]).reshape(3, slab, nz, ny, HDIM)
    stacked = stacked.transpose(2, 3, 0, 4, 1).reshape(nz, ny * head, slab)
    w_qkv = gather_group(spread_z(stacked))
    w_qkv = w_qkv.transpose(2, 1, 0, 3).reshape(ny, head, width)
    w_qkv = jnp.concatenate([take(w_qkv, yi), take(w_qkv, 1 - yi)], axis=0)

    late = lax.optimization_barrier((w_gate, w_up, w_down, w_out, cotangent, x_last))
    w_gate_, w_up_, w_down_, w_out_, cotangent_ = late[:5]

    def gather_rows(weight):
        got = gather_group(spread_z(weight.reshape(slab, nz, units).transpose(1, 0, 2)))
        return got.transpose(1, 0, 2, 3).reshape(width, units)

    wo = lax.all_gather(w_out_, WIDE, axis=0, tiled=False)
    wo = wo.transpose(1, 0, 2).reshape(w_out.shape[0], width)
    wg, wu = gather_rows(w_gate_), gather_rows(w_up_)
    wd = gather_group(spread_z(w_down_.reshape(nz, units, slab)))
    wd = wd.transpose(2, 1, 0, 3).reshape(units, width)
    cot_chunks, _ = gather_chunks(cotangent_)

    ancestor, starts, parent_len, ancestor_len = segment_tables(segment_ids, parents)
    q_blocks = [(z * nq + qi) * ny + (yi ^ dy) for dy in range(ny) for z in zs]
    k_blocks = [(z * nq + q) * ny + (yi ^ dy) for q in range(nq) for dy in range(ny) for z in zs]
    segments = segment_ids.reshape(-1, rows)
    k_seg = jnp.stack([take(segments, b) for b in k_blocks])
    k_pos = jnp.stack(k_blocks).astype(jnp.int32)
    q_tiles, k_tiles = len(q_blocks), len(k_blocks)
    of_queries = lambda a: lax.dynamic_slice_in_dim(a, qi * q_tiles, q_tiles, 0)
    flat = k_seg.reshape(-1)
    labels = jnp.arange(-(-parents.shape[0] // 16) * 16, dtype=jnp.int32)[None, :, None]
    places = k_pos[:, None] * rows + jnp.arange(rows, dtype=jnp.int32)[None]
    places = places + lookup(parent_len + ancestor_len - starts, flat).reshape(k_tiles, rows)
    k_own = labels == k_seg[:, None]
    q_seen = of_queries(
        k_own
        | (labels == lookup(parents, flat).reshape(k_tiles, 1, rows))
        | (labels == lookup(ancestor, flat).reshape(k_tiles, 1, rows))
    )
    q_mask = jnp.where(q_seen, 0.0, masked_fill).astype(BF16)
    k_mask = k_own.astype(BF16)
    q_pos = of_queries(k_pos)
    shown = jnp.any(jnp.any(q_seen, axis=2)[:, None] & jnp.any(k_own, axis=2)[None], axis=2)
    shown = shown & (k_pos[None, :] <= q_pos[:, None])
    number = jnp.arange(k_tiles, dtype=jnp.int32)
    earlier = number[None, None, :] < number[None, :, None]
    before = jnp.sum((shown[:, None, :] & earlier).astype(jnp.int32), axis=2)
    chosen = shown[:, None, :] & (before[:, None, :] == number[None, :, None])
    visible = jnp.sum(jnp.where(chosen, number[None, None, :], 0), axis=2, dtype=jnp.int32)
    slots = jnp.stack([z * ny + (yi ^ dy) for dy in range(ny) for z in zs]).astype(jnp.int32)
    q_info = jnp.concatenate([q_pos, slots, (qi * q_tiles).reshape(1).astype(jnp.int32)])
    tables = (
        visible.reshape(-1),
        jnp.sum(shown.astype(jnp.int32), axis=1, dtype=jnp.int32),
        q_info,
        k_pos,
    )
    frequency = rope_base ** (-2.0 * jnp.arange(HALF, dtype=F32) / HDIM)
    angles = places.astype(F32)[:, None, :] * frequency[None, :, None]
    cosine, sine = jnp.cos(angles), jnp.sin(angles)
    cos_q, sin_q = of_queries(cosine), of_queries(sine)

    buffers, mine, theirs, scale1 = None, [], [], []
    for s in range(nz):
        inputs = (*x_chunks[s], gain1, w_qkv, cos_q[s], sin_q[s])
        normed1, own, other, scale = chunk_call(
            qkv_kernel,
            "qkv",
            where[s],
            inputs,
            buffers,
            [(group_rows, width)],
            [shape((head, rows), BF16), shape((head, rows), BF16), shape((rows, 1), F32)],
            4 * rows * width * head,
        )
        buffers = [normed1]
        mine.append(own)
        theirs.append(swap(other, "y"))
        scale1.append(scale)
    queries = jnp.stack(mine + theirs)
    keys = queries
    if nq > 1:
        keys = lax.all_gather(queries, "q", axis=0, tiled=True)
    att_low, att, log_norm, peak = attend(tables, queries, q_mask, keys, k_mask)

    att_t = lax.all_to_all(att_low, ("z", "y"), split_axis=0, concat_axis=0, tiled=True)
    att_t = att_t.reshape(nz * ny * HDIM, rows)
    keep, send = small_call(
        project_kernel,
        "project",
        where[0],
        (att_t, wo),
        [shape((2, rows, cols), BF16)] * 2,
        2 * rows * width * att_t.shape[0],
    )
    residual_mid = hidden_in.astype(F32) + scatter_narrow(keep, send)
    mid_block = residual_mid.astype(BF16)
    mid_chunks, _ = gather_chunks(mid_block)

    buffers, out_parts, back_parts, gain2_term = None, [], [], 0.0
    whole = [(group_rows, width)] * 2 + [(group_rows, units)] * 3
    for s in range(nz):
        results = chunk_call(
            ffn_kernel,
            "feed_forward",
            where[s],
            (*mid_chunks[s], *cot_chunks[s], gain2, wg, wu, wd),
            buffers,
            whole,
            [shape((2, rows, cols), BF16)] * 2
            + [shape((2, rows + EXTRA, cols), BF16)] * 2
            + [shape((1, width), F32), shape((rows, 1), F32)],
            12 * rows * width * units,
        )
        buffers = results[:5]
        out_parts.append(results[5:7])
        back_parts.append(results[7:9])
        gain2_term = gain2_term + results[9]
        if s == 0:
            scale2 = results[10]
    normed2, cot_rows, hidden, grad_gate_lin, grad_up_lin = buffers
    summed2 = scatter_chunks(back_parts)
    hidden_out = (residual_mid + scatter_chunks(out_parts)).astype(BF16)

    def norm_back(summed, gain, block, rstd):
        gain = lax.dynamic_slice_in_dim(gain, own_columns * cols, cols, 1)
        mean = summed[rows, :rows].reshape(rows, 1) / width
        return rstd * (summed[:rows] * gain - block.astype(F32) * rstd * mean)

    grad_mid = cotangent.astype(F32) + norm_back(summed2, gain2, mid_block, scale2)
    branch = grad_mid.astype(BF16)
    branch_x = swap(branch, "x")
    pieces = (branch, swap(branch, "c"), branch_x, swap(branch_x, "c"))

    grad_att, wo_back = small_call(
        project_back_kernel,
        "project_back",
        where[0],
        (*pieces, att_t, wo),
        [shape(att_t.shape, BF16), shape(wo.shape, BF16)],
        4 * rows * width * att_t.shape[0],
    )
    grad_att = grad_att.reshape(nz * ny, HDIM, rows)
    grad_att = lax.all_to_all(grad_att, ("z", "y"), split_axis=0, concat_axis=0, tiled=True)
    grad_q, grad_kv = attend_back(
        tables, queries, q_mask, keys, k_mask, grad_att, att, log_norm, cosine, sine
    )
    if nq > 1:
        grad_kv = lax.psum_scatter(grad_kv, "q", scatter_dimension=0, tiled=True)
    back = jnp.concatenate([grad_q, grad_kv], axis=1)
    order = list(range(1, nz)) + [0]
    other_back = {s: swap(back[nz + s], "y") for s in order}
    parts, gain1_term = [None] * nz, 0.0
    for s in order:
        keep, send, term = small_call(
            qkv_back_kernel,
            "qkv_back",
            where[s],
            (*x_chunks[s], scale1[s], gain1, w_qkv, back[s], other_back[s]),
            [shape((2, rows + EXTRA, cols), BF16)] * 2 + [shape((1, width), F32)],
            4 * rows * width * head,
        )
        parts[s] = (keep, send)
        gain1_term = gain1_term + term
    summed1 = scatter_chunks(parts)
    grad_in = (grad_mid + norm_back(summed1, gain1, hidden_in, scale1[0])).astype(BF16)

    def units_back(grad):
        parts = grad.astype(BF16).reshape(nz, groups, slab, units).transpose(1, 0, 2, 3)
        parts = spread_z(scatter_groups(parts).astype(BF16))
        return parts.transpose(1, 0, 2).reshape(slab, nz * units).astype(F32)

    grad_wg = units_back(dot(normed2, grad_gate_lin, 0, 0))
    grad_wu = units_back(dot(normed2, grad_up_lin, 0, 0))
    down = dot(hidden, cot_rows, 0, 0).astype(BF16).reshape(units, nz, groups, slab)
    down = spread_z(scatter_groups(down.transpose(2, 1, 0, 3)).astype(BF16))
    grad_wd = down.reshape(nz * units, slab).astype(F32)
    wo_back = wo_back.reshape(-1, nz * groups, slab).transpose(1, 0, 2)
    grad_wo = lax.psum_scatter(wo_back, WIDE, scatter_dimension=0, tiled=False).astype(F32)

    def absolute(chunks):
        stacked = jnp.stack([chunks[-s % nz] for s in range(nz)])
        return jnp.roll(stacked, zi, axis=0)

    back_own = absolute([back[s] for s in range(nz)])
    back_other = absolute([other_back[s] for s in range(nz)])
    back_abs = jnp.stack([pick(yi, back_own, back_other), pick(yi, back_other, back_own)])
    back_abs = back_abs.transpose(0, 2, 1, 3).reshape(ny * head, group_rows)
    grad_qkv = dot(back_abs, normed1, 1, 0).astype(BF16).reshape(ny * head, nz, groups, slab)
    grad_qkv = spread_z(scatter_groups(grad_qkv.transpose(2, 1, 0, 3)).astype(BF16))
    grad_qkv = grad_qkv.reshape(nz, ny, 3, HDIM, slab).transpose(2, 4, 0, 1, 3)
    grad_qkv = grad_qkv.reshape(3, slab, nz * ny * HDIM).astype(F32)

    terms = jnp.concatenate([gain1_term, gain2_term], axis=0)
    terms = sum_small(terms, ("c", "x", "y", "z", "q"))
    terms = lax.dynamic_slice_in_dim(terms, (zi * groups + group) * slab, slab, 1)

    peak_slots = jnp.zeros((nz * groups,), F32)
    peak_slots = lax.dynamic_update_slice(
        peak_slots, jnp.max(peak).reshape(1), (zi * groups + group,)
    )
    peaks = sum_small(peak_slots, ("y", "z", "q")).reshape(nz, nq, ny)
    head_peaks = jnp.max(peaks, axis=1).reshape(nz * ny)
    factor = jnp.sqrt(clip_limit / jnp.maximum(head_peaks, clip_limit))
    column_factor = jnp.repeat(factor, HDIM)
    return (
        hidden_out,
        grad_in,
        grad_qkv[0],
        grad_qkv[1],
        grad_qkv[2],
        grad_wo,
        grad_wg,
        grad_wu,
        grad_wd,
        terms[0],
        terms[1],
        w_query.astype(F32) * column_factor[None, :],
        w_key.astype(F32) * column_factor[None, :],
        head_peaks,
    )


def solution(mesh):
    wide, narrow = mesh.devices.shape
    sizes = (4, wide // 8, 2, narrow // 2, 2)
    fine = Mesh(mesh.devices.reshape(sizes), ("z", "q", "y", "x", "c"))
    both = P(WIDE, NARROW)
    turned = P(NARROW, WIDE)
    return jax.shard_map(
        functools.partial(on_device, sizes),
        mesh=fine,
        in_specs=(
            both, P(WIDE), both, both, both, turned, P(WIDE), both, both, turned, both, P(), P()
        ),
        out_specs=(
            both, both, both, both, both, turned, both, both, turned,
            P(WIDE), P(WIDE), both, both, P(NARROW),
        ),
        check_vma=False,
    )
```

time: 2030 us -> 764 us (0.38)
  waiting for transfers between devices: 1520 us -> 254 us
  matrix products: 243 us -> 24.5 us
  Pallas kernels: 0 us -> 126 us
  starting transfers between devices: 2.08 us -> 123 us
  blocking collectives: 85.3 us -> 16.5 us
  local copies, waits for them, and re-layouts: 78.2 us -> 121 us
    reduce_scatter x11 -> x1, waiting for transfers between devices: 808 us -> 0.01 us  [on_device(): lax.psum_scatter(wo_back, WIDE, scatter_dimension=0, tiled=False)]
    all_gather x12 -> x1, waiting for transfers between devices: 623 us -> 0.02 us  [on_device(): wo = lax.all_gather(w_out_, WIDE, axis=0, tiled=False)]
    dot_general x53 -> x4, matrix products: 243 us -> 24.5 us  [dot(): lax.dot_general(left, right, (((left_dim,), (right_dim,)), ((), ())), pre...]
    ppermute x0 -> x110, waiting for transfers between devices: none -> 203 us  [the longest x86 121 us: swap(): return lax.ppermute(array, axis, [(0, 1), (1, 0)])]
    pallas_call x0 -> x16, Pallas kernels: none -> 126 us  [the longest x8 64.8 us: chunk_call(): pl.pallas_call(kernel, grid_spec=pltpu.PrefetchScalarGridSpec(num_scalar_...]
    psum x2 -> x0, waiting for transfers between devices: 80.9 us -> none  [the longest x1 40.4 us: on_device(): lax.psum(partial_ffn.astype(jnp.bfloat16), 'narrow').astype(jnp.float32)]
    ppermute x0 -> x110, starting transfers between devices: none -> 79.5 us  [the longest x86 53.5 us: swap(): return lax.ppermute(array, axis, [(0, 1), (1, 0)])]
    all_to_all x0 -> x9, waiting for transfers between devices: none -> 50.1 us  [the longest x1 26.5 us: on_device(): lax.all_to_all(grad_att, ('z', 'y'), split_axis=0, concat_axis=0, tiled=T...]
  transfers between devices with their start and end apart: 25 -> 121, of which waited for: 22 -> 32; matrix products, arithmetic and copies ran while one was open for 10% -> 24% of each run, Pallas kernels for 0% -> 17%
where the time goes in v1:
time: 764 us; the launch traced here: 758 us
  waiting for transfers between devices  254 us (33%)
  Pallas kernels  126 us (16%)
  starting transfers between devices  123 us (16%)
  local copies, waits for them, and re-layouts  121 us (16%)
  other arithmetic  76.3 us (10%)
  matrix products  24.5 us (3%)
  between operations  17 us (2%)
  blocking collectives  16.5 us (2%)
    ppermute x86, waiting for transfers between devices, swap(): return lax.ppermute(array, axis, [(0, 1), (1, 0)])  121 us
    ppermute x18, waiting for transfers between devices, ring(): return lax.ppermute(array, 'z', [(i, (i + 1) % size) for i in range(size)])  66.9 us
    pallas_call x8, Pallas kernels, chunk_call(): pl.pallas_call(kernel, grid_spec=pltpu.PrefetchScalarGridSpec(num_scalar_...  64.8 us
    unnamed x363, local copies, waits for them, and re-layouts  54.5 us
    ppermute x86, starting transfers between devices, swap(): return lax.ppermute(array, axis, [(0, 1), (1, 0)])  53.5 us
    all_to_all x8, starting transfers between devices, spread_z(): return lax.all_to_all(parts, 'z', split_axis=0, concat_axis=0, tiled=True)  37.5 us
    all_to_all x1, waiting for transfers between devices, on_device(): lax.all_to_all(grad_att, ('z', 'y'), split_axis=0, concat_axis=0, tiled=T...  26.5 us
    dot_general x4, matrix products, dot(): lax.dot_general(left, right, (((left_dim,), (right_dim,)), ((), ())), pre...  24.5 us
  transfers between devices with their start and end apart: 121, of which 32 were waited for; matrix products, arithmetic and copies ran while one was open for 24% of the time, Pallas kernels for 17%

profile of v1, /device:TPU:0, one launch (start us, length us, event | category | flops | bytes accessed | tf_op | source)
XLA Modules:
  0.0 758.4 jit_solution(18164292862966066773)
XLA Ops:
  19.1 4.2 all-to-all-start
  32.2 20.1 %all-to-all-done = bf16[4,384,256]{2,1,0:T(8,128)(2,1)} async-done(((bf16[4,384,256]{2,1,0:T(8,128)(2,1)}), bf16[4,384,256]{2,1,0:T(8,128)(2,1)}, u32[]{:S(2)}, u32[]{:S(2)}) %all-to-all-start) | async-done | bytes 786464 | tf_op jit(solution)/shard_map/all_to_all | solution.py:522
  55.5 7.3 collective-permute-done.4
  69.8 4.3 all-to-all-start.2
  89.2 5.3 collective-permute-done.13.refs_2_
  112.0 4.6 qkv.6
  118.3 4.6 qkv.7
  125.5 5.3 all-to-all-start.3
  141.4 17.8 %attend.1 = (bf16[8,64,384]{2,1,0:T(8,128)(2,1)S(1)}, f32[8,64,384]{2,1,0:T(8,128)S(1)}, f32[8,1,384]{2,1,0:T(1,128)S(1)}, f32[8,1,384]{2,1,0:T(1,128)S(1)}) custom-call(s32[64]{0:T(128)S(1)} %copy-done.118, s32[8]{0:T(128)S(1)} %copy-done.116, s32[17]{0:T(128)S(1)} %copy-done.120, s32[8]{0:T(128)S(1)} %stack.199.k_pos, bf16[8,192,384]{2,1,0:T(8,128)(2,1)S(1)} %copy-done.89, ...), custom_call_target="tpu_custom_call" | custom-call | flops 1811939328 | bytes 3145728 | tf_op jit(solution)/shard_map/attend/pallas_call | solution.py:161
  161.7 16.5 %all_to_all.50 = bf16[8,64,384]{2,1,0:T(8,128)(2,1)} all-to-all(bf16[8,64,384]{2,1,0:T(8,128)(2,1)S(1)} %get-tuple-element.110), channel_id=1, replica_groups=mesh['z'=4,'q'=1,'y'=2,'x'=2,'c'=2] {'z','y'}, dimensions={0} | all-to-all | bytes 786432 | tf_op jit(solution)/shard_map/all_to_all | solution.py:636
  178.2 4.3 all-to-all-start.4
  197.0 18.2 %collective-permute-done.107 = f32[8]{0:T(128)S(1)} collective-permute-done((f32[8]{0:T(128)S(1)}, f32[8]{0:T(128)S(1)}, u32[]{:S(2)}, u32[]{:S(2)}) %collective-permute-start.107) | collective-permute-done | bytes 64 | tf_op jit(solution)/shard_map/ppermute | solution.py:62
  228.3 4.7 collective-permute-done.24
  233.7 32.8 %collective-permute-done.33 = bf16[4,512,256]{2,1,0:T(8,128)(2,1)S(1)} collective-permute-done((bf16[4,512,256]{2,1,0:T(8,128)(2,1)}, bf16[4,512,256]{2,1,0:T(8,128)(2,1)S(1)}, u32[]{:S(2)}, u32[]{:S(2)}) %collective-permute-start.33) | collective-permute-done | bytes 1048608 | tf_op jit(solution)/shard_map/ppermute | solution.py:62
  272.1 4.5 reshape.371.refs_11_
  283.6 7.2 collective-permute-done.43.refs_4_
  292.4 6.8 collective-permute-done.36.refs_0_
  300.7 12.2 %feed_forward.4 = (bf16[1536,2048]{1,0:T(8,128)(2,1)}, bf16[1536,2048]{1,0:T(8,128)(2,1)}, bf16[1536,512]{1,0:T(8,128)(2,1)}, bf16[1536,512]{1,0:T(8,128)(2,1)},...) custom-call(s32[2]{0:T(128)S(1)} %copy-done.114, ...), custom_call_target="tpu_custom_call" | custom-call | flops 4831838208 | bytes 8388608 | tf_op jit(solution)/shard_map/feed_forward/pallas_call | solution.py:355
  329.5 6.2 collective-permute-done.37.refs_0_
  340.4 12.0 %feed_forward.5 = (bf16[1536,2048]{1,0:T(8,128)(2,1)}, bf16[1536,2048]{1,0:T(8,128)(2,1)}, bf16[1536,512]{1,0:T(8,128)(2,1)}, bf16[1536,512]{1,0:T(8,128)(2,1)},...) custom-call(s32[2]{0:T(128)S(1)} %copy-done.104, ...), custom_call_target="tpu_custom_call", output_to_operand_aliasing={{0}: (13, {}), {1}: (14, {}), {2}: (15, {}), {3}: (16, {}),... | custom-call | flops 4831838208 | bytes 8388608 | tf_op jit(solution)/shard_map/feed_forward/pallas_call | solution.py:355
  358.2 8.9 %collective-permute-done.38.refs_0_ = bf16[384,512]{1,0:T(8,128)(2,1)S(1)} collective-permute-done((bf16[384,512]{1,0:T(8,128)(2,1)}, bf16[384,512]{1,0:T(8,128)(2,1)S(1)}, u32[]{:S(2)}, u32[]{:S(2)}) %collective-permute-start.38) | collective-permute-done | bytes 393248 | tf_op jit(solution)/shard_map/ppermute | solution.py:66
  367.7 12.1 %feed_forward.6 = (bf16[1536,2048]{1,0:T(8,128)(2,1)}, bf16[1536,2048]{1,0:T(8,128)(2,1)}, bf16[1536,512]{1,0:T(8,128)(2,1)}, bf16[1536,512]{1,0:T(8,128)(2,1)},...) custom-call(s32[2]{0:T(128)S(1)} %copy-done.110, ...), custom_call_target="tpu_custom_call", output_to_operand_aliasing={{0}: (13, {}), {1}: (14, {}), {2}: (15, {}), {3}: (16, {}),... | custom-call | flops 4831838208 | bytes 8388608 | tf_op jit(solution)/shard_map/feed_forward/pallas_call | solution.py:355
  385.9 11.9 %feed_forward.7 = (bf16[1536,2048]{1,0:T(8,128)(2,1)}, bf16[1536,2048]{1,0:T(8,128)(2,1)}, bf16[1536,512]{1,0:T(8,128)(2,1)}, bf16[1536,512]{1,0:T(8,128)(2,1)},...) custom-call(s32[2]{0:T(128)S(1)} %copy-done.107, ...), custom_call_target="tpu_custom_call", output_to_operand_aliasing={{0}: (13, {}), {1}: (14, {}), {2}: (15, {}), {3}: (16, {}),... | custom-call | flops 4831838208 | bytes 8388608 | tf_op jit(solution)/shard_map/feed_forward/pallas_call | solution.py:355
  397.9 8.6 %convolution_convert_fusion.1 = bf16[2048,512]{1,0:T(8,128)(2,1)} fusion(bf16[1536,2048]{1,0:T(8,128)(2,1)} %get-tuple-element.169, bf16[1536,512]{1,0:T(8,128)(2,1)} %get-tuple-element.171), kind=kOutput, calls=%fused_computation.1 | convolution fusion | flops 3222274048 | bytes 9961472 | tf_op jit(solution)/shard_map/dot_general | solution.py:52
  406.5 4.7 convolution_convert_fusion.2
  411.2 4.7 convolution_convert_fusion
  418.5 4.5 reshape.378
  429.6 15.0 %collective-permute-done.76 = bf16[400,512]{1,0:T(8,128)(2,1)S(1)} collective-permute-done((bf16[400,512]{1,0:T(8,128)(2,1)S(1)}, bf16[400,512]{1,0:T(8,128)(2,1)S(1)}, u32[]{:S(2)}, u32[]{:S(2)}) %collective-permute-start.76) | collective-permute-done | bytes 409632 | tf_op jit(solution)/shard_map/ppermute | solution.py:62
  446.8 8.9 %collective-permute-done.74 = bf16[400,512]{1,0:T(8,128)(2,1)S(1)} collective-permute-done((bf16[400,512]{1,0:T(8,128)(2,1)S(1)}, bf16[400,512]{1,0:T(8,128)(2,1)S(1)}, u32[]{:S(2)}, u32[]{:S(2)}) %collective-permute-start.74) | collective-permute-done | bytes 409632 | tf_op jit(solution)/shard_map/ppermute | solution.py:62
  458.3 5.7 constant_dynamic-slice_fusion.3
  473.4 15.8 %collective-permute-done.79 = bf16[400,512]{1,0:T(8,128)(2,1)S(1)} collective-permute-done((bf16[400,512]{1,0:T(8,128)(2,1)S(1)}, bf16[400,512]{1,0:T(8,128)(2,1)S(1)}, u32[]{:S(2)}, u32[]{:S(2)}) %collective-permute-start.79) | collective-permute-done | bytes 409632 | tf_op jit(solution)/shard_map/ppermute | solution.py:66
  495.6 4.5 collective-permute-done.81.p2
  505.6 4.5 project_back.1
  512.1 6.2 all-to-all-start.5
  527.3 26.5 %all-to-all-done.5.grads = bf16[8,64,384]{2,1,0:T(8,128)(2,1)} async-done(((bf16[8,64,384]{2,1,0:T(8,128)(2,1)}), bf16[8,64,384]{2,1,0:T(8,128)(2,1)}, u32[]{:S(2)}, u32[]{:S(2)}) %all-to-all-start.5) | async-done | bytes 393248 | tf_op jit(solution)/shard_map/all_to_all | solution.py:694
  553.7 5.8 all-to-all-start.9
  580.5 22.5 %attend_back.1 = (bf16[8,64,384]{2,1,0:T(8,128)(2,1)S(1)}, bf16[8,128,384]{2,1,0:T(8,128)(2,1)S(1)}) custom-call(s32[64]{0:T(128)S(1)} %copy-done.119, s32[8]{0:T(128)S(1)} %copy-done.117, s32[17]{0:T(128)S(1)} %copy-done.121, s32[8]{0:T(128)S(1)} %copy-done.102, bf16[8,192,384]{2,1,0:T(8,128)(2,1)S(1)} %copy-done.90, bf16[8,16,384]{2,1,0:T(8,128)(2,1)S(1)} %copy-done.86, ...), custom_call_target="tpu_custom_call" | custom-call | flops 3623878656 | bytes 6291456 | tf_op jit(solution)/shard_map/attend_back/pallas_call | solution.py:272
  607.4 4.2 all-to-all-start.8
  614.6 4.9 collective-permute-done.83.refs_8_
  644.7 4.5 all-to-all-start.7
  649.2 6.5 convolution_convert_fusion.3
  659.8 4.4 constant_dynamic-slice_fusion.5
  685.0 4.9 all-to-all-start.6
  693.8 9.6 %collective-permute-done.94 = bf16[400,512]{1,0:T(8,128)(2,1)S(1)} collective-permute-done((bf16[400,512]{1,0:T(8,128)(2,1)S(1)}, bf16[400,512]{1,0:T(8,128)(2,1)S(1)}, u32[]{:S(2)}, u32[]{:S(2)}) %collective-permute-start.94) | collective-permute-done | bytes 409632 | tf_op jit(solution)/shard_map/ppermute | solution.py:62
  707.7 6.5 collective-permute-done.91
  721.2 4.5 collective-permute-done.88
  725.7 5.1 collective-permute-done.96
  735.1 9.5 %collective-permute-done.97 = bf16[400,512]{1,0:T(8,128)(2,1)} collective-permute-done((bf16[400,512]{1,0:T(8,128)(2,1)}, bf16[400,512]{1,0:T(8,128)(2,1)}, u32[]{:S(2)}, u32[]{:S(2)}) %collective-permute-start.97) | collective-permute-done | bytes 409632 | tf_op jit(solution)/shard_map/ppermute | solution.py:66
  (730 shorter events, 307.3 us)
Async XLA Ops:
  7.2 68.3 %collective-permute-start.1 = (bf16[384,512]{1,0:T(8,128)(2,1)}, bf16[384,512]{1,0:T(8,128)(2,1)S(1)}, u32[]{:S(2)}, u32[]{:S(2)}) collective-permute-start(bf16[384,512]{1,0:T(8,128)(2,1)} %refs_0_.3), channel_id=1, source_target_pairs={{0,2},{2,0},{1,3},{3,1},{4,6},{6,4},{5,7},{7,5},{8,10},{10,8},{9,1... | collective-permute-start | bytes 1179656 | tf_op jit(solution)/shard_map/ppermute | solution.py:62
  10.2 71.1 %collective-permute-start = (bf16[384,512]{1,0:T(8,128)(2,1)}, bf16[384,512]{1,0:T(8,128)(2,1)S(1)}, u32[]{:S(2)}, u32[]{:S(2)}) collective-permute-start(bf16[384,512]{1,0:T(8,128)(2,1)} %refs_0_.3), channel_id=1, source_target_pairs={{0,1},{1,0},{2,3},{3,2},{4,5},{5,4},{6,7},{7,6},{8,9},{9,8},{10,11... | collective-permute-start | bytes 1179656 | tf_op jit(solution)/shard_map/ppermute | solution.py:62
  13.1 39.6 %collective-permute-start.3 = (f32[8,2,256]{2,0,1:T(8,128)S(1)}, f32[8,2,256]{2,0,1:T(8,128)S(1)}, u32[]{:S(2)}, u32[]{:S(2)}) collective-permute-start(f32[8,2,256]{2,0,1:T(8,128)S(1)} %dynamic_update_slice.10), channel_id=1, source_target_pairs={{0,4},{4,0},{1,5},{5,1},{2,6},{6,2},{3,7},{7,3},{8,12},{12,8},{9,1... | collective-permute-start | bytes 49160 | tf_op jit(solution)/shard_map/ppermute | solution.py:62
  19.1 33.2 %all-to-all-start = ((bf16[4,384,256]{2,1,0:T(8,128)(2,1)}), bf16[4,384,256]{2,1,0:T(8,128)(2,1)}, u32[]{:S(2)}, u32[]{:S(2)}) async-start(bf16[4,384,256]{2,1,0:T(8,128)(2,1)} %bitcast.15), calls=%async_computation | async-start | bytes 1572864 | tf_op jit(solution)/shard_map/all_to_all | solution.py:522
  52.2 26.1 %collective-permute-start.6 = (bf16[4,384,256]{2,1,0:T(8,128)(2,1)}, bf16[4,384,256]{2,1,0:T(8,128)(2,1)}, u32[]{:S(2)}, u32[]{:S(2)}) collective-permute-start(bf16[4,384,256]{2,1,0:T(8,128)(2,1)} %all-to-all-done), channel_id=1, source_target_pairs={{0,4},{4,0},{1,5},{5,1},{2,6},{6,2},{3,7},{7,3},{8,12},{12,8},{9,1... | collective-permute-start | bytes 2359304 | tf_op jit(solution)/shard_map/ppermute | solution.py:62
  69.8 55.7 %all-to-all-start.2 = ((bf16[4,256,512]{2,1,0:T(8,128)(2,1)}), bf16[4,256,512]{2,1,0:T(8,128)(2,1)}, u32[]{:S(2)}, u32[]{:S(2)}) async-start(bf16[4,256,512]{2,1,0:T(8,128)(2,1)} %bitcast.376), calls=%async_computation.2 | async-start | bytes 2097152 | tf_op jit(solution)/shard_map/all_to_all | solution.py:522
  74.0 108.5 %all-gather.3.cloned.1.call-start = ((), (), s32[]{:S(2)}) async-start(), calls=%async_computation.12 | async-start | bytes 2359296 | tf_op jit(solution)/shard_map/all_gather | solution.py:565
  105.5 28.2 %collective-permute-start.19 = (bf16[192,384]{1,0:T(8,128)(2,1)}, bf16[192,384]{1,0:T(8,128)(2,1)}, u32[]{:S(2)}, u32[]{:S(2)}) collective-permute-start(bf16[192,384]{1,0:T(8,128)(2,1)} %get-tuple-element.106), channel_id=1, source_target_pairs={{0,4},{4,0},{1,5},{5,1},{2,6},{6,2},{3,7},{7,3},{8,12},{12,8},{9,1... | collective-permute-start | bytes 442376 | tf_op jit(solution)/shard_map/ppermute | solution.py:62
  125.5 36.3 %all-to-all-start.3 = ((bf16[4,256,512]{2,1,0:T(8,128)(2,1)}), bf16[4,256,512]{2,1,0:T(8,128)(2,1)}, u32[]{:S(2)}, u32[]{:S(2)}) async-start(bf16[4,256,512]{2,1,0:T(8,128)(2,1)} %bitcast.375), calls=%async_computation.3 | async-start | bytes 2097152 | tf_op jit(solution)/shard_map/all_to_all | solution.py:522
  178.2 42.9 %all-to-all-start.4 = ((bf16[4,512,256]{2,1,0:T(8,128)(2,1)}), bf16[4,512,256]{2,1,0:T(8,128)(2,1)}, u32[]{:S(2)}, u32[]{:S(2)}) async-start(bf16[4,512,256]{2,1,0:T(8,128)(2,1)} %bitcast.391), calls=%async_computation.4 | async-start | bytes 2097152 | tf_op jit(solution)/shard_map/all_to_all | solution.py:522
  189.3 31.9 %collective-permute-start.23 = (bf16[2,384,512]{2,1,0:T(8,128)(2,1)}, bf16[2,384,512]{2,1,0:T(8,128)(2,1)}, u32[]{:S(2)}, u32[]{:S(2)}) collective-permute-start(bf16[2,384,512]{2,1,0:T(8,128)(2,1)} %get-tuple-element.113), channel_id=1, source_target_pairs={{0,1},{1,0},{2,3},{3,2},{4,5},{5,4},{6,7},{7,6},{8,9},{9,8},{10,11... | collective-permute-start | bytes 2359304 | tf_op jit(solution)/shard_map/ppermute | solution.py:62
  189.3 34.5 %collective-permute-start.31 = (bf16[4,256,512]{2,1,0:T(8,128)(2,1)}, bf16[4,256,512]{2,1,0:T(8,128)(2,1)}, u32[]{:S(2)}, u32[]{:S(2)}) collective-permute-start(bf16[4,256,512]{2,1,0:T(8,128)(2,1)} %all-to-all-done.2), channel_id=1, source_target_pairs={{0,4},{4,0},{1,5},{5,1},{2,6},{6,2},{3,7},{7,3},{8,12},{12,8},{9,1... | collective-permute-start | bytes 3145736 | tf_op jit(solution)/shard_map/ppermute | solution.py:62
  191.5 36.3 %collective-permute-start.29 = (bf16[384,512]{1,0:T(8,128)(2,1)}, bf16[384,512]{1,0:T(8,128)(2,1)}, u32[]{:S(2)}, u32[]{:S(2)}) collective-permute-start(bf16[384,512]{1,0:T(8,128)(2,1)} %refs_4_), channel_id=1, source_target_pairs={{0,2},{2,0},{1,3},{3,1},{4,6},{6,4},{5,7},{7,5},{8,10},{10,8},{9,1... | collective-permute-start | bytes 1179656 | tf_op jit(solution)/shard_map/ppermute | solution.py:62
  192.0 35.7 %collective-permute-start.42 = (bf16[384,512]{1,0:T(8,128)(2,1)}, bf16[384,512]{1,0:T(8,128)(2,1)}, u32[]{:S(2)}, u32[]{:S(2)}) collective-permute-start(bf16[384,512]{1,0:T(8,128)(2,1)} %refs_4_), channel_id=1, source_target_pairs={{0,8},{8,16},{16,24},{24,0},{1,9},{9,17},{17,25},{25,1},{2,10},{10... | collective-permute-start | bytes 1179656 | tf_op jit(solution)/shard_map/ppermute | solution.py:66
  220.0 58.3 %collective-permute-start.32 = (bf16[4,256,512]{2,1,0:T(8,128)(2,1)}, bf16[4,256,512]{2,1,0:T(8,128)(2,1)}, u32[]{:S(2)}, u32[]{:S(2)}) collective-permute-start(bf16[4,256,512]{2,1,0:T(8,128)(2,1)} %all-to-all-done.3), channel_id=1, source_target_pairs={{0,4},{4,0},{1,5},{5,1},{2,6},{6,2},{3,7},{7,3},{8,12},{12,8},{9,1... | collective-permute-start | bytes 3145736 | tf_op jit(solution)/shard_map/ppermute | solution.py:62
  221.1 45.4 %collective-permute-start.33 = (bf16[4,512,256]{2,1,0:T(8,128)(2,1)}, bf16[4,512,256]{2,1,0:T(8,128)(2,1)S(1)}, u32[]{:S(2)}, u32[]{:S(2)}) collective-permute-start(bf16[4,512,256]{2,1,0:T(8,128)(2,1)} %all-to-all-done.4), channel_id=1, source_target_pairs={{0,4},{4,0},{1,5},{5,1},{2,6},{6,2},{3,7},{7,3},{8,12},{12,8},{9,1... | collective-permute-start | bytes 3145736 | tf_op jit(solution)/shard_map/ppermute | solution.py:62
  227.8 48.8 %collective-permute-start.28 = (bf16[384,512]{1,0:T(8,128)(2,1)}, bf16[384,512]{1,0:T(8,128)(2,1)}, u32[]{:S(2)}, u32[]{:S(2)}) collective-permute-start(bf16[384,512]{1,0:T(8,128)(2,1)} %refs_4_), channel_id=1, source_target_pairs={{0,1},{1,0},{2,3},{3,2},{4,5},{5,4},{6,7},{7,6},{8,9},{9,8},{10,11... | collective-permute-start | bytes 1179656 | tf_op jit(solution)/shard_map/ppermute | solution.py:62
  227.8 50.5 %collective-permute-start.30 = (bf16[384,512]{1,0:T(8,128)(2,1)}, bf16[384,512]{1,0:T(8,128)(2,1)}, u32[]{:S(2)}, u32[]{:S(2)}) collective-permute-start(bf16[384,512]{1,0:T(8,128)(2,1)} %collective-permute-done.29.refs_6_), channel_id=1, source_target_pairs={{0,1},{1,0},{2,3},{3,2},{4,5},{5,4},{6,7},{7,6},{8,9},{9,8},{10,11... | collective-permute-start | bytes 1179656 | tf_op jit(solution)/shard_map/ppermute | solution.py:62
  233.0 50.2 %collective-permute-start.58 = (bf16[384,512]{1,0:T(8,128)(2,1)}, bf16[384,512]{1,0:T(8,128)(2,1)}, u32[]{:S(2)}, u32[]{:S(2)}) collective-permute-start(bf16[384,512]{1,0:T(8,128)(2,1)} %collective-permute-done.42.refs_4_), channel_id=1, source_target_pairs={{0,2},{2,0},{1,3},{3,1},{4,6},{6,4},{5,7},{7,5},{8,10},{10,8},{9,1... | collective-permute-start | bytes 1179656 | tf_op jit(solution)/shard_map/ppermute | solution.py:62
  283.2 32.9 %collective-permute-start.57 = (bf16[384,512]{1,0:T(8,128)(2,1)}, bf16[384,512]{1,0:T(8,128)(2,1)S(1)}, u32[]{:S(2)}, u32[]{:S(2)}) collective-permute-start(bf16[384,512]{1,0:T(8,128)(2,1)} %collective-permute-done.42.refs_4_), channel_id=1, source_target_pairs={{0,1},{1,0},{2,3},{3,2},{4,5},{5,4},{6,7},{7,6},{8,9},{9,8},{10,11... | collective-permute-start | bytes 1179656 | tf_op jit(solution)/shard_map/ppermute | solution.py:62
  290.8 31.3 %collective-permute-start.52 = (bf16[384,512]{1,0:T(8,128)(2,1)}, bf16[384,512]{1,0:T(8,128)(2,1)}, u32[]{:S(2)}, u32[]{:S(2)}) collective-permute-start(bf16[384,512]{1,0:T(8,128)(2,1)} %collective-permute-done.43.refs_4_), channel_id=1, source_target_pairs={{0,2},{2,0},{1,3},{3,1},{4,6},{6,4},{5,7},{7,5},{8,10},{10,8},{9,1... | collective-permute-start | bytes 1179656 | tf_op jit(solution)/shard_map/ppermute | solution.py:62
  292.2 36.7 %collective-permute-start.44 = (bf16[384,512]{1,0:T(8,128)(2,1)}, bf16[384,512]{1,0:T(8,128)(2,1)}, u32[]{:S(2)}, u32[]{:S(2)}) collective-permute-start(bf16[384,512]{1,0:T(8,128)(2,1)} %collective-permute-done.43.refs_4_), channel_id=1, source_target_pairs={{0,8},{8,16},{16,24},{24,0},{1,9},{9,17},{17,25},{25,1},{2,10},{10... | collective-permute-start | bytes 1179656 | tf_op jit(solution)/shard_map/ppermute | solution.py:66
  322.1 33.2 %collective-permute-start.34 = (bf16[2,384,512]{2,1,0:T(8,128)(2,1)}, bf16[2,384,512]{2,1,0:T(8,128)(2,1)}, u32[]{:S(2)}, u32[]{:S(2)}) collective-permute-start(bf16[2,384,512]{2,1,0:T(8,128)(2,1)} %get-tuple-element.119), channel_id=1, source_target_pairs={{0,1},{1,0},{2,3},{3,2},{4,5},{5,4},{6,7},{7,6},{8,9},{9,8},{10,11... | collective-permute-start | bytes 2359304 | tf_op jit(solution)/shard_map/ppermute | solution.py:62
  352.4 27.8 %collective-permute-start.69 = (bf16[2,400,512]{2,1,0:T(8,128)(2,1)S(1)}, bf16[2,400,512]{2,1,0:T(8,128)(2,1)S(1)}, u32[]{:S(2)}, u32[]{:S(2)}) collective-permute-start(bf16[2,400,512]{2,1,0:T(8,128)(2,1)S(1)} %copy-done.168), channel_id=1, source_target_pairs={{0,1},{1,0},{2,3},{3,2},{4,5},{5,4},{6,7},{7,6},{8,9},{9,8},{10,11... | collective-permute-start | bytes 2457608 | tf_op jit(solution)/shard_map/ppermute | solution.py:62
  357.7 26.0 %collective-permute-start.45 = (bf16[384,512]{1,0:T(8,128)(2,1)}, bf16[384,512]{1,0:T(8,128)(2,1)S(1)}, u32[]{:S(2)}, u32[]{:S(2)}) collective-permute-start(bf16[384,512]{1,0:T(8,128)(2,1)} %collective-permute-done.44.refs_4_), channel_id=1, source_target_pairs={{0,1},{1,0},{2,3},{3,2},{4,5},{5,4},{6,7},{7,6},{8,9},{9,8},{10,11... | collective-permute-start | bytes 1179656 | tf_op jit(solution)/shard_map/ppermute | solution.py:62
  367.2 57.0 %collective-permute-start.75 = (bf16[2,400,512]{2,1,0:T(8,128)(2,1)}, bf16[2,400,512]{2,1,0:T(8,128)(2,1)}, u32[]{:S(2)}, u32[]{:S(2)}) collective-permute-start(bf16[2,400,512]{2,1,0:T(8,128)(2,1)} %get-tuple-element.149), channel_id=1, source_target_pairs={{0,1},{1,0},{2,3},{3,2},{4,5},{5,4},{6,7},{7,6},{8,9},{9,8},{10,11... | collective-permute-start | bytes 2457608 | tf_op jit(solution)/shard_map/ppermute | solution.py:62
  383.7 32.3 %collective-permute-start.64 = (bf16[2,384,512]{2,1,0:T(8,128)(2,1)S(1)}, bf16[2,384,512]{2,1,0:T(8,128)(2,1)}, u32[]{:S(2)}, u32[]{:S(2)}) collective-permute-start(bf16[2,384,512]{2,1,0:T(8,128)(2,1)S(1)} %get-tuple-element.140), channel_id=1, source_target_pairs={{0,1},{1,0},{2,3},{3,2},{4,5},{5,4},{6,7},{7,6},{8,9},{9,8},{10,11... | collective-permute-start | bytes 2359304 | tf_op jit(solution)/shard_map/ppermute | solution.py:62
  383.9 42.7 %collective-permute-start.73 = (bf16[2,400,512]{2,1,0:T(8,128)(2,1)}, bf16[2,400,512]{2,1,0:T(8,128)(2,1)}, u32[]{:S(2)}, u32[]{:S(2)}) collective-permute-start(bf16[2,400,512]{2,1,0:T(8,128)(2,1)} %get-tuple-element.147), channel_id=1, source_target_pairs={{0,1},{1,0},{2,3},{3,2},{4,5},{5,4},{6,7},{7,6},{8,9},{9,8},{10,11... | collective-permute-start | bytes 2457608 | tf_op jit(solution)/shard_map/ppermute | solution.py:62
  384.2 86.0 %collective-permute-start.62 = (bf16[2,384,512]{2,1,0:T(8,128)(2,1)}, bf16[2,384,512]{2,1,0:T(8,128)(2,1)}, u32[]{:S(2)}, u32[]{:S(2)}) collective-permute-start(bf16[2,384,512]{2,1,0:T(8,128)(2,1)} %get-tuple-element.138), channel_id=1, source_target_pairs={{0,1},{1,0},{2,3},{3,2},{4,5},{5,4},{6,7},{7,6},{8,9},{9,8},{10,11... | collective-permute-start | bytes 2359304 | tf_op jit(solution)/shard_map/ppermute | solution.py:62
  384.4 87.4 %collective-permute-start.70 = (bf16[400,512]{1,0:T(8,128)(2,1)}, bf16[400,512]{1,0:T(8,128)(2,1)}, u32[]{:S(2)}, u32[]{:S(2)}) collective-permute-start(bf16[400,512]{1,0:T(8,128)(2,1)} %fusion.59), channel_id=1, source_target_pairs={{0,2},{2,0},{1,3},{3,1},{4,6},{6,4},{5,7},{7,5},{8,10},{10,8},{9,1... | collective-permute-start | bytes 1228808 | tf_op jit(solution)/shard_map/ppermute | solution.py:62
  416.0 29.3 %collective-permute-start.71 = (bf16[2,400,512]{2,1,0:T(8,128)(2,1)}, bf16[2,400,512]{2,1,0:T(8,128)(2,1)}, u32[]{:S(2)}, u32[]{:S(2)}) collective-permute-start(bf16[2,400,512]{2,1,0:T(8,128)(2,1)} %get-tuple-element.145), channel_id=1, source_target_pairs={{0,1},{1,0},{2,3},{3,2},{4,5},{5,4},{6,7},{7,6},{8,9},{9,8},{10,11... | collective-permute-start | bytes 2457608 | tf_op jit(solution)/shard_map/ppermute | solution.py:62
  424.2 41.2 %collective-permute-start.65 = (bf16[384,512]{1,0:T(8,128)(2,1)S(1)}, bf16[384,512]{1,0:T(8,128)(2,1)S(1)}, u32[]{:S(2)}, u32[]{:S(2)}) collective-permute-start(bf16[384,512]{1,0:T(8,128)(2,1)S(1)} %fusion.71), channel_id=1, source_target_pairs={{0,2},{2,0},{1,3},{3,1},{4,6},{6,4},{5,7},{7,5},{8,10},{10,8},{9,1... | collective-permute-start | bytes 1179656 | tf_op jit(solution)/shard_map/ppermute | solution.py:62
  465.4 58.8 %collective-permute-start.101 = (bf16[4,512,256]{2,1,0:T(8,128)(2,1)}, bf16[4,512,256]{2,1,0:T(8,128)(2,1)}, u32[]{:S(2)}, u32[]{:S(2)}) collective-permute-start(bf16[4,512,256]{2,1,0:T(8,128)(2,1)} %bitcast.340), channel_id=1, source_target_pairs={{0,4},{4,0},{1,5},{5,1},{2,6},{6,2},{3,7},{7,3},{8,12},{12,8},{9,1... | collective-permute-start | bytes 3145736 | tf_op jit(solution)/shard_map/ppermute | solution.py:62
  466.6 51.8 %collective-permute-start.60 = (bf16[2,384,512]{2,1,0:T(8,128)(2,1)}, bf16[2,384,512]{2,1,0:T(8,128)(2,1)}, u32[]{:S(2)}, u32[]{:S(2)}) collective-permute-start(bf16[2,384,512]{2,1,0:T(8,128)(2,1)} %get-tuple-element.136), channel_id=1, source_target_pairs={{0,1},{1,0},{2,3},{3,2},{4,5},{5,4},{6,7},{7,6},{8,9},{9,8},{10,11... | collective-permute-start | bytes 2359304 | tf_op jit(solution)/shard_map/ppermute | solution.py:62
  471.8 29.3 %collective-permute-start.63 = (bf16[384,512]{1,0:T(8,128)(2,1)S(1)}, bf16[384,512]{1,0:T(8,128)(2,1)S(1)}, u32[]{:S(2)}, u32[]{:S(2)}) collective-permute-start(bf16[384,512]{1,0:T(8,128)(2,1)S(1)} %fusion.70), channel_id=1, source_target_pairs={{0,2},{2,0},{1,3},{3,1},{4,6},{6,4},{5,7},{7,5},{8,10},{10,8},{9,1... | collective-permute-start | bytes 1179656 | tf_op jit(solution)/shard_map/ppermute | solution.py:62
  501.2 58.4 %collective-permute-start.100 = (bf16[4,256,512]{2,1,0:T(8,128)(2,1)}, bf16[4,256,512]{2,1,0:T(8,128)(2,1)}, u32[]{:S(2)}, u32[]{:S(2)}) collective-permute-start(bf16[4,256,512]{2,1,0:T(8,128)(2,1)} %dynamic-slice_bitcast_fusion), channel_id=1, source_target_pairs={{0,4},{4,0},{1,5},{5,1},{2,6},{6,2},{3,7},{7,3},{8,12},{12,8},{9,1... | collective-permute-start | bytes 3145736 | tf_op jit(solution)/shard_map/ppermute | solution.py:62
  503.1 243.0 %collective-permute-start.35 = (bf16[384,512]{1,0:T(8,128)(2,1)}, bf16[384,512]{1,0:T(8,128)(2,1)}, u32[]{:S(2)}, u32[]{:S(2)}) collective-permute-start(bf16[384,512]{1,0:T(8,128)(2,1)} %fusion.68), channel_id=1, source_target_pairs={{0,2},{2,0},{1,3},{3,1},{4,6},{6,4},{5,7},{7,5},{8,10},{10,8},{9,1... | collective-permute-start | bytes 1179656 | tf_op jit(solution)/shard_map/ppermute | solution.py:62
  504.6 57.9 %collective-permute-start.99 = (bf16[4,256,512]{2,1,0:T(8,128)(2,1)}, bf16[4,256,512]{2,1,0:T(8,128)(2,1)}, u32[]{:S(2)}, u32[]{:S(2)}) collective-permute-start(bf16[4,256,512]{2,1,0:T(8,128)(2,1)} %dynamic-slice_bitcast_fusion.1), channel_id=1, source_target_pairs={{0,4},{4,0},{1,5},{5,1},{2,6},{6,2},{3,7},{7,3},{8,12},{12,8},{9,1... | collective-permute-start | bytes 3145736 | tf_op jit(solution)/shard_map/ppermute | solution.py:62
  512.1 41.6 %all-to-all-start.5 = ((bf16[8,64,384]{2,1,0:T(8,128)(2,1)}), bf16[8,64,384]{2,1,0:T(8,128)(2,1)}, u32[]{:S(2)}, u32[]{:S(2)}) async-start(bf16[8,64,384]{2,1,0:T(8,128)(2,1)} %bitcast.357), calls=%async_computation.5 | async-start | bytes 786432 | tf_op jit(solution)/shard_map/all_to_all | solution.py:694
  518.4 46.9 %collective-permute-start.67 = (bf16[384,512]{1,0:T(8,128)(2,1)}, bf16[384,512]{1,0:T(8,128)(2,1)}, u32[]{:S(2)}, u32[]{:S(2)}) collective-permute-start(bf16[384,512]{1,0:T(8,128)(2,1)} %fusion.36), channel_id=1, source_target_pairs={{0,8},{8,16},{16,24},{24,0},{1,9},{9,17},{17,25},{25,1},{2,10},{10... | collective-permute-start | bytes 1179656 | tf_op jit(solution)/shard_map/ppermute | solution.py:66
  524.1 41.2 %collective-permute-start.61 = (bf16[384,512]{1,0:T(8,128)(2,1)}, bf16[384,512]{1,0:T(8,128)(2,1)}, u32[]{:S(2)}, u32[]{:S(2)}) collective-permute-start(bf16[384,512]{1,0:T(8,128)(2,1)} %fusion.69), channel_id=1, source_target_pairs={{0,2},{2,0},{1,3},{3,1},{4,6},{6,4},{5,7},{7,5},{8,10},{10,8},{9,1... | collective-permute-start | bytes 1179656 | tf_op jit(solution)/shard_map/ppermute | solution.py:62
  553.7 53.7 %all-to-all-start.9 = ((bf16[4,512,256]{2,1,0:T(8,128)(2,1)}), bf16[4,512,256]{2,1,0:T(8,128)(2,1)}, u32[]{:S(2)}, u32[]{:S(2)}) async-start(bf16[4,512,256]{2,1,0:T(8,128)(2,1)} %fusion), calls=%async_computation.10 | async-start | bytes 2097152 | tf_op jit(solution)/shard_map/all_to_all | solution.py:522
  559.5 189.8 %reduce-scatter.2.cloned.1.call-start = ((), (), s32[]{:S(2)}) async-start(), calls=%async_computation.11 | async-start | bytes 2359296 | tf_op jit(solution)/shard_map/reduce_scatter | solution.py:729
  567.4 178.8 %collective-permute-start.68 = (bf16[384,512]{1,0:T(8,128)(2,1)}, bf16[384,512]{1,0:T(8,128)(2,1)}, u32[]{:S(2)}, u32[]{:S(2)}) collective-permute-start(bf16[384,512]{1,0:T(8,128)(2,1)} %fusion.39), channel_id=1, source_target_pairs={{0,8},{8,16},{16,24},{24,0},{1,9},{9,17},{17,25},{25,1},{2,10},{10... | collective-permute-start | bytes 1179656 | tf_op jit(solution)/shard_map/ppermute | solution.py:66
  607.4 37.2 %all-to-all-start.8 = ((bf16[4,256,512]{2,1,0:T(8,128)(2,1)}), bf16[4,256,512]{2,1,0:T(8,128)(2,1)}, u32[]{:S(2)}, u32[]{:S(2)}) async-start(bf16[4,256,512]{2,1,0:T(8,128)(2,1)} %fusion.1), calls=%async_computation.9 | async-start | bytes 2097152 | tf_op jit(solution)/shard_map/all_to_all | solution.py:522
  644.7 31.2 %all-to-all-start.7 = ((bf16[4,256,512]{2,1,0:T(8,128)(2,1)}), bf16[4,256,512]{2,1,0:T(8,128)(2,1)}, u32[]{:S(2)}, u32[]{:S(2)}) async-start(bf16[4,256,512]{2,1,0:T(8,128)(2,1)} %fusion.2), calls=%async_computation.8 | async-start | bytes 2097152 | tf_op jit(solution)/shard_map/all_to_all | solution.py:522
  685.0 46.7 %all-to-all-start.6 = ((bf16[4,384,256]{2,1,0:T(8,128)(2,1)}), bf16[4,384,256]{2,1,0:T(8,128)(2,1)S(1)}, u32[]{:S(2)}, u32[]{:S(2)}) async-start(bf16[4,384,256]{2,1,0:T(8,128)(2,1)} %fusion.3), calls=%async_computation.6 | async-start | bytes 1572864 | tf_op jit(solution)/shard_map/all_to_all | solution.py:522
  689.9 28.4 %collective-permute-start.84 = (bf16[2,400,512]{2,1,0:T(8,128)(2,1)}, bf16[2,400,512]{2,1,0:T(8,128)(2,1)S(1)}, u32[]{:S(2)}, u32[]{:S(2)}) collective-permute-start(bf16[2,400,512]{2,1,0:T(8,128)(2,1)} %copy-done.122), channel_id=1, source_target_pairs={{0,1},{1,0},{2,3},{3,2},{4,5},{5,4},{6,7},{7,6},{8,9},{9,8},{10,11... | collective-permute-start | bytes 2457608 | tf_op jit(solution)/shard_map/ppermute | solution.py:62
  (244 other events, 2298.8 us)
Sparse Core Ops, SparseCore 0:
  77.0 72.0 all-gather.2
  571.2 78.7 reduce-scatter.1

commit v2 on v1

v2 whole, which is shorter than its diff:
```python
import functools

import jax
import jax.numpy as jnp
from jax import lax
from jax.experimental import pallas as pl
from jax.experimental.pallas import tpu as pltpu
from jax.sharding import Mesh
from jax.sharding import PartitionSpec as P

HDIM = 64
HALF = HDIM // 2

eps_norm = 1e-05
rope_base = 130000.0
clip_limit = 5.0
masked_fill = -1e30

F32 = jnp.float32
BF16 = jnp.bfloat16
WIDE = ("z", "q", "y")
GROUP = ("q", "y")
NARROW = ("x", "c")
VMEM_BYTES = 60 * 2**20
EXTRA = 16


def lookup(lookup_table, indices):
    labels = jnp.arange(lookup_table.shape[0], dtype=jnp.int32)
    return jnp.sum(
        jnp.where(indices[:, None] == labels[None, :], lookup_table[None, :], 0),
        axis=1,
        dtype=jnp.int32,
    )


def segment_tables(segment_ids, parents):
    labels = jnp.arange(parents.shape[0], dtype=jnp.int32)
    counts = jnp.sum(
        (segment_ids[:, None] == labels[None, :]).astype(jnp.int32), axis=0, dtype=jnp.int32
    )
    starts = jnp.sum(
        jnp.where(labels[None, :] < labels[:, None], counts[None, :], 0), axis=1, dtype=jnp.int32
    )
    ancestor = lookup(parents, parents)
    parent_len = jnp.where(parents != labels, lookup(counts, parents), 0)
    ancestor_len = jnp.where(ancestor != parents, lookup(counts, ancestor), 0)
    return (ancestor, starts, parent_len, ancestor_len)


def dot(left, right, left_dim, right_dim):
    return lax.dot_general(
        left, right, (((left_dim,), (right_dim,)), ((), ())), preferred_element_type=F32
    )


def take(array, index, axis=0):
    return lax.dynamic_index_in_dim(array, index, axis, keepdims=False)


def swap(array, axis):
    return lax.ppermute(array, axis, [(0, 1), (1, 0)])


def ring(array, size):
    return lax.ppermute(array, "z", [(i, (i + 1) % size) for i in range(size)])


def pick(flag, first, second):
    return jnp.where(flag == 0, first, second)


def together(*values):
    return lax.optimization_barrier(values)


def params():
    return pltpu.CompilerParams(vmem_limit_bytes=VMEM_BYTES)


def cost(time):
    return pl.CostEstimate(flops=int(time * 1e9), bytes_accessed=1000, transcendentals=0)


def shape(dims, dtype):
    return jax.ShapeDtypeStruct(dims, dtype)


def full(dims):
    return pl.BlockSpec(dims, lambda *_: (0,) * len(dims))


def fill_tiles(sources, mask, held, k_ext, values_t):
    if len(sources) == 1:
        held[...] = sources[0][...]
    else:
        for t, source in enumerate(sources):
            held[t] = source[...]
    for t in range(held.shape[0]):
        tile = held[t].astype(F32)
        spare = k_ext.shape[2] - HDIM - mask.shape[1]
        parts = [tile[HDIM : 2 * HDIM], mask[t].astype(F32)]
        parts.append(jnp.zeros((spare, tile.shape[1]), F32))
        k_ext[t] = jnp.concatenate(parts, axis=0).T.astype(BF16)
        if values_t is not None:
            values_t[t] = jnp.concatenate(
                [tile[2 * HDIM :], jnp.zeros((HDIM, tile.shape[1]), F32)], axis=0
            ).T.astype(BF16)


def query_ext(q, mask, depth):
    spare = depth - HDIM - mask.shape[1]
    return jnp.concatenate([q, mask[0], jnp.zeros((spare, q.shape[1]), BF16)], axis=0)


def attend_kernel(visible, counts, q_pos, k_pos, *refs):
    q_mask, k_mask, low, out, log_norm, peak, held, k_ext = refs[-8:]
    i = pl.program_id(0)
    tiles, _, width = held.shape

    @pl.when(i == 0)
    def _():
        fill_tiles(refs[:-8], k_mask, held, k_ext, None)

    mine = q_pos[pl.num_programs(0) * 2]
    q_tile = query_ext(held[mine + i, :HDIM], q_mask, k_ext.shape[2])
    relative = lax.broadcasted_iota(jnp.int32, (width, width), 0) - lax.broadcasted_iota(
        jnp.int32, (width, width), 1
    )

    def step(n, carry):
        high, total, acc = carry
        j = visible[i * tiles + n]
        scores = dot(k_ext[j], q_tile, 1, 0)
        scores = jnp.where(relative <= (q_pos[i] - k_pos[j]) * width, scores, masked_fill)
        new_high = jnp.maximum(high, jnp.max(scores, axis=0, keepdims=True))
        weights = jnp.exp(scores - new_high)
        shrink = jnp.exp(high - new_high)
        total = total * shrink + jnp.sum(weights, axis=0, keepdims=True)
        acc = acc * shrink + dot(held[j, 2 * HDIM :], weights.astype(BF16), 1, 0)
        return new_high, total, acc

    high, total, acc = lax.fori_loop(
        0,
        counts[i],
        step,
        (
            jnp.full((1, width), masked_fill, F32),
            jnp.zeros((1, width), F32),
            jnp.zeros((HDIM, width), F32),
        ),
    )
    result = acc / total
    out[0] = result
    low[0] = result.astype(BF16)
    log_norm[0] = high + jnp.log(total)
    peak[0] = high


def attend(tables, tiles, q_mask, k_mask):
    q_tiles, labels, width = q_mask.shape
    k_tiles = k_mask.shape[0]
    part = lambda i, *_: (i, 0, 0)
    placed = lambda i, visible, counts, q_pos, k_pos: (q_pos[i + q_tiles], 0, 0)
    return pl.pallas_call(
        attend_kernel,
        grid_spec=pltpu.PrefetchScalarGridSpec(
            num_scalar_prefetch=4,
            grid=(q_tiles,),
            in_specs=[full(a.shape) for a in tiles]
            + [pl.BlockSpec((1, labels, width), part), full(k_mask.shape)],
            out_specs=[
                pl.BlockSpec((1, HDIM, width), placed),
                pl.BlockSpec((1, HDIM, width), part),
                pl.BlockSpec((1, 1, width), part),
                pl.BlockSpec((1, 1, width), part),
            ],
            scratch_shapes=[
                pltpu.VMEM((k_tiles, 3 * HDIM, width), BF16),
                pltpu.VMEM((k_tiles, width, 2 * HDIM), BF16),
            ],
        ),
        out_shape=[
            shape((q_tiles, HDIM, width), BF16),
            shape((q_tiles, HDIM, width), F32),
            shape((q_tiles, 1, width), F32),
            shape((q_tiles, 1, width), F32),
        ],
        compiler_params=params(),
        cost_estimate=cost(18),
        name="attend",
    )(*tables, *tiles, q_mask, k_mask)


def attend_back_kernel(visible, counts, q_pos, k_pos, *refs):
    q_mask, k_mask, grads, out, log_norm, cosine, sine, back = refs[-13:-5]
    held, k_ext, values_t, acc_k, acc_v = refs[-5:]
    i = pl.program_id(0)
    tiles, _, width = held.shape

    @pl.when(i == 0)
    def _():
        fill_tiles(refs[:-13], k_mask, held, k_ext, values_t)
        acc_k[...] = jnp.zeros_like(acc_k)
        acc_v[...] = jnp.zeros_like(acc_v)

    mine = q_pos[pl.num_programs(0) * 2]
    q_rows = held[mine + i, :HDIM]
    q_tile = query_ext(q_rows, q_mask, k_ext.shape[2])
    g_tile = grads[0]
    g_ext = jnp.concatenate([g_tile, jnp.zeros_like(g_tile)], axis=0)
    lse = log_norm[0]
    delta = jnp.sum(g_tile.astype(F32) * out[0], axis=0, keepdims=True)
    relative = lax.broadcasted_iota(jnp.int32, (width, width), 0) - lax.broadcasted_iota(
        jnp.int32, (width, width), 1
    )

    def step(n, acc):
        j = visible[i * tiles + n]
        scores = dot(k_ext[j], q_tile, 1, 0)
        scores = jnp.where(relative <= (q_pos[i] - k_pos[j]) * width, scores, masked_fill)
        probs = jnp.exp(scores - lse)
        grad_probs = dot(values_t[j], g_ext, 1, 0)
        grad_scores = (probs * (grad_probs - delta)).astype(BF16)
        acc_v[j] += dot(g_tile, probs.astype(BF16), 1, 1)
        acc_k[j] += dot(q_rows, grad_scores, 1, 1)
        return acc + dot(held[j, HDIM : 2 * HDIM], grad_scores, 1, 0)

    acc = lax.fori_loop(0, counts[i], step, jnp.zeros((HDIM, width), F32))

    def put_unrotated(grad, t, base):
        first, second, c, s = grad[:HALF], grad[HALF:], cosine[t], sine[t]
        back[t, base : base + HALF] = (first * c + second * s).astype(BF16)
        back[t, base + HALF : base + HDIM] = (second * c - first * s).astype(BF16)

    put_unrotated(acc * HDIM ** (-0.5), mine + i, 0)

    @pl.when(i == pl.num_programs(0) - 1)
    def _():
        for t in range(tiles):
            put_unrotated(acc_k[t], t, HDIM)
            back[t, 2 * HDIM :] = acc_v[t].astype(BF16)


def attend_back(tables, tiles, q_mask, k_mask, grads, out, log_norm, cosine, sine):
    q_tiles, labels, width = q_mask.shape
    k_tiles = k_mask.shape[0]
    part = lambda i, *_: (i, 0, 0)
    placed = lambda i, visible, counts, q_pos, k_pos: (q_pos[i + q_tiles], 0, 0)
    return pl.pallas_call(
        attend_back_kernel,
        grid_spec=pltpu.PrefetchScalarGridSpec(
            num_scalar_prefetch=4,
            grid=(q_tiles,),
            in_specs=[full(a.shape) for a in tiles]
            + [
                pl.BlockSpec((1, labels, width), part),
                full(k_mask.shape),
                pl.BlockSpec((1, HDIM, width), placed),
                pl.BlockSpec((1, HDIM, width), part),
                pl.BlockSpec((1, 1, width), part),
                full(cosine.shape),
                full(sine.shape),
            ],
            out_specs=full((k_tiles, 3 * HDIM, width)),
            scratch_shapes=[
                pltpu.VMEM((k_tiles, 3 * HDIM, width), BF16),
                pltpu.VMEM((k_tiles, width, 2 * HDIM), BF16),
                pltpu.VMEM((k_tiles, width, 2 * HDIM), BF16),
                pltpu.VMEM((k_tiles, HDIM, width), F32),
                pltpu.VMEM((k_tiles, HDIM, width), F32),
            ],
        ),
        out_shape=shape((k_tiles, 3 * HDIM, width), BF16),
        compiler_params=params(),
        cost_estimate=cost(22),
        name="attend_back",
    )(*tables, *tiles, q_mask, k_mask, grads, out, log_norm, cosine, sine)


def row_scale(pieces, width):
    squares = 0.0
    for piece in pieces:
        values = piece[...].astype(F32)
        squares = squares + jnp.sum(values * values, axis=1, keepdims=True)
    return lax.rsqrt(squares / width + eps_norm)


def aligned(start, size):
    return pl.ds(pl.multiple_of(start, size), size)


def block_of(where, k):
    return where[0] ^ k


def half_columns(where, h, wide):
    return aligned((h ^ where[1]) * wide, wide)


def put_normed(where, pieces, rstd, gain, normed):
    cols = pieces[0].shape[1]
    half = cols // 2
    for k, piece in enumerate(pieces):
        block = block_of(where, k)
        values = piece[...].astype(F32) * rstd * gain[:, aligned(block * cols, cols)]
        for part in range(2):
            columns = aligned((part * 4 + block) * half, half)
            normed[:, columns] = values[:, part * half : (part + 1) * half].astype(BF16)


def qkv_kernel(where, *refs):
    pieces, (gain, w_first, w_second, cosine, sine) = refs[:4], refs[4:9]
    normed, mine, other, scale = refs[-4:]
    rows, cols = pieces[0].shape
    half = cols // 2
    rstd = row_scale(pieces, 4 * cols)
    scale[...] = rstd
    put_normed(where, pieces, rstd, gain, normed)
    c, s = cosine[...], sine[...]
    features = 3 * HDIM
    for out, head in ((mine, where[2]), (other, 1 - where[2])):
        span = aligned(head * features, features)
        lin = 0.0
        for h, weights in enumerate((w_first, w_second)):
            for z in range(4):
                columns = aligned(((h ^ where[1]) * 4 + z) * half, half)
                lin = lin + dot(weights[z, span, :], normed[:, columns], 1, 1)
        for part, factor in ((0, HDIM ** (-0.5)), (1, 1.0)):
            base = part * HDIM
            first, second = lin[base : base + HALF], lin[base + HALF : base + HDIM]
            out[base : base + HALF] = ((first * c - second * s) * factor).astype(BF16)
            out[base + HALF : base + HDIM] = ((second * c + first * s) * factor).astype(BF16)
        out[2 * HDIM :] = lin[2 * HDIM :].astype(BF16)


def chunk_call(kernel, name, time, where, s, inputs, buffers, whole_shapes, out_shapes, held=False):
    def spec(dims, how):
        rest = (0,) * (len(dims) - 1)
        if how == "whole":
            return full(dims)
        if how == "there":
            return pl.BlockSpec(memory_space=pl.ANY)
        block = (dims[0] // 4, *dims[1:])
        if how == "chunk":
            return pl.BlockSpec(block, lambda i, where: (s, *rest))
        return pl.BlockSpec(block, lambda i, where: (where[3], *rest))

    in_specs = [spec(a.shape, how) for a, how in inputs]
    arrays = [a for a, _ in inputs]
    aliases = {}
    if buffers is not None:
        for n, buffer in enumerate(buffers):
            aliases[1 + len(arrays)] = n
            in_specs.append(pl.BlockSpec(memory_space=pl.ANY))
            arrays.append(buffer)
    out_specs = [spec(dims, how) for dims, how in whole_shapes]
    out_specs += [full(a.shape) for a in out_shapes]
    scratch = []
    if held:
        there = [a for a, how in inputs if how == "there"]
        rows = sum(a.shape[0] for a in there)
        scratch = [
            pltpu.VMEM((rows, there[0].shape[1]), BF16),
            pltpu.SemaphoreType.DMA((len(there),)),
        ]
    return pl.pallas_call(
        kernel,
        grid_spec=pltpu.PrefetchScalarGridSpec(
            num_scalar_prefetch=1,
            grid=(1,),
            in_specs=in_specs,
            out_specs=out_specs,
            scratch_shapes=scratch,
        ),
        out_shape=[shape(dims, BF16) for dims, _ in whole_shapes] + list(out_shapes),
        input_output_aliases=aliases,
        compiler_params=params(),
        cost_estimate=cost(time),
        name=name,
    )(where, *arrays)


def fetch(weights, held, sems):
    copies, start = [], 0
    for n, weight in enumerate(weights):
        rows = weight.shape[0]
        copies.append(pltpu.make_async_copy(weight, held.at[pl.ds(start, rows)], sems.at[n]))
        copies[-1].start()
        start += rows
    return copies


def ffn_kernel(where, *refs):
    normed, hidden, gates, ups, scale, held, sems = refs[-7:]
    mids, gain, weights = refs[:4], refs[4], refs[5 : 5 + sems.shape[0]]
    rows, cols = mids[0].shape
    units, wide = hidden.shape[1], 2 * cols
    copies = fetch(weights, held, sems)
    rstd = row_scale(mids, 4 * cols)
    scale[...] = rstd
    put_normed(where, mids, rstd, gain, normed)
    for copy in copies:
        copy.wait()
    step = 256
    for n in range(0, units, step):
        span = slice(n, n + step)
        gate = up = 0.0
        for h in range(2):
            values = normed[:, half_columns(where, h, wide)]
            gate = gate + dot(values, held[h * wide : (h + 1) * wide, span], 1, 0)
            up = up + dot(values, held[(h + 2) * wide : (h + 3) * wide, span], 1, 0)
        hidden[:, span] = (gate * jax.nn.sigmoid(gate) * up).astype(BF16)
        gates[:, span] = gate
        ups[:, span] = up


def ffn_back_kernel(where, *refs):
    cots, normed, hidden, gates, ups = refs[:5]
    cot_rows, grad_gate, grad_up, out, keep_back, send_back, gain_term, held, sems = refs[-9:]
    count = sems.shape[0]
    rows, units = hidden.shape
    cols = cots.shape[2]
    half, wide = cols // 2, 2 * cols
    copies = fetch(refs[5 : 5 + count], held, sems)
    for block in range(4):
        for part in range(2):
            start = (part * 4 + block) * half
            cot_rows[:, start : start + half] = cots[block, :, part * half : (part + 1) * half]
    for copy in copies[: count // 2]:
        copy.wait()
    step = 256
    for n in range(0, units, step):
        span = slice(n, n + step)
        grad_hidden = 0.0
        for h in range(2):
            grad_hidden = grad_hidden + dot(
                cot_rows[:, half_columns(where, h, wide)], held[h * wide : (h + 1) * wide, span], 1, 0
            )
        gate, up = gates[:, span], ups[:, span]
        sigmoid = jax.nn.sigmoid(gate)
        grad_gate[:, span] = (
            grad_hidden * up * sigmoid * (1.0 + gate * (1.0 - sigmoid))
        ).astype(BF16)
        grad_up[:, span] = (grad_hidden * (gate * sigmoid)).astype(BF16)
    for copy in copies[count // 2 :]:
        copy.wait()
    row_term = 0.0
    for k in range(4):
        block = block_of(where, k)
        back = (keep_back, send_back)[k % 2]
        for h in range(2):
            part = aligned((h ^ where[1]) * half, half)
            of_down, of_gate, of_up = [
                held[aligned((n + h) * wide + block * half, half), :] for n in (0, 2, 4)
            ]
            out[block, :, part] = dot(hidden[...], of_down, 1, 1).astype(BF16)
            partial = dot(grad_gate[...], of_gate, 1, 1) + dot(grad_up[...], of_up, 1, 1)
            back[k // 2, :rows, part] = partial.astype(BF16)
            columns = aligned(((h ^ where[1]) * 4 + block) * half, half)
            terms = partial * normed[:, columns].astype(F32)
            gain_term[:, columns] = jnp.sum(terms, axis=0, keepdims=True)
            row_term = row_term + jnp.sum(terms, axis=1, keepdims=True)
    put_row_term(row_term, cols, keep_back, send_back)


def put_row_term(row_term, cols, keep, send):
    rows = row_term.shape[0]
    line = jnp.broadcast_to(row_term, (rows, 128)).T[:EXTRA]
    line = jnp.concatenate([line, jnp.zeros((EXTRA, cols - rows), F32)], axis=1).astype(BF16)
    for ref in (keep, send):
        ref[0, rows:] = line
        ref[1, rows:] = line


def qkv_back_kernel(where, normed, mine, other, w_first, w_second, keep, send, gain_term):
    rows, cols = normed.shape[0], keep.shape[2]
    half = cols // 2
    features = 3 * HDIM
    row_term = 0.0
    for k in range(4):
        block = block_of(where, k)
        back = (keep, send)[k % 2]
        for h, weights in enumerate((w_first, w_second)):
            part = aligned((h ^ where[1]) * half, half)
            partial = 0.0
            for grads, head in ((mine, where[2]), (other, 1 - where[2])):
                span = aligned(head * features, features)
                partial = partial + dot(grads[0], weights[block, span, :], 0, 0)
            back[k // 2, :rows, part] = partial.astype(BF16)
            columns = aligned(((h ^ where[1]) * 4 + block) * half, half)
            terms = partial * normed[:, columns].astype(F32)
            gain_term[:, columns] = jnp.sum(terms, axis=0, keepdims=True)
            row_term = row_term + jnp.sum(terms, axis=1, keepdims=True)
    put_row_term(row_term, cols, keep, send)


def qkv_weights_kernel(where, normed, *refs):
    own, other, outs = refs[0], refs[1], refs[2:]
    count = other.shape[0]
    half = outs[0].shape[2]
    rows, features = own.shape[2], 3 * HDIM
    for h, out in enumerate(outs):
        for z in range(4):
            columns = aligned(((h ^ where[1]) * 4 + z) * half, half)
            for grads, head in ((own, where[2]), (other, 1 - where[2])):
                total = 0.0
                for s in range(count):
                    total = total + dot(
                        grads[s], normed[s * rows : (s + 1) * rows, columns], 1, 0
                    )
                out[z, aligned(head * features, features), :] = total.astype(BF16)


def project_kernel(where, attended, weights, keep, send):
    half = weights.shape[2]
    for k in range(4):
        for part in range(2):
            (keep, send)[k % 2][k // 2, :, part * half : (part + 1) * half] = dot(
                attended[...], weights[block_of(where, k) * 2 + part], 0, 0
            ).astype(BF16)


def project_back_kernel(where, p0, p1, p2, p3, attended, weights, grad_att, grad_weights):
    half = weights.shape[2]
    total = 0.0
    for k, piece in enumerate((p0, p1, p2, p3)):
        for part in range(2):
            b = block_of(where, k) * 2 + part
            values = piece[:, part * half : (part + 1) * half]
            total = total + dot(weights[b], values, 1, 1)
            grad_weights[b] = dot(attended[...], values, 1, 0).astype(BF16)
    grad_att[...] = total.astype(BF16)


def columns_kernel(where, parts, out):
    for z in range(parts.shape[0]):
        out[:, z * parts.shape[2] : (z + 1) * parts.shape[2]] = parts[z].astype(F32)


def turned_kernel(where, parts, out):
    size = parts.shape[2]
    for z in range(parts.shape[0]):
        out[z * size : (z + 1) * size, :] = parts[z].astype(F32).T


def qkv_out_kernel(where, parts, *outs):
    features = 3 * HDIM
    for z in range(parts.shape[0]):
        for n, out in enumerate(outs):
            heads = [parts[z, h * features + n * HDIM : h * features + (n + 1) * HDIM] for h in (0, 1)]
            both = jnp.concatenate(heads, axis=0).astype(F32)
            out[:, z * 2 * HDIM : (z + 1) * 2 * HDIM] = both.T


def small_call(kernel, name, time, where, inputs, out_shapes, specs=None):
    specs = specs or {}
    return pl.pallas_call(
        kernel,
        grid_spec=pltpu.PrefetchScalarGridSpec(
            num_scalar_prefetch=1,
            grid=(1,),
            in_specs=[specs.get(n) or full(a.shape) for n, a in enumerate(inputs)],
            out_specs=[full(s.shape) for s in out_shapes],
        ),
        out_shape=list(out_shapes),
        compiler_params=params(),
        cost_estimate=cost(time),
        name=name,
    )(where, *inputs)


def on_device(
    sizes,
    hidden_in,
    gain_attn,
    w_query,
    w_key,
    w_value,
    w_out,
    gain_ffn,
    w_gate,
    w_up,
    w_down,
    cotangent,
    segment_ids,
    parents,
):
    nz, nq, ny, nx, nc = sizes
    rows, cols = hidden_in.shape
    groups = nq * ny
    group_rows = nz * rows
    width = cols * nx * nc
    half = cols // 2
    slab = gain_attn.shape[0]
    head = 3 * HDIM
    units = w_gate.shape[1] // nz

    zi, qi, yi, xi, ci = [lax.axis_index(a) for a in ("z", "q", "y", "x", "c")]
    group = qi * ny + yi
    own_columns = xi * nc + ci
    zs = [(zi - s) % nz for s in range(nz)]
    flip = yi if nq == 1 else 0 * yi
    where = [jnp.stack([own_columns, flip, yi, z]).astype(jnp.int32) for z in zs]

    def scatter_narrow(keep, send):
        held = keep.astype(F32) + swap(send, "c").astype(F32)
        return held[0] + swap(held[1].astype(BF16), "x").astype(F32)

    def first_sum(keep, received):
        held = keep.astype(F32) + received.astype(F32)
        return held[0], held[1].astype(BF16)

    def spread_z(parts):
        return lax.all_to_all(parts, "z", split_axis=0, concat_axis=0, tiled=True)

    def gather_rows(parts):
        n = parts.shape[2]
        if nq == 1:
            return parts.reshape(-1, n), swap(parts, "y").reshape(-1, n)
        got = lax.all_gather(parts, GROUP, axis=0, tiled=False)
        got = got.reshape(2, groups // 2, nz, slab, n).transpose(0, 2, 1, 3, 4)
        return tuple(got.reshape(2, nz * half, n))

    def swap_part(parts, n):
        part = parts[n * nz // 2 : (n + 1) * nz // 2]
        return swap(part, "y") if nq == 1 else part

    def join_rows(parts, swapped):
        if nq > 1:
            return gather_rows(parts)
        return [a.reshape(-1, units) for a in (parts, *swapped)]

    def gather_lanes(parts):
        n = parts.shape[1]
        if nq == 1:
            return parts, swap(parts, "y")
        got = lax.all_gather(parts, GROUP, axis=0, tiled=False)
        got = got.reshape(2, groups // 2, nz, n, slab).transpose(0, 2, 3, 1, 4)
        return tuple(got.reshape(2, nz, n, half))

    def exchange_rows(grad):
        if nq == 1:
            return swap(take(grad.reshape(2, -1, grad.shape[1]), 1 - yi), "y")
        n = grad.shape[1]
        parts = grad.reshape(2, nz, groups // 2, slab, n).transpose(0, 2, 1, 3, 4)
        return lax.psum_scatter(
            parts.reshape(groups, nz, slab, n), GROUP, scatter_dimension=0, tiled=False
        )

    def add_rows(grad, received):
        if nq == 1:
            own = take(grad.reshape(2, -1, grad.shape[1]), yi)
            received = (own.astype(F32) + received.astype(F32)).astype(BF16)
        return received.reshape(nz, slab, -1)

    def exchange_lanes(second):
        return swap(second, "y") if nq == 1 else second

    def scatter_lanes(first, second):
        n = first.shape[1]
        if nq == 1:
            return (first.astype(F32) + second.astype(F32)).astype(BF16)
        both = jnp.stack([first, second]).reshape(2, nz, n, groups // 2, slab)
        both = both.transpose(0, 3, 1, 2, 4).reshape(groups, nz, n, slab)
        return lax.psum_scatter(both, GROUP, scatter_dimension=0, tiled=False)

    def sum_small(values, axes):
        for axis in axes:
            if axis == "z":
                for bit in (1, 2):
                    values = values + lax.ppermute(values, "z", [(i, i ^ bit) for i in range(nz)])
            elif axis == "q":
                values = lax.psum(values, "q") if nq > 1 else values
            else:
                values = values + swap(values, axis)
        return values

    stacked = jnp.stack([w_query, w_key, w_value]).reshape(3, slab, nz, ny, HDIM)
    stacked = stacked.transpose(2, 3, 0, 4, 1).reshape(nz, ny * head, slab)
    both_gains = jnp.concatenate(
        [gain_attn[None], gain_ffn[None], jnp.zeros((EXTRA - 2, slab), BF16)], axis=0
    )
    both_gains = jnp.broadcast_to(both_gains[None], (nz, EXTRA, slab))
    stacked = jnp.concatenate([stacked, both_gains], axis=1)
    z1, x0, c0, stacked, segment_ids, parents = together(
        ring(hidden_in, nz),
        swap(hidden_in, "x"),
        swap(hidden_in, "c"),
        stacked,
        segment_ids,
        parents,
    )

    ancestor, starts, parent_len, ancestor_len = segment_tables(segment_ids, parents)
    q_blocks = [(z * nq + qi) * ny + (yi ^ dy) for dy in range(ny) for z in zs]
    k_blocks = [(z * nq + q) * ny + (yi ^ dy) for q in range(nq) for dy in range(ny) for z in zs]
    segments = segment_ids.reshape(-1, rows)
    k_seg = jnp.stack([take(segments, b) for b in k_blocks])
    k_pos = jnp.stack(k_blocks).astype(jnp.int32)
    q_tiles, k_tiles = len(q_blocks), len(k_blocks)
    of_queries = lambda a: lax.dynamic_slice_in_dim(a, qi * q_tiles, q_tiles, 0)
    flat = k_seg.reshape(-1)
    labels = jnp.arange(-(-parents.shape[0] // 16) * 16, dtype=jnp.int32)[None, :, None]
    places = k_pos[:, None] * rows + jnp.arange(rows, dtype=jnp.int32)[None]
    places = places + lookup(parent_len + ancestor_len - starts, flat).reshape(k_tiles, rows)
    k_own = labels == k_seg[:, None]
    q_seen = of_queries(
        k_own
        | (labels == lookup(parents, flat).reshape(k_tiles, 1, rows))
        | (labels == lookup(ancestor, flat).reshape(k_tiles, 1, rows))
    )
    q_mask = jnp.where(q_seen, 0.0, masked_fill).astype(BF16)
    k_mask = k_own.astype(BF16)
    q_pos = of_queries(k_pos)
    shown = jnp.any(jnp.any(q_seen, axis=2)[:, None] & jnp.any(k_own, axis=2)[None], axis=2)
    shown = shown & (k_pos[None, :] <= q_pos[:, None])
    number = jnp.arange(k_tiles, dtype=jnp.int32)
    earlier = number[None, None, :] < number[None, :, None]
    before = jnp.sum((shown[:, None, :] & earlier).astype(jnp.int32), axis=2)
    chosen = shown[:, None, :] & (before[:, None, :] == number[None, :, None])
    visible = jnp.sum(jnp.where(chosen, number[None, None, :], 0), axis=2, dtype=jnp.int32)
    slots = jnp.stack([z * ny + (yi ^ dy) for dy in range(ny) for z in zs]).astype(jnp.int32)
    q_info = jnp.concatenate([q_pos, slots, (qi * q_tiles).reshape(1).astype(jnp.int32)])
    tables = (
        visible.reshape(-1),
        jnp.sum(shown.astype(jnp.int32), axis=1, dtype=jnp.int32),
        q_info,
        k_pos,
    )
    frequency = rope_base ** (-2.0 * jnp.arange(HALF, dtype=F32) / HDIM)
    angles = places.astype(F32)[:, None, :] * frequency[None, :, None]
    cosine, sine = jnp.cos(angles), jnp.sin(angles)
    cos_q, sin_q = of_queries(cosine), of_queries(sine)

    z2, x1, c1, cx0, w_qkv, (tables, q_mask, k_mask, cosine, sine, cos_q, sin_q) = together(
        ring(z1, nz),
        swap(z1, "x"),
        swap(z1, "c"),
        swap(x0, "c"),
        spread_z(stacked),
        (tables, q_mask, k_mask, cosine, sine, cos_q, sin_q),
    )
    z3, x2, c2, cx1, w_qkv, w_gate_, cotangent_, w_out_ = together(
        ring(z2, nz),
        swap(z2, "x"),
        swap(z2, "c"),
        swap(x1, "c"),
        gather_lanes(w_qkv),
        w_gate,
        cotangent,
        w_out,
    )
    x3, c3, cx2 = swap(z3, "x"), swap(z3, "c"), swap(x2, "c")
    x_chunks = [
        (hidden_in, c0, x0, cx0),
        (z1, c1, x1, cx1),
        (z2, c2, x2, cx2),
        (z3, c3, x3, swap(x3, "c")),
    ]
    gains = [w[:, ny * head : ny * head + 2].astype(F32) for w in w_qkv]
    gains = jnp.stack([pick(flip, *gains), pick(flip, gains[1], gains[0])], axis=1)
    gains = gains.transpose(2, 0, 1, 3).reshape(2, width)
    gain1, gain2 = gains[:1], gains[1:]

    wo = lax.all_gather(w_out_, WIDE, axis=0, tiled=False)
    if nq > 1:
        wo = wo.reshape(nz * 2, groups // 2, -1, slab).transpose(0, 2, 1, 3)
        wo = wo.reshape(nz * 2, -1, half)
    of_units = lambda w: spread_z(w.reshape(slab, nz, units).transpose(1, 0, 2))
    cot = lax.all_gather(cotangent_, ("z", *NARROW), axis=0, tiled=False)

    buffers, mine, theirs, scale1 = None, [], [], []
    for s in range(nz):
        normed1, own, other, scale = chunk_call(
            qkv_kernel,
            "qkv",
            5,
            where[s],
            s,
            [(a, "whole") for a in (*x_chunks[s], gain1, *w_qkv, cos_q[s], sin_q[s])],
            buffers,
            [((group_rows, width), "chunk")],
            [shape((head, rows), BF16), shape((head, rows), BF16), shape((rows, 1), F32)],
        )
        buffers = [normed1]
        mine.append(own)
        theirs.append(swap(other, "y"))
        scale1.append(scale)
    tiles, gate_parts, w_up_, w_down_ = together(
        mine + theirs, of_units(w_gate_), w_up, w_down.T
    )
    if nq > 1:
        tiles = [lax.all_gather(jnp.stack(tiles), "q", axis=0, tiled=True)]
    (att_low, att, log_norm, peak), up_parts, w_gates, w_down_ = together(
        attend(tables, tiles, q_mask, k_mask), of_units(w_up_), gather_rows(gate_parts), w_down_
    )

    att_t = lax.all_to_all(att_low, ("z", "y"), split_axis=0, concat_axis=0, tiled=True)
    att_t, w_down_ = together(att_t, w_down_)
    att_t = att_t.reshape(nz * ny * HDIM, rows)
    keep, send = small_call(
        project_kernel,
        "project",
        4,
        where[0],
        (att_t, wo),
        [shape((2, rows, cols), BF16)] * 2,
    )
    residual_mid = hidden_in.astype(F32) + scatter_narrow(keep, send)
    down_parts = of_units(w_down_)
    mid_block = residual_mid.astype(BF16)

    def forward(s, pieces, buffers):
        results = chunk_call(
            ffn_kernel,
            "feed_forward",
            7,
            where[s],
            s,
            [(a, "whole") for a in (*pieces, gain2)] + [(w, "there") for w in (*w_gates, *w_ups)],
            buffers,
            [((group_rows, width), "chunk"), ((group_rows, units), "chunk")],
            [shape((rows, units), F32)] * 2 + [shape((rows, 1), F32)],
            held=True,
        )
        return results[:2], results[2:]

    def backward(s, normed2, hidden, kept, buffers):
        results = chunk_call(
            ffn_back_kernel,
            "feed_forward_back",
            10,
            where[s],
            s,
            [(cot, "place"), (normed2, "chunk"), (hidden, "chunk")]
            + [(a, "whole") for a in kept[:2]]
            + [(w, "there") for w in (*w_downs, *w_gates, *w_ups)],
            buffers,
            [
                ((group_rows, width), "chunk"),
                ((group_rows, units), "chunk"),
                ((group_rows, units), "chunk"),
                ((nz * nx * nc, rows, cols), "place"),
            ],
            [shape((2, rows + EXTRA, cols), BF16)] * 2 + [shape((1, width), F32)],
            held=True,
        )
        return results[:4], results[4:]

    z0 = mid_block
    z1, x0, c0, up_a = together(
        ring(z0, nz), swap(z0, "x"), swap(z0, "c"), swap_part(up_parts, 0)
    )
    z2, x1, c1, cx0, up_b, down_parts = together(
        ring(z1, nz),
        swap(z1, "x"),
        swap(z1, "c"),
        swap(x0, "c"),
        swap_part(up_parts, 1),
        down_parts,
    )
    w_ups = join_rows(up_parts, (up_a, up_b))
    z3, x2, c2, cx1, down_a, (saved, kept0) = together(
        ring(z2, nz),
        swap(z2, "x"),
        swap(z2, "c"),
        swap(x1, "c"),
        swap_part(down_parts, 0),
        forward(0, (z0, c0, x0, cx0), None),
    )
    x3, c3, cx2, down_b, (saved, kept1) = together(
        swap(z3, "x"),
        swap(z3, "c"),
        swap(x2, "c"),
        swap_part(down_parts, 1),
        forward(1, (z1, c1, x1, cx1), saved),
    )
    w_downs = join_rows(down_parts, (down_a, down_b))
    saved, kept2 = forward(2, (z2, c2, x2, cx2), saved)
    cx3, saved, kept2, (buffers, part1) = together(
        swap(x3, "c"), saved, kept2, backward(1, *saved, kept1, None)
    )
    saved, kept3 = forward(3, (z3, c3, x3, cx3), saved)
    got1, saved, kept3, (buffers, part2) = together(
        swap(part1[1], "c"), saved, kept3, backward(2, *saved, kept2, buffers)
    )
    normed2, hidden = saved
    own1, send1 = first_sum(part1[0], got1)
    own1, got1, got2, (buffers, part3) = together(
        own1,
        swap(send1, "x"),
        swap(part2[1], "c"),
        backward(3, *saved, kept3, buffers),
    )
    own2, send2 = first_sum(part2[0], got2)
    sum1 = (own1 + got1.astype(F32)).astype(BF16)
    carried, own2, got2, got3, (buffers, part0) = together(
        ring(sum1, nz),
        own2,
        swap(send2, "x"),
        swap(part3[1], "c"),
        backward(0, *saved, kept0, buffers),
    )
    cot_rows, grad_gate_lin, grad_up_lin, out_parts = buffers
    own3, send3 = first_sum(part3[0], got3)
    sum2 = (own2 + got2.astype(F32) + carried.astype(F32)).astype(BF16)
    carried, own3, got3, got0, down = together(
        ring(sum2, nz),
        own3,
        swap(send3, "x"),
        swap(part0[1], "c"),
        dot(cot_rows, hidden, 0, 0).astype(BF16),
    )
    own0, send0 = first_sum(part0[0], got0)
    sum3 = (own3 + got3.astype(F32) + carried.astype(F32)).astype(BF16)
    carried, own0, got0, gate, down_got, grad_up_lin = together(
        ring(sum3, nz),
        own0,
        swap(send0, "x"),
        dot(normed2, grad_gate_lin, 0, 0).astype(BF16),
        exchange_rows(down),
        grad_up_lin,
    )
    summed2 = own0 + got0.astype(F32) + carried.astype(F32)
    scale2 = kept0[2]
    terms2 = part0[2] + part1[2] + part2[2] + part3[2]

    def norm_back(summed, gain, block, rstd):
        gain = lax.dynamic_slice_in_dim(gain, own_columns * cols, cols, 1)
        mean = summed[rows, :rows].reshape(rows, 1) / width
        return rstd * (summed[:rows] * gain - block.astype(F32) * rstd * mean)

    grad_mid = cotangent.astype(F32) + norm_back(summed2, gain2, mid_block, scale2)
    branch = grad_mid.astype(BF16)
    branch_x = swap(branch, "x")
    branch_c, branch_cx = swap(branch, "c"), swap(branch_x, "c")
    branch_x, branch_c, branch_cx, gate_got, up, terms2 = together(
        branch_x,
        branch_c,
        branch_cx,
        exchange_rows(gate),
        dot(normed2, grad_up_lin, 0, 0).astype(BF16),
        terms2,
    )
    down = add_rows(down, down_got)
    gate = add_rows(gate, gate_got)
    pieces = (branch, branch_c, branch_x, branch_cx)

    grad_att, wo_back = small_call(
        project_back_kernel,
        "project_back",
        6,
        where[0],
        (*pieces, att_t, wo),
        [shape(att_t.shape, BF16), shape(wo.shape, BF16)],
    )
    grad_att = grad_att.reshape(nz * ny, HDIM, rows)
    grad_att, up, terms2, got2, down, gate = together(
        lax.all_to_all(grad_att, ("z", "y"), split_axis=0, concat_axis=0, tiled=True),
        up,
        terms2,
        swap(terms2, "c"),
        down,
        gate,
    )
    terms2 = terms2 + got2
    back, down, up_got, gate, terms2, got2 = together(
        attend_back(tables, tiles, q_mask, k_mask, grad_att, att, log_norm, cosine, sine),
        spread_z(down),
        exchange_rows(up),
        gate,
        terms2,
        swap(terms2, "x"),
    )
    up = add_rows(up, up_got)
    peak_slots = jnp.zeros((1, nz * groups), F32)
    peak_slots = lax.dynamic_update_slice(
        peak_slots, jnp.max(peak).reshape(1, 1), (0, zi * groups + group)
    )
    terms2 = sum_small(jnp.concatenate([terms2 + got2, peak_slots], axis=1), ("q",))
    if nq > 1:
        grad_q = of_queries(back)[:, :HDIM]
        grad_kv = lax.psum_scatter(back[:, HDIM:], "q", scatter_dimension=0, tiled=True)
        back = jnp.concatenate([grad_q, grad_kv], axis=1)
    def qkv_back(s, place):
        chunk = pl.BlockSpec((1, head, rows), lambda i, where: (s, 0, 0))
        specs = {0: pl.BlockSpec((rows, width), lambda i, where: (s, 0)), 1: chunk, 2: chunk}
        return small_call(
            qkv_back_kernel,
            "qkv_back",
            5,
            place,
            (normed1, back, other_back, *w_qkv),
            [shape((2, rows + EXTRA, cols), BF16)] * 2 + [shape((1, width), F32)],
            specs,
        )

    other_back, place, gate, got2 = together(
        swap(back[nz:], "y"), where[1], gate, swap(terms2, "y")
    )
    terms2 = terms2 + got2
    part1, place = together(qkv_back(1, place), where[2])
    got1, part2, gate, up, place, got2 = together(
        swap(part1[1], "c"),
        qkv_back(2, place),
        spread_z(gate),
        up,
        where[3],
        lax.ppermute(terms2, "z", [(i, i ^ 1) for i in range(nz)]),
    )
    terms2 = terms2 + got2
    own1, send1 = first_sum(part1[0], got1)
    own1, got1, got2, part3, qkv_grads, place, got_terms = together(
        own1,
        swap(send1, "x"),
        swap(part2[1], "c"),
        qkv_back(3, place),
        small_call(
            qkv_weights_kernel,
            "qkv_weights",
            8,
            place,
            (normed1, back, other_back),
            [shape((nz, ny * head, half), BF16)] * 2,
        ),
        where[0],
        lax.ppermute(terms2, "z", [(i, i ^ 2) for i in range(nz)]),
    )
    terms2 = terms2 + got_terms
    terms2, peaks = terms2[:, :width], terms2[0, width:]
    own2, send2 = first_sum(part2[0], got2)
    sum1 = (own1 + got1.astype(F32)).astype(BF16)
    carried, own2, got2, got3, part0, qkv_own, qkv_got, up = together(
        ring(sum1, nz),
        own2,
        swap(send2, "x"),
        swap(part3[1], "c"),
        qkv_back(0, place),
        qkv_grads[0],
        exchange_lanes(qkv_grads[1]),
        spread_z(up),
    )
    qkv_grads = spread_z(scatter_lanes(qkv_own, qkv_got))
    own3, send3 = first_sum(part3[0], got3)
    sum2 = (own2 + got2.astype(F32) + carried.astype(F32)).astype(BF16)
    terms1 = part0[2] + part1[2] + part2[2] + part3[2]
    terms1 = terms1 + swap(terms1, "c")
    carried, own3, got3, got0, terms1, terms1_x = together(
        ring(sum2, nz),
        own3,
        swap(send3, "x"),
        swap(part0[1], "c"),
        terms1,
        swap(terms1, "x"),
    )
    own0, send0 = first_sum(part0[0], got0)
    sum3 = (own3 + got3.astype(F32) + carried.astype(F32)).astype(BF16)
    terms1 = sum_small(terms1 + terms1_x, ("y", "q"))
    terms1_z = lax.ppermute(terms1, "z", [(i, i ^ 1) for i in range(nz)])
    carried, own0, got0, terms1, terms1_z = together(
        ring(sum3, nz), own0, swap(send0, "x"), terms1, terms1_z
    )
    terms1 = terms1 + terms1_z
    terms1 = terms1 + lax.ppermute(terms1, "z", [(i, i ^ 2) for i in range(nz)])
    summed1 = own0 + got0.astype(F32) + carried.astype(F32)
    grad_in = (grad_mid + norm_back(summed1, gain1, hidden_in, scale1[0])).astype(BF16)

    def laid_out(kernel, time, parts, *dims):
        return small_call(kernel, "lay_out", time, where[0], (parts,), [shape(d, F32) for d in dims])

    [grad_wd] = laid_out(turned_kernel, 3, down, (nz * units, slab))
    [grad_wg] = laid_out(columns_kernel, 2, gate, (slab, nz * units))
    [grad_wu] = laid_out(columns_kernel, 2, up, (slab, nz * units))
    branch_ffn = lax.psum_scatter(out_parts, ("z", *NARROW), scatter_dimension=0, tiled=False)
    hidden_out = (residual_mid + branch_ffn.astype(F32)).astype(BF16)
    if nq > 1:
        wo_back = wo_back.reshape(nz * 2, -1, groups // 2, slab).transpose(0, 2, 1, 3)
        wo_back = wo_back.reshape(nz * groups, -1, slab)
    grad_wo = lax.psum_scatter(wo_back, WIDE, scatter_dimension=0, tiled=False).astype(F32)
    grad_qkv = laid_out(qkv_out_kernel, 3, qkv_grads, *[(slab, nz * ny * HDIM)] * 3)

    gain_terms = jnp.concatenate([terms1, terms2], axis=0).reshape(2, 2, nz, half)
    gain_terms = gain_terms.transpose(0, 2, 1, 3).reshape(2, width) / gains
    terms = lax.dynamic_slice_in_dim(gain_terms, (zi * groups + group) * slab, slab, 1)
    peaks = peaks.reshape(nz, nq, ny)
    head_peaks = jnp.max(peaks, axis=1).reshape(nz * ny)
    factor = jnp.sqrt(clip_limit / jnp.maximum(head_peaks, clip_limit))
    column_factor = jnp.repeat(factor, HDIM)
    return (
        hidden_out,
        grad_in,
        grad_qkv[0],
        grad_qkv[1],
        grad_qkv[2],
        grad_wo,
        grad_wg,
        grad_wu,
        grad_wd,
        terms[0],
        terms[1],
        w_query.astype(F32) * column_factor[None, :],
        w_key.astype(F32) * column_factor[None, :],
        head_peaks,
    )


def solution(mesh):
    wide, narrow = mesh.devices.shape
    sizes = (4, wide // 8, 2, narrow // 2, 2)
    fine = Mesh(mesh.devices.reshape(sizes), ("z", "q", "y", "x", "c"))
    both = P(WIDE, NARROW)
    turned = P(NARROW, WIDE)
    return jax.shard_map(
        functools.partial(on_device, sizes),
        mesh=fine,
        in_specs=(
            both, P(WIDE), both, both, both, turned, P(WIDE), both, both, turned, both, P(), P()
        ),
        out_specs=(
            both, both, both, both, both, turned, both, both, turned,
            P(WIDE), P(WIDE), both, both, P(NARROW),
        ),
        check_vma=False,
    )
```

time: 764 us -> 668 us (0.87)
  local copies, waits for them, and re-layouts: 121 us -> 28.5 us
  Pallas kernels: 126 us -> 193 us
  other arithmetic: 76.3 us -> 46.2 us
  waiting for transfers between devices: 254 us -> 232 us
  starting transfers between devices: 123 us -> 107 us
  matrix products: 24.5 us -> 15 us
  blocking collectives: 16.5 us -> 24.9 us
    all_to_all x8, waiting for transfers between devices: 23.6 us -> 73.2 us  [spread_z(): return lax.all_to_all(parts, 'z', split_axis=0, concat_axis=0, tiled=True)]
    unnamed x363 -> x169, local copies, waits for them, and re-layouts: 54.5 us -> 9.88 us
    pallas_call x6 -> x11, Pallas kernels: 21.3 us -> 55 us  [small_call(): pl.pallas_call(kernel, grid_spec=pltpu.PrefetchScalarGridSpec(num_scalar_...]
    pallas_call x8 -> x12, Pallas kernels: 64.8 us -> 97.5 us  [chunk_call(): pl.pallas_call(kernel, grid_spec=pltpu.PrefetchScalarGridSpec(num_scalar_...]
    ppermute x86 -> x66, waiting for transfers between devices: 121 us -> 89.1 us  [swap(): return lax.ppermute(array, axis, [(0, 1), (1, 0)])]
    ppermute x18 -> x12, waiting for transfers between devices: 66.9 us -> 40.3 us  [ring(): return lax.ppermute(array, 'z', [(i, (i + 1) % size) for i in range(size)])]
    all_to_all x1, waiting for transfers between devices: 26.5 us -> 6.85 us  [on_device(): lax.all_to_all(grad_att, ('z', 'y'), split_axis=0, concat_axis=0, tiled=T...]
    reshape x7 -> x3, local copies, waits for them, and re-layouts: 21.7 us -> 3.54 us  [on_device(): of_units = lambda w: spread_z(w.reshape(slab, nz, units).transpose(1, 0, 2))]
  transfers between devices with their start and end apart: 121 -> 95, of which waited for: 32 -> 41; matrix products, arithmetic and copies ran while one was open for 24% -> 12% of each run, Pallas kernels for 17% -> 28%
where the time goes in v2:
time: 668 us; the launch traced here: 662 us
  waiting for transfers between devices  232 us (35%)
  Pallas kernels  193 us (29%)
  starting transfers between devices  107 us (16%)
  other arithmetic  46.2 us (7%)
  local copies, waits for them, and re-layouts  28.5 us (4%)
  blocking collectives  24.9 us (4%)
  between operations  15.7 us (2%)
  matrix products  15 us (2%)
    pallas_call x12, Pallas kernels, chunk_call(): pl.pallas_call(kernel, grid_spec=pltpu.PrefetchScalarGridSpec(num_scalar_...  97.5 us
    ppermute x66, waiting for transfers between devices, swap(): return lax.ppermute(array, axis, [(0, 1), (1, 0)])  89.1 us
    all_to_all x8, waiting for transfers between devices, spread_z(): return lax.all_to_all(parts, 'z', split_axis=0, concat_axis=0, tiled=True)  73.2 us
    pallas_call x11, Pallas kernels, small_call(): pl.pallas_call(kernel, grid_spec=pltpu.PrefetchScalarGridSpec(num_scalar_...  55 us
    ppermute x66, starting transfers between devices, swap(): return lax.ppermute(array, axis, [(0, 1), (1, 0)])  44.3 us
    ppermute x12, waiting for transfers between devices, ring(): return lax.ppermute(array, 'z', [(i, (i + 1) % size) for i in range(size)])  40.3 us
    all_to_all x8, starting transfers between devices, spread_z(): return lax.all_to_all(parts, 'z', split_axis=0, concat_axis=0, tiled=True)  33.1 us
    all_to_all x1, blocking collectives, on_device(): lax.all_to_all(att_low, ('z', 'y'), split_axis=0, concat_axis=0, tiled=True)  24.9 us
  transfers between devices with their start and end apart: 95, of which 41 were waited for; matrix products, arithmetic and copies ran while one was open for 12% of the time, Pallas kernels for 28%

profile of v2, /device:TPU:0, one launch (start us, length us, event | category | flops | bytes accessed | tf_op | source)
XLA Modules:
  0.0 661.8 jit_solution(8880657723576567722)
XLA Ops:
  23.9 5.1 all-to-all-start
  37.7 16.5 %all-to-all-done.refs_5_.w_first = bf16[4,400,256]{2,1,0:T(8,128)(2,1)S(1)} async-done(((bf16[4,400,256]{2,1,0:T(8,128)(2,1)}), bf16[4,400,256]{2,1,0:T(8,128)(2,1)S(1)}, u32[]{:S(2)}, u32[]{:S(2)}) %all-to-all-start) | async-done | bytes 819232 | tf_op jit(solution)/shard_map/all_to_all | solution.py:615
  58.4 9.2 %collective-permute-done.8.refs_2_ = bf16[384,512]{1,0:T(8,128)(2,1)} collective-permute-done((bf16[384,512]{1,0:T(8,128)(2,1)}, bf16[384,512]{1,0:T(8,128)(2,1)}, u32[]{:S(2)}, u32[]{:S(2)}) %collective-permute-start.8) | collective-permute-done | bytes 393248 | tf_op jit(solution)/shard_map/ppermute | solution.py:62
  85.5 5.7 qkv.4
  92.7 5.8 qkv.5
  99.0 5.7 qkv.6
  107.1 5.9 qkv.7
  114.3 8.4 %collective-permute-done.19.refs_7_ = bf16[192,384]{1,0:T(8,128)(2,1)S(1)} collective-permute-done((bf16[192,384]{1,0:T(8,128)(2,1)}, bf16[192,384]{1,0:T(8,128)(2,1)S(1)}, u32[]{:S(2)}, u32[]{:S(2)}) %collective-permute-start.19) | collective-permute-done | bytes 147488 | tf_op jit(solution)/shard_map/ppermute | solution.py:62
  132.5 18.3 %attend.1 = (bf16[8,64,384]{2,1,0:T(8,128)(2,1)}, f32[8,64,384]{2,1,0:T(8,128)}, f32[8,1,384]{2,1,0:T(1,128)}, f32[8,1,384]{2,1,0:T(1,128)}) custom-call(s32[64]{0:T(128)} %reshape.319.visible, s32[8]{0:T(128)} %get-tuple-element.303.counts, s32[17]{0:T(128)} %concatenate.23.q_pos, s32[8]{0:T(128)} %copy-done.61, ...), custom_call_target="tpu_custom_call" | custom-call | flops 17999998976 | bytes 1000 | tf_op jit(solution)/shard_map/attend/pallas_call | solution.py:165
  150.8 5.1 collective-permute-done.20
  155.9 13.2 %all-to-all-done.2 = bf16[4,256,512]{2,1,0:T(8,128)(2,1)S(1)} async-done(((bf16[4,256,512]{2,1,0:T(8,128)(2,1)}), bf16[4,256,512]{2,1,0:T(8,128)(2,1)S(1)}, u32[]{:S(2)}, u32[]{:S(2)}) %all-to-all-start.2) | async-done | bytes 1048608 | tf_op jit(solution)/shard_map/all_to_all | solution.py:615
  169.2 24.9 %all_to_all.50 = bf16[8,64,384]{2,1,0:T(8,128)(2,1)} all-to-all(bf16[8,64,384]{2,1,0:T(8,128)(2,1)} %get-tuple-element.349), channel_id=1, replica_groups=mesh['z'=4,'q'=1,'y'=2,'x'=2,'c'=2] {'z','y'}, dimensions={0} | all-to-all | bytes 786432 | tf_op jit(solution)/shard_map/all_to_all | solution.py:799
  206.9 9.5 %collective-permute-done.22 = bf16[384,512]{1,0:T(8,128)(2,1)S(1)} collective-permute-done((bf16[384,512]{1,0:T(8,128)(2,1)S(1)}, bf16[384,512]{1,0:T(8,128)(2,1)S(1)}, u32[]{:S(2)}, u32[]{:S(2)}) %collective-permute-start.22) | collective-permute-done | bytes 393248 | tf_op jit(solution)/shard_map/ppermute | solution.py:62
  220.4 8.0 %collective-permute-done.24.refs_2_ = bf16[384,512]{1,0:T(8,128)(2,1)} collective-permute-done((bf16[384,512]{1,0:T(8,128)(2,1)S(1)}, bf16[384,512]{1,0:T(8,128)(2,1)}, u32[]{:S(2)}, u32[]{:S(2)}) %collective-permute-start.24) | collective-permute-done | bytes 393248 | tf_op jit(solution)/shard_map/ppermute | solution.py:62
  228.4 6.1 collective-permute-done.23.refs_0_
  235.0 4.7 collective-permute-start.27
  239.8 9.5 %all-to-all-done.4 = bf16[4,256,512]{2,1,0:T(8,128)(2,1)S(1)} async-done(((bf16[4,256,512]{2,1,0:T(8,128)(2,1)}), bf16[4,256,512]{2,1,0:T(8,128)(2,1)S(1)}, u32[]{:S(2)}, u32[]{:S(2)}) %all-to-all-start.4) | async-done | bytes 1048608 | tf_op jit(solution)/shard_map/all_to_all | solution.py:615
  255.2 7.4 %feed_forward.4 = (bf16[1536,2048]{1,0:T(8,128)(2,1)}, bf16[1536,512]{1,0:T(8,128)(2,1)}, f32[384,512]{1,0:T(8,128)}, f32[384,512]{1,0:T(8,128)}, f32[384,1]{1,0:T(8,128)}) custom-call(s32[4]{0:T(128)} %get-tuple-element.541.where, bf16[384,512]{1,0:T(8,128)(2,1)} %copy-done.14, bf16[384,512]{1,0:T(8,128)(2,1)} %copy-done.67, ...), custom_call_target="tpu_custom_call" | custom-call | flops 7000000000 | bytes 1000 | tf_op jit(solution)/shard_map/feed_forward/pallas_call | solution.py:367
  269.8 7.4 %feed_forward.5 = (bf16[1536,2048]{1,0:T(8,128)(2,1)}, bf16[1536,512]{1,0:T(8,128)(2,1)}, f32[384,512]{1,0:T(8,128)}, f32[384,512]{1,0:T(8,128)}, f32[384,1]{1,0:T(8,128)}) custom-call(s32[4]{0:T(128)} %get-tuple-element.512.where, bf16[384,512]{1,0:T(8,128)(2,1)} %collective-permute-done.23.refs_0_, ...), custom_call_target="tpu_custom_call", output_to_operand_aliasing={{0}: (11, {}), {1}: (12, {})} | custom-call | flops 7000000000 | bytes 1000 | tf_op jit(solution)/shard_map/feed_forward/pallas_call | solution.py:367
  280.0 7.4 %feed_forward.6 = (bf16[1536,2048]{1,0:T(8,128)(2,1)}, bf16[1536,512]{1,0:T(8,128)(2,1)}, f32[384,512]{1,0:T(8,128)}, f32[384,512]{1,0:T(8,128)}, f32[384,1]{1,0:T(8,128)}) custom-call(s32[4]{0:T(128)} %get-tuple-element.520.where, bf16[384,512]{1,0:T(8,128)(2,1)} %collective-permute-done.27.refs_0_, ...), custom_call_target="tpu_custom_call", output_to_operand_aliasing={{0}: (11, {}), {1}: (12, {})} | custom-call | flops 7000000000 | bytes 1000 | tf_op jit(solution)/shard_map/feed_forward/pallas_call | solution.py:367
  287.4 11.2 %feed_forward_back.4 = (bf16[1536,2048]{1,0:T(8,128)(2,1)}, bf16[1536,512]{1,0:T(8,128)(2,1)}, bf16[1536,512]{1,0:T(8,128)(2,1)}, bf16[16,384,512]{2,1,0:T(8,128...) custom-call(s32[4]{0:T(128)} %get-tuple-element.512.where, ...), custom_call_target="tpu_custom_call" | custom-call | flops 10000000000 | bytes 1000 | tf_op jit(solution)/shard_map/feed_forward_back/pallas_call | solution.py:367
  299.4 7.5 %feed_forward.7 = (bf16[1536,2048]{1,0:T(8,128)(2,1)}, bf16[1536,512]{1,0:T(8,128)(2,1)}, f32[384,512]{1,0:T(8,128)}, f32[384,512]{1,0:T(8,128)}, f32[384,1]{1,0:T(8,128)}) custom-call(s32[4]{0:T(128)} %get-tuple-element.529.where, bf16[384,512]{1,0:T(8,128)(2,1)} %collective-permute-done.32.refs_0_, ...), custom_call_target="tpu_custom_call", output_to_operand_aliasing={{0}: (11, {}), {1}: (12, {})} | custom-call | flops 7000000000 | bytes 1000 | tf_op jit(solution)/shard_map/feed_forward/pallas_call | solution.py:367
  306.9 11.2 %feed_forward_back.5 = (bf16[1536,2048]{1,0:T(8,128)(2,1)}, bf16[1536,512]{1,0:T(8,128)(2,1)}, bf16[1536,512]{1,0:T(8,128)(2,1)}, bf16[16,384,512]{2,1,0:T(8,128...) custom-call(s32[4]{0:T(128)} %get-tuple-element.520.where, ...), custom_call_target="tpu_custom_call", output_to_operand_aliasing={{0}: (14, {}), {1}: (15, {}), {2}: (16, {}), {3}: (17, {})} | custom-call | flops 10000000000 | bytes 1000 | tf_op jit(solution)/shard_map/feed_forward_back/pallas_call | solution.py:367
  319.2 11.1 %feed_forward_back.6 = (bf16[1536,2048]{1,0:T(8,128)(2,1)}, bf16[1536,512]{1,0:T(8,128)(2,1)}, bf16[1536,512]{1,0:T(8,128)(2,1)}, bf16[16,384,512]{2,1,0:T(8,128...) custom-call(s32[4]{0:T(128)} %get-tuple-element.529.where, ...), custom_call_target="tpu_custom_call", output_to_operand_aliasing={{0}: (14, {}), {1}: (15, {}), {2}: (16, {}), {3}: (17, {})} | custom-call | flops 10000000000 | bytes 1000 | tf_op jit(solution)/shard_map/feed_forward_back/pallas_call | solution.py:367
  335.7 11.2 %feed_forward_back.7 = (bf16[1536,2048]{1,0:T(8,128)(2,1)}, bf16[1536,512]{1,0:T(8,128)(2,1)}, bf16[1536,512]{1,0:T(8,128)(2,1)}, bf16[16,384,512]{2,1,0:T(8,128...) custom-call(s32[4]{0:T(128)} %get-tuple-element.541.where, ...), custom_call_target="tpu_custom_call", output_to_operand_aliasing={{0}: (14, {}), {1}: (15, {}), {2}: (16, {}), {3}: (17, {})} | custom-call | flops 10000000000 | bytes 1000 | tf_op jit(solution)/shard_map/feed_forward_back/pallas_call | solution.py:367
  351.6 6.7 %convolution_convert_fusion.2 = bf16[2048,512]{1,0:T(8,128)(2,1)S(1)} fusion(bf16[1536,2048]{1,0:T(8,128)(2,1)} %get-tuple-element.470, bf16[1536,512]{1,0:T(8,128)(2,1)S(1)} %copy-done.3), kind=kOutput, calls=%fused_computation.2 | convolution fusion | flops 3222274048 | bytes 9961472 | tf_op jit(solution)/shard_map/dot_general | solution.py:52
  369.9 5.9 collective-permute-done.51
  375.8 12.5 %collective-permute-done.53 = bf16[1024,512]{1,0:T(8,128)(2,1)S(1)} collective-permute-done((bf16[1024,512]{1,0:T(8,128)(2,1)S(1)}, bf16[1024,512]{1,0:T(8,128)(2,1)S(1)}, u32[]{:S(2)}, u32[]{:S(2)}) %collective-permute-start.53) | collective-permute-done | bytes 1048608 | tf_op jit(solution)/shard_map/ppermute | solution.py:62
  392.6 5.3 collective-permute-done.54.p2
  397.9 4.7 convolution_convert_fusion
  404.1 9.5 %collective-permute-done.57 = bf16[1024,512]{1,0:T(8,128)(2,1)} collective-permute-done((bf16[1024,512]{1,0:T(8,128)(2,1)S(1)}, bf16[1024,512]{1,0:T(8,128)(2,1)}, u32[]{:S(2)}, u32[]{:S(2)}) %collective-permute-start.57) | collective-permute-done | bytes 1048608 | tf_op jit(solution)/shard_map/ppermute | solution.py:62
  413.6 6.6 %project_back.1 = (bf16[512,384]{1,0:T(8,128)(2,1)}, bf16[8,512,256]{2,1,0:T(8,128)(2,1)}) custom-call(s32[4]{0:T(128)} %get-tuple-element.541.where, bf16[384,512]{1,0:T(8,128)(2,1)} %copy-done.43, bf16[384,512]{1,0:T(8,128)(2,1)} %copy-done.75, bf16[384,512]{1,0:T(8,128)(2,1)} %copy-done.73, bf16[384,512]{1,0:T(8,128)(2,1)} %copy-done.76, ...), custom_call_target="tpu_custom_call" | custom-call | flops 6000000000 | bytes 1000 | tf_op jit(solution)/shard_map/project_back/pallas_call | solution.py:558
  420.3 6.1 all-to-all-start.5
  433.9 6.9 %all-to-all-done.5.refs_10_ = bf16[8,64,384]{2,1,0:T(8,128)(2,1)S(1)} async-done(((bf16[8,64,384]{2,1,0:T(8,128)(2,1)}), bf16[8,64,384]{2,1,0:T(8,128)(2,1)S(1)}, u32[]{:S(2)}, u32[]{:S(2)}) %all-to-all-start.5) | async-done | bytes 393248 | tf_op jit(solution)/shard_map/all_to_all | solution.py:960
  449.6 22.3 %attend_back.1.mine.refs_0_ = bf16[8,192,384]{2,1,0:T(8,128)(2,1)} custom-call(s32[64]{0:T(128)} %reshape.319.visible, s32[8]{0:T(128)} %get-tuple-element.303.counts, s32[17]{0:T(128)} %concatenate.23.q_pos, s32[8]{0:T(128)} %copy-done.61, bf16[192,384]{1,0:T(8,128)(2,1)} %get-tuple-element.332.refs_0_, bf16[192,384]{1,0:T(8,128)(2,1)} %get-tuple-element.333.refs_1_, ...), custom_call_target="tpu_custom_call" | custom-call | flops 22000001024 | bytes 1000 | tf_op jit(solution)/shard_map/attend_back/pallas_call | solution.py:250
  484.2 6.4 collective-permute-done.62
  495.2 5.3 qkv_back.4
  502.5 5.3 qkv_back.5
  507.8 5.2 reduce-scatter.5.cloned.1.call-done
  516.9 8.8 %all-to-all-done.7.parts = bf16[4,256,512]{2,1,0:T(8,128)(2,1)S(1)} async-done(((bf16[4,256,512]{2,1,0:T(8,128)(2,1)}), bf16[4,256,512]{2,1,0:T(8,128)(2,1)S(1)}, u32[]{:S(2)}, u32[]{:S(2)}) %all-to-all-start.7) | async-done | bytes 1048608 | tf_op jit(solution)/shard_map/all_to_all | solution.py:615
  536.5 8.4 %qkv_weights.1 = (bf16[4,384,256]{2,1,0:T(8,128)(2,1)}, bf16[4,384,256]{2,1,0:T(8,128)(2,1)}) custom-call(s32[4]{0:T(128)} %get-tuple-element.529.where, bf16[1536,2048]{1,0:T(8,128)(2,1)} %get-tuple-element.513.normed, bf16[8,192,384]{2,1,0:T(8,128)(2,1)} %attend_back.1.mine.refs_0_, bf16[4,192,384]{2,1,0:T(8,128)(2,1)} %copy-done.63), custom_call_target="tpu_custom_call" | custom-call | flops 8000000000 | bytes 1000 | tf_op jit(solution)/shard_map/qkv_weights/pallas_call | solution.py:558
  544.8 5.9 qkv_back.6
  555.3 14.0 %collective-permute-done.67 = f32[1,2056]{1,0:T(1,128)S(1)} collective-permute-done((f32[1,2056]{1,0:T(1,128)S(1)}, f32[1,2056]{1,0:T(1,128)S(1)}, u32[]{:S(2)}, u32[]{:S(2)}) %collective-permute-start.67) | collective-permute-done | bytes 8256 | tf_op jit(solution)/shard_map/ppermute | solution.py:1028
  576.5 5.4 qkv_back.7
  581.9 7.9 %collective-permute-done.68 = bf16[400,512]{1,0:T(8,128)(2,1)} collective-permute-done((bf16[400,512]{1,0:T(8,128)(2,1)}, bf16[400,512]{1,0:T(8,128)(2,1)}, u32[]{:S(2)}, u32[]{:S(2)}) %collective-permute-start.68) | collective-permute-done | bytes 409632 | tf_op jit(solution)/shard_map/ppermute | solution.py:66
  598.2 4.8 all-to-all-start.9
  609.7 6.3 collective-permute-done.72
  624.9 19.6 %all-to-all-done.9.parts = bf16[4,384,256]{2,1,0:T(8,128)(2,1)S(1)} async-done(((bf16[4,384,256]{2,1,0:T(8,128)(2,1)}), bf16[4,384,256]{2,1,0:T(8,128)(2,1)S(1)}, u32[]{:S(2)}, u32[]{:S(2)}) %all-to-all-start.9) | async-done | bytes 786464 | tf_op jit(solution)/shard_map/all_to_all | solution.py:615
  (474 shorter events, 220.4 us)
Async XLA Ops:
  23.9 30.4 %all-to-all-start = ((bf16[4,400,256]{2,1,0:T(8,128)(2,1)}), bf16[4,400,256]{2,1,0:T(8,128)(2,1)S(1)}, u32[]{:S(2)}, u32[]{:S(2)}) async-start(bf16[4,400,256]{2,1,0:T(8,128)(2,1)} %pad_maximum_fusion), calls=%async_computation | async-start | bytes 1638400 | tf_op jit(solution)/shard_map/all_to_all | solution.py:615
  29.0 165.0 %all-gather.5.cloned.1.call-start = ((), (), s32[]{:S(2)}) async-start(), calls=%async_computation.14 | async-start | bytes 2359296 | tf_op jit(solution)/shard_map/all_gather | solution.py:766
  54.2 20.3 %collective-permute-start.11 = (bf16[4,400,256]{2,1,0:T(8,128)(2,1)S(1)}, bf16[4,400,256]{2,1,0:T(8,128)(2,1)}, u32[]{:S(2)}, u32[]{:S(2)}) collective-permute-start(bf16[4,400,256]{2,1,0:T(8,128)(2,1)S(1)} %all-to-all-done.refs_5_.w_first), channel_id=1, source_target_pairs={{0,4},{4,0},{1,5},{5,1},{2,6},{6,2},{3,7},{7,3},{8,12},{12,8},{9,1... | collective-permute-start | bytes 2457608 | tf_op jit(solution)/shard_map/ppermute | solution.py:62
  74.6 212.9 %all-gather.7.cloned.1.call-start = ((), (), s32[]{:S(2)}) async-start(), calls=%async_computation.15 | async-start | bytes 6684672 | tf_op jit(solution)/shard_map/all_gather | solution.py:771
  77.3 21.8 %collective-permute-start.14 = (bf16[384,512]{1,0:T(8,128)(2,1)}, bf16[384,512]{1,0:T(8,128)(2,1)S(1)}, u32[]{:S(2)}, u32[]{:S(2)}) collective-permute-start(bf16[384,512]{1,0:T(8,128)(2,1)} %collective-permute-done.7.refs_0_), channel_id=1, source_target_pairs={{0,2},{2,0},{1,3},{3,1},{4,6},{6,4},{5,7},{7,5},{8,10},{10,8},{9,1... | collective-permute-start | bytes 1179656 | tf_op jit(solution)/shard_map/ppermute | solution.py:62
  78.7 27.6 %collective-permute-start.13 = (bf16[384,512]{1,0:T(8,128)(2,1)}, bf16[384,512]{1,0:T(8,128)(2,1)}, u32[]{:S(2)}, u32[]{:S(2)}) collective-permute-start(bf16[384,512]{1,0:T(8,128)(2,1)} %collective-permute-done.7.refs_0_), channel_id=1, source_target_pairs={{0,1},{1,0},{2,3},{3,2},{4,5},{5,4},{6,7},{7,6},{8,9},{9,8},{10,11... | collective-permute-start | bytes 1179656 | tf_op jit(solution)/shard_map/ppermute | solution.py:62
  80.2 18.9 %collective-permute-start.12 = (bf16[384,512]{1,0:T(8,128)(2,1)}, bf16[384,512]{1,0:T(8,128)(2,1)}, u32[]{:S(2)}, u32[]{:S(2)}) collective-permute-start(bf16[384,512]{1,0:T(8,128)(2,1)} %collective-permute-done.8.refs_2_), channel_id=1, source_target_pairs={{0,1},{1,0},{2,3},{3,2},{4,5},{5,4},{6,7},{7,6},{8,9},{9,8},{10,11... | collective-permute-start | bytes 1179656 | tf_op jit(solution)/shard_map/ppermute | solution.py:62
  81.8 44.7 %all-to-all-start.1 = ((bf16[4,256,512]{2,1,0:T(8,128)(2,1)}), bf16[4,256,512]{2,1,0:T(8,128)(2,1)S(1)}, u32[]{:S(2)}, u32[]{:S(2)}) async-start(bf16[4,256,512]{2,1,0:T(8,128)(2,1)} %bitcast.160), calls=%async_computation.1 | async-start | bytes 2097152 | tf_op jit(solution)/shard_map/all_to_all | solution.py:615
  91.2 22.5 %collective-permute-start.16 = (bf16[192,384]{1,0:T(8,128)(2,1)}, bf16[192,384]{1,0:T(8,128)(2,1)S(1)}, u32[]{:S(2)}, u32[]{:S(2)}) collective-permute-start(bf16[192,384]{1,0:T(8,128)(2,1)} %get-tuple-element.327), channel_id=1, source_target_pairs={{0,4},{4,0},{1,5},{5,1},{2,6},{6,2},{3,7},{7,3},{8,12},{12,8},{9,1... | collective-permute-start | bytes 442376 | tf_op jit(solution)/shard_map/ppermute | solution.py:62
  98.5 15.2 %collective-permute-start.17 = (bf16[192,384]{1,0:T(8,128)(2,1)}, bf16[192,384]{1,0:T(8,128)(2,1)S(1)}, u32[]{:S(2)}, u32[]{:S(2)}) collective-permute-start(bf16[192,384]{1,0:T(8,128)(2,1)} %get-tuple-element.328), channel_id=1, source_target_pairs={{0,4},{4,0},{1,5},{5,1},{2,6},{6,2},{3,7},{7,3},{8,12},{12,8},{9,1... | collective-permute-start | bytes 442376 | tf_op jit(solution)/shard_map/ppermute | solution.py:62
  127.6 41.6 %all-to-all-start.2 = ((bf16[4,256,512]{2,1,0:T(8,128)(2,1)}), bf16[4,256,512]{2,1,0:T(8,128)(2,1)S(1)}, u32[]{:S(2)}, u32[]{:S(2)}) async-start(bf16[4,256,512]{2,1,0:T(8,128)(2,1)} %bitcast.158), calls=%async_computation.2 | async-start | bytes 2097152 | tf_op jit(solution)/shard_map/all_to_all | solution.py:615
  131.1 24.8 %collective-permute-start.20 = (bf16[4,256,512]{2,1,0:T(8,128)(2,1)S(1)}, bf16[4,256,512]{2,1,0:T(8,128)(2,1)S(1)}, u32[]{:S(2)}, u32[]{:S(2)}) collective-permute-start(bf16[4,256,512]{2,1,0:T(8,128)(2,1)S(1)} %all-to-all-done.1), channel_id=1, source_target_pairs={{0,4},{4,0},{1,5},{5,1},{2,6},{6,2},{3,7},{7,3},{8,12},{12,8},{9,1... | collective-permute-start | bytes 3145736 | tf_op jit(solution)/shard_map/ppermute | solution.py:62
  199.9 49.4 %all-to-all-start.4 = ((bf16[4,256,512]{2,1,0:T(8,128)(2,1)}), bf16[4,256,512]{2,1,0:T(8,128)(2,1)S(1)}, u32[]{:S(2)}, u32[]{:S(2)}) async-start(bf16[4,256,512]{2,1,0:T(8,128)(2,1)} %bitcast.40), calls=%async_computation.4 | async-start | bytes 2097152 | tf_op jit(solution)/shard_map/all_to_all | solution.py:615
  203.6 309.4 %reduce-scatter.5.cloned.1.call-start = ((), (), s32[]{:S(2)}) async-start(), calls=%async_computation.13 | async-start | bytes 2359296 | tf_op jit(solution)/shard_map/reduce_scatter | solution.py:1080
  205.2 15.1 %collective-permute-start.26 = (bf16[2,256,512]{2,1,0:T(8,128)(2,1)S(1)}, bf16[2,256,512]{2,1,0:T(8,128)(2,1)S(1)}, u32[]{:S(2)}, u32[]{:S(2)}) collective-permute-start(bf16[2,256,512]{2,1,0:T(8,128)(2,1)S(1)} %get-tuple-element.599), channel_id=1, source_target_pairs={{0,4},{4,0},{1,5},{5,1},{2,6},{6,2},{3,7},{7,3},{8,12},{12,8},{9,1... | collective-permute-start | bytes 1572872 | tf_op jit(solution)/shard_map/ppermute | solution.py:62
  217.1 17.4 %collective-permute-start.23 = (bf16[384,512]{1,0:T(8,128)(2,1)S(1)}, bf16[384,512]{1,0:T(8,128)(2,1)}, u32[]{:S(2)}, u32[]{:S(2)}) collective-permute-start(bf16[384,512]{1,0:T(8,128)(2,1)S(1)} %fusion.22.refs_0_), channel_id=1, source_target_pairs={{0,8},{8,16},{16,24},{24,0},{1,9},{9,17},{17,25},{25,1},{2,10},{10... | collective-permute-start | bytes 1179656 | tf_op jit(solution)/shard_map/ppermute | solution.py:66
  218.7 21.0 %collective-permute-start.31 = (bf16[2,256,512]{2,1,0:T(8,128)(2,1)S(1)}, bf16[2,256,512]{2,1,0:T(8,128)(2,1)S(1)}, u32[]{:S(2)}, u32[]{:S(2)}) collective-permute-start(bf16[2,256,512]{2,1,0:T(8,128)(2,1)S(1)} %get-tuple-element.598), channel_id=1, source_target_pairs={{0,4},{4,0},{1,5},{5,1},{2,6},{6,2},{3,7},{7,3},{8,12},{12,8},{9,1... | collective-permute-start | bytes 1572872 | tf_op jit(solution)/shard_map/ppermute | solution.py:62
  234.5 14.8 %collective-permute-start.30 = (bf16[384,512]{1,0:T(8,128)(2,1)}, bf16[384,512]{1,0:T(8,128)(2,1)}, u32[]{:S(2)}, u32[]{:S(2)}) collective-permute-start(bf16[384,512]{1,0:T(8,128)(2,1)} %collective-permute-done.24.refs_2_), channel_id=1, source_target_pairs={{0,1},{1,0},{2,3},{3,2},{4,5},{5,4},{6,7},{7,6},{8,9},{9,8},{10,11... | collective-permute-start | bytes 1179656 | tf_op jit(solution)/shard_map/ppermute | solution.py:62
  234.5 14.8 %collective-permute-start.29 = (bf16[384,512]{1,0:T(8,128)(2,1)}, bf16[384,512]{1,0:T(8,128)(2,1)}, u32[]{:S(2)}, u32[]{:S(2)}) collective-permute-start(bf16[384,512]{1,0:T(8,128)(2,1)} %collective-permute-done.23.refs_0_), channel_id=1, source_target_pairs={{0,1},{1,0},{2,3},{3,2},{4,5},{5,4},{6,7},{7,6},{8,9},{9,8},{10,11... | collective-permute-start | bytes 1179656 | tf_op jit(solution)/shard_map/ppermute | solution.py:62
  262.6 16.4 %collective-permute-start.40 = (bf16[2,256,512]{2,1,0:T(8,128)(2,1)S(1)}, bf16[2,256,512]{2,1,0:T(8,128)(2,1)S(1)}, u32[]{:S(2)}, u32[]{:S(2)}) collective-permute-start(bf16[2,256,512]{2,1,0:T(8,128)(2,1)S(1)} %get-tuple-element.596), channel_id=1, source_target_pairs={{0,4},{4,0},{1,5},{5,1},{2,6},{6,2},{3,7},{7,3},{8,12},{12,8},{9,1... | collective-permute-start | bytes 1572872 | tf_op jit(solution)/shard_map/ppermute | solution.py:62
  280.0 18.7 %collective-permute-start.41 = (bf16[384,512]{1,0:T(8,128)(2,1)S(1)}, bf16[384,512]{1,0:T(8,128)(2,1)S(1)}, u32[]{:S(2)}, u32[]{:S(2)}) collective-permute-start(bf16[384,512]{1,0:T(8,128)(2,1)S(1)} %collective-permute-done.37.refs_2_), channel_id=1, source_target_pairs={{0,1},{1,0},{2,3},{3,2},{4,5},{5,4},{6,7},{7,6},{8,9},{9,8},{10,11... | collective-permute-start | bytes 1179656 | tf_op jit(solution)/shard_map/ppermute | solution.py:62
  298.6 19.5 %collective-permute-start.42 = (bf16[2,400,512]{2,1,0:T(8,128)(2,1)}, bf16[2,400,512]{2,1,0:T(8,128)(2,1)S(1)}, u32[]{:S(2)}, u32[]{:S(2)}) collective-permute-start(bf16[2,400,512]{2,1,0:T(8,128)(2,1)} %get-tuple-element.405), channel_id=1, source_target_pairs={{0,1},{1,0},{2,3},{3,2},{4,5},{5,4},{6,7},{7,6},{8,9},{9,8},{10,11... | collective-permute-start | bytes 2457608 | tf_op jit(solution)/shard_map/ppermute | solution.py:62
  330.6 16.4 %collective-permute-start.45 = (bf16[400,512]{1,0:T(8,128)(2,1)S(1)}, bf16[400,512]{1,0:T(8,128)(2,1)}, u32[]{:S(2)}, u32[]{:S(2)}) collective-permute-start(bf16[400,512]{1,0:T(8,128)(2,1)S(1)} %add_convert_fusion.6), channel_id=1, source_target_pairs={{0,8},{8,16},{16,24},{24,0},{1,9},{9,17},{17,25},{25,1},{2,10},{10... | collective-permute-start | bytes 1228808 | tf_op jit(solution)/shard_map/ppermute | solution.py:66
  364.4 24.0 %collective-permute-start.53 = (bf16[1024,512]{1,0:T(8,128)(2,1)S(1)}, bf16[1024,512]{1,0:T(8,128)(2,1)S(1)}, u32[]{:S(2)}, u32[]{:S(2)}) collective-permute-start(bf16[1024,512]{1,0:T(8,128)(2,1)S(1)} %dynamic-slice_bitcast_fusion.2), channel_id=1, source_target_pairs={{0,4},{4,0},{1,5},{5,1},{2,6},{6,2},{3,7},{7,3},{8,12},{12,8},{9,1... | collective-permute-start | bytes 3145736 | tf_op jit(solution)/shard_map/ppermute | solution.py:62
  390.7 22.9 %collective-permute-start.57 = (bf16[1024,512]{1,0:T(8,128)(2,1)S(1)}, bf16[1024,512]{1,0:T(8,128)(2,1)}, u32[]{:S(2)}, u32[]{:S(2)}) collective-permute-start(bf16[1024,512]{1,0:T(8,128)(2,1)S(1)} %dynamic-slice_bitcast_fusion.1), channel_id=1, source_target_pairs={{0,4},{4,0},{1,5},{5,1},{2,6},{6,2},{3,7},{7,3},{8,12},{12,8},{9,1... | collective-permute-start | bytes 3145736 | tf_op jit(solution)/shard_map/ppermute | solution.py:62
  420.3 20.5 %all-to-all-start.5 = ((bf16[8,64,384]{2,1,0:T(8,128)(2,1)}), bf16[8,64,384]{2,1,0:T(8,128)(2,1)S(1)}, u32[]{:S(2)}, u32[]{:S(2)}) async-start(bf16[8,64,384]{2,1,0:T(8,128)(2,1)} %bitcast.62), calls=%async_computation.6 | async-start | bytes 786432 | tf_op jit(solution)/shard_map/all_to_all | solution.py:960
  426.4 225.0 %reduce-scatter.3.cloned.1.call-start = ((), (), s32[]{:S(2)}) async-start(), calls=%async_computation.12 | async-start | bytes 6684672 | tf_op jit(solution)/shard_map/reduce_scatter | solution.py:1075
  440.8 33.8 %all-to-all-start.6 = ((bf16[4,256,512]{2,1,0:T(8,128)(2,1)}), bf16[4,256,512]{2,1,0:T(8,128)(2,1)}, u32[]{:S(2)}, u32[]{:S(2)}) async-start(bf16[4,256,512]{2,1,0:T(8,128)(2,1)} %bitcast.64), calls=%async_computation.7 | async-start | bytes 2097152 | tf_op jit(solution)/shard_map/all_to_all | solution.py:615
  445.1 26.8 %collective-permute-start.60 = (f32[1,2048]{1,0:T(1,128)S(1)}, f32[1,2048]{1,0:T(1,128)S(1)}, u32[]{:S(2)}, u32[]{:S(2)}) collective-permute-start(f32[1,2048]{1,0:T(1,128)S(1)} %add.332), channel_id=1, source_target_pairs={{0,2},{2,0},{1,3},{3,1},{4,6},{6,4},{5,7},{7,5},{8,10},{10,8},{9,1... | collective-permute-start | bytes 24584 | tf_op jit(solution)/shard_map/ppermute | solution.py:62
  446.4 26.2 %collective-permute-start.59 = (bf16[1024,512]{1,0:T(8,128)(2,1)S(1)}, bf16[1024,512]{1,0:T(8,128)(2,1)}, u32[]{:S(2)}, u32[]{:S(2)}) collective-permute-start(bf16[1024,512]{1,0:T(8,128)(2,1)S(1)} %dynamic-slice_bitcast_fusion), channel_id=1, source_target_pairs={{0,4},{4,0},{1,5},{5,1},{2,6},{6,2},{3,7},{7,3},{8,12},{12,8},{9,1... | collective-permute-start | bytes 3145736 | tf_op jit(solution)/shard_map/ppermute | solution.py:62
  475.7 14.9 %collective-permute-start.61 = (bf16[4,192,384]{2,1,0:T(8,128)(2,1)S(1)}, bf16[4,192,384]{2,1,0:T(8,128)(2,1)S(1)}, u32[]{:S(2)}, u32[]{:S(2)}) collective-permute-start(bf16[4,192,384]{2,1,0:T(8,128)(2,1)S(1)} %slice.174), channel_id=1, source_target_pairs={{0,4},{4,0},{1,5},{5,1},{2,6},{6,2},{3,7},{7,3},{8,12},{12,8},{9,1... | collective-permute-start | bytes 1769480 | tf_op jit(solution)/shard_map/ppermute | solution.py:62
  491.5 34.2 %all-to-all-start.7 = ((bf16[4,256,512]{2,1,0:T(8,128)(2,1)}), bf16[4,256,512]{2,1,0:T(8,128)(2,1)S(1)}, u32[]{:S(2)}, u32[]{:S(2)}) async-start(bf16[4,256,512]{2,1,0:T(8,128)(2,1)} %bitcast.66), calls=%async_computation.8 | async-start | bytes 2097152 | tf_op jit(solution)/shard_map/all_to_all | solution.py:615
  500.4 16.5 %collective-permute-start.63 = (bf16[2,400,512]{2,1,0:T(8,128)(2,1)}, bf16[2,400,512]{2,1,0:T(8,128)(2,1)S(1)}, u32[]{:S(2)}, u32[]{:S(2)}) collective-permute-start(bf16[2,400,512]{2,1,0:T(8,128)(2,1)} %get-tuple-element.519), channel_id=1, source_target_pairs={{0,1},{1,0},{2,3},{3,2},{4,5},{5,4},{6,7},{7,6},{8,9},{9,8},{10,11... | collective-permute-start | bytes 2457608 | tf_op jit(solution)/shard_map/ppermute | solution.py:62
  500.4 16.5 %collective-permute-start.64 = (f32[1,2056]{1,0:T(1,128)S(1)}, f32[1,2056]{1,0:T(1,128)S(1)}, u32[]{:S(2)}, u32[]{:S(2)}) collective-permute-start(f32[1,2056]{1,0:T(1,128)S(1)} %fusion.36), channel_id=1, source_target_pairs={{0,8},{8,0},{16,24},{24,16},{1,9},{9,1},{17,25},{25,17},{2,10},{10... | collective-permute-start | bytes 24680 | tf_op jit(solution)/shard_map/ppermute | solution.py:1010
  525.7 64.1 %all-to-all-start.8 = ((bf16[4,256,512]{2,1,0:T(8,128)(2,1)}), bf16[4,256,512]{2,1,0:T(8,128)(2,1)}, u32[]{:S(2)}, u32[]{:S(2)}) async-start(bf16[4,256,512]{2,1,0:T(8,128)(2,1)} %bitcast.71), calls=%async_computation.9 | async-start | bytes 2097152 | tf_op jit(solution)/shard_map/all_to_all | solution.py:615
  530.1 39.2 %collective-permute-start.67 = (f32[1,2056]{1,0:T(1,128)S(1)}, f32[1,2056]{1,0:T(1,128)S(1)}, u32[]{:S(2)}, u32[]{:S(2)}) collective-permute-start(f32[1,2056]{1,0:T(1,128)S(1)} %add.339), channel_id=1, source_target_pairs={{0,16},{8,24},{16,0},{24,8},{1,17},{9,25},{17,1},{25,9},{2,18},{10... | collective-permute-start | bytes 24680 | tf_op jit(solution)/shard_map/ppermute | solution.py:1028
  535.5 33.8 %collective-permute-start.65 = (bf16[400,512]{1,0:T(8,128)(2,1)}, bf16[400,512]{1,0:T(8,128)(2,1)S(1)}, u32[]{:S(2)}, u32[]{:S(2)}) collective-permute-start(bf16[400,512]{1,0:T(8,128)(2,1)} %fusion.17), channel_id=1, source_target_pairs={{0,2},{2,0},{1,3},{3,1},{4,6},{6,4},{5,7},{7,5},{8,10},{10,8},{9,1... | collective-permute-start | bytes 1228808 | tf_op jit(solution)/shard_map/ppermute | solution.py:62
  536.5 32.8 %collective-permute-start.66 = (bf16[2,400,512]{2,1,0:T(8,128)(2,1)}, bf16[2,400,512]{2,1,0:T(8,128)(2,1)}, u32[]{:S(2)}, u32[]{:S(2)}) collective-permute-start(bf16[2,400,512]{2,1,0:T(8,128)(2,1)} %get-tuple-element.528), channel_id=1, source_target_pairs={{0,1},{1,0},{2,3},{3,2},{4,5},{5,4},{6,7},{7,6},{8,9},{9,8},{10,11... | collective-permute-start | bytes 2457608 | tf_op jit(solution)/shard_map/ppermute | solution.py:62
  570.8 19.0 %collective-permute-start.68 = (bf16[400,512]{1,0:T(8,128)(2,1)}, bf16[400,512]{1,0:T(8,128)(2,1)}, u32[]{:S(2)}, u32[]{:S(2)}) collective-permute-start(bf16[400,512]{1,0:T(8,128)(2,1)} %add_convert_fusion.3), channel_id=1, source_target_pairs={{0,8},{8,16},{16,24},{24,0},{1,9},{9,17},{17,25},{25,1},{2,10},{10... | collective-permute-start | bytes 1228808 | tf_op jit(solution)/shard_map/ppermute | solution.py:66
  571.9 18.0 %collective-permute-start.71 = (bf16[4,384,256]{2,1,0:T(8,128)(2,1)}, bf16[4,384,256]{2,1,0:T(8,128)(2,1)}, u32[]{:S(2)}, u32[]{:S(2)}) collective-permute-start(bf16[4,384,256]{2,1,0:T(8,128)(2,1)} %get-tuple-element.546), channel_id=1, source_target_pairs={{0,4},{4,0},{1,5},{5,1},{2,6},{6,2},{3,7},{7,3},{8,12},{12,8},{9,1... | collective-permute-start | bytes 2359304 | tf_op jit(solution)/shard_map/ppermute | solution.py:62
  572.6 17.2 %collective-permute-start.70 = (bf16[2,400,512]{2,1,0:T(8,128)(2,1)}, bf16[2,400,512]{2,1,0:T(8,128)(2,1)}, u32[]{:S(2)}, u32[]{:S(2)}) collective-permute-start(bf16[2,400,512]{2,1,0:T(8,128)(2,1)} %get-tuple-element.540), channel_id=1, source_target_pairs={{0,1},{1,0},{2,3},{3,2},{4,5},{5,4},{6,7},{7,6},{8,9},{9,8},{10,11... | collective-permute-start | bytes 2457608 | tf_op jit(solution)/shard_map/ppermute | solution.py:62
  592.8 23.2 %collective-permute-start.72 = (bf16[400,512]{1,0:T(8,128)(2,1)}, bf16[400,512]{1,0:T(8,128)(2,1)}, u32[]{:S(2)}, u32[]{:S(2)}) collective-permute-start(bf16[400,512]{1,0:T(8,128)(2,1)} %add_convert_fusion.2), channel_id=1, source_target_pairs={{0,8},{8,16},{16,24},{24,0},{1,9},{9,17},{17,25},{25,1},{2,10},{10... | collective-permute-start | bytes 1228808 | tf_op jit(solution)/shard_map/ppermute | solution.py:66
  592.8 23.2 %collective-permute-start.74 = (bf16[2,400,512]{2,1,0:T(8,128)(2,1)}, bf16[2,400,512]{2,1,0:T(8,128)(2,1)}, u32[]{:S(2)}, u32[]{:S(2)}) collective-permute-start(bf16[2,400,512]{2,1,0:T(8,128)(2,1)} %get-tuple-element.553), channel_id=1, source_target_pairs={{0,1},{1,0},{2,3},{3,2},{4,5},{5,4},{6,7},{7,6},{8,9},{9,8},{10,11... | collective-permute-start | bytes 2457608 | tf_op jit(solution)/shard_map/ppermute | solution.py:62
  595.4 20.5 %collective-permute-start.73 = (bf16[400,512]{1,0:T(8,128)(2,1)}, bf16[400,512]{1,0:T(8,128)(2,1)}, u32[]{:S(2)}, u32[]{:S(2)}) collective-permute-start(bf16[400,512]{1,0:T(8,128)(2,1)} %fusion.19), channel_id=1, source_target_pairs={{0,2},{2,0},{1,3},{3,1},{4,6},{6,4},{5,7},{7,5},{8,10},{10,8},{9,1... | collective-permute-start | bytes 1228808 | tf_op jit(solution)/shard_map/ppermute | solution.py:62
  598.2 46.3 %all-to-all-start.9 = ((bf16[4,384,256]{2,1,0:T(8,128)(2,1)}), bf16[4,384,256]{2,1,0:T(8,128)(2,1)S(1)}, u32[]{:S(2)}, u32[]{:S(2)}) async-start(bf16[4,384,256]{2,1,0:T(8,128)(2,1)} %add_convert_fusion), calls=%async_computation.10 | async-start | bytes 1572864 | tf_op jit(solution)/shard_map/all_to_all | solution.py:615
  619.5 29.1 %collective-permute-start.77 = (bf16[400,512]{1,0:T(8,128)(2,1)}, bf16[400,512]{1,0:T(8,128)(2,1)}, u32[]{:S(2)}, u32[]{:S(2)}) collective-permute-start(bf16[400,512]{1,0:T(8,128)(2,1)} %add_convert_fusion.1), channel_id=1, source_target_pairs={{0,8},{8,16},{16,24},{24,0},{1,9},{9,17},{17,25},{25,1},{2,10},{10... | collective-permute-start | bytes 1228808 | tf_op jit(solution)/shard_map/ppermute | solution.py:66
  621.8 26.9 %collective-permute-start.78 = (bf16[400,512]{1,0:T(8,128)(2,1)}, bf16[400,512]{1,0:T(8,128)(2,1)}, u32[]{:S(2)}, u32[]{:S(2)}) collective-permute-start(bf16[400,512]{1,0:T(8,128)(2,1)} %fusion.20), channel_id=1, source_target_pairs={{0,2},{2,0},{1,3},{3,1},{4,6},{6,4},{5,7},{7,5},{8,10},{10,8},{9,1... | collective-permute-start | bytes 1228808 | tf_op jit(solution)/shard_map/ppermute | solution.py:62
  622.7 25.9 %collective-permute-start.80 = (f32[1,2048]{1,0:T(1,128)S(1)}, f32[1,2048]{1,0:T(1,128)S(1)}, u32[]{:S(2)}, u32[]{:S(2)}) collective-permute-start(f32[1,2048]{1,0:T(1,128)S(1)} %add.353), channel_id=1, source_target_pairs={{0,8},{8,0},{16,24},{24,16},{1,9},{9,1},{17,25},{25,17},{2,10},{10... | collective-permute-start | bytes 24584 | tf_op jit(solution)/shard_map/ppermute | solution.py:1060
  (131 other events, 1458.8 us)
Sparse Core Ops, SparseCore 0:
  74.7 61.4 all-gather.4
  138.4 80.8 all-gather.6
  420.4 92.5 reduce-scatter.4
  516.8 111.3 reduce-scatter.2

commit v3 on v2

--- a/solution.py
+++ b/solution.py
@@ -334,7 +334,9 @@
         out[2 * HDIM :] = lin[2 * HDIM :].astype(BF16)
 
 
-def chunk_call(kernel, name, time, where, s, inputs, buffers, whole_shapes, out_shapes, held=False):
+def chunk_call(
+    kernel, name, time, where, s, inputs, buffers, whole_shapes, out_shapes, scratch=(), out_there=0
+):
     def spec(dims, how):
         rest = (0,) * (len(dims) - 1)
         if how == "whole":
@@ -355,15 +357,10 @@
             in_specs.append(pl.BlockSpec(memory_space=pl.ANY))
             arrays.append(buffer)
     out_specs = [spec(dims, how) for dims, how in whole_shapes]
-    out_specs += [full(a.shape) for a in out_shapes]
-    scratch = []
-    if held:
-        there = [a for a, how in inputs if how == "there"]
-        rows = sum(a.shape[0] for a in there)
-        scratch = [
-            pltpu.VMEM((rows, there[0].shape[1]), BF16),
-            pltpu.SemaphoreType.DMA((len(there),)),
-        ]
+    out_specs += [
+        pl.BlockSpec(memory_space=pl.ANY) if n < out_there else full(a.shape)
+        for n, a in enumerate(out_shapes)
+    ]
     return pl.pallas_call(
         kernel,
         grid_spec=pltpu.PrefetchScalarGridSpec(
@@ -371,7 +368,7 @@
             grid=(1,),
             in_specs=in_specs,
             out_specs=out_specs,
-            scratch_shapes=scratch,
+            scratch_shapes=list(scratch),
         ),
         out_shape=[shape(dims, BF16) for dims, _ in whole_shapes] + list(out_shapes),
         input_output_aliases=aliases,
@@ -381,93 +378,215 @@
     )(where, *arrays)
 
 
-def fetch(weights, held, sems):
-    copies, start = [], 0
+def fetch(weights, held, sems, first=0, start=0):
+    copies = []
     for n, weight in enumerate(weights):
         rows = weight.shape[0]
-        copies.append(pltpu.make_async_copy(weight, held.at[pl.ds(start, rows)], sems.at[n]))
+        copies.append(
+            pltpu.make_async_copy(weight, held.at[pl.ds(start, rows)], sems.at[first + n])
+        )
         copies[-1].start()
         start += rows
     return copies
 
 
-def ffn_kernel(where, *refs):
-    normed, hidden, gates, ups, scale, held, sems = refs[-7:]
-    mids, gain, weights = refs[:4], refs[4], refs[5 : 5 + sems.shape[0]]
-    rows, cols = mids[0].shape
-    units, wide = hidden.shape[1], 2 * cols
-    copies = fetch(weights, held, sems)
-    rstd = row_scale(mids, 4 * cols)
-    scale[...] = rstd
-    put_normed(where, mids, rstd, gain, normed)
+class Sends:
+    def __init__(self, sems):
+        self.sems, self.copies = sems, []
+
+    def start(self, source, target):
+        self.copies.append(pltpu.make_async_copy(source, target, self.sems.at[len(self.copies)]))
+        self.copies[-1].start()
+
+    def wait(self):
+        for copy in self.copies:
+            copy.wait()
+
+
+def load(pairs, sems, first):
+    copies = [
+        pltpu.make_async_copy(source, target, sems.at[first + n])
+        for n, (source, target) in enumerate(pairs)
+    ]
+    for copy in copies:
+        copy.start()
+    return copies
+
+
+def wait_all(copies):
     for copy in copies:
         copy.wait()
+
+
+def ffn_kernel(chunks, count, where, *refs):
+    pieces, gain, weights = refs[:8], refs[8], refs[9 : 9 + count]
+    outs = refs[-16:-8]
+    mids, normed_all, hidden_all, gates_all, ups_all, held, sems, out_sems = refs[-8:]
+    normed_out, hidden_out, scales = outs[0], outs[1], outs[6:]
+    rows, cols = mids.shape[2:]
+    units, wide = hidden_all.shape[2], 2 * cols
+    come = [
+        load([(pieces[4 * i + k], mids.at[i, k]) for k in range(4)], sems, count + 4 * i)
+        for i in range(2)
+    ]
+    copies = fetch(weights, held, sems)
+    sends = Sends(out_sems)
     step = 256
-    for n in range(0, units, step):
-        span = slice(n, n + step)
-        gate = up = 0.0
-        for h in range(2):
-            values = normed[:, half_columns(where, h, wide)]
-            gate = gate + dot(values, held[h * wide : (h + 1) * wide, span], 1, 0)
-            up = up + dot(values, held[(h + 2) * wide : (h + 3) * wide, span], 1, 0)
-        hidden[:, span] = (gate * jax.nn.sigmoid(gate) * up).astype(BF16)
-        gates[:, span] = gate
-        ups[:, span] = up
-
-
-def ffn_back_kernel(where, *refs):
-    cots, normed, hidden, gates, ups = refs[:5]
-    cot_rows, grad_gate, grad_up, out, keep_back, send_back, gain_term, held, sems = refs[-9:]
-    count = sems.shape[0]
-    rows, units = hidden.shape
+    for i in range(2):
+        chunk = pl.ds(chunks[i] * rows, rows)
+        normed, hidden = normed_all.at[i], hidden_all.at[i]
+        gates, ups = gates_all.at[i], ups_all.at[i]
+        gates_out, ups_out = outs[2 + 2 * i], outs[3 + 2 * i]
+        wait_all(come[i])
+        blocks = [mids.at[i, k] for k in range(4)]
+        rstd = row_scale(blocks, 4 * cols)
+        scales[i][...] = rstd
+        put_normed(where, blocks, rstd, gain, normed)
+        sends.start(normed, normed_out.at[chunk])
+        if i == 0:
+            wait_all(copies)
+        for n in range(0, units, step):
+            span = slice(n, n + step)
+            columns = pl.ds(n, step)
+            gate = up = 0.0
+            for h in range(2):
+                values = normed[:, half_columns(where, h, wide)]
+                gate = gate + dot(values, held[h * wide : (h + 1) * wide, span], 1, 0)
+                up = up + dot(values, held[(h + 2) * wide : (h + 3) * wide, span], 1, 0)
+            gates[:, span] = gate
+            ups[:, span] = up
+            sends.start(gates.at[:, columns], gates_out.at[:, columns])
+            sends.start(ups.at[:, columns], ups_out.at[:, columns])
+            hidden[:, span] = (gate * jax.nn.sigmoid(gate) * up).astype(BF16)
+            sends.start(hidden.at[:, columns], hidden_out.at[chunk, columns])
+    sends.wait()
+
+
+def arrange_kernel(zs, cots, cot_rows):
     cols = cots.shape[2]
-    half, wide = cols // 2, 2 * cols
-    copies = fetch(refs[5 : 5 + count], held, sems)
+    half = cols // 2
     for block in range(4):
         for part in range(2):
             start = (part * 4 + block) * half
             cot_rows[:, start : start + half] = cots[block, :, part * half : (part + 1) * half]
-    for copy in copies[: count // 2]:
-        copy.wait()
+
+
+def arrange(cot, zs):
+    blocks, rows, cols = cot.shape
+    return pl.pallas_call(
+        arrange_kernel,
+        grid_spec=pltpu.PrefetchScalarGridSpec(
+            num_scalar_prefetch=1,
+            grid=(4,),
+            in_specs=[pl.BlockSpec((blocks // 4, rows, cols), lambda s, zs: (zs[s], 0, 0))],
+            out_specs=pl.BlockSpec((rows, 4 * cols), lambda s, zs: (s, 0)),
+        ),
+        out_shape=shape((4 * rows, 4 * cols), BF16),
+        compiler_params=params(),
+        cost_estimate=cost(5),
+        name="arrange",
+    )(zs, cot)
+
+
+def ffn_back_kernel(chunks, downs, count, where, *refs):
+    weights, kept = refs[:count], refs[count : count + 4]
+    all_cot, all_hidden, all_normed = refs[count + 4 : count + 7]
+    grad_gate_out, grad_up_out, out = refs[-21:-18]
+    backs, gain_term = refs[-18:-14], refs[-14]
+    held, cot_all, gate_up, hidden_in, normed_in, sems = refs[-13:-7]
+    grad_gates, grad_ups, out_held, back_held, lines, out_sems, line_sems = refs[-7:]
+    rows, units = grad_gates.shape[1:]
+    cols = out_held.shape[3]
+    half, wide = cols // 2, 2 * cols
     step = 256
-    for n in range(0, units, step):
-        span = slice(n, n + step)
-        grad_hidden = 0.0
-        for h in range(2):
-            grad_hidden = grad_hidden + dot(
-                cot_rows[:, half_columns(where, h, wide)], held[h * wide : (h + 1) * wide, span], 1, 0
-            )
-        gate, up = gates[:, span], ups[:, span]
-        sigmoid = jax.nn.sigmoid(gate)
-        grad_gate[:, span] = (
-            grad_hidden * up * sigmoid * (1.0 + gate * (1.0 - sigmoid))
-        ).astype(BF16)
-        grad_up[:, span] = (grad_hidden * (gate * sigmoid)).astype(BF16)
-    for copy in copies[count // 2 :]:
-        copy.wait()
-    row_term = 0.0
-    for k in range(4):
-        block = block_of(where, k)
-        back = (keep_back, send_back)[k % 2]
-        for h in range(2):
-            part = aligned((h ^ where[1]) * half, half)
-            of_down, of_gate, of_up = [
-                held[aligned((n + h) * wide + block * half, half), :] for n in (0, 2, 4)
-            ]
-            out[block, :, part] = dot(hidden[...], of_down, 1, 1).astype(BF16)
-            partial = dot(grad_gate[...], of_gate, 1, 1) + dot(grad_up[...], of_up, 1, 1)
-            back[k // 2, :rows, part] = partial.astype(BF16)
-            columns = aligned(((h ^ where[1]) * 4 + block) * half, half)
-            terms = partial * normed[:, columns].astype(F32)
-            gain_term[:, columns] = jnp.sum(terms, axis=0, keepdims=True)
-            row_term = row_term + jnp.sum(terms, axis=1, keepdims=True)
-    put_row_term(row_term, cols, keep_back, send_back)
+    spans = [pl.ds(s * rows, rows) for s in chunks]
+    early = load([(all_cot.at[spans[0]], cot_all.at[0])], sems, count)
+    early += fetch(weights[:downs], held, sems)
+    early += load([(kept[0], gate_up.at[0, 0]), (kept[1], gate_up.at[0, 1])], sems, count + 1)
+    late = load(
+        [(all_hidden.at[spans[0]], hidden_in.at[0]), (all_normed.at[spans[0]], normed_in.at[0])],
+        sems,
+        count + 3,
+    )
+    late += fetch(weights[downs:], held, sems, downs, 2 * wide)
+    second = load(
+        [
+            (all_cot.at[spans[1]], cot_all.at[1]),
+            (kept[2], gate_up.at[1, 0]),
+            (kept[3], gate_up.at[1, 1]),
+            (all_hidden.at[spans[1]], hidden_in.at[1]),
+            (all_normed.at[spans[1]], normed_in.at[1]),
+        ],
+        sems,
+        count + 5,
+    )
+    sends, tails = Sends(out_sems), Sends(line_sems)
+    for i in range(2):
+        cot_rows, hidden, normed = cot_all.at[i], hidden_in.at[i], normed_in.at[i]
+        gates, ups = gate_up.at[i, 0], gate_up.at[i, 1]
+        grad_gate, grad_up = grad_gates.at[i], grad_ups.at[i]
+        place = where[3 + i]
+        wait_all(early if i == 0 else second)
+        for n in range(0, units, step):
+            span = slice(n, n + step)
+            columns = pl.ds(n, step)
+            grad_hidden = 0.0
+            for h in range(2):
+                grad_hidden = grad_hidden + dot(
+                    cot_rows[:, half_columns(where, h, wide)],
+                    held[h * wide : (h + 1) * wide, span],
+                    1,
+                    0,
+                )
+            gate, up = gates[:, span], ups[:, span]
+            sigmoid = jax.nn.sigmoid(gate)
+            grad_gate[:, span] = (
+                grad_hidden * up * sigmoid * (1.0 + gate * (1.0 - sigmoid))
+            ).astype(BF16)
+            grad_up[:, span] = (grad_hidden * (gate * sigmoid)).astype(BF16)
+            sends.start(grad_gate.at[:, columns], grad_gate_out.at[spans[i], columns])
+            sends.start(grad_up.at[:, columns], grad_up_out.at[spans[i], columns])
+        if i == 0:
+            wait_all(late)
+        row_term = 0.0
+        for k in range(4):
+            block = block_of(where, k)
+            back = backs[2 * i + k % 2]
+            for h in range(2):
+                part = aligned((h ^ where[1]) * half, half)
+                of_down, of_gate, of_up = [
+                    held[aligned((n + h) * wide + block * half, half), :] for n in (0, 2, 4)
+                ]
+                out_held[i, k, :, part] = dot(hidden[...], of_down, 1, 1).astype(BF16)
+                partial = dot(grad_gate[...], of_gate, 1, 1) + dot(grad_up[...], of_up, 1, 1)
+                back_held[i, k, :, part] = partial.astype(BF16)
+                columns = aligned(((h ^ where[1]) * 4 + block) * half, half)
+                terms = partial * normed[:, columns].astype(F32)
+                column_term = jnp.sum(terms, axis=0, keepdims=True)
+                if i == 0:
+                    gain_term[:, columns] = column_term
+                else:
+                    gain_term[:, columns] += column_term
+                row_term = row_term + jnp.sum(terms, axis=1, keepdims=True)
+            sends.start(out_held.at[i, k], out.at[place * 4 + block])
+            sends.start(back_held.at[i, k], back.at[k // 2, pl.ds(0, rows)])
+        lines[i] = row_line(row_term, cols)
+        for back in backs[2 * i : 2 * i + 2]:
+            for x in range(2):
+                tails.start(lines.at[i], back.at[x, pl.ds(rows, EXTRA)])
+    sends.wait()
+    tails.wait()
+
+
+def row_line(row_term, cols):
+    rows = row_term.shape[0]
+    line = jnp.broadcast_to(row_term, (rows, 128)).T[:EXTRA]
+    return jnp.concatenate([line, jnp.zeros((EXTRA, cols - rows), F32)], axis=1).astype(BF16)
 
 
 def put_row_term(row_term, cols, keep, send):
     rows = row_term.shape[0]
-    line = jnp.broadcast_to(row_term, (rows, 128)).T[:EXTRA]
-    line = jnp.concatenate([line, jnp.zeros((EXTRA, cols - rows), F32)], axis=1).astype(BF16)
+    line = row_line(row_term, cols)
     for ref in (keep, send):
         ref[0, rows:] = line
         ref[1, rows:] = line
@@ -533,15 +652,30 @@
     grad_att[...] = total.astype(BF16)
 
 
-def columns_kernel(where, parts, out):
-    for z in range(parts.shape[0]):
-        out[:, z * parts.shape[2] : (z + 1) * parts.shape[2]] = parts[z].astype(F32)
-
-
-def turned_kernel(where, parts, out):
-    size = parts.shape[2]
-    for z in range(parts.shape[0]):
-        out[z * size : (z + 1) * size, :] = parts[z].astype(F32).T
+def columns_kernel(parts, out):
+    out[...] = parts[0].astype(F32)
+
+
+def turned_kernel(parts, out):
+    out[...] = parts[0].astype(F32).T
+
+
+def lay_out(parts, turned):
+    nz, n, m = parts.shape
+    if turned:
+        kernel, dims, block, place = turned_kernel, (nz * m, n), (m, n), lambda z: (z, 0)
+    else:
+        kernel, dims, block, place = columns_kernel, (n, nz * m), (n, m), lambda z: (0, z)
+    return pl.pallas_call(
+        kernel,
+        grid=(nz,),
+        in_specs=[pl.BlockSpec((1, n, m), lambda z: (z, 0, 0))],
+        out_specs=pl.BlockSpec(block, place),
+        out_shape=shape(dims, F32),
+        compiler_params=params(),
+        cost_estimate=cost(2),
+        name="lay_out",
+    )(parts)
 
 
 def qkv_out_kernel(where, parts, *outs):
@@ -811,42 +945,68 @@
     down_parts = of_units(w_down_)
     mid_block = residual_mid.astype(BF16)
 
-    def forward(s, pieces, buffers):
+    def forward(chunks, pieces, buffers):
         results = chunk_call(
-            ffn_kernel,
+            functools.partial(ffn_kernel, chunks, len(w_gates) + len(w_ups)),
             "feed_forward",
-            7,
-            where[s],
-            s,
-            [(a, "whole") for a in (*pieces, gain2)] + [(w, "there") for w in (*w_gates, *w_ups)],
+            9,
+            where[0],
+            0,
+            [(a, "there") for a in pieces]
+            + [(gain2, "whole")]
+            + [(w, "there") for w in (*w_gates, *w_ups)],
             buffers,
-            [((group_rows, width), "chunk"), ((group_rows, units), "chunk")],
-            [shape((rows, units), F32)] * 2 + [shape((rows, 1), F32)],
-            held=True,
+            [((group_rows, width), "there"), ((group_rows, units), "there")],
+            [shape((rows, units), F32)] * 4 + [shape((rows, 1), F32)] * 2,
+            [
+                pltpu.VMEM((2, 4, rows, cols), BF16),
+                pltpu.VMEM((2, rows, width), BF16),
+                pltpu.VMEM((2, rows, units), BF16),
+                pltpu.VMEM((2, rows, units), F32),
+                pltpu.VMEM((2, rows, units), F32),
+                pltpu.VMEM((8 * cols, units), BF16),
+                pltpu.SemaphoreType.DMA((len(w_gates) + len(w_ups) + 8,)),
+                pltpu.SemaphoreType.DMA((2 + 6 * units // 256,)),
+            ],
+            4,
         )
         return results[:2], results[2:]
 
-    def backward(s, normed2, hidden, kept, buffers):
+    def backward(chunks, saved, kept, buffers):
+        weights = (*w_downs, *w_gates, *w_ups)
+        places = jnp.concatenate([where[0][:3], jnp.stack([zs[s] for s in chunks]).astype(jnp.int32)])
         results = chunk_call(
-            ffn_back_kernel,
+            functools.partial(ffn_back_kernel, chunks, len(w_downs), len(weights)),
             "feed_forward_back",
-            10,
-            where[s],
-            s,
-            [(cot, "place"), (normed2, "chunk"), (hidden, "chunk")]
-            + [(a, "whole") for a in kept[:2]]
-            + [(w, "there") for w in (*w_downs, *w_gates, *w_ups)],
+            15,
+            places,
+            0,
+            [(a, "there") for a in (*weights, *kept, cot_rows, saved[1], saved[0])],
             buffers,
             [
-                ((group_rows, width), "chunk"),
-                ((group_rows, units), "chunk"),
-                ((group_rows, units), "chunk"),
-                ((nz * nx * nc, rows, cols), "place"),
+                ((group_rows, units), "there"),
+                ((group_rows, units), "there"),
+                ((nz * nx * nc, rows, cols), "there"),
             ],
-            [shape((2, rows + EXTRA, cols), BF16)] * 2 + [shape((1, width), F32)],
-            held=True,
+            [shape((2, rows + EXTRA, cols), BF16)] * 4 + [shape((1, width), F32)],
+            [
+                pltpu.VMEM((12 * cols, units), BF16),
+                pltpu.VMEM((2, rows, width), BF16),
+                pltpu.VMEM((2, 2, rows, units), F32),
+                pltpu.VMEM((2, rows, units), BF16),
+                pltpu.VMEM((2, rows, width), BF16),
+                pltpu.SemaphoreType.DMA((len(weights) + 10,)),
+                pltpu.VMEM((2, rows, units), BF16),
+                pltpu.VMEM((2, rows, units), BF16),
+                pltpu.VMEM((2, 4, rows, cols), BF16),
+                pltpu.VMEM((2, 4, rows, cols), BF16),
+                pltpu.VMEM((2, EXTRA, cols), BF16),
+                pltpu.SemaphoreType.DMA((16 + 4 * units // 256,)),
+                pltpu.SemaphoreType.DMA((8,)),
+            ],
+            4,
         )
-        return results[:4], results[4:]
+        return results[:3], results[3:7], results[7]
 
     z0 = mid_block
     z1, x0, c0, up_a = together(
@@ -861,70 +1021,70 @@
         down_parts,
     )
     w_ups = join_rows(up_parts, (up_a, up_b))
-    z3, x2, c2, cx1, down_a, (saved, kept0) = together(
+    z3, x2, c2, cx1, down_a, cot_rows = together(
         ring(z2, nz),
         swap(z2, "x"),
         swap(z2, "c"),
         swap(x1, "c"),
         swap_part(down_parts, 0),
-        forward(0, (z0, c0, x0, cx0), None),
-    )
-    x3, c3, cx2, down_b, (saved, kept1) = together(
+        arrange(cot, jnp.stack(zs).astype(jnp.int32)),
+    )
+    x3, c3, cx2, down_b, (saved, kept01) = together(
         swap(z3, "x"),
         swap(z3, "c"),
         swap(x2, "c"),
         swap_part(down_parts, 1),
-        forward(1, (z1, c1, x1, cx1), saved),
+        forward((0, 1), (z0, c0, x0, cx0, z1, c1, x1, cx1), None),
     )
     w_downs = join_rows(down_parts, (down_a, down_b))
-    saved, kept2 = forward(2, (z2, c2, x2, cx2), saved)
-    cx3, saved, kept2, (buffers, part1) = together(
-        swap(x3, "c"), saved, kept2, backward(1, *saved, kept1, None)
-    )
-    saved, kept3 = forward(3, (z3, c3, x3, cx3), saved)
-    got1, saved, kept3, (buffers, part2) = together(
-        swap(part1[1], "c"), saved, kept3, backward(2, *saved, kept2, buffers)
-    )
+    cx3 = swap(x3, "c")
+    saved, kept23 = forward((2, 3), (z2, c2, x2, cx2, z3, c3, x3, cx3), saved)
+    buffers, back12, terms12 = backward((1, 2), saved, (*kept01[2:4], *kept23[:2]), None)
+    part1, part2 = back12[:2], back12[2:]
+    got1, part1, part2 = together(swap(part1[1], "c"), part1, part2)
     normed2, hidden = saved
     own1, send1 = first_sum(part1[0], got1)
-    own1, got1, got2, (buffers, part3) = together(
+    own1, got1, got2, (buffers, back30, terms30) = together(
         own1,
         swap(send1, "x"),
         swap(part2[1], "c"),
-        backward(3, *saved, kept3, buffers),
-    )
+        backward((3, 0), saved, (*kept23[2:4], *kept01[:2]), buffers),
+    )
+    part3, part0 = back30[:2], back30[2:]
     own2, send2 = first_sum(part2[0], got2)
     sum1 = (own1 + got1.astype(F32)).astype(BF16)
-    carried, own2, got2, got3, (buffers, part0) = together(
+    carried, own2, got2, got3, down = together(
         ring(sum1, nz),
         own2,
         swap(send2, "x"),
         swap(part3[1], "c"),
-        backward(0, *saved, kept0, buffers),
-    )
-    cot_rows, grad_gate_lin, grad_up_lin, out_parts = buffers
+        dot(cot_rows, hidden, 0, 0).astype(BF16),
+    )
+    grad_gate_lin, grad_up_lin, out_parts = buffers
     own3, send3 = first_sum(part3[0], got3)
     sum2 = (own2 + got2.astype(F32) + carried.astype(F32)).astype(BF16)
-    carried, own3, got3, got0, down = together(
+    carried, own3, got3, got0, down_got, gate, grad_up_lin = together(
         ring(sum2, nz),
         own3,
         swap(send3, "x"),
         swap(part0[1], "c"),
-        dot(cot_rows, hidden, 0, 0).astype(BF16),
+        exchange_rows(down),
+        dot(normed2, grad_gate_lin, 0, 0).astype(BF16),
+        grad_up_lin,
     )
     own0, send0 = first_sum(part0[0], got0)
     sum3 = (own3 + got3.astype(F32) + carried.astype(F32)).astype(BF16)
-    carried, own0, got0, gate, down_got, grad_up_lin = together(
+    down = add_rows(down, down_got)
+    gate_got = exchange_rows(gate)
+    carried, own0, got0, up = together(
         ring(sum3, nz),
         own0,
         swap(send0, "x"),
-        dot(normed2, grad_gate_lin, 0, 0).astype(BF16),
-        exchange_rows(down),
-        grad_up_lin,
+        dot(normed2, grad_up_lin, 0, 0).astype(BF16),
     )
     summed2 = own0 + got0.astype(F32) + carried.astype(F32)
-    scale2 = kept0[2]
-    terms2 = part0[2] + part1[2] + part2[2] + part3[2]
+    scale2 = kept01[4]
+    terms2 = terms12 + terms30
 
     def norm_back(summed, gain, block, rstd):
         gain = lax.dynamic_slice_in_dim(gain, own_columns * cols, cols, 1)
@@ -935,16 +1095,11 @@
     branch = grad_mid.astype(BF16)
     branch_x = swap(branch, "x")
     branch_c, branch_cx = swap(branch, "c"), swap(branch_x, "c")
-    branch_x, branch_c, branch_cx, gate_got, up, terms2 = together(
-        branch_x,
-        branch_c,
-        branch_cx,
-        exchange_rows(gate),
-        dot(normed2, grad_up_lin, 0, 0).astype(BF16),
-        terms2,
-    )
-    down = add_rows(down, down_got)
+    branch_x, branch_c, branch_cx, gate_got, up = together(
+        branch_x, branch_c, branch_cx, gate_got, up
+    )
     gate = add_rows(gate, gate_got)
+    up_got = exchange_rows(up)
     pieces = (branch, branch_c, branch_x, branch_cx)
 
     grad_att, wo_back = small_call(
@@ -956,29 +1111,16 @@
         [shape(att_t.shape, BF16), shape(wo.shape, BF16)],
     )
     grad_att = grad_att.reshape(nz * ny, HDIM, rows)
-    grad_att, up, terms2, got2, down, gate = together(
-        lax.all_to_all(grad_att, ("z", "y"), split_axis=0, concat_axis=0, tiled=True),
-        up,
-        terms2,
-        swap(terms2, "c"),
-        down,
-        gate,
-    )
-    terms2 = terms2 + got2
-    back, down, up_got, gate, terms2, got2 = together(
+    grad_att, down = together(
+        lax.all_to_all(grad_att, ("z", "y"), split_axis=0, concat_axis=0, tiled=True), down
+    )
+    back, down, up_got, gate = together(
         attend_back(tables, tiles, q_mask, k_mask, grad_att, att, log_norm, cosine, sine),
         spread_z(down),
-        exchange_rows(up),
+        up_got,
         gate,
-        terms2,
-        swap(terms2, "x"),
     )
     up = add_rows(up, up_got)
-    peak_slots = jnp.zeros((1, nz * groups), F32)
-    peak_slots = lax.dynamic_update_slice(
-        peak_slots, jnp.max(peak).reshape(1, 1), (0, zi * groups + group)
-    )
-    terms2 = sum_small(jnp.concatenate([terms2 + got2, peak_slots], axis=1), ("q",))
     if nq > 1:
         grad_q = of_queries(back)[:, :HDIM]
         grad_kv = lax.psum_scatter(back[:, HDIM:], "q", scatter_dimension=0, tiled=True)
@@ -996,26 +1138,11 @@
             specs,
         )
 
-    other_back, place, gate, got2 = together(
-        swap(back[nz:], "y"), where[1], gate, swap(terms2, "y")
-    )
-    terms2 = terms2 + got2
+    other_back, place = together(swap(back[nz:], "y"), where[1])
     part1, place = together(qkv_back(1, place), where[2])
-    got1, part2, gate, up, place, got2 = together(
+    got1, part2, qkv_grads, gate, place = together(
         swap(part1[1], "c"),
         qkv_back(2, place),
-        spread_z(gate),
-        up,
-        where[3],
-        lax.ppermute(terms2, "z", [(i, i ^ 1) for i in range(nz)]),
-    )
-    terms2 = terms2 + got2
-    own1, send1 = first_sum(part1[0], got1)
-    own1, got1, got2, part3, qkv_grads, place, got_terms = together(
-        own1,
-        swap(send1, "x"),
-        swap(part2[1], "c"),
-        qkv_back(3, place),
         small_call(
             qkv_weights_kernel,
             "qkv_weights",
@@ -1024,27 +1151,35 @@
             (normed1, back, other_back),
             [shape((nz, ny * head, half), BF16)] * 2,
         ),
+        spread_z(gate),
+        where[3],
+    )
+    own1, send1 = first_sum(part1[0], got1)
+    own1, got1, got2, part3, qkv_own, qkv_got, place = together(
+        own1,
+        swap(send1, "x"),
+        swap(part2[1], "c"),
+        qkv_back(3, place),
+        qkv_grads[0],
+        exchange_lanes(qkv_grads[1]),
         where[0],
-        lax.ppermute(terms2, "z", [(i, i ^ 2) for i in range(nz)]),
-    )
-    terms2 = terms2 + got_terms
-    terms2, peaks = terms2[:, :width], terms2[0, width:]
+    )
     own2, send2 = first_sum(part2[0], got2)
     sum1 = (own1 + got1.astype(F32)).astype(BF16)
-    carried, own2, got2, got3, part0, qkv_own, qkv_got, up = together(
+    carried, own2, got2, got3, part0, qkv_grads, up = together(
         ring(sum1, nz),
         own2,
         swap(send2, "x"),
         swap(part3[1], "c"),
         qkv_back(0, place),
-        qkv_grads[0],
-        exchange_lanes(qkv_grads[1]),
+        scatter_lanes(qkv_own, qkv_got),
         spread_z(up),
     )
-    qkv_grads = spread_z(scatter_lanes(qkv_own, qkv_got))
+    qkv_grads = spread_z(qkv_grads)
     own3, send3 = first_sum(part3[0], got3)
     sum2 = (own2 + got2.astype(F32) + carried.astype(F32)).astype(BF16)
     terms1 = part0[2] + part1[2] + part2[2] + part3[2]
+    terms1 = jnp.concatenate([terms1, terms2], axis=0)
     terms1 = terms1 + swap(terms1, "c")
     carried, own3, got3, got0, terms1, terms1_x = together(
         ring(sum2, nz),
@@ -1056,7 +1191,12 @@
     )
     own0, send0 = first_sum(part0[0], got0)
     sum3 = (own3 + got3.astype(F32) + carried.astype(F32)).astype(BF16)
-    terms1 = sum_small(terms1 + terms1_x, ("y", "q"))
+    peak_slots = jnp.zeros((nz * groups, 2 * width // (nz * groups)), F32)
+    peak_slots = lax.dynamic_update_slice(
+        peak_slots, jnp.broadcast_to(jnp.max(peak), (1, peak_slots.shape[1])), (zi * groups + group, 0)
+    )
+    terms1 = jnp.stack([terms1 + terms1_x, peak_slots.reshape(2, width)])
+    terms1 = sum_small(terms1, ("y", "q"))
     terms1_z = lax.ppermute(terms1, "z", [(i, i ^ 1) for i in range(nz)])
     carried, own0, got0, terms1, terms1_z = together(
         ring(sum3, nz), own0, swap(send0, "x"), terms1, terms1_z
@@ -1066,21 +1206,26 @@
     summed1 = own0 + got0.astype(F32) + carried.astype(F32)
     grad_in = (grad_mid + norm_back(summed1, gain1, hidden_in, scale1[0])).astype(BF16)
 
-    def laid_out(kernel, time, parts, *dims):
-        return small_call(kernel, "lay_out", time, where[0], (parts,), [shape(d, F32) for d in dims])
-
-    [grad_wd] = laid_out(turned_kernel, 3, down, (nz * units, slab))
-    [grad_wg] = laid_out(columns_kernel, 2, gate, (slab, nz * units))
-    [grad_wu] = laid_out(columns_kernel, 2, up, (slab, nz * units))
+    grad_wd = lay_out(down, True)
+    grad_wg = lay_out(gate, False)
+    grad_wu = lay_out(up, False)
     branch_ffn = lax.psum_scatter(out_parts, ("z", *NARROW), scatter_dimension=0, tiled=False)
     hidden_out = (residual_mid + branch_ffn.astype(F32)).astype(BF16)
     if nq > 1:
         wo_back = wo_back.reshape(nz * 2, -1, groups // 2, slab).transpose(0, 2, 1, 3)
         wo_back = wo_back.reshape(nz * groups, -1, slab)
     grad_wo = lax.psum_scatter(wo_back, WIDE, scatter_dimension=0, tiled=False).astype(F32)
-    grad_qkv = laid_out(qkv_out_kernel, 3, qkv_grads, *[(slab, nz * ny * HDIM)] * 3)
-
-    gain_terms = jnp.concatenate([terms1, terms2], axis=0).reshape(2, 2, nz, half)
+    grad_qkv = small_call(
+        qkv_out_kernel,
+        "lay_out_qkv",
+        3,
+        where[0],
+        (qkv_grads,),
+        [shape((slab, nz * ny * HDIM), F32)] * 3,
+    )
+
+    peaks = terms1[1].reshape(nz * groups, -1)[:, 0]
+    gain_terms = terms1[0].reshape(2, 2, nz, half)
     gain_terms = gain_terms.transpose(0, 2, 1, 3).reshape(2, width) / gains
     terms = lax.dynamic_slice_in_dim(gain_terms, (zi * groups + group) * slab, slab, 1)
     peaks = peaks.reshape(nz, nq, ny)

time: 668 us -> 638 us (0.955)
  Pallas kernels: 193 us -> 178 us
  waiting for transfers between devices: 232 us -> 220 us
    pallas_call x12 -> x8, Pallas kernels: 97.5 us -> 72.2 us  [chunk_call(): pl.pallas_call(kernel, grid_spec=pltpu.PrefetchScalarGridSpec(num_scalar_...]
    ppermute x12, waiting for transfers between devices: 40.3 us -> 62.4 us  [ring(): return lax.ppermute(array, 'z', [(i, (i + 1) % size) for i in range(size)])]
    ppermute x66 -> x63, waiting for transfers between devices: 89.1 us -> 68.5 us  [swap(): return lax.ppermute(array, axis, [(0, 1), (1, 0)])]
    pallas_call x0 -> x4, Pallas kernels: none -> 18.4 us  [the longest x3 11 us: lay_out(): pl.pallas_call(kernel, grid=(nz,), in_specs=[pl.BlockSpec((1, n, m), lamb...]
    ppermute x2 -> x0, waiting for transfers between devices: 16.1 us -> none  [the longest x1 14 us: on_device(): lax.ppermute(terms2, 'z', [(i, i ^ 2) for i in range(nz)])]
    pallas_call x11 -> x8, Pallas kernels: 55 us -> 44.1 us  [small_call(): pl.pallas_call(kernel, grid_spec=pltpu.PrefetchScalarGridSpec(num_scalar_...]
    all_to_all x8, waiting for transfers between devices: 73.2 us -> 81 us  [spread_z(): return lax.all_to_all(parts, 'z', split_axis=0, concat_axis=0, tiled=True)]
    ppermute x66 -> x63, starting transfers between devices: 44.3 us -> 45.1 us  [swap(): return lax.ppermute(array, axis, [(0, 1), (1, 0)])]
  transfers between devices with their start and end apart: 95 -> 90, of which waited for: 41 -> 32; matrix products, arithmetic and copies ran while one was open for 12% -> 13% of each run, Pallas kernels for 28% -> 23%
where the time goes in v3:
time: 638 us; the launch traced here: 631 us
  waiting for transfers between devices  220 us (34%)
  Pallas kernels  178 us (28%)
  starting transfers between devices  101 us (16%)
  other arithmetic  46.2 us (7%)
  local copies, waits for them, and re-layouts  31.5 us (5%)
  blocking collectives  24.3 us (4%)
  between operations  15.5 us (2%)
  matrix products  15.2 us (2%)
    all_to_all x8, waiting for transfers between devices, spread_z(): return lax.all_to_all(parts, 'z', split_axis=0, concat_axis=0, tiled=True)  81 us
    pallas_call x8, Pallas kernels, chunk_call(): pl.pallas_call(kernel, grid_spec=pltpu.PrefetchScalarGridSpec(num_scalar_...  72.2 us
    ppermute x63, waiting for transfers between devices, swap(): return lax.ppermute(array, axis, [(0, 1), (1, 0)])  68.5 us
    ppermute x12, waiting for transfers between devices, ring(): return lax.ppermute(array, 'z', [(i, (i + 1) % size) for i in range(size)])  62.4 us
    ppermute x63, starting transfers between devices, swap(): return lax.ppermute(array, axis, [(0, 1), (1, 0)])  45.1 us
    pallas_call x8, Pallas kernels, small_call(): pl.pallas_call(kernel, grid_spec=pltpu.PrefetchScalarGridSpec(num_scalar_...  44.1 us
    all_to_all x8, starting transfers between devices, spread_z(): return lax.all_to_all(parts, 'z', split_axis=0, concat_axis=0, tiled=True)  31.2 us
    all_to_all x1, blocking collectives, on_device(): lax.all_to_all(att_low, ('z', 'y'), split_axis=0, concat_axis=0, tiled=True)  24.3 us
  transfers between devices with their start and end apart: 90, of which 32 were waited for; matrix products, arithmetic and copies ran while one was open for 13% of the time, Pallas kernels for 23%

profile of v3, /device:TPU:0, one launch (start us, length us, event | category | flops | bytes accessed | tf_op | source)
XLA Modules:
  0.0 631.3 jit_solution(14965236848065394952)
XLA Ops:
  24.9 4.1 all-to-all-start
  34.9 16.5 %all-to-all-done.refs_5_.w_first = bf16[4,400,256]{2,1,0:T(8,128)(2,1)S(1)} async-done(((bf16[4,400,256]{2,1,0:T(8,128)(2,1)}), bf16[4,400,256]{2,1,0:T(8,128)(2,1)S(1)}, u32[]{:S(2)}, u32[]{:S(2)}) %all-to-all-start) | async-done | bytes 819232 | tf_op jit(solution)/shard_map/all_to_all | solution.py:749
  54.7 10.8 %collective-permute-done.7.refs_0_ = bf16[384,512]{1,0:T(8,128)(2,1)S(1)} collective-permute-done((bf16[384,512]{1,0:T(8,128)(2,1)}, bf16[384,512]{1,0:T(8,128)(2,1)S(1)}, u32[]{:S(2)}, u32[]{:S(2)}) %collective-permute-start.7) | collective-permute-done | bytes 393248 | tf_op jit(solution)/shard_map/ppermute | solution.py:66
  67.7 3.9 collective-permute-done.11.refs_6_.w_second
  82.0 5.7 qkv.4
  89.3 5.7 qkv.5
  95.5 5.7 qkv.6
  103.6 5.9 qkv.7
  111.0 8.3 %collective-permute-done.19.refs_7_ = bf16[192,384]{1,0:T(8,128)(2,1)S(1)} collective-permute-done((bf16[192,384]{1,0:T(8,128)(2,1)}, bf16[192,384]{1,0:T(8,128)(2,1)S(1)}, u32[]{:S(2)}, u32[]{:S(2)}) %collective-permute-start.19) | collective-permute-done | bytes 147488 | tf_op jit(solution)/shard_map/ppermute | solution.py:62
  119.2 4.1 all-to-all-done.1
  129.3 19.3 %attend.1 = (bf16[8,64,384]{2,1,0:T(8,128)(2,1)}, f32[8,64,384]{2,1,0:T(8,128)}, f32[8,1,384]{2,1,0:T(1,128)}, f32[8,1,384]{2,1,0:T(1,128)}) custom-call(s32[64]{0:T(128)} %reshape.313.visible, s32[8]{0:T(128)} %get-tuple-element.250.counts, s32[17]{0:T(128)} %concatenate.29.q_pos, s32[8]{0:T(128)} %copy-done.51, ...), custom_call_target="tpu_custom_call" | custom-call | flops 17999998976 | bytes 1000 | tf_op jit(solution)/shard_map/attend/pallas_call | solution.py:165
  148.6 4.3 collective-permute-done.20
  152.9 13.0 %all-to-all-done.2 = bf16[4,256,512]{2,1,0:T(8,128)(2,1)S(1)} async-done(((bf16[4,256,512]{2,1,0:T(8,128)(2,1)}), bf16[4,256,512]{2,1,0:T(8,128)(2,1)S(1)}, u32[]{:S(2)}, u32[]{:S(2)}) %all-to-all-start.2) | async-done | bytes 1048608 | tf_op jit(solution)/shard_map/all_to_all | solution.py:749
  165.9 24.3 %all_to_all.50 = bf16[8,64,384]{2,1,0:T(8,128)(2,1)} all-to-all(bf16[8,64,384]{2,1,0:T(8,128)(2,1)} %get-tuple-element.296), channel_id=1, replica_groups=mesh['z'=4,'q'=1,'y'=2,'x'=2,'c'=2] {'z','y'}, dimensions={0} | all-to-all | bytes 786432 | tf_op jit(solution)/shard_map/all_to_all | solution.py:933
  190.2 4.5 project.1
  203.9 8.8 %collective-permute-done.22 = bf16[384,512]{1,0:T(8,128)(2,1)S(1)} collective-permute-done((bf16[384,512]{1,0:T(8,128)(2,1)S(1)}, bf16[384,512]{1,0:T(8,128)(2,1)S(1)}, u32[]{:S(2)}, u32[]{:S(2)}) %collective-permute-start.22) | collective-permute-done | bytes 393248 | tf_op jit(solution)/shard_map/ppermute | solution.py:62
  216.9 13.4 %collective-permute-done.23.refs_4_ = bf16[384,512]{1,0:T(8,128)(2,1)S(1)} collective-permute-done((bf16[384,512]{1,0:T(8,128)(2,1)S(1)}, bf16[384,512]{1,0:T(8,128)(2,1)S(1)}, u32[]{:S(2)}, u32[]{:S(2)}) %collective-permute-start.23) | collective-permute-done | bytes 393248 | tf_op jit(solution)/shard_map/ppermute | solution.py:66
  230.4 4.8 collective-permute-start.27
  236.6 8.6 %all-to-all-done.4 = bf16[4,256,512]{2,1,0:T(8,128)(2,1)S(1)} async-done(((bf16[4,256,512]{2,1,0:T(8,128)(2,1)}), bf16[4,256,512]{2,1,0:T(8,128)(2,1)S(1)}, u32[]{:S(2)}, u32[]{:S(2)}) %all-to-all-start.4) | async-done | bytes 1048608 | tf_op jit(solution)/shard_map/all_to_all | solution.py:749
  253.1 7.3 %arrange.1.refs_12_ = bf16[1536,2048]{1,0:T(8,128)(2,1)} custom-call(s32[4]{0:T(128)} %add_add_fusion.1.zs, bf16[16,384,512]{2,1,0:T(8,128)(2,1)} %bitcast.193), custom_call_target="tpu_custom_call" | custom-call | flops 5000000000 | bytes 1000 | tf_op jit(solution)/shard_map/arrange/pallas_call | solution.py:476
  262.9 10.8 %feed_forward.2 = (bf16[1536,2048]{1,0:T(8,128)(2,1)}, bf16[1536,512]{1,0:T(8,128)(2,1)}, f32[384,512]{1,0:T(8,128)}, f32[384,512]{1,0:T(8,128)}, f32[384,512]{1...) custom-call(s32[4]{0:T(128)} %get-tuple-element.434.where, bf16[384,512]{1,0:T(8,128)(2,1)} %copy-done.5, ...), custom_call_target="tpu_custom_call" | custom-call | flops 8999999488 | bytes 1000 | tf_op jit(solution)/shard_map/feed_forward/pallas_call | solution.py:364
  276.9 10.9 %feed_forward.3 = (bf16[1536,2048]{1,0:T(8,128)(2,1)}, bf16[1536,512]{1,0:T(8,128)(2,1)}, f32[384,512]{1,0:T(8,128)}, f32[384,512]{1,0:T(8,128)}, f32[384,512]{1...) custom-call(s32[4]{0:T(128)} %get-tuple-element.434.where, ...), custom_call_target="tpu_custom_call", output_to_operand_aliasing={{0}: (15, {}), {1}: (16, {})} | custom-call | flops 8999999488 | bytes 1000 | tf_op jit(solution)/shard_map/feed_forward/pallas_call | solution.py:364
  287.8 13.9 %feed_forward_back.2 = (bf16[1536,512]{1,0:T(8,128)(2,1)}, bf16[1536,512]{1,0:T(8,128)(2,1)}, bf16[16,384,512]{2,1,0:T(8,128)(2,1)}, bf16[2,400,512]{2,1,0:T(8,1...) custom-call(s32[5]{0:T(128)} %concatenate.30.where, ...), custom_call_target="tpu_custom_call" | custom-call | flops 15000000512 | bytes 1000 | tf_op jit(solution)/shard_map/feed_forward_back/pallas_call | solution.py:364
  306.9 13.6 %feed_forward_back.3 = (bf16[1536,512]{1,0:T(8,128)(2,1)}, bf16[1536,512]{1,0:T(8,128)(2,1)}, bf16[16,384,512]{2,1,0:T(8,128)(2,1)}, bf16[2,400,512]{2,1,0:T(8,1...) custom-call(s32[5]{0:T(128)} %concatenate.31.where, ...), custom_call_target="tpu_custom_call", output_to_operand_aliasing={{0}: (16, {}), {1}: (17, {}), {2}: (18, {})} | custom-call | flops 15000000512 | bytes 1000 | tf_op jit(solution)/shard_map/feed_forward_back/pallas_call | solution.py:364
  324.9 6.9 %convolution_convert_fusion.2 = bf16[2048,512]{1,0:T(8,128)(2,1)S(1)} fusion(bf16[1536,2048]{1,0:T(8,128)(2,1)} %arrange.1.refs_12_, bf16[1536,512]{1,0:T(8,128)(2,1)S(1)} %copy-done.82), kind=kOutput, calls=%fused_computation.2 | convolution fusion | flops 3222274048 | bytes 9961472 | tf_op jit(solution)/shard_map/dot_general | solution.py:52
  342.7 6.1 collective-permute-done.48
  348.8 13.1 %collective-permute-done.51 = bf16[1024,512]{1,0:T(8,128)(2,1)S(1)} collective-permute-done((bf16[1024,512]{1,0:T(8,128)(2,1)S(1)}, bf16[1024,512]{1,0:T(8,128)(2,1)S(1)}, u32[]{:S(2)}, u32[]{:S(2)}) %collective-permute-start.51) | collective-permute-done | bytes 1048608 | tf_op jit(solution)/shard_map/ppermute | solution.py:62
  365.0 4.6 convolution_convert_fusion
  375.2 7.3 %collective-permute-done.54.p2 = bf16[384,512]{1,0:T(8,128)(2,1)S(1)} collective-permute-done((bf16[384,512]{1,0:T(8,128)(2,1)S(1)}, bf16[384,512]{1,0:T(8,128)(2,1)S(1)}, u32[]{:S(2)}, u32[]{:S(2)}) %collective-permute-start.54) | collective-permute-done | bytes 393248 | tf_op jit(solution)/shard_map/ppermute | solution.py:62
  382.6 9.6 %collective-permute-done.57 = bf16[1024,512]{1,0:T(8,128)(2,1)S(1)} collective-permute-done((bf16[1024,512]{1,0:T(8,128)(2,1)S(1)}, bf16[1024,512]{1,0:T(8,128)(2,1)S(1)}, u32[]{:S(2)}, u32[]{:S(2)}) %collective-permute-start.57) | collective-permute-done | bytes 1048608 | tf_op jit(solution)/shard_map/ppermute | solution.py:62
  393.2 6.6 %project_back.1 = (bf16[512,384]{1,0:T(8,128)(2,1)}, bf16[8,512,256]{2,1,0:T(8,128)(2,1)}) custom-call(s32[4]{0:T(128)} %get-tuple-element.434.where, bf16[384,512]{1,0:T(8,128)(2,1)} %copy-done.36, bf16[384,512]{1,0:T(8,128)(2,1)} %copy-done.75, bf16[384,512]{1,0:T(8,128)(2,1)} %copy-done.73, bf16[384,512]{1,0:T(8,128)(2,1)} %collective-permute-done.56.p3, ...), custom_call_target="tpu_custom_call" | custom-call | flops 6000000000 | bytes 1000 | tf_op jit(solution)/shard_map/project_back/pallas_call | solution.py:692
  399.9 4.4 all-to-all-start.5
  410.4 7.2 %all-to-all-done.5.refs_10_ = bf16[8,64,384]{2,1,0:T(8,128)(2,1)S(1)} async-done(((bf16[8,64,384]{2,1,0:T(8,128)(2,1)}), bf16[8,64,384]{2,1,0:T(8,128)(2,1)S(1)}, u32[]{:S(2)}, u32[]{:S(2)}) %all-to-all-start.5) | async-done | bytes 393248 | tf_op jit(solution)/shard_map/all_to_all | solution.py:1115
  417.6 4.3 all-to-all-start.6
  422.0 24.1 %attend_back.1.mine.refs_0_ = bf16[8,192,384]{2,1,0:T(8,128)(2,1)} custom-call(s32[64]{0:T(128)} %reshape.313.visible, s32[8]{0:T(128)} %get-tuple-element.250.counts, s32[17]{0:T(128)} %concatenate.29.q_pos, s32[8]{0:T(128)} %copy-done.51, bf16[192,384]{1,0:T(8,128)(2,1)} %get-tuple-element.279.refs_0_, bf16[192,384]{1,0:T(8,128)(2,1)} %get-tuple-element.280.refs_1_, ...), custom_call_target="tpu_custom_call" | custom-call | flops 22000001024 | bytes 1000 | tf_op jit(solution)/shard_map/attend_back/pallas_call | solution.py:250
  446.1 6.5 %all-to-all-done.6.parts = bf16[4,256,512]{2,1,0:T(8,128)(2,1)} async-done(((bf16[4,256,512]{2,1,0:T(8,128)(2,1)}), bf16[4,256,512]{2,1,0:T(8,128)(2,1)}, u32[]{:S(2)}, u32[]{:S(2)}) %all-to-all-start.6) | async-done | bytes 1048608 | tf_op jit(solution)/shard_map/all_to_all | solution.py:749
  468.0 5.3 qkv_back.4
  473.3 8.3 %qkv_weights.1 = (bf16[4,384,256]{2,1,0:T(8,128)(2,1)}, bf16[4,384,256]{2,1,0:T(8,128)(2,1)}) custom-call(s32[4]{0:T(128)} %get-tuple-element.414.where, bf16[1536,2048]{1,0:T(8,128)(2,1)} %get-tuple-element.407.normed, bf16[8,192,384]{2,1,0:T(8,128)(2,1)} %attend_back.1.mine.refs_0_, bf16[4,192,384]{2,1,0:T(8,128)(2,1)} %collective-permute-done.59.other.refs_1_), custom_call_target="tpu_custom_call" | custom-call | flops 8000000000 | bytes 1000 | tf_op jit(solution)/shard_map/qkv_weights/pallas_call | solution.py:692
  481.6 5.3 qkv_back.5
  486.8 6.7 %all-to-all-done.7.parts = bf16[4,256,512]{2,1,0:T(8,128)(2,1)S(1)} async-done(((bf16[4,256,512]{2,1,0:T(8,128)(2,1)}), bf16[4,256,512]{2,1,0:T(8,128)(2,1)S(1)}, u32[]{:S(2)}, u32[]{:S(2)}) %all-to-all-start.7) | async-done | bytes 1048608 | tf_op jit(solution)/shard_map/all_to_all | solution.py:749
  493.5 4.2 all-to-all-start.8
  503.2 5.4 qkv_back.6
  515.1 7.8 %collective-permute-done.63 = bf16[4,384,256]{2,1,0:T(8,128)(2,1)} collective-permute-done((bf16[4,384,256]{2,1,0:T(8,128)(2,1)}, bf16[4,384,256]{2,1,0:T(8,128)(2,1)}, u32[]{:S(2)}, u32[]{:S(2)}) %collective-permute-start.63) | collective-permute-done | bytes 786464 | tf_op jit(solution)/shard_map/ppermute | solution.py:62
  532.1 5.4 qkv_back.7
  537.5 12.8 %collective-permute-done.64 = bf16[400,512]{1,0:T(8,128)(2,1)} collective-permute-done((bf16[400,512]{1,0:T(8,128)(2,1)}, bf16[400,512]{1,0:T(8,128)(2,1)}, u32[]{:S(2)}, u32[]{:S(2)}) %collective-permute-start.64) | collective-permute-done | bytes 409632 | tf_op jit(solution)/shard_map/ppermute | solution.py:66
  558.0 4.2 all-to-all-start.9
  569.1 9.6 %collective-permute-done.67 = bf16[400,512]{1,0:T(8,128)(2,1)} collective-permute-done((bf16[400,512]{1,0:T(8,128)(2,1)}, bf16[400,512]{1,0:T(8,128)(2,1)}, u32[]{:S(2)}, u32[]{:S(2)}) %collective-permute-start.67) | collective-permute-done | bytes 409632 | tf_op jit(solution)/shard_map/ppermute | solution.py:66
  586.8 25.7 %all-to-all-done.9.parts = bf16[4,384,256]{2,1,0:T(8,128)(2,1)} async-done(((bf16[4,384,256]{2,1,0:T(8,128)(2,1)}), bf16[4,384,256]{2,1,0:T(8,128)(2,1)}, u32[]{:S(2)}, u32[]{:S(2)}) %all-to-all-start.9) | async-done | bytes 786464 | tf_op jit(solution)/shard_map/all_to_all | solution.py:749
  (467 shorter events, 186.2 us)
Async XLA Ops:
  7.2 14.4 %collective-permute-start = (bf16[384,512]{1,0:T(8,128)(2,1)}, bf16[384,512]{1,0:T(8,128)(2,1)S(1)}, u32[]{:S(2)}, u32[]{:S(2)}) collective-permute-start(bf16[384,512]{1,0:T(8,128)(2,1)} %refs_0_.1), channel_id=1, source_target_pairs={{0,8},{8,16},{16,24},{24,0},{1,9},{9,17},{17,25},{25,1},{2,10},{10... | collective-permute-start | bytes 1179656 | tf_op jit(solution)/shard_map/ppermute | solution.py:66
  24.9 26.4 %all-to-all-start = ((bf16[4,400,256]{2,1,0:T(8,128)(2,1)}), bf16[4,400,256]{2,1,0:T(8,128)(2,1)S(1)}, u32[]{:S(2)}, u32[]{:S(2)}) async-start(bf16[4,400,256]{2,1,0:T(8,128)(2,1)} %pad_maximum_fusion), calls=%async_computation | async-start | bytes 1638400 | tf_op jit(solution)/shard_map/all_to_all | solution.py:749
  29.0 161.2 %all-gather.5.cloned.1.call-start = ((), (), s32[]{:S(2)}) async-start(), calls=%async_computation.14 | async-start | bytes 2359296 | tf_op jit(solution)/shard_map/all_gather | solution.py:900
  51.3 20.2 %collective-permute-start.11 = (bf16[4,400,256]{2,1,0:T(8,128)(2,1)S(1)}, bf16[4,400,256]{2,1,0:T(8,128)(2,1)S(1)}, u32[]{:S(2)}, u32[]{:S(2)}) collective-permute-start(bf16[4,400,256]{2,1,0:T(8,128)(2,1)S(1)} %all-to-all-done.refs_5_.w_first), channel_id=1, source_target_pairs={{0,4},{4,0},{1,5},{5,1},{2,6},{6,2},{3,7},{7,3},{8,12},{12,8},{9,1... | collective-permute-start | bytes 2457608 | tf_op jit(solution)/shard_map/ppermute | solution.py:62
  71.6 181.5 %all-gather.7.cloned.1.call-start = ((), (), s32[]{:S(2)}) async-start(), calls=%async_computation.15 | async-start | bytes 6684672 | tf_op jit(solution)/shard_map/all_gather | solution.py:905
  74.3 28.5 %collective-permute-start.13 = (bf16[384,512]{1,0:T(8,128)(2,1)}, bf16[384,512]{1,0:T(8,128)(2,1)}, u32[]{:S(2)}, u32[]{:S(2)}) collective-permute-start(bf16[384,512]{1,0:T(8,128)(2,1)} %copy-done.63), channel_id=1, source_target_pairs={{0,1},{1,0},{2,3},{3,2},{4,5},{5,4},{6,7},{7,6},{8,9},{9,8},{10,11... | collective-permute-start | bytes 1179656 | tf_op jit(solution)/shard_map/ppermute | solution.py:62
  74.3 21.2 %collective-permute-start.14 = (bf16[384,512]{1,0:T(8,128)(2,1)}, bf16[384,512]{1,0:T(8,128)(2,1)}, u32[]{:S(2)}, u32[]{:S(2)}) collective-permute-start(bf16[384,512]{1,0:T(8,128)(2,1)} %copy-done.63), channel_id=1, source_target_pairs={{0,2},{2,0},{1,3},{3,1},{4,6},{6,4},{5,7},{7,5},{8,10},{10,8},{9,1... | collective-permute-start | bytes 1179656 | tf_op jit(solution)/shard_map/ppermute | solution.py:62
  76.9 18.6 %collective-permute-start.12 = (bf16[384,512]{1,0:T(8,128)(2,1)}, bf16[384,512]{1,0:T(8,128)(2,1)}, u32[]{:S(2)}, u32[]{:S(2)}) collective-permute-start(bf16[384,512]{1,0:T(8,128)(2,1)} %copy-done.65), channel_id=1, source_target_pairs={{0,1},{1,0},{2,3},{3,2},{4,5},{5,4},{6,7},{7,6},{8,9},{9,8},{10,11... | collective-permute-start | bytes 1179656 | tf_op jit(solution)/shard_map/ppermute | solution.py:62
  78.2 45.1 %all-to-all-start.1 = ((bf16[4,256,512]{2,1,0:T(8,128)(2,1)}), bf16[4,256,512]{2,1,0:T(8,128)(2,1)S(1)}, u32[]{:S(2)}, u32[]{:S(2)}) async-start(bf16[4,256,512]{2,1,0:T(8,128)(2,1)} %bitcast.160), calls=%async_computation.1 | async-start | bytes 2097152 | tf_op jit(solution)/shard_map/all_to_all | solution.py:749
  87.7 22.5 %collective-permute-start.16 = (bf16[192,384]{1,0:T(8,128)(2,1)}, bf16[192,384]{1,0:T(8,128)(2,1)S(1)}, u32[]{:S(2)}, u32[]{:S(2)}) collective-permute-start(bf16[192,384]{1,0:T(8,128)(2,1)} %get-tuple-element.274), channel_id=1, source_target_pairs={{0,4},{4,0},{1,5},{5,1},{2,6},{6,2},{3,7},{7,3},{8,12},{12,8},{9,1... | collective-permute-start | bytes 442376 | tf_op jit(solution)/shard_map/ppermute | solution.py:62
  95.0 15.2 %collective-permute-start.17 = (bf16[192,384]{1,0:T(8,128)(2,1)}, bf16[192,384]{1,0:T(8,128)(2,1)S(1)}, u32[]{:S(2)}, u32[]{:S(2)}) collective-permute-start(bf16[192,384]{1,0:T(8,128)(2,1)} %get-tuple-element.275), channel_id=1, source_target_pairs={{0,4},{4,0},{1,5},{5,1},{2,6},{6,2},{3,7},{7,3},{8,12},{12,8},{9,1... | collective-permute-start | bytes 442376 | tf_op jit(solution)/shard_map/ppermute | solution.py:62
  124.5 41.4 %all-to-all-start.2 = ((bf16[4,256,512]{2,1,0:T(8,128)(2,1)}), bf16[4,256,512]{2,1,0:T(8,128)(2,1)S(1)}, u32[]{:S(2)}, u32[]{:S(2)}) async-start(bf16[4,256,512]{2,1,0:T(8,128)(2,1)} %bitcast.158), calls=%async_computation.2 | async-start | bytes 2097152 | tf_op jit(solution)/shard_map/all_to_all | solution.py:749
  128.0 24.8 %collective-permute-start.20 = (bf16[4,256,512]{2,1,0:T(8,128)(2,1)S(1)}, bf16[4,256,512]{2,1,0:T(8,128)(2,1)S(1)}, u32[]{:S(2)}, u32[]{:S(2)}) collective-permute-start(bf16[4,256,512]{2,1,0:T(8,128)(2,1)S(1)} %all-to-all-done.1), channel_id=1, source_target_pairs={{0,4},{4,0},{1,5},{5,1},{2,6},{6,2},{3,7},{7,3},{8,12},{12,8},{9,1... | collective-permute-start | bytes 3145736 | tf_op jit(solution)/shard_map/ppermute | solution.py:62
  196.1 49.2 %all-to-all-start.4 = ((bf16[4,256,512]{2,1,0:T(8,128)(2,1)}), bf16[4,256,512]{2,1,0:T(8,128)(2,1)S(1)}, u32[]{:S(2)}, u32[]{:S(2)}) async-start(bf16[4,256,512]{2,1,0:T(8,128)(2,1)} %bitcast.40), calls=%async_computation.4 | async-start | bytes 2097152 | tf_op jit(solution)/shard_map/all_to_all | solution.py:749
  199.6 313.7 %reduce-scatter.5.cloned.1.call-start = ((), (), s32[]{:S(2)}) async-start(), calls=%async_computation.13 | async-start | bytes 2359296 | tf_op jit(solution)/shard_map/reduce_scatter | solution.py:1217
  202.1 14.9 %collective-permute-start.26 = (bf16[2,256,512]{2,1,0:T(8,128)(2,1)S(1)}, bf16[2,256,512]{2,1,0:T(8,128)(2,1)S(1)}, u32[]{:S(2)}, u32[]{:S(2)}) collective-permute-start(bf16[2,256,512]{2,1,0:T(8,128)(2,1)S(1)} %get-tuple-element.491), channel_id=1, source_target_pairs={{0,4},{4,0},{1,5},{5,1},{2,6},{6,2},{3,7},{7,3},{8,12},{12,8},{9,1... | collective-permute-start | bytes 1572872 | tf_op jit(solution)/shard_map/ppermute | solution.py:62
  212.9 17.5 %collective-permute-start.23 = (bf16[384,512]{1,0:T(8,128)(2,1)S(1)}, bf16[384,512]{1,0:T(8,128)(2,1)S(1)}, u32[]{:S(2)}, u32[]{:S(2)}) collective-permute-start(bf16[384,512]{1,0:T(8,128)(2,1)S(1)} %fusion.22.refs_0_), channel_id=1, source_target_pairs={{0,8},{8,16},{16,24},{24,0},{1,9},{9,17},{17,25},{25,1},{2,10},{10... | collective-permute-start | bytes 1179656 | tf_op jit(solution)/shard_map/ppermute | solution.py:66
  214.6 15.8 %collective-permute-start.24 = (bf16[384,512]{1,0:T(8,128)(2,1)S(1)}, bf16[384,512]{1,0:T(8,128)(2,1)}, u32[]{:S(2)}, u32[]{:S(2)}) collective-permute-start(bf16[384,512]{1,0:T(8,128)(2,1)S(1)} %fusion.22.refs_0_), channel_id=1, source_target_pairs={{0,2},{2,0},{1,3},{3,1},{4,6},{6,4},{5,7},{7,5},{8,10},{10,8},{9,1... | collective-permute-start | bytes 1179656 | tf_op jit(solution)/shard_map/ppermute | solution.py:62
  215.4 15.0 %collective-permute-start.25 = (bf16[384,512]{1,0:T(8,128)(2,1)S(1)}, bf16[384,512]{1,0:T(8,128)(2,1)}, u32[]{:S(2)}, u32[]{:S(2)}) collective-permute-start(bf16[384,512]{1,0:T(8,128)(2,1)S(1)} %fusion.22.refs_0_), channel_id=1, source_target_pairs={{0,1},{1,0},{2,3},{3,2},{4,5},{5,4},{6,7},{7,6},{8,9},{9,8},{10,11... | collective-permute-start | bytes 1179656 | tf_op jit(solution)/shard_map/ppermute | solution.py:62
  215.4 21.3 %collective-permute-start.31 = (bf16[2,256,512]{2,1,0:T(8,128)(2,1)S(1)}, bf16[2,256,512]{2,1,0:T(8,128)(2,1)S(1)}, u32[]{:S(2)}, u32[]{:S(2)}) collective-permute-start(bf16[2,256,512]{2,1,0:T(8,128)(2,1)S(1)} %get-tuple-element.490), channel_id=1, source_target_pairs={{0,4},{4,0},{1,5},{5,1},{2,6},{6,2},{3,7},{7,3},{8,12},{12,8},{9,1... | collective-permute-start | bytes 1572872 | tf_op jit(solution)/shard_map/ppermute | solution.py:62
  230.4 14.8 %collective-permute-start.27 = (bf16[384,512]{1,0:T(8,128)(2,1)S(1)}, bf16[384,512]{1,0:T(8,128)(2,1)S(1)}, u32[]{:S(2)}, u32[]{:S(2)}) collective-permute-start(bf16[384,512]{1,0:T(8,128)(2,1)S(1)} %collective-permute-done.23.refs_4_), channel_id=1, source_target_pairs={{0,8},{8,16},{16,24},{24,0},{1,9},{9,17},{17,25},{25,1},{2,10},{10... | collective-permute-start | bytes 1179656 | tf_op jit(solution)/shard_map/ppermute | solution.py:66
  246.1 15.2 %collective-permute-start.36 = (bf16[2,256,512]{2,1,0:T(8,128)(2,1)S(1)}, bf16[2,256,512]{2,1,0:T(8,128)(2,1)}, u32[]{:S(2)}, u32[]{:S(2)}) collective-permute-start(bf16[2,256,512]{2,1,0:T(8,128)(2,1)S(1)} %get-tuple-element.489), channel_id=1, source_target_pairs={{0,4},{4,0},{1,5},{5,1},{2,6},{6,2},{3,7},{7,3},{8,12},{12,8},{9,1... | collective-permute-start | bytes 1572872 | tf_op jit(solution)/shard_map/ppermute | solution.py:62
  305.7 14.8 %collective-permute-start.43 = (bf16[400,512]{1,0:T(8,128)(2,1)S(1)}, bf16[400,512]{1,0:T(8,128)(2,1)}, u32[]{:S(2)}, u32[]{:S(2)}) collective-permute-start(bf16[400,512]{1,0:T(8,128)(2,1)S(1)} %fusion.13), channel_id=1, source_target_pairs={{0,2},{2,0},{1,3},{3,1},{4,6},{6,4},{5,7},{7,5},{8,10},{10,8},{9,1... | collective-permute-start | bytes 1228808 | tf_op jit(solution)/shard_map/ppermute | solution.py:62
  306.9 13.7 %collective-permute-start.44 = (bf16[2,400,512]{2,1,0:T(8,128)(2,1)}, bf16[2,400,512]{2,1,0:T(8,128)(2,1)}, u32[]{:S(2)}, u32[]{:S(2)}) collective-permute-start(bf16[2,400,512]{2,1,0:T(8,128)(2,1)} %get-tuple-element.348), channel_id=1, source_target_pairs={{0,1},{1,0},{2,3},{3,2},{4,5},{5,4},{6,7},{7,6},{8,9},{9,8},{10,11... | collective-permute-start | bytes 2457608 | tf_op jit(solution)/shard_map/ppermute | solution.py:62
  321.8 13.8 %collective-permute-start.45 = (bf16[400,512]{1,0:T(8,128)(2,1)S(1)}, bf16[400,512]{1,0:T(8,128)(2,1)S(1)}, u32[]{:S(2)}, u32[]{:S(2)}) collective-permute-start(bf16[400,512]{1,0:T(8,128)(2,1)S(1)} %add_convert_fusion.6), channel_id=1, source_target_pairs={{0,8},{8,16},{16,24},{24,0},{1,9},{9,17},{17,25},{25,1},{2,10},{10... | collective-permute-start | bytes 1228808 | tf_op jit(solution)/shard_map/ppermute | solution.py:66
  337.5 24.4 %collective-permute-start.51 = (bf16[1024,512]{1,0:T(8,128)(2,1)S(1)}, bf16[1024,512]{1,0:T(8,128)(2,1)S(1)}, u32[]{:S(2)}, u32[]{:S(2)}) collective-permute-start(bf16[1024,512]{1,0:T(8,128)(2,1)S(1)} %dynamic-slice_bitcast_fusion.2), channel_id=1, source_target_pairs={{0,4},{4,0},{1,5},{5,1},{2,6},{6,2},{3,7},{7,3},{8,12},{12,8},{9,1... | collective-permute-start | bytes 3145736 | tf_op jit(solution)/shard_map/ppermute | solution.py:62
  369.7 22.5 %collective-permute-start.57 = (bf16[1024,512]{1,0:T(8,128)(2,1)S(1)}, bf16[1024,512]{1,0:T(8,128)(2,1)S(1)}, u32[]{:S(2)}, u32[]{:S(2)}) collective-permute-start(bf16[1024,512]{1,0:T(8,128)(2,1)S(1)} %dynamic-slice_bitcast_fusion.1), channel_id=1, source_target_pairs={{0,4},{4,0},{1,5},{5,1},{2,6},{6,2},{3,7},{7,3},{8,12},{12,8},{9,1... | collective-permute-start | bytes 3145736 | tf_op jit(solution)/shard_map/ppermute | solution.py:62
  399.9 17.7 %all-to-all-start.5 = ((bf16[8,64,384]{2,1,0:T(8,128)(2,1)}), bf16[8,64,384]{2,1,0:T(8,128)(2,1)S(1)}, u32[]{:S(2)}, u32[]{:S(2)}) async-start(bf16[8,64,384]{2,1,0:T(8,128)(2,1)} %bitcast.62), calls=%async_computation.6 | async-start | bytes 786432 | tf_op jit(solution)/shard_map/all_to_all | solution.py:1115
  407.0 39.0 %collective-permute-start.58 = (bf16[1024,512]{1,0:T(8,128)(2,1)S(1)}, bf16[1024,512]{1,0:T(8,128)(2,1)}, u32[]{:S(2)}, u32[]{:S(2)}) collective-permute-start(bf16[1024,512]{1,0:T(8,128)(2,1)S(1)} %dynamic-slice_bitcast_fusion), channel_id=1, source_target_pairs={{0,4},{4,0},{1,5},{5,1},{2,6},{6,2},{3,7},{7,3},{8,12},{12,8},{9,1... | collective-permute-start | bytes 3145736 | tf_op jit(solution)/shard_map/ppermute | solution.py:62
  417.6 35.0 %all-to-all-start.6 = ((bf16[4,256,512]{2,1,0:T(8,128)(2,1)}), bf16[4,256,512]{2,1,0:T(8,128)(2,1)}, u32[]{:S(2)}, u32[]{:S(2)}) async-start(bf16[4,256,512]{2,1,0:T(8,128)(2,1)} %bitcast.64), calls=%async_computation.7 | async-start | bytes 2097152 | tf_op jit(solution)/shard_map/all_to_all | solution.py:749
  421.9 196.5 %reduce-scatter.3.cloned.1.call-start = ((), (), s32[]{:S(2)}) async-start(), calls=%async_computation.12 | async-start | bytes 6684672 | tf_op jit(solution)/shard_map/reduce_scatter | solution.py:1212
  453.7 14.3 %collective-permute-start.59 = (bf16[4,192,384]{2,1,0:T(8,128)(2,1)S(1)}, bf16[4,192,384]{2,1,0:T(8,128)(2,1)}, u32[]{:S(2)}, u32[]{:S(2)}) collective-permute-start(bf16[4,192,384]{2,1,0:T(8,128)(2,1)S(1)} %slice.180), channel_id=1, source_target_pairs={{0,4},{4,0},{1,5},{5,1},{2,6},{6,2},{3,7},{7,3},{8,12},{12,8},{9,1... | collective-permute-start | bytes 1769480 | tf_op jit(solution)/shard_map/ppermute | solution.py:62
  457.5 36.0 %all-to-all-start.7 = ((bf16[4,256,512]{2,1,0:T(8,128)(2,1)}), bf16[4,256,512]{2,1,0:T(8,128)(2,1)S(1)}, u32[]{:S(2)}, u32[]{:S(2)}) async-start(bf16[4,256,512]{2,1,0:T(8,128)(2,1)} %bitcast.68), calls=%async_computation.8 | async-start | bytes 2097152 | tf_op jit(solution)/shard_map/all_to_all | solution.py:749
  473.3 24.5 %collective-permute-start.60 = (bf16[2,400,512]{2,1,0:T(8,128)(2,1)}, bf16[2,400,512]{2,1,0:T(8,128)(2,1)S(1)}, u32[]{:S(2)}, u32[]{:S(2)}) collective-permute-start(bf16[2,400,512]{2,1,0:T(8,128)(2,1)} %get-tuple-element.413), channel_id=1, source_target_pairs={{0,1},{1,0},{2,3},{3,2},{4,5},{5,4},{6,7},{7,6},{8,9},{9,8},{10,11... | collective-permute-start | bytes 2457608 | tf_op jit(solution)/shard_map/ppermute | solution.py:62
  493.5 44.0 %all-to-all-start.8 = ((bf16[4,256,512]{2,1,0:T(8,128)(2,1)}), bf16[4,256,512]{2,1,0:T(8,128)(2,1)}, u32[]{:S(2)}, u32[]{:S(2)}) async-start(bf16[4,256,512]{2,1,0:T(8,128)(2,1)} %bitcast.74), calls=%async_computation.9 | async-start | bytes 2097152 | tf_op jit(solution)/shard_map/all_to_all | solution.py:749
  501.1 14.0 %collective-permute-start.61 = (bf16[400,512]{1,0:T(8,128)(2,1)}, bf16[400,512]{1,0:T(8,128)(2,1)}, u32[]{:S(2)}, u32[]{:S(2)}) collective-permute-start(bf16[400,512]{1,0:T(8,128)(2,1)} %fusion.17), channel_id=1, source_target_pairs={{0,2},{2,0},{1,3},{3,1},{4,6},{6,4},{5,7},{7,5},{8,10},{10,8},{9,1... | collective-permute-start | bytes 1228808 | tf_op jit(solution)/shard_map/ppermute | solution.py:62
  502.6 20.3 %collective-permute-start.62 = (bf16[2,400,512]{2,1,0:T(8,128)(2,1)}, bf16[2,400,512]{2,1,0:T(8,128)(2,1)}, u32[]{:S(2)}, u32[]{:S(2)}) collective-permute-start(bf16[2,400,512]{2,1,0:T(8,128)(2,1)} %get-tuple-element.422), channel_id=1, source_target_pairs={{0,1},{1,0},{2,3},{3,2},{4,5},{5,4},{6,7},{7,6},{8,9},{9,8},{10,11... | collective-permute-start | bytes 2457608 | tf_op jit(solution)/shard_map/ppermute | solution.py:62
  502.6 20.3 %collective-permute-start.63 = (bf16[4,384,256]{2,1,0:T(8,128)(2,1)}, bf16[4,384,256]{2,1,0:T(8,128)(2,1)}, u32[]{:S(2)}, u32[]{:S(2)}) collective-permute-start(bf16[4,384,256]{2,1,0:T(8,128)(2,1)} %get-tuple-element.428), channel_id=1, source_target_pairs={{0,4},{4,0},{1,5},{5,1},{2,6},{6,2},{3,7},{7,3},{8,12},{12,8},{9,1... | collective-permute-start | bytes 2359304 | tf_op jit(solution)/shard_map/ppermute | solution.py:62
  522.8 27.5 %collective-permute-start.66 = (bf16[2,400,512]{2,1,0:T(8,128)(2,1)}, bf16[2,400,512]{2,1,0:T(8,128)(2,1)}, u32[]{:S(2)}, u32[]{:S(2)}) collective-permute-start(bf16[2,400,512]{2,1,0:T(8,128)(2,1)} %get-tuple-element.433), channel_id=1, source_target_pairs={{0,1},{1,0},{2,3},{3,2},{4,5},{5,4},{6,7},{7,6},{8,9},{9,8},{10,11... | collective-permute-start | bytes 2457608 | tf_op jit(solution)/shard_map/ppermute | solution.py:62
  527.1 23.2 %collective-permute-start.64 = (bf16[400,512]{1,0:T(8,128)(2,1)}, bf16[400,512]{1,0:T(8,128)(2,1)}, u32[]{:S(2)}, u32[]{:S(2)}) collective-permute-start(bf16[400,512]{1,0:T(8,128)(2,1)} %add_convert_fusion.3), channel_id=1, source_target_pairs={{0,8},{8,16},{16,24},{24,0},{1,9},{9,17},{17,25},{25,1},{2,10},{10... | collective-permute-start | bytes 1228808 | tf_op jit(solution)/shard_map/ppermute | solution.py:66
  529.2 21.1 %collective-permute-start.65 = (bf16[400,512]{1,0:T(8,128)(2,1)}, bf16[400,512]{1,0:T(8,128)(2,1)}, u32[]{:S(2)}, u32[]{:S(2)}) collective-permute-start(bf16[400,512]{1,0:T(8,128)(2,1)} %fusion.18), channel_id=1, source_target_pairs={{0,2},{2,0},{1,3},{3,1},{4,6},{6,4},{5,7},{7,5},{8,10},{10,8},{9,1... | collective-permute-start | bytes 1228808 | tf_op jit(solution)/shard_map/ppermute | solution.py:62
  550.4 28.4 %collective-permute-start.69 = (bf16[2,400,512]{2,1,0:T(8,128)(2,1)}, bf16[2,400,512]{2,1,0:T(8,128)(2,1)}, u32[]{:S(2)}, u32[]{:S(2)}) collective-permute-start(bf16[2,400,512]{2,1,0:T(8,128)(2,1)} %get-tuple-element.446), channel_id=1, source_target_pairs={{0,1},{1,0},{2,3},{3,2},{4,5},{5,4},{6,7},{7,6},{8,9},{9,8},{10,11... | collective-permute-start | bytes 2457608 | tf_op jit(solution)/shard_map/ppermute | solution.py:62
  556.0 22.8 %collective-permute-start.67 = (bf16[400,512]{1,0:T(8,128)(2,1)}, bf16[400,512]{1,0:T(8,128)(2,1)}, u32[]{:S(2)}, u32[]{:S(2)}) collective-permute-start(bf16[400,512]{1,0:T(8,128)(2,1)} %add_convert_fusion.2), channel_id=1, source_target_pairs={{0,8},{8,16},{16,24},{24,0},{1,9},{9,17},{17,25},{25,1},{2,10},{10... | collective-permute-start | bytes 1228808 | tf_op jit(solution)/shard_map/ppermute | solution.py:66
  557.5 21.3 %collective-permute-start.68 = (bf16[400,512]{1,0:T(8,128)(2,1)}, bf16[400,512]{1,0:T(8,128)(2,1)}, u32[]{:S(2)}, u32[]{:S(2)}) collective-permute-start(bf16[400,512]{1,0:T(8,128)(2,1)} %fusion.19), channel_id=1, source_target_pairs={{0,2},{2,0},{1,3},{3,1},{4,6},{6,4},{5,7},{7,5},{8,10},{10,8},{9,1... | collective-permute-start | bytes 1228808 | tf_op jit(solution)/shard_map/ppermute | solution.py:62
  558.0 54.5 %all-to-all-start.9 = ((bf16[4,384,256]{2,1,0:T(8,128)(2,1)}), bf16[4,384,256]{2,1,0:T(8,128)(2,1)}, u32[]{:S(2)}, u32[]{:S(2)}) async-start(bf16[4,384,256]{2,1,0:T(8,128)(2,1)} %add_convert_fusion), calls=%async_computation.10 | async-start | bytes 1572864 | tf_op jit(solution)/shard_map/all_to_all | solution.py:749
  584.9 30.8 %collective-permute-start.72 = (bf16[400,512]{1,0:T(8,128)(2,1)}, bf16[400,512]{1,0:T(8,128)(2,1)}, u32[]{:S(2)}, u32[]{:S(2)}) collective-permute-start(bf16[400,512]{1,0:T(8,128)(2,1)} %add_convert_fusion.1), channel_id=1, source_target_pairs={{0,8},{8,16},{16,24},{24,0},{1,9},{9,17},{17,25},{25,1},{2,10},{10... | collective-permute-start | bytes 1228808 | tf_op jit(solution)/shard_map/ppermute | solution.py:66
  584.9 30.8 %collective-permute-start.73 = (bf16[400,512]{1,0:T(8,128)(2,1)}, bf16[400,512]{1,0:T(8,128)(2,1)}, u32[]{:S(2)}, u32[]{:S(2)}) collective-permute-start(bf16[400,512]{1,0:T(8,128)(2,1)} %fusion.20), channel_id=1, source_target_pairs={{0,2},{2,0},{1,3},{3,1},{4,6},{6,4},{5,7},{7,5},{8,10},{10,8},{9,1... | collective-permute-start | bytes 1228808 | tf_op jit(solution)/shard_map/ppermute | solution.py:62
  586.0 29.7 %collective-permute-start.75 = (f32[2,2,2048]{2,1,0:T(2,128)S(1)}, f32[2,2,2048]{2,1,0:T(2,128)S(1)}, u32[]{:S(2)}, u32[]{:S(2)}) collective-permute-start(f32[2,2,2048]{2,1,0:T(2,128)S(1)} %fusion.37), channel_id=1, source_target_pairs={{0,8},{8,0},{16,24},{24,16},{1,9},{9,1},{17,25},{25,17},{2,10},{10... | collective-permute-start | bytes 98312 | tf_op jit(solution)/shard_map/ppermute | solution.py:1200
  (127 other events, 1503.6 us)
Sparse Core Ops, SparseCore 0:
  71.7 60.4 all-gather.4
  134.5 80.6 all-gather.6
  400.0 92.8 reduce-scatter.4
  496.6 121.2 reduce-scatter.2

commit v4 on v3

--- a/solution.py
+++ b/solution.py
@@ -128,11 +128,11 @@
         jnp.int32, (width, width), 1
     )
 
-    def step(n, carry):
+    def one_tile(j, carry, diagonal):
         high, total, acc = carry
-        j = visible[i * tiles + n]
         scores = dot(k_ext[j], q_tile, 1, 0)
-        scores = jnp.where(relative <= (q_pos[i] - k_pos[j]) * width, scores, masked_fill)
+        if diagonal:
+            scores = jnp.where(relative <= 0, scores, masked_fill)
         new_high = jnp.maximum(high, jnp.max(scores, axis=0, keepdims=True))
         weights = jnp.exp(scores - new_high)
         shrink = jnp.exp(high - new_high)
@@ -140,15 +140,16 @@
         acc = acc * shrink + dot(held[j, 2 * HDIM :], weights.astype(BF16), 1, 0)
         return new_high, total, acc
 
+    start = (
+        jnp.full((1, width), masked_fill, F32),
+        jnp.zeros((1, width), F32),
+        jnp.zeros((HDIM, width), F32),
+    )
     high, total, acc = lax.fori_loop(
         0,
         counts[i],
-        step,
-        (
-            jnp.full((1, width), masked_fill, F32),
-            jnp.zeros((1, width), F32),
-            jnp.zeros((HDIM, width), F32),
-        ),
+        lambda n, carry: one_tile(visible[i * tiles + n], carry, False),
+        one_tile(mine + i, start, True),
     )
     result = acc / total
     out[0] = result
@@ -215,10 +216,10 @@
         jnp.int32, (width, width), 1
     )
 
-    def step(n, acc):
-        j = visible[i * tiles + n]
+    def one_tile(j, acc, diagonal):
         scores = dot(k_ext[j], q_tile, 1, 0)
-        scores = jnp.where(relative <= (q_pos[i] - k_pos[j]) * width, scores, masked_fill)
+        if diagonal:
+            scores = jnp.where(relative <= 0, scores, masked_fill)
         probs = jnp.exp(scores - lse)
         grad_probs = dot(values_t[j], g_ext, 1, 0)
         grad_scores = (probs * (grad_probs - delta)).astype(BF16)
@@ -226,7 +227,12 @@
         acc_k[j] += dot(q_rows, grad_scores, 1, 1)
         return acc + dot(held[j, HDIM : 2 * HDIM], grad_scores, 1, 0)
 
-    acc = lax.fori_loop(0, counts[i], step, jnp.zeros((HDIM, width), F32))
+    acc = lax.fori_loop(
+        0,
+        counts[i],
+        lambda n, acc: one_tile(visible[i * tiles + n], acc, False),
+        one_tile(mine + i, jnp.zeros((HDIM, width), F32), True),
+    )
 
     def put_unrotated(grad, t, base):
         first, second, c, s = grad[:HALF], grad[HALF:], cosine[t], sine[t]
@@ -848,7 +854,7 @@
     k_mask = k_own.astype(BF16)
     q_pos = of_queries(k_pos)
     shown = jnp.any(jnp.any(q_seen, axis=2)[:, None] & jnp.any(k_own, axis=2)[None], axis=2)
-    shown = shown & (k_pos[None, :] <= q_pos[:, None])
+    shown = shown & (k_pos[None, :] < q_pos[:, None])
     number = jnp.arange(k_tiles, dtype=jnp.int32)
     earlier = number[None, None, :] < number[None, :, None]
     before = jnp.sum((shown[:, None, :] & earlier).astype(jnp.int32), axis=2)

time: 638 us -> 638 us (level)
  no operation moved by 1% of the time
where the time goes in v4:
time: 638 us; the launch traced here: 631 us
  waiting for transfers between devices  223 us (35%)
  Pallas kernels  175 us (27%)
  starting transfers between devices  101 us (16%)
  other arithmetic  46.2 us (7%)
  local copies, waits for them, and re-layouts  31.5 us (5%)
  blocking collectives  24.3 us (4%)
  between operations  15.5 us (2%)
  matrix products  15.2 us (2%)
    all_to_all x8, waiting for transfers between devices, spread_z(): return lax.all_to_all(parts, 'z', split_axis=0, concat_axis=0, tiled=True)  83.3 us
    pallas_call x8, Pallas kernels, chunk_call(): pl.pallas_call(kernel, grid_spec=pltpu.PrefetchScalarGridSpec(num_scalar_...  72.2 us
    ppermute x63, waiting for transfers between devices, swap(): return lax.ppermute(array, axis, [(0, 1), (1, 0)])  69.7 us
    ppermute x12, waiting for transfers between devices, ring(): return lax.ppermute(array, 'z', [(i, (i + 1) % size) for i in range(size)])  62.4 us
    ppermute x63, starting transfers between devices, swap(): return lax.ppermute(array, axis, [(0, 1), (1, 0)])  45.1 us
    pallas_call x8, Pallas kernels, small_call(): pl.pallas_call(kernel, grid_spec=pltpu.PrefetchScalarGridSpec(num_scalar_...  44.1 us
    all_to_all x8, starting transfers between devices, spread_z(): return lax.all_to_all(parts, 'z', split_axis=0, concat_axis=0, tiled=True)  31.2 us
    all_to_all x1, blocking collectives, on_device(): lax.all_to_all(att_low, ('z', 'y'), split_axis=0, concat_axis=0, tiled=True)  24.3 us
  transfers between devices with their start and end apart: 90, of which 32 were waited for; matrix products, arithmetic and copies ran while one was open for 13% of the time, Pallas kernels for 23%

profile of v4, /device:TPU:0, one launch (start us, length us, event | category | flops | bytes accessed | tf_op | source)
XLA Modules:
  0.0 631.3 jit_solution(15806424805433992780)
XLA Ops:
  24.9 4.1 all-to-all-start
  34.9 16.5 %all-to-all-done.refs_5_.w_first = bf16[4,400,256]{2,1,0:T(8,128)(2,1)S(1)} async-done(((bf16[4,400,256]{2,1,0:T(8,128)(2,1)}), bf16[4,400,256]{2,1,0:T(8,128)(2,1)S(1)}, u32[]{:S(2)}, u32[]{:S(2)}) %all-to-all-start) | async-done | bytes 819232 | tf_op jit(solution)/shard_map/all_to_all | solution.py:755
  54.7 10.8 %collective-permute-done.7.refs_0_ = bf16[384,512]{1,0:T(8,128)(2,1)S(1)} collective-permute-done((bf16[384,512]{1,0:T(8,128)(2,1)}, bf16[384,512]{1,0:T(8,128)(2,1)S(1)}, u32[]{:S(2)}, u32[]{:S(2)}) %collective-permute-start.7) | collective-permute-done | bytes 393248 | tf_op jit(solution)/shard_map/ppermute | solution.py:66
  67.7 3.9 collective-permute-done.11.refs_6_.w_second
  82.0 5.7 qkv.4
  89.3 5.7 qkv.5
  95.5 5.7 qkv.6
  103.6 5.9 qkv.7
  111.0 8.3 %collective-permute-done.19.refs_7_ = bf16[192,384]{1,0:T(8,128)(2,1)S(1)} collective-permute-done((bf16[192,384]{1,0:T(8,128)(2,1)}, bf16[192,384]{1,0:T(8,128)(2,1)S(1)}, u32[]{:S(2)}, u32[]{:S(2)}) %collective-permute-start.19) | collective-permute-done | bytes 147488 | tf_op jit(solution)/shard_map/ppermute | solution.py:62
  119.2 4.1 all-to-all-done.1
  129.3 18.1 %attend.1 = (bf16[8,64,384]{2,1,0:T(8,128)(2,1)}, f32[8,64,384]{2,1,0:T(8,128)}, f32[8,1,384]{2,1,0:T(1,128)}, f32[8,1,384]{2,1,0:T(1,128)}) custom-call(s32[64]{0:T(128)} %reshape.313.visible, s32[8]{0:T(128)} %get-tuple-element.250.counts, s32[17]{0:T(128)} %concatenate.29.q_pos, s32[8]{0:T(128)} %copy-done.51, ...), custom_call_target="tpu_custom_call" | custom-call | flops 17999998976 | bytes 1000 | tf_op jit(solution)/shard_map/attend/pallas_call | solution.py:166
  147.4 5.5 collective-permute-done.20
  152.9 13.0 %all-to-all-done.2 = bf16[4,256,512]{2,1,0:T(8,128)(2,1)S(1)} async-done(((bf16[4,256,512]{2,1,0:T(8,128)(2,1)}), bf16[4,256,512]{2,1,0:T(8,128)(2,1)S(1)}, u32[]{:S(2)}, u32[]{:S(2)}) %all-to-all-start.2) | async-done | bytes 1048608 | tf_op jit(solution)/shard_map/all_to_all | solution.py:755
  165.9 24.3 %all_to_all.50 = bf16[8,64,384]{2,1,0:T(8,128)(2,1)} all-to-all(bf16[8,64,384]{2,1,0:T(8,128)(2,1)} %get-tuple-element.296), channel_id=1, replica_groups=mesh['z'=4,'q'=1,'y'=2,'x'=2,'c'=2] {'z','y'}, dimensions={0} | all-to-all | bytes 786432 | tf_op jit(solution)/shard_map/all_to_all | solution.py:939
  190.2 4.5 project.1
  203.9 8.8 %collective-permute-done.22 = bf16[384,512]{1,0:T(8,128)(2,1)S(1)} collective-permute-done((bf16[384,512]{1,0:T(8,128)(2,1)S(1)}, bf16[384,512]{1,0:T(8,128)(2,1)S(1)}, u32[]{:S(2)}, u32[]{:S(2)}) %collective-permute-start.22) | collective-permute-done | bytes 393248 | tf_op jit(solution)/shard_map/ppermute | solution.py:62
  216.9 13.4 %collective-permute-done.23.refs_4_ = bf16[384,512]{1,0:T(8,128)(2,1)S(1)} collective-permute-done((bf16[384,512]{1,0:T(8,128)(2,1)S(1)}, bf16[384,512]{1,0:T(8,128)(2,1)S(1)}, u32[]{:S(2)}, u32[]{:S(2)}) %collective-permute-start.23) | collective-permute-done | bytes 393248 | tf_op jit(solution)/shard_map/ppermute | solution.py:66
  230.4 4.8 collective-permute-start.27
  236.6 8.6 %all-to-all-done.4 = bf16[4,256,512]{2,1,0:T(8,128)(2,1)S(1)} async-done(((bf16[4,256,512]{2,1,0:T(8,128)(2,1)}), bf16[4,256,512]{2,1,0:T(8,128)(2,1)S(1)}, u32[]{:S(2)}, u32[]{:S(2)}) %all-to-all-start.4) | async-done | bytes 1048608 | tf_op jit(solution)/shard_map/all_to_all | solution.py:755
  253.1 7.3 %arrange.1.refs_12_ = bf16[1536,2048]{1,0:T(8,128)(2,1)} custom-call(s32[4]{0:T(128)} %add_add_fusion.1.zs, bf16[16,384,512]{2,1,0:T(8,128)(2,1)} %bitcast.193), custom_call_target="tpu_custom_call" | custom-call | flops 5000000000 | bytes 1000 | tf_op jit(solution)/shard_map/arrange/pallas_call | solution.py:482
  262.9 10.8 %feed_forward.2 = (bf16[1536,2048]{1,0:T(8,128)(2,1)}, bf16[1536,512]{1,0:T(8,128)(2,1)}, f32[384,512]{1,0:T(8,128)}, f32[384,512]{1,0:T(8,128)}, f32[384,512]{1...) custom-call(s32[4]{0:T(128)} %get-tuple-element.434.where, bf16[384,512]{1,0:T(8,128)(2,1)} %copy-done.5, ...), custom_call_target="tpu_custom_call" | custom-call | flops 8999999488 | bytes 1000 | tf_op jit(solution)/shard_map/feed_forward/pallas_call | solution.py:370
  276.9 10.9 %feed_forward.3 = (bf16[1536,2048]{1,0:T(8,128)(2,1)}, bf16[1536,512]{1,0:T(8,128)(2,1)}, f32[384,512]{1,0:T(8,128)}, f32[384,512]{1,0:T(8,128)}, f32[384,512]{1...) custom-call(s32[4]{0:T(128)} %get-tuple-element.434.where, ...), custom_call_target="tpu_custom_call", output_to_operand_aliasing={{0}: (15, {}), {1}: (16, {})} | custom-call | flops 8999999488 | bytes 1000 | tf_op jit(solution)/shard_map/feed_forward/pallas_call | solution.py:370
  287.8 13.9 %feed_forward_back.2 = (bf16[1536,512]{1,0:T(8,128)(2,1)}, bf16[1536,512]{1,0:T(8,128)(2,1)}, bf16[16,384,512]{2,1,0:T(8,128)(2,1)}, bf16[2,400,512]{2,1,0:T(8,1...) custom-call(s32[5]{0:T(128)} %concatenate.30.where, ...), custom_call_target="tpu_custom_call" | custom-call | flops 15000000512 | bytes 1000 | tf_op jit(solution)/shard_map/feed_forward_back/pallas_call | solution.py:370
  306.9 13.6 %feed_forward_back.3 = (bf16[1536,512]{1,0:T(8,128)(2,1)}, bf16[1536,512]{1,0:T(8,128)(2,1)}, bf16[16,384,512]{2,1,0:T(8,128)(2,1)}, bf16[2,400,512]{2,1,0:T(8,1...) custom-call(s32[5]{0:T(128)} %concatenate.31.where, ...), custom_call_target="tpu_custom_call", output_to_operand_aliasing={{0}: (16, {}), {1}: (17, {}), {2}: (18, {})} | custom-call | flops 15000000512 | bytes 1000 | tf_op jit(solution)/shard_map/feed_forward_back/pallas_call | solution.py:370
  324.9 6.9 %convolution_convert_fusion.2 = bf16[2048,512]{1,0:T(8,128)(2,1)S(1)} fusion(bf16[1536,2048]{1,0:T(8,128)(2,1)} %arrange.1.refs_12_, bf16[1536,512]{1,0:T(8,128)(2,1)S(1)} %copy-done.82), kind=kOutput, calls=%fused_computation.2 | convolution fusion | flops 3222274048 | bytes 9961472 | tf_op jit(solution)/shard_map/dot_general | solution.py:52
  342.7 6.1 collective-permute-done.48
  348.8 13.1 %collective-permute-done.51 = bf16[1024,512]{1,0:T(8,128)(2,1)S(1)} collective-permute-done((bf16[1024,512]{1,0:T(8,128)(2,1)S(1)}, bf16[1024,512]{1,0:T(8,128)(2,1)S(1)}, u32[]{:S(2)}, u32[]{:S(2)}) %collective-permute-start.51) | collective-permute-done | bytes 1048608 | tf_op jit(solution)/shard_map/ppermute | solution.py:62
  365.0 4.6 convolution_convert_fusion
  375.2 7.3 %collective-permute-done.54.p2 = bf16[384,512]{1,0:T(8,128)(2,1)S(1)} collective-permute-done((bf16[384,512]{1,0:T(8,128)(2,1)S(1)}, bf16[384,512]{1,0:T(8,128)(2,1)S(1)}, u32[]{:S(2)}, u32[]{:S(2)}) %collective-permute-start.54) | collective-permute-done | bytes 393248 | tf_op jit(solution)/shard_map/ppermute | solution.py:62
  382.6 9.6 %collective-permute-done.57 = bf16[1024,512]{1,0:T(8,128)(2,1)S(1)} collective-permute-done((bf16[1024,512]{1,0:T(8,128)(2,1)S(1)}, bf16[1024,512]{1,0:T(8,128)(2,1)S(1)}, u32[]{:S(2)}, u32[]{:S(2)}) %collective-permute-start.57) | collective-permute-done | bytes 1048608 | tf_op jit(solution)/shard_map/ppermute | solution.py:62
  393.2 6.6 %project_back.1 = (bf16[512,384]{1,0:T(8,128)(2,1)}, bf16[8,512,256]{2,1,0:T(8,128)(2,1)}) custom-call(s32[4]{0:T(128)} %get-tuple-element.434.where, bf16[384,512]{1,0:T(8,128)(2,1)} %copy-done.36, bf16[384,512]{1,0:T(8,128)(2,1)} %copy-done.75, bf16[384,512]{1,0:T(8,128)(2,1)} %copy-done.73, bf16[384,512]{1,0:T(8,128)(2,1)} %collective-permute-done.56.p3, ...), custom_call_target="tpu_custom_call" | custom-call | flops 6000000000 | bytes 1000 | tf_op jit(solution)/shard_map/project_back/pallas_call | solution.py:698
  399.9 4.4 all-to-all-start.5
  410.4 7.2 %all-to-all-done.5.refs_10_ = bf16[8,64,384]{2,1,0:T(8,128)(2,1)S(1)} async-done(((bf16[8,64,384]{2,1,0:T(8,128)(2,1)}), bf16[8,64,384]{2,1,0:T(8,128)(2,1)S(1)}, u32[]{:S(2)}, u32[]{:S(2)}) %all-to-all-start.5) | async-done | bytes 393248 | tf_op jit(solution)/shard_map/all_to_all | solution.py:1121
  417.6 4.3 all-to-all-start.6
  422.0 21.9 %attend_back.1.mine.refs_0_ = bf16[8,192,384]{2,1,0:T(8,128)(2,1)} custom-call(s32[64]{0:T(128)} %reshape.313.visible, s32[8]{0:T(128)} %get-tuple-element.250.counts, s32[17]{0:T(128)} %concatenate.29.q_pos, s32[8]{0:T(128)} %copy-done.51, bf16[192,384]{1,0:T(8,128)(2,1)} %get-tuple-element.279.refs_0_, bf16[192,384]{1,0:T(8,128)(2,1)} %get-tuple-element.280.refs_1_, ...), custom_call_target="tpu_custom_call" | custom-call | flops 22000001024 | bytes 1000 | tf_op jit(solution)/shard_map/attend_back/pallas_call | solution.py:256
  443.9 8.7 %all-to-all-done.6.parts = bf16[4,256,512]{2,1,0:T(8,128)(2,1)} async-done(((bf16[4,256,512]{2,1,0:T(8,128)(2,1)}), bf16[4,256,512]{2,1,0:T(8,128)(2,1)}, u32[]{:S(2)}, u32[]{:S(2)}) %all-to-all-start.6) | async-done | bytes 1048608 | tf_op jit(solution)/shard_map/all_to_all | solution.py:755
  468.0 5.3 qkv_back.4
  473.3 8.3 %qkv_weights.1 = (bf16[4,384,256]{2,1,0:T(8,128)(2,1)}, bf16[4,384,256]{2,1,0:T(8,128)(2,1)}) custom-call(s32[4]{0:T(128)} %get-tuple-element.414.where, bf16[1536,2048]{1,0:T(8,128)(2,1)} %get-tuple-element.407.normed, bf16[8,192,384]{2,1,0:T(8,128)(2,1)} %attend_back.1.mine.refs_0_, bf16[4,192,384]{2,1,0:T(8,128)(2,1)} %collective-permute-done.59.other.refs_1_), custom_call_target="tpu_custom_call" | custom-call | flops 8000000000 | bytes 1000 | tf_op jit(solution)/shard_map/qkv_weights/pallas_call | solution.py:698
  481.6 5.3 qkv_back.5
  486.8 6.7 %all-to-all-done.7.parts = bf16[4,256,512]{2,1,0:T(8,128)(2,1)S(1)} async-done(((bf16[4,256,512]{2,1,0:T(8,128)(2,1)}), bf16[4,256,512]{2,1,0:T(8,128)(2,1)S(1)}, u32[]{:S(2)}, u32[]{:S(2)}) %all-to-all-start.7) | async-done | bytes 1048608 | tf_op jit(solution)/shard_map/all_to_all | solution.py:755
  493.5 4.2 all-to-all-start.8
  503.2 5.4 qkv_back.6
  515.1 7.8 %collective-permute-done.63 = bf16[4,384,256]{2,1,0:T(8,128)(2,1)} collective-permute-done((bf16[4,384,256]{2,1,0:T(8,128)(2,1)}, bf16[4,384,256]{2,1,0:T(8,128)(2,1)}, u32[]{:S(2)}, u32[]{:S(2)}) %collective-permute-start.63) | collective-permute-done | bytes 786464 | tf_op jit(solution)/shard_map/ppermute | solution.py:62
  532.1 5.4 qkv_back.7
  537.5 12.8 %collective-permute-done.64 = bf16[400,512]{1,0:T(8,128)(2,1)} collective-permute-done((bf16[400,512]{1,0:T(8,128)(2,1)}, bf16[400,512]{1,0:T(8,128)(2,1)}, u32[]{:S(2)}, u32[]{:S(2)}) %collective-permute-start.64) | collective-permute-done | bytes 409632 | tf_op jit(solution)/shard_map/ppermute | solution.py:66
  558.1 4.2 all-to-all-start.9
  569.1 9.6 %collective-permute-done.67 = bf16[400,512]{1,0:T(8,128)(2,1)} collective-permute-done((bf16[400,512]{1,0:T(8,128)(2,1)}, bf16[400,512]{1,0:T(8,128)(2,1)}, u32[]{:S(2)}, u32[]{:S(2)}) %collective-permute-start.67) | collective-permute-done | bytes 409632 | tf_op jit(solution)/shard_map/ppermute | solution.py:66
  586.8 25.7 %all-to-all-done.9.parts = bf16[4,384,256]{2,1,0:T(8,128)(2,1)} async-done(((bf16[4,384,256]{2,1,0:T(8,128)(2,1)}), bf16[4,384,256]{2,1,0:T(8,128)(2,1)}, u32[]{:S(2)}, u32[]{:S(2)}) %all-to-all-start.9) | async-done | bytes 786464 | tf_op jit(solution)/shard_map/all_to_all | solution.py:755
  (467 shorter events, 186.2 us)
Async XLA Ops:
  7.2 14.4 %collective-permute-start = (bf16[384,512]{1,0:T(8,128)(2,1)}, bf16[384,512]{1,0:T(8,128)(2,1)S(1)}, u32[]{:S(2)}, u32[]{:S(2)}) collective-permute-start(bf16[384,512]{1,0:T(8,128)(2,1)} %refs_0_.1), channel_id=1, source_target_pairs={{0,8},{8,16},{16,24},{24,0},{1,9},{9,17},{17,25},{25,1},{2,10},{10... | collective-permute-start | bytes 1179656 | tf_op jit(solution)/shard_map/ppermute | solution.py:66
  24.9 26.4 %all-to-all-start = ((bf16[4,400,256]{2,1,0:T(8,128)(2,1)}), bf16[4,400,256]{2,1,0:T(8,128)(2,1)S(1)}, u32[]{:S(2)}, u32[]{:S(2)}) async-start(bf16[4,400,256]{2,1,0:T(8,128)(2,1)} %pad_maximum_fusion), calls=%async_computation | async-start | bytes 1638400 | tf_op jit(solution)/shard_map/all_to_all | solution.py:755
  29.0 161.2 %all-gather.5.cloned.1.call-start = ((), (), s32[]{:S(2)}) async-start(), calls=%async_computation.14 | async-start | bytes 2359296 | tf_op jit(solution)/shard_map/all_gather | solution.py:906
  51.3 20.2 %collective-permute-start.11 = (bf16[4,400,256]{2,1,0:T(8,128)(2,1)S(1)}, bf16[4,400,256]{2,1,0:T(8,128)(2,1)S(1)}, u32[]{:S(2)}, u32[]{:S(2)}) collective-permute-start(bf16[4,400,256]{2,1,0:T(8,128)(2,1)S(1)} %all-to-all-done.refs_5_.w_first), channel_id=1, source_target_pairs={{0,4},{4,0},{1,5},{5,1},{2,6},{6,2},{3,7},{7,3},{8,12},{12,8},{9,1... | collective-permute-start | bytes 2457608 | tf_op jit(solution)/shard_map/ppermute | solution.py:62
  71.6 181.5 %all-gather.7.cloned.1.call-start = ((), (), s32[]{:S(2)}) async-start(), calls=%async_computation.15 | async-start | bytes 6684672 | tf_op jit(solution)/shard_map/all_gather | solution.py:911
  74.3 28.5 %collective-permute-start.13 = (bf16[384,512]{1,0:T(8,128)(2,1)}, bf16[384,512]{1,0:T(8,128)(2,1)}, u32[]{:S(2)}, u32[]{:S(2)}) collective-permute-start(bf16[384,512]{1,0:T(8,128)(2,1)} %copy-done.63), channel_id=1, source_target_pairs={{0,1},{1,0},{2,3},{3,2},{4,5},{5,4},{6,7},{7,6},{8,9},{9,8},{10,11... | collective-permute-start | bytes 1179656 | tf_op jit(solution)/shard_map/ppermute | solution.py:62
  74.3 21.2 %collective-permute-start.14 = (bf16[384,512]{1,0:T(8,128)(2,1)}, bf16[384,512]{1,0:T(8,128)(2,1)}, u32[]{:S(2)}, u32[]{:S(2)}) collective-permute-start(bf16[384,512]{1,0:T(8,128)(2,1)} %copy-done.63), channel_id=1, source_target_pairs={{0,2},{2,0},{1,3},{3,1},{4,6},{6,4},{5,7},{7,5},{8,10},{10,8},{9,1... | collective-permute-start | bytes 1179656 | tf_op jit(solution)/shard_map/ppermute | solution.py:62
  76.9 18.6 %collective-permute-start.12 = (bf16[384,512]{1,0:T(8,128)(2,1)}, bf16[384,512]{1,0:T(8,128)(2,1)}, u32[]{:S(2)}, u32[]{:S(2)}) collective-permute-start(bf16[384,512]{1,0:T(8,128)(2,1)} %copy-done.65), channel_id=1, source_target_pairs={{0,1},{1,0},{2,3},{3,2},{4,5},{5,4},{6,7},{7,6},{8,9},{9,8},{10,11... | collective-permute-start | bytes 1179656 | tf_op jit(solution)/shard_map/ppermute | solution.py:62
  78.2 45.1 %all-to-all-start.1 = ((bf16[4,256,512]{2,1,0:T(8,128)(2,1)}), bf16[4,256,512]{2,1,0:T(8,128)(2,1)S(1)}, u32[]{:S(2)}, u32[]{:S(2)}) async-start(bf16[4,256,512]{2,1,0:T(8,128)(2,1)} %bitcast.160), calls=%async_computation.1 | async-start | bytes 2097152 | tf_op jit(solution)/shard_map/all_to_all | solution.py:755
  87.7 22.5 %collective-permute-start.16 = (bf16[192,384]{1,0:T(8,128)(2,1)}, bf16[192,384]{1,0:T(8,128)(2,1)S(1)}, u32[]{:S(2)}, u32[]{:S(2)}) collective-permute-start(bf16[192,384]{1,0:T(8,128)(2,1)} %get-tuple-element.274), channel_id=1, source_target_pairs={{0,4},{4,0},{1,5},{5,1},{2,6},{6,2},{3,7},{7,3},{8,12},{12,8},{9,1... | collective-permute-start | bytes 442376 | tf_op jit(solution)/shard_map/ppermute | solution.py:62
  95.0 15.2 %collective-permute-start.17 = (bf16[192,384]{1,0:T(8,128)(2,1)}, bf16[192,384]{1,0:T(8,128)(2,1)S(1)}, u32[]{:S(2)}, u32[]{:S(2)}) collective-permute-start(bf16[192,384]{1,0:T(8,128)(2,1)} %get-tuple-element.275), channel_id=1, source_target_pairs={{0,4},{4,0},{1,5},{5,1},{2,6},{6,2},{3,7},{7,3},{8,12},{12,8},{9,1... | collective-permute-start | bytes 442376 | tf_op jit(solution)/shard_map/ppermute | solution.py:62
  124.5 41.4 %all-to-all-start.2 = ((bf16[4,256,512]{2,1,0:T(8,128)(2,1)}), bf16[4,256,512]{2,1,0:T(8,128)(2,1)S(1)}, u32[]{:S(2)}, u32[]{:S(2)}) async-start(bf16[4,256,512]{2,1,0:T(8,128)(2,1)} %bitcast.158), calls=%async_computation.2 | async-start | bytes 2097152 | tf_op jit(solution)/shard_map/all_to_all | solution.py:755
  128.0 24.8 %collective-permute-start.20 = (bf16[4,256,512]{2,1,0:T(8,128)(2,1)S(1)}, bf16[4,256,512]{2,1,0:T(8,128)(2,1)S(1)}, u32[]{:S(2)}, u32[]{:S(2)}) collective-permute-start(bf16[4,256,512]{2,1,0:T(8,128)(2,1)S(1)} %all-to-all-done.1), channel_id=1, source_target_pairs={{0,4},{4,0},{1,5},{5,1},{2,6},{6,2},{3,7},{7,3},{8,12},{12,8},{9,1... | collective-permute-start | bytes 3145736 | tf_op jit(solution)/shard_map/ppermute | solution.py:62
  196.1 49.2 %all-to-all-start.4 = ((bf16[4,256,512]{2,1,0:T(8,128)(2,1)}), bf16[4,256,512]{2,1,0:T(8,128)(2,1)S(1)}, u32[]{:S(2)}, u32[]{:S(2)}) async-start(bf16[4,256,512]{2,1,0:T(8,128)(2,1)} %bitcast.40), calls=%async_computation.4 | async-start | bytes 2097152 | tf_op jit(solution)/shard_map/all_to_all | solution.py:755
  199.6 313.7 %reduce-scatter.5.cloned.1.call-start = ((), (), s32[]{:S(2)}) async-start(), calls=%async_computation.13 | async-start | bytes 2359296 | tf_op jit(solution)/shard_map/reduce_scatter | solution.py:1223
  202.1 14.9 %collective-permute-start.26 = (bf16[2,256,512]{2,1,0:T(8,128)(2,1)S(1)}, bf16[2,256,512]{2,1,0:T(8,128)(2,1)S(1)}, u32[]{:S(2)}, u32[]{:S(2)}) collective-permute-start(bf16[2,256,512]{2,1,0:T(8,128)(2,1)S(1)} %get-tuple-element.491), channel_id=1, source_target_pairs={{0,4},{4,0},{1,5},{5,1},{2,6},{6,2},{3,7},{7,3},{8,12},{12,8},{9,1... | collective-permute-start | bytes 1572872 | tf_op jit(solution)/shard_map/ppermute | solution.py:62
  212.9 17.5 %collective-permute-start.23 = (bf16[384,512]{1,0:T(8,128)(2,1)S(1)}, bf16[384,512]{1,0:T(8,128)(2,1)S(1)}, u32[]{:S(2)}, u32[]{:S(2)}) collective-permute-start(bf16[384,512]{1,0:T(8,128)(2,1)S(1)} %fusion.22.refs_0_), channel_id=1, source_target_pairs={{0,8},{8,16},{16,24},{24,0},{1,9},{9,17},{17,25},{25,1},{2,10},{10... | collective-permute-start | bytes 1179656 | tf_op jit(solution)/shard_map/ppermute | solution.py:66
  214.6 15.8 %collective-permute-start.24 = (bf16[384,512]{1,0:T(8,128)(2,1)S(1)}, bf16[384,512]{1,0:T(8,128)(2,1)}, u32[]{:S(2)}, u32[]{:S(2)}) collective-permute-start(bf16[384,512]{1,0:T(8,128)(2,1)S(1)} %fusion.22.refs_0_), channel_id=1, source_target_pairs={{0,2},{2,0},{1,3},{3,1},{4,6},{6,4},{5,7},{7,5},{8,10},{10,8},{9,1... | collective-permute-start | bytes 1179656 | tf_op jit(solution)/shard_map/ppermute | solution.py:62
  215.4 15.0 %collective-permute-start.25 = (bf16[384,512]{1,0:T(8,128)(2,1)S(1)}, bf16[384,512]{1,0:T(8,128)(2,1)}, u32[]{:S(2)}, u32[]{:S(2)}) collective-permute-start(bf16[384,512]{1,0:T(8,128)(2,1)S(1)} %fusion.22.refs_0_), channel_id=1, source_target_pairs={{0,1},{1,0},{2,3},{3,2},{4,5},{5,4},{6,7},{7,6},{8,9},{9,8},{10,11... | collective-permute-start | bytes 1179656 | tf_op jit(solution)/shard_map/ppermute | solution.py:62
  215.4 21.3 %collective-permute-start.31 = (bf16[2,256,512]{2,1,0:T(8,128)(2,1)S(1)}, bf16[2,256,512]{2,1,0:T(8,128)(2,1)S(1)}, u32[]{:S(2)}, u32[]{:S(2)}) collective-permute-start(bf16[2,256,512]{2,1,0:T(8,128)(2,1)S(1)} %get-tuple-element.490), channel_id=1, source_target_pairs={{0,4},{4,0},{1,5},{5,1},{2,6},{6,2},{3,7},{7,3},{8,12},{12,8},{9,1... | collective-permute-start | bytes 1572872 | tf_op jit(solution)/shard_map/ppermute | solution.py:62
  230.4 14.8 %collective-permute-start.27 = (bf16[384,512]{1,0:T(8,128)(2,1)S(1)}, bf16[384,512]{1,0:T(8,128)(2,1)S(1)}, u32[]{:S(2)}, u32[]{:S(2)}) collective-permute-start(bf16[384,512]{1,0:T(8,128)(2,1)S(1)} %collective-permute-done.23.refs_4_), channel_id=1, source_target_pairs={{0,8},{8,16},{16,24},{24,0},{1,9},{9,17},{17,25},{25,1},{2,10},{10... | collective-permute-start | bytes 1179656 | tf_op jit(solution)/shard_map/ppermute | solution.py:66
  246.1 15.2 %collective-permute-start.36 = (bf16[2,256,512]{2,1,0:T(8,128)(2,1)S(1)}, bf16[2,256,512]{2,1,0:T(8,128)(2,1)}, u32[]{:S(2)}, u32[]{:S(2)}) collective-permute-start(bf16[2,256,512]{2,1,0:T(8,128)(2,1)S(1)} %get-tuple-element.489), channel_id=1, source_target_pairs={{0,4},{4,0},{1,5},{5,1},{2,6},{6,2},{3,7},{7,3},{8,12},{12,8},{9,1... | collective-permute-start | bytes 1572872 | tf_op jit(solution)/shard_map/ppermute | solution.py:62
  305.7 14.8 %collective-permute-start.43 = (bf16[400,512]{1,0:T(8,128)(2,1)S(1)}, bf16[400,512]{1,0:T(8,128)(2,1)}, u32[]{:S(2)}, u32[]{:S(2)}) collective-permute-start(bf16[400,512]{1,0:T(8,128)(2,1)S(1)} %fusion.13), channel_id=1, source_target_pairs={{0,2},{2,0},{1,3},{3,1},{4,6},{6,4},{5,7},{7,5},{8,10},{10,8},{9,1... | collective-permute-start | bytes 1228808 | tf_op jit(solution)/shard_map/ppermute | solution.py:62
  306.9 13.7 %collective-permute-start.44 = (bf16[2,400,512]{2,1,0:T(8,128)(2,1)}, bf16[2,400,512]{2,1,0:T(8,128)(2,1)}, u32[]{:S(2)}, u32[]{:S(2)}) collective-permute-start(bf16[2,400,512]{2,1,0:T(8,128)(2,1)} %get-tuple-element.348), channel_id=1, source_target_pairs={{0,1},{1,0},{2,3},{3,2},{4,5},{5,4},{6,7},{7,6},{8,9},{9,8},{10,11... | collective-permute-start | bytes 2457608 | tf_op jit(solution)/shard_map/ppermute | solution.py:62
  321.8 13.8 %collective-permute-start.45 = (bf16[400,512]{1,0:T(8,128)(2,1)S(1)}, bf16[400,512]{1,0:T(8,128)(2,1)S(1)}, u32[]{:S(2)}, u32[]{:S(2)}) collective-permute-start(bf16[400,512]{1,0:T(8,128)(2,1)S(1)} %add_convert_fusion.6), channel_id=1, source_target_pairs={{0,8},{8,16},{16,24},{24,0},{1,9},{9,17},{17,25},{25,1},{2,10},{10... | collective-permute-start | bytes 1228808 | tf_op jit(solution)/shard_map/ppermute | solution.py:66
  337.5 24.4 %collective-permute-start.51 = (bf16[1024,512]{1,0:T(8,128)(2,1)S(1)}, bf16[1024,512]{1,0:T(8,128)(2,1)S(1)}, u32[]{:S(2)}, u32[]{:S(2)}) collective-permute-start(bf16[1024,512]{1,0:T(8,128)(2,1)S(1)} %dynamic-slice_bitcast_fusion.2), channel_id=1, source_target_pairs={{0,4},{4,0},{1,5},{5,1},{2,6},{6,2},{3,7},{7,3},{8,12},{12,8},{9,1... | collective-permute-start | bytes 3145736 | tf_op jit(solution)/shard_map/ppermute | solution.py:62
  369.7 22.5 %collective-permute-start.57 = (bf16[1024,512]{1,0:T(8,128)(2,1)S(1)}, bf16[1024,512]{1,0:T(8,128)(2,1)S(1)}, u32[]{:S(2)}, u32[]{:S(2)}) collective-permute-start(bf16[1024,512]{1,0:T(8,128)(2,1)S(1)} %dynamic-slice_bitcast_fusion.1), channel_id=1, source_target_pairs={{0,4},{4,0},{1,5},{5,1},{2,6},{6,2},{3,7},{7,3},{8,12},{12,8},{9,1... | collective-permute-start | bytes 3145736 | tf_op jit(solution)/shard_map/ppermute | solution.py:62
  399.9 17.7 %all-to-all-start.5 = ((bf16[8,64,384]{2,1,0:T(8,128)(2,1)}), bf16[8,64,384]{2,1,0:T(8,128)(2,1)S(1)}, u32[]{:S(2)}, u32[]{:S(2)}) async-start(bf16[8,64,384]{2,1,0:T(8,128)(2,1)} %bitcast.62), calls=%async_computation.6 | async-start | bytes 786432 | tf_op jit(solution)/shard_map/all_to_all | solution.py:1121
  407.0 36.8 %collective-permute-start.58 = (bf16[1024,512]{1,0:T(8,128)(2,1)S(1)}, bf16[1024,512]{1,0:T(8,128)(2,1)}, u32[]{:S(2)}, u32[]{:S(2)}) collective-permute-start(bf16[1024,512]{1,0:T(8,128)(2,1)S(1)} %dynamic-slice_bitcast_fusion), channel_id=1, source_target_pairs={{0,4},{4,0},{1,5},{5,1},{2,6},{6,2},{3,7},{7,3},{8,12},{12,8},{9,1... | collective-permute-start | bytes 3145736 | tf_op jit(solution)/shard_map/ppermute | solution.py:62
  417.6 35.0 %all-to-all-start.6 = ((bf16[4,256,512]{2,1,0:T(8,128)(2,1)}), bf16[4,256,512]{2,1,0:T(8,128)(2,1)}, u32[]{:S(2)}, u32[]{:S(2)}) async-start(bf16[4,256,512]{2,1,0:T(8,128)(2,1)} %bitcast.64), calls=%async_computation.7 | async-start | bytes 2097152 | tf_op jit(solution)/shard_map/all_to_all | solution.py:755
  421.9 196.5 %reduce-scatter.3.cloned.1.call-start = ((), (), s32[]{:S(2)}) async-start(), calls=%async_computation.12 | async-start | bytes 6684672 | tf_op jit(solution)/shard_map/reduce_scatter | solution.py:1218
  453.7 14.2 %collective-permute-start.59 = (bf16[4,192,384]{2,1,0:T(8,128)(2,1)S(1)}, bf16[4,192,384]{2,1,0:T(8,128)(2,1)}, u32[]{:S(2)}, u32[]{:S(2)}) collective-permute-start(bf16[4,192,384]{2,1,0:T(8,128)(2,1)S(1)} %slice.180), channel_id=1, source_target_pairs={{0,4},{4,0},{1,5},{5,1},{2,6},{6,2},{3,7},{7,3},{8,12},{12,8},{9,1... | collective-permute-start | bytes 1769480 | tf_op jit(solution)/shard_map/ppermute | solution.py:62
  457.5 36.0 %all-to-all-start.7 = ((bf16[4,256,512]{2,1,0:T(8,128)(2,1)}), bf16[4,256,512]{2,1,0:T(8,128)(2,1)S(1)}, u32[]{:S(2)}, u32[]{:S(2)}) async-start(bf16[4,256,512]{2,1,0:T(8,128)(2,1)} %bitcast.68), calls=%async_computation.8 | async-start | bytes 2097152 | tf_op jit(solution)/shard_map/all_to_all | solution.py:755
  473.3 24.5 %collective-permute-start.60 = (bf16[2,400,512]{2,1,0:T(8,128)(2,1)}, bf16[2,400,512]{2,1,0:T(8,128)(2,1)S(1)}, u32[]{:S(2)}, u32[]{:S(2)}) collective-permute-start(bf16[2,400,512]{2,1,0:T(8,128)(2,1)} %get-tuple-element.413), channel_id=1, source_target_pairs={{0,1},{1,0},{2,3},{3,2},{4,5},{5,4},{6,7},{7,6},{8,9},{9,8},{10,11... | collective-permute-start | bytes 2457608 | tf_op jit(solution)/shard_map/ppermute | solution.py:62
  493.5 44.0 %all-to-all-start.8 = ((bf16[4,256,512]{2,1,0:T(8,128)(2,1)}), bf16[4,256,512]{2,1,0:T(8,128)(2,1)}, u32[]{:S(2)}, u32[]{:S(2)}) async-start(bf16[4,256,512]{2,1,0:T(8,128)(2,1)} %bitcast.74), calls=%async_computation.9 | async-start | bytes 2097152 | tf_op jit(solution)/shard_map/all_to_all | solution.py:755
  501.1 13.9 %collective-permute-start.61 = (bf16[400,512]{1,0:T(8,128)(2,1)}, bf16[400,512]{1,0:T(8,128)(2,1)}, u32[]{:S(2)}, u32[]{:S(2)}) collective-permute-start(bf16[400,512]{1,0:T(8,128)(2,1)} %fusion.17), channel_id=1, source_target_pairs={{0,2},{2,0},{1,3},{3,1},{4,6},{6,4},{5,7},{7,5},{8,10},{10,8},{9,1... | collective-permute-start | bytes 1228808 | tf_op jit(solution)/shard_map/ppermute | solution.py:62
  502.5 20.3 %collective-permute-start.62 = (bf16[2,400,512]{2,1,0:T(8,128)(2,1)}, bf16[2,400,512]{2,1,0:T(8,128)(2,1)}, u32[]{:S(2)}, u32[]{:S(2)}) collective-permute-start(bf16[2,400,512]{2,1,0:T(8,128)(2,1)} %get-tuple-element.422), channel_id=1, source_target_pairs={{0,1},{1,0},{2,3},{3,2},{4,5},{5,4},{6,7},{7,6},{8,9},{9,8},{10,11... | collective-permute-start | bytes 2457608 | tf_op jit(solution)/shard_map/ppermute | solution.py:62
  502.6 20.3 %collective-permute-start.63 = (bf16[4,384,256]{2,1,0:T(8,128)(2,1)}, bf16[4,384,256]{2,1,0:T(8,128)(2,1)}, u32[]{:S(2)}, u32[]{:S(2)}) collective-permute-start(bf16[4,384,256]{2,1,0:T(8,128)(2,1)} %get-tuple-element.428), channel_id=1, source_target_pairs={{0,4},{4,0},{1,5},{5,1},{2,6},{6,2},{3,7},{7,3},{8,12},{12,8},{9,1... | collective-permute-start | bytes 2359304 | tf_op jit(solution)/shard_map/ppermute | solution.py:62
  522.8 27.5 %collective-permute-start.66 = (bf16[2,400,512]{2,1,0:T(8,128)(2,1)}, bf16[2,400,512]{2,1,0:T(8,128)(2,1)}, u32[]{:S(2)}, u32[]{:S(2)}) collective-permute-start(bf16[2,400,512]{2,1,0:T(8,128)(2,1)} %get-tuple-element.433), channel_id=1, source_target_pairs={{0,1},{1,0},{2,3},{3,2},{4,5},{5,4},{6,7},{7,6},{8,9},{9,8},{10,11... | collective-permute-start | bytes 2457608 | tf_op jit(solution)/shard_map/ppermute | solution.py:62
  527.1 23.2 %collective-permute-start.64 = (bf16[400,512]{1,0:T(8,128)(2,1)}, bf16[400,512]{1,0:T(8,128)(2,1)}, u32[]{:S(2)}, u32[]{:S(2)}) collective-permute-start(bf16[400,512]{1,0:T(8,128)(2,1)} %add_convert_fusion.3), channel_id=1, source_target_pairs={{0,8},{8,16},{16,24},{24,0},{1,9},{9,17},{17,25},{25,1},{2,10},{10... | collective-permute-start | bytes 1228808 | tf_op jit(solution)/shard_map/ppermute | solution.py:66
  529.2 21.1 %collective-permute-start.65 = (bf16[400,512]{1,0:T(8,128)(2,1)}, bf16[400,512]{1,0:T(8,128)(2,1)}, u32[]{:S(2)}, u32[]{:S(2)}) collective-permute-start(bf16[400,512]{1,0:T(8,128)(2,1)} %fusion.18), channel_id=1, source_target_pairs={{0,2},{2,0},{1,3},{3,1},{4,6},{6,4},{5,7},{7,5},{8,10},{10,8},{9,1... | collective-permute-start | bytes 1228808 | tf_op jit(solution)/shard_map/ppermute | solution.py:62
  550.4 28.4 %collective-permute-start.69 = (bf16[2,400,512]{2,1,0:T(8,128)(2,1)}, bf16[2,400,512]{2,1,0:T(8,128)(2,1)}, u32[]{:S(2)}, u32[]{:S(2)}) collective-permute-start(bf16[2,400,512]{2,1,0:T(8,128)(2,1)} %get-tuple-element.446), channel_id=1, source_target_pairs={{0,1},{1,0},{2,3},{3,2},{4,5},{5,4},{6,7},{7,6},{8,9},{9,8},{10,11... | collective-permute-start | bytes 2457608 | tf_op jit(solution)/shard_map/ppermute | solution.py:62
  556.0 22.8 %collective-permute-start.67 = (bf16[400,512]{1,0:T(8,128)(2,1)}, bf16[400,512]{1,0:T(8,128)(2,1)}, u32[]{:S(2)}, u32[]{:S(2)}) collective-permute-start(bf16[400,512]{1,0:T(8,128)(2,1)} %add_convert_fusion.2), channel_id=1, source_target_pairs={{0,8},{8,16},{16,24},{24,0},{1,9},{9,17},{17,25},{25,1},{2,10},{10... | collective-permute-start | bytes 1228808 | tf_op jit(solution)/shard_map/ppermute | solution.py:66
  557.5 21.3 %collective-permute-start.68 = (bf16[400,512]{1,0:T(8,128)(2,1)}, bf16[400,512]{1,0:T(8,128)(2,1)}, u32[]{:S(2)}, u32[]{:S(2)}) collective-permute-start(bf16[400,512]{1,0:T(8,128)(2,1)} %fusion.19), channel_id=1, source_target_pairs={{0,2},{2,0},{1,3},{3,1},{4,6},{6,4},{5,7},{7,5},{8,10},{10,8},{9,1... | collective-permute-start | bytes 1228808 | tf_op jit(solution)/shard_map/ppermute | solution.py:62
  558.1 54.4 %all-to-all-start.9 = ((bf16[4,384,256]{2,1,0:T(8,128)(2,1)}), bf16[4,384,256]{2,1,0:T(8,128)(2,1)}, u32[]{:S(2)}, u32[]{:S(2)}) async-start(bf16[4,384,256]{2,1,0:T(8,128)(2,1)} %add_convert_fusion), calls=%async_computation.10 | async-start | bytes 1572864 | tf_op jit(solution)/shard_map/all_to_all | solution.py:755
  584.9 30.8 %collective-permute-start.72 = (bf16[400,512]{1,0:T(8,128)(2,1)}, bf16[400,512]{1,0:T(8,128)(2,1)}, u32[]{:S(2)}, u32[]{:S(2)}) collective-permute-start(bf16[400,512]{1,0:T(8,128)(2,1)} %add_convert_fusion.1), channel_id=1, source_target_pairs={{0,8},{8,16},{16,24},{24,0},{1,9},{9,17},{17,25},{25,1},{2,10},{10... | collective-permute-start | bytes 1228808 | tf_op jit(solution)/shard_map/ppermute | solution.py:66
  584.9 30.8 %collective-permute-start.73 = (bf16[400,512]{1,0:T(8,128)(2,1)}, bf16[400,512]{1,0:T(8,128)(2,1)}, u32[]{:S(2)}, u32[]{:S(2)}) collective-permute-start(bf16[400,512]{1,0:T(8,128)(2,1)} %fusion.20), channel_id=1, source_target_pairs={{0,2},{2,0},{1,3},{3,1},{4,6},{6,4},{5,7},{7,5},{8,10},{10,8},{9,1... | collective-permute-start | bytes 1228808 | tf_op jit(solution)/shard_map/ppermute | solution.py:62
  586.0 29.7 %collective-permute-start.75 = (f32[2,2,2048]{2,1,0:T(2,128)S(1)}, f32[2,2,2048]{2,1,0:T(2,128)S(1)}, u32[]{:S(2)}, u32[]{:S(2)}) collective-permute-start(f32[2,2,2048]{2,1,0:T(2,128)S(1)} %fusion.37), channel_id=1, source_target_pairs={{0,8},{8,0},{16,24},{24,16},{1,9},{9,1},{17,25},{25,17},{2,10},{10... | collective-permute-start | bytes 98312 | tf_op jit(solution)/shard_map/ppermute | solution.py:1206
  (127 other events, 1503.6 us)
Sparse Core Ops, SparseCore 0:
  71.7 60.4 all-gather.4
  134.5 80.6 all-gather.6
  400.0 92.8 reduce-scatter.4
  496.6 121.2 reduce-scatter.2

commit v5 on v4

--- a/solution.py
+++ b/solution.py
@@ -497,7 +497,7 @@
 def ffn_back_kernel(chunks, downs, count, where, *refs):
     weights, kept = refs[:count], refs[count : count + 4]
     all_cot, all_hidden, all_normed = refs[count + 4 : count + 7]
-    grad_gate_out, grad_up_out, out = refs[-21:-18]
+    grad_gate_out, grad_up_out = refs[-20:-18]
     backs, gain_term = refs[-18:-14], refs[-14]
     held, cot_all, gate_up, hidden_in, normed_in, sems = refs[-13:-7]
     grad_gates, grad_ups, out_held, back_held, lines, out_sems, line_sems = refs[-7:]
@@ -531,7 +531,6 @@
         cot_rows, hidden, normed = cot_all.at[i], hidden_in.at[i], normed_in.at[i]
         gates, ups = gate_up.at[i, 0], gate_up.at[i, 1]
         grad_gate, grad_up = grad_gates.at[i], grad_ups.at[i]
-        place = where[3 + i]
         wait_all(early if i == 0 else second)
         for n in range(0, units, step):
             span = slice(n, n + step)
@@ -574,7 +573,7 @@
                 else:
                     gain_term[:, columns] += column_term
                 row_term = row_term + jnp.sum(terms, axis=1, keepdims=True)
-            sends.start(out_held.at[i, k], out.at[place * 4 + block])
+            sends.start(out_held.at[i, k], back.at[k // 2, pl.ds(rows + EXTRA, rows)])
             sends.start(back_held.at[i, k], back.at[k // 2, pl.ds(0, rows)])
         lines[i] = row_line(row_term, cols)
         for back in backs[2 * i : 2 * i + 2]:
@@ -980,21 +979,19 @@
 
     def backward(chunks, saved, kept, buffers):
         weights = (*w_downs, *w_gates, *w_ups)
-        places = jnp.concatenate([where[0][:3], jnp.stack([zs[s] for s in chunks]).astype(jnp.int32)])
         results = chunk_call(
             functools.partial(ffn_back_kernel, chunks, len(w_downs), len(weights)),
             "feed_forward_back",
             15,
-            places,
+            where[0],
             0,
             [(a, "there") for a in (*weights, *kept, cot_rows, saved[1], saved[0])],
             buffers,
             [
                 ((group_rows, units), "there"),
                 ((group_rows, units), "there"),
-                ((nz * nx * nc, rows, cols), "there"),
             ],
-            [shape((2, rows + EXTRA, cols), BF16)] * 4 + [shape((1, width), F32)],
+            [shape((2, 2 * rows + EXTRA, cols), BF16)] * 4 + [shape((1, width), F32)],
             [
                 pltpu.VMEM((12 * cols, units), BF16),
                 pltpu.VMEM((2, rows, width), BF16),
@@ -1012,7 +1009,7 @@
             ],
             4,
         )
-        return results[:3], results[3:7], results[7]
+        return results[:2], results[2:6], results[6]
 
     z0 = mid_block
     z1, x0, c0, up_a = together(
@@ -1066,7 +1063,7 @@
         swap(part3[1], "c"),
         dot(cot_rows, hidden, 0, 0).astype(BF16),
     )
-    grad_gate_lin, grad_up_lin, out_parts = buffers
+    grad_gate_lin, grad_up_lin = buffers
     own3, send3 = first_sum(part3[0], got3)
     sum2 = (own2 + got2.astype(F32) + carried.astype(F32)).astype(BF16)
     carried, own3, got3, got0, down_got, gate, grad_up_lin = together(
@@ -1116,15 +1113,16 @@
         (*pieces, att_t, wo),
         [shape(att_t.shape, BF16), shape(wo.shape, BF16)],
     )
+    grad_att, wo_back, down = together(grad_att, wo_back, spread_z(down))
     grad_att = grad_att.reshape(nz * ny, HDIM, rows)
-    grad_att, down = together(
-        lax.all_to_all(grad_att, ("z", "y"), split_axis=0, concat_axis=0, tiled=True), down
-    )
-    back, down, up_got, gate = together(
+    grad_att, gate = together(
+        lax.all_to_all(grad_att, ("z", "y"), split_axis=0, concat_axis=0, tiled=True), gate
+    )
+    gate = spread_z(gate)
+    back, up_got, up = together(
         attend_back(tables, tiles, q_mask, k_mask, grad_att, att, log_norm, cosine, sine),
-        spread_z(down),
         up_got,
-        gate,
+        up,
     )
     up = add_rows(up, up_got)
     if nq > 1:
@@ -1144,9 +1142,9 @@
             specs,
         )
 
-    other_back, place = together(swap(back[nz:], "y"), where[1])
+    other_back, place, gate = together(swap(back[nz:], "y"), where[1], gate)
     part1, place = together(qkv_back(1, place), where[2])
-    got1, part2, qkv_grads, gate, place = together(
+    got1, part2, qkv_grads, up, place = together(
         swap(part1[1], "c"),
         qkv_back(2, place),
         small_call(
@@ -1157,7 +1155,7 @@
             (normed1, back, other_back),
             [shape((nz, ny * head, half), BF16)] * 2,
         ),
-        spread_z(gate),
+        spread_z(up),
         where[3],
     )
     own1, send1 = first_sum(part1[0], got1)
@@ -1172,28 +1170,27 @@
     )
     own2, send2 = first_sum(part2[0], got2)
     sum1 = (own1 + got1.astype(F32)).astype(BF16)
-    carried, own2, got2, got3, part0, qkv_grads, up = together(
+    carried, own2, got2, got3, part0 = together(
         ring(sum1, nz),
         own2,
         swap(send2, "x"),
         swap(part3[1], "c"),
         qkv_back(0, place),
-        scatter_lanes(qkv_own, qkv_got),
-        spread_z(up),
-    )
-    qkv_grads = spread_z(qkv_grads)
+    )
+    qkv_grads = spread_z(scatter_lanes(qkv_own, qkv_got))
     own3, send3 = first_sum(part3[0], got3)
     sum2 = (own2 + got2.astype(F32) + carried.astype(F32)).astype(BF16)
     terms1 = part0[2] + part1[2] + part2[2] + part3[2]
     terms1 = jnp.concatenate([terms1, terms2], axis=0)
     terms1 = terms1 + swap(terms1, "c")
-    carried, own3, got3, got0, terms1, terms1_x = together(
+    carried, own3, got3, got0, terms1, terms1_x, qkv_grads = together(
         ring(sum2, nz),
         own3,
         swap(send3, "x"),
         swap(part0[1], "c"),
         terms1,
         swap(terms1, "x"),
+        qkv_grads,
     )
     own0, send0 = first_sum(part0[0], got0)
     sum3 = (own3 + got3.astype(F32) + carried.astype(F32)).astype(BF16)
@@ -1215,7 +1212,7 @@
     grad_wd = lay_out(down, True)
     grad_wg = lay_out(gate, False)
     grad_wu = lay_out(up, False)
-    branch_ffn = lax.psum_scatter(out_parts, ("z", *NARROW), scatter_dimension=0, tiled=False)
+    branch_ffn = summed2[rows + EXTRA :]
     hidden_out = (residual_mid + branch_ffn.astype(F32)).astype(BF16)
     if nq > 1:
         wo_back = wo_back.reshape(nz * 2, -1, groups // 2, slab).transpose(0, 2, 1, 3)

time: 638 us -> 633 us (level)
  waiting for transfers between devices: 223 us -> 206 us
    all_to_all x8, waiting for transfers between devices: 83.3 us -> 59.2 us  [spread_z(): return lax.all_to_all(parts, 'z', split_axis=0, concat_axis=0, tiled=True)]
    unnamed x174 -> x184, local copies, waits for them, and re-layouts: 11.4 us -> 13.2 us
  transfers between devices with their start and end apart: 90 -> 89, of which waited for: 32 -> 33; matrix products, arithmetic and copies ran while one was open for 13% -> 13% of each run, Pallas kernels for 23% -> 24%
where the time goes in v5:
time: 633 us; the launch traced here: 626 us
  waiting for transfers between devices  206 us (33%)
  Pallas kernels  175 us (28%)
  starting transfers between devices  105 us (17%)
  other arithmetic  46.4 us (7%)
  local copies, waits for them, and re-layouts  35.5 us (6%)
  blocking collectives  25.1 us (4%)
  matrix products  18.5 us (3%)
  between operations  15.5 us (2%)
    ppermute x63, waiting for transfers between devices, swap(): return lax.ppermute(array, axis, [(0, 1), (1, 0)])  76 us
    pallas_call x8, Pallas kernels, chunk_call(): pl.pallas_call(kernel, grid_spec=pltpu.PrefetchScalarGridSpec(num_scalar_...  72.3 us
    all_to_all x8, waiting for transfers between devices, spread_z(): return lax.all_to_all(parts, 'z', split_axis=0, concat_axis=0, tiled=True)  59.2 us
    ppermute x12, waiting for transfers between devices, ring(): return lax.ppermute(array, 'z', [(i, (i + 1) % size) for i in range(size)])  56.3 us
    ppermute x63, starting transfers between devices, swap(): return lax.ppermute(array, axis, [(0, 1), (1, 0)])  45.8 us
    pallas_call x8, Pallas kernels, small_call(): pl.pallas_call(kernel, grid_spec=pltpu.PrefetchScalarGridSpec(num_scalar_...  43.9 us
    all_to_all x8, starting transfers between devices, spread_z(): return lax.all_to_all(parts, 'z', split_axis=0, concat_axis=0, tiled=True)  33.6 us
    all_to_all x1, blocking collectives, on_device(): lax.all_to_all(att_low, ('z', 'y'), split_axis=0, concat_axis=0, tiled=True)  25.1 us
  transfers between devices with their start and end apart: 89, of which 33 were waited for; matrix products, arithmetic and copies ran while one was open for 13% of the time, Pallas kernels for 24%

profile of v5, /device:TPU:0, one launch (start us, length us, event | category | flops | bytes accessed | tf_op | source)
XLA Modules:
  0.0 626.1 jit_solution(11817671785418679569)
XLA Ops:
  24.9 4.1 all-to-all-start
  34.9 16.4 %all-to-all-done.refs_5_.w_first = bf16[4,400,256]{2,1,0:T(8,128)(2,1)S(1)} async-done(((bf16[4,400,256]{2,1,0:T(8,128)(2,1)}), bf16[4,400,256]{2,1,0:T(8,128)(2,1)S(1)}, u32[]{:S(2)}, u32[]{:S(2)}) %all-to-all-start) | async-done | bytes 819232 | tf_op jit(solution)/shard_map/all_to_all | solution.py:754
  54.7 10.8 %collective-permute-done.7.refs_0_ = bf16[384,512]{1,0:T(8,128)(2,1)S(1)} collective-permute-done((bf16[384,512]{1,0:T(8,128)(2,1)}, bf16[384,512]{1,0:T(8,128)(2,1)S(1)}, u32[]{:S(2)}, u32[]{:S(2)}) %collective-permute-start.7) | collective-permute-done | bytes 393248 | tf_op jit(solution)/shard_map/ppermute | solution.py:66
  67.7 3.9 collective-permute-done.11.refs_6_.w_second
  82.0 5.7 qkv.4
  89.2 5.7 qkv.5
  96.2 5.7 qkv.6
  104.2 5.9 qkv.7
  111.4 8.5 %collective-permute-done.19.refs_7_ = bf16[192,384]{1,0:T(8,128)(2,1)S(1)} collective-permute-done((bf16[192,384]{1,0:T(8,128)(2,1)}, bf16[192,384]{1,0:T(8,128)(2,1)S(1)}, u32[]{:S(2)}, u32[]{:S(2)}) %collective-permute-start.19) | collective-permute-done | bytes 147488 | tf_op jit(solution)/shard_map/ppermute | solution.py:62
  129.3 18.6 %attend.1 = (bf16[8,64,384]{2,1,0:T(8,128)(2,1)}, f32[8,64,384]{2,1,0:T(8,128)}, f32[8,1,384]{2,1,0:T(1,128)}, f32[8,1,384]{2,1,0:T(1,128)}) custom-call(s32[64]{0:T(128)} %reshape.313.visible, s32[8]{0:T(128)} %get-tuple-element.249.counts, s32[17]{0:T(128)} %concatenate.20.q_pos, s32[8]{0:T(128)} %copy-done.54, ...), custom_call_target="tpu_custom_call" | custom-call | flops 17999998976 | bytes 1000 | tf_op jit(solution)/shard_map/attend/pallas_call | solution.py:166
  147.9 4.8 collective-permute-done.20
  152.6 13.6 %all-to-all-done.2 = bf16[4,256,512]{2,1,0:T(8,128)(2,1)S(1)} async-done(((bf16[4,256,512]{2,1,0:T(8,128)(2,1)}), bf16[4,256,512]{2,1,0:T(8,128)(2,1)S(1)}, u32[]{:S(2)}, u32[]{:S(2)}) %all-to-all-start.2) | async-done | bytes 1048608 | tf_op jit(solution)/shard_map/all_to_all | solution.py:754
  166.3 25.1 %all_to_all.50 = bf16[8,64,384]{2,1,0:T(8,128)(2,1)} all-to-all(bf16[8,64,384]{2,1,0:T(8,128)(2,1)} %get-tuple-element.295), channel_id=1, replica_groups=mesh['z'=4,'q'=1,'y'=2,'x'=2,'c'=2] {'z','y'}, dimensions={0} | all-to-all | bytes 786432 | tf_op jit(solution)/shard_map/all_to_all | solution.py:938
  191.4 4.5 project.1
  204.9 9.0 %collective-permute-done.22 = bf16[384,512]{1,0:T(8,128)(2,1)S(1)} collective-permute-done((bf16[384,512]{1,0:T(8,128)(2,1)S(1)}, bf16[384,512]{1,0:T(8,128)(2,1)S(1)}, u32[]{:S(2)}, u32[]{:S(2)}) %collective-permute-start.22) | collective-permute-done | bytes 393248 | tf_op jit(solution)/shard_map/ppermute | solution.py:62
  217.9 13.8 %collective-permute-done.23.refs_4_ = bf16[384,512]{1,0:T(8,128)(2,1)S(1)} collective-permute-done((bf16[384,512]{1,0:T(8,128)(2,1)S(1)}, bf16[384,512]{1,0:T(8,128)(2,1)S(1)}, u32[]{:S(2)}, u32[]{:S(2)}) %collective-permute-start.23) | collective-permute-done | bytes 393248 | tf_op jit(solution)/shard_map/ppermute | solution.py:66
  231.7 4.8 collective-permute-start.27
  237.7 8.9 %all-to-all-done.4 = bf16[4,256,512]{2,1,0:T(8,128)(2,1)S(1)} async-done(((bf16[4,256,512]{2,1,0:T(8,128)(2,1)}), bf16[4,256,512]{2,1,0:T(8,128)(2,1)S(1)}, u32[]{:S(2)}, u32[]{:S(2)}) %all-to-all-start.4) | async-done | bytes 1048608 | tf_op jit(solution)/shard_map/all_to_all | solution.py:754
  254.0 7.0 %arrange.1.refs_12_ = bf16[1536,2048]{1,0:T(8,128)(2,1)} custom-call(s32[4]{0:T(128)} %add_add_fusion.1.zs, bf16[16,384,512]{2,1,0:T(8,128)(2,1)} %bitcast.192), custom_call_target="tpu_custom_call" | custom-call | flops 5000000000 | bytes 1000 | tf_op jit(solution)/shard_map/arrange/pallas_call | solution.py:482
  264.0 11.0 %feed_forward.2 = (bf16[1536,2048]{1,0:T(8,128)(2,1)}, bf16[1536,512]{1,0:T(8,128)(2,1)}, f32[384,512]{1,0:T(8,128)}, f32[384,512]{1,0:T(8,128)}, f32[384,512]{1...) custom-call(s32[4]{0:T(128)} %get-tuple-element.433.where, bf16[384,512]{1,0:T(8,128)(2,1)} %copy-done.6, ...), custom_call_target="tpu_custom_call" | custom-call | flops 8999999488 | bytes 1000 | tf_op jit(solution)/shard_map/feed_forward/pallas_call | solution.py:370
  277.6 10.9 %feed_forward.3 = (bf16[1536,2048]{1,0:T(8,128)(2,1)}, bf16[1536,512]{1,0:T(8,128)(2,1)}, f32[384,512]{1,0:T(8,128)}, f32[384,512]{1,0:T(8,128)}, f32[384,512]{1...) custom-call(s32[4]{0:T(128)} %get-tuple-element.433.where, ...), custom_call_target="tpu_custom_call", output_to_operand_aliasing={{0}: (15, {}), {1}: (16, {})} | custom-call | flops 8999999488 | bytes 1000 | tf_op jit(solution)/shard_map/feed_forward/pallas_call | solution.py:370
  288.5 13.9 %feed_forward_back.2 = (bf16[1536,512]{1,0:T(8,128)(2,1)}, bf16[1536,512]{1,0:T(8,128)(2,1)}, bf16[2,784,512]{2,1,0:T(8,128)(2,1)}, bf16[2,784,512]{2,1,0:T(8,12...) custom-call(s32[4]{0:T(128)} %get-tuple-element.433.where, ...), custom_call_target="tpu_custom_call" | custom-call | flops 15000000512 | bytes 1000 | tf_op jit(solution)/shard_map/feed_forward_back/pallas_call | solution.py:370
  312.1 13.4 %feed_forward_back.3 = (bf16[1536,512]{1,0:T(8,128)(2,1)}, bf16[1536,512]{1,0:T(8,128)(2,1)}, bf16[2,784,512]{2,1,0:T(8,128)(2,1)}, bf16[2,784,512]{2,1,0:T(8,12...) custom-call(s32[4]{0:T(128)} %get-tuple-element.433.where, ...), custom_call_target="tpu_custom_call", output_to_operand_aliasing={{0}: (16, {}), {1}: (17, {})} | custom-call | flops 15000000512 | bytes 1000 | tf_op jit(solution)/shard_map/feed_forward_back/pallas_call | solution.py:370
  325.7 5.3 collective-permute-done.43
  335.2 6.8 %convolution_convert_fusion.2 = bf16[2048,512]{1,0:T(8,128)(2,1)S(1)} fusion(bf16[1536,2048]{1,0:T(8,128)(2,1)} %arrange.1.refs_12_, bf16[1536,512]{1,0:T(8,128)(2,1)S(1)} %copy-done.87), kind=kOutput, calls=%fused_computation.6 | convolution fusion | flops 3222274048 | bytes 9961472 | tf_op jit(solution)/shard_map/dot_general | solution.py:52
  342.4 9.9 %collective-permute-done.45 = bf16[784,512]{1,0:T(8,128)(2,1)S(1)} collective-permute-done((bf16[784,512]{1,0:T(8,128)(2,1)S(1)}, bf16[784,512]{1,0:T(8,128)(2,1)S(1)}, u32[]{:S(2)}, u32[]{:S(2)}) %collective-permute-start.45) | collective-permute-done | bytes 802848 | tf_op jit(solution)/shard_map/ppermute | solution.py:66
  362.6 13.1 %collective-permute-done.48 = bf16[784,512]{1,0:T(8,128)(2,1)S(1)} collective-permute-done((bf16[784,512]{1,0:T(8,128)(2,1)S(1)}, bf16[784,512]{1,0:T(8,128)(2,1)S(1)}, u32[]{:S(2)}, u32[]{:S(2)}) %collective-permute-start.48) | collective-permute-done | bytes 802848 | tf_op jit(solution)/shard_map/ppermute | solution.py:66
  375.8 5.5 collective-permute-done.51
  389.3 4.5 all-to-all-start.5
  393.7 8.0 %convolution_convert_fusion = bf16[2048,512]{1,0:T(8,128)(2,1)} fusion(bf16[1536,2048]{1,0:T(8,128)(2,1)} %get-tuple-element.340.refs_14_, bf16[1536,512]{1,0:T(8,128)(2,1)} %get-tuple-element.380), kind=kOutput, calls=%fused_computation.4 | convolution fusion | flops 3222274048 | bytes 9961472 | tf_op jit(solution)/shard_map/dot_general | solution.py:52
  401.8 4.6 collective-permute-done.52
  410.1 7.0 %collective-permute-done.54.p2 = bf16[384,512]{1,0:T(8,128)(2,1)S(1)} collective-permute-done((bf16[384,512]{1,0:T(8,128)(2,1)S(1)}, bf16[384,512]{1,0:T(8,128)(2,1)S(1)}, u32[]{:S(2)}, u32[]{:S(2)}) %collective-permute-start.54) | collective-permute-done | bytes 393248 | tf_op jit(solution)/shard_map/ppermute | solution.py:62
  419.6 6.6 %project_back.1 = (bf16[512,384]{1,0:T(8,128)(2,1)}, bf16[8,512,256]{2,1,0:T(8,128)(2,1)}) custom-call(s32[4]{0:T(128)} %get-tuple-element.433.where, bf16[384,512]{1,0:T(8,128)(2,1)} %copy-done.38, bf16[384,512]{1,0:T(8,128)(2,1)} %copy-done.79, bf16[384,512]{1,0:T(8,128)(2,1)} %copy-done.78, bf16[384,512]{1,0:T(8,128)(2,1)} %copy-done.81, ...), custom_call_target="tpu_custom_call" | custom-call | flops 6000000000 | bytes 1000 | tf_op jit(solution)/shard_map/project_back/pallas_call | solution.py:697
  426.3 5.9 all-to-all-start.6
  438.2 5.9 all-to-all-done.6.refs_10_
  444.2 4.2 all-to-all-start.7
  448.5 22.0 %attend_back.1.mine.refs_0_ = bf16[8,192,384]{2,1,0:T(8,128)(2,1)} custom-call(s32[64]{0:T(128)} %reshape.313.visible, s32[8]{0:T(128)} %get-tuple-element.249.counts, s32[17]{0:T(128)} %concatenate.20.q_pos, s32[8]{0:T(128)} %copy-done.54, bf16[192,384]{1,0:T(8,128)(2,1)} %get-tuple-element.278.refs_0_, bf16[192,384]{1,0:T(8,128)(2,1)} %get-tuple-element.279.refs_1_, ...), custom_call_target="tpu_custom_call" | custom-call | flops 22000001024 | bytes 1000 | tf_op jit(solution)/shard_map/attend_back/pallas_call | solution.py:256
  482.4 5.0 all-to-all-start.8
  489.0 5.2 qkv_back.4
  494.2 5.2 qkv_back.5
  503.1 8.4 %qkv_weights.1 = (bf16[4,384,256]{2,1,0:T(8,128)(2,1)}, bf16[4,384,256]{2,1,0:T(8,128)(2,1)}) custom-call(s32[4]{0:T(128)} %get-tuple-element.412.where, bf16[1536,2048]{1,0:T(8,128)(2,1)} %get-tuple-element.405.normed, bf16[8,192,384]{2,1,0:T(8,128)(2,1)} %attend_back.1.mine.refs_0_, bf16[4,192,384]{2,1,0:T(8,128)(2,1)} %collective-permute-done.59.other.refs_1_), custom_call_target="tpu_custom_call" | custom-call | flops 8000000000 | bytes 1000 | tf_op jit(solution)/shard_map/qkv_weights/pallas_call | solution.py:697
  511.5 14.4 %all-to-all-done.8.parts = bf16[4,256,512]{2,1,0:T(8,128)(2,1)S(1)} async-done(((bf16[4,256,512]{2,1,0:T(8,128)(2,1)}), bf16[4,256,512]{2,1,0:T(8,128)(2,1)S(1)}, u32[]{:S(2)}, u32[]{:S(2)}) %all-to-all-start.8) | async-done | bytes 1048608 | tf_op jit(solution)/shard_map/all_to_all | solution.py:754
  536.0 5.4 qkv_back.6
  541.4 12.0 %collective-permute-done.63 = bf16[4,384,256]{2,1,0:T(8,128)(2,1)} collective-permute-done((bf16[4,384,256]{2,1,0:T(8,128)(2,1)}, bf16[4,384,256]{2,1,0:T(8,128)(2,1)}, u32[]{:S(2)}, u32[]{:S(2)}) %collective-permute-start.63) | collective-permute-done | bytes 786464 | tf_op jit(solution)/shard_map/ppermute | solution.py:62
  560.2 4.9 all-to-all-start.9
  565.1 5.3 qkv_back.7
  582.6 9.8 %collective-permute-done.71 = f32[2,2048]{1,0:T(2,128)S(1)} collective-permute-done((f32[2,2048]{1,0:T(2,128)S(1)}, f32[2,2048]{1,0:T(2,128)S(1)}, u32[]{:S(2)}, u32[]{:S(2)}) %collective-permute-start.71) | collective-permute-done | bytes 16416 | tf_op jit(solution)/shard_map/ppermute | solution.py:62
  606.1 4.8 collective-permute-done.75
  (472 shorter events, 194.5 us)
Async XLA Ops:
  24.9 26.4 %all-to-all-start = ((bf16[4,400,256]{2,1,0:T(8,128)(2,1)}), bf16[4,400,256]{2,1,0:T(8,128)(2,1)S(1)}, u32[]{:S(2)}, u32[]{:S(2)}) async-start(bf16[4,400,256]{2,1,0:T(8,128)(2,1)} %pad_maximum_fusion), calls=%async_computation | async-start | bytes 1638400 | tf_op jit(solution)/shard_map/all_to_all | solution.py:754
  29.0 162.4 %all-gather.5.cloned.1.call-start = ((), (), s32[]{:S(2)}) async-start(), calls=%async_computation.12 | async-start | bytes 2359296 | tf_op jit(solution)/shard_map/all_gather | solution.py:905
  51.3 20.2 %collective-permute-start.11 = (bf16[4,400,256]{2,1,0:T(8,128)(2,1)S(1)}, bf16[4,400,256]{2,1,0:T(8,128)(2,1)S(1)}, u32[]{:S(2)}, u32[]{:S(2)}) collective-permute-start(bf16[4,400,256]{2,1,0:T(8,128)(2,1)S(1)} %all-to-all-done.refs_5_.w_first), channel_id=1, source_target_pairs={{0,4},{4,0},{1,5},{5,1},{2,6},{6,2},{3,7},{7,3},{8,12},{12,8},{9,1... | collective-permute-start | bytes 2457608 | tf_op jit(solution)/shard_map/ppermute | solution.py:62
  71.6 182.4 %all-gather.7.cloned.1.call-start = ((), (), s32[]{:S(2)}) async-start(), calls=%async_computation.13 | async-start | bytes 6684672 | tf_op jit(solution)/shard_map/all_gather | solution.py:910
  74.4 29.1 %collective-permute-start.13 = (bf16[384,512]{1,0:T(8,128)(2,1)}, bf16[384,512]{1,0:T(8,128)(2,1)}, u32[]{:S(2)}, u32[]{:S(2)}) collective-permute-start(bf16[384,512]{1,0:T(8,128)(2,1)} %copy-done.66), channel_id=1, source_target_pairs={{0,1},{1,0},{2,3},{3,2},{4,5},{5,4},{6,7},{7,6},{8,9},{9,8},{10,11... | collective-permute-start | bytes 1179656 | tf_op jit(solution)/shard_map/ppermute | solution.py:62
  74.4 21.0 %collective-permute-start.14 = (bf16[384,512]{1,0:T(8,128)(2,1)}, bf16[384,512]{1,0:T(8,128)(2,1)}, u32[]{:S(2)}, u32[]{:S(2)}) collective-permute-start(bf16[384,512]{1,0:T(8,128)(2,1)} %copy-done.66), channel_id=1, source_target_pairs={{0,2},{2,0},{1,3},{3,1},{4,6},{6,4},{5,7},{7,5},{8,10},{10,8},{9,1... | collective-permute-start | bytes 1179656 | tf_op jit(solution)/shard_map/ppermute | solution.py:62
  77.0 18.5 %collective-permute-start.12 = (bf16[384,512]{1,0:T(8,128)(2,1)}, bf16[384,512]{1,0:T(8,128)(2,1)S(1)}, u32[]{:S(2)}, u32[]{:S(2)}) collective-permute-start(bf16[384,512]{1,0:T(8,128)(2,1)} %copy-done.68), channel_id=1, source_target_pairs={{0,1},{1,0},{2,3},{3,2},{4,5},{5,4},{6,7},{7,6},{8,9},{9,8},{10,11... | collective-permute-start | bytes 1179656 | tf_op jit(solution)/shard_map/ppermute | solution.py:62
  78.2 44.9 %all-to-all-start.1 = ((bf16[4,256,512]{2,1,0:T(8,128)(2,1)}), bf16[4,256,512]{2,1,0:T(8,128)(2,1)S(1)}, u32[]{:S(2)}, u32[]{:S(2)}) async-start(bf16[4,256,512]{2,1,0:T(8,128)(2,1)} %bitcast.158), calls=%async_computation.1 | async-start | bytes 2097152 | tf_op jit(solution)/shard_map/all_to_all | solution.py:754
  87.7 23.0 %collective-permute-start.16 = (bf16[192,384]{1,0:T(8,128)(2,1)}, bf16[192,384]{1,0:T(8,128)(2,1)S(1)}, u32[]{:S(2)}, u32[]{:S(2)}) collective-permute-start(bf16[192,384]{1,0:T(8,128)(2,1)} %get-tuple-element.273), channel_id=1, source_target_pairs={{0,4},{4,0},{1,5},{5,1},{2,6},{6,2},{3,7},{7,3},{8,12},{12,8},{9,1... | collective-permute-start | bytes 442376 | tf_op jit(solution)/shard_map/ppermute | solution.py:62
  95.0 15.8 %collective-permute-start.17 = (bf16[192,384]{1,0:T(8,128)(2,1)}, bf16[192,384]{1,0:T(8,128)(2,1)S(1)}, u32[]{:S(2)}, u32[]{:S(2)}) collective-permute-start(bf16[192,384]{1,0:T(8,128)(2,1)} %get-tuple-element.274), channel_id=1, source_target_pairs={{0,4},{4,0},{1,5},{5,1},{2,6},{6,2},{3,7},{7,3},{8,12},{12,8},{9,1... | collective-permute-start | bytes 442376 | tf_op jit(solution)/shard_map/ppermute | solution.py:62
  124.3 41.9 %all-to-all-start.2 = ((bf16[4,256,512]{2,1,0:T(8,128)(2,1)}), bf16[4,256,512]{2,1,0:T(8,128)(2,1)S(1)}, u32[]{:S(2)}, u32[]{:S(2)}) async-start(bf16[4,256,512]{2,1,0:T(8,128)(2,1)} %bitcast.156), calls=%async_computation.2 | async-start | bytes 2097152 | tf_op jit(solution)/shard_map/all_to_all | solution.py:754
  127.9 24.8 %collective-permute-start.20 = (bf16[4,256,512]{2,1,0:T(8,128)(2,1)S(1)}, bf16[4,256,512]{2,1,0:T(8,128)(2,1)S(1)}, u32[]{:S(2)}, u32[]{:S(2)}) collective-permute-start(bf16[4,256,512]{2,1,0:T(8,128)(2,1)S(1)} %all-to-all-done.1), channel_id=1, source_target_pairs={{0,4},{4,0},{1,5},{5,1},{2,6},{6,2},{3,7},{7,3},{8,12},{12,8},{9,1... | collective-permute-start | bytes 3145736 | tf_op jit(solution)/shard_map/ppermute | solution.py:62
  197.2 49.4 %all-to-all-start.4 = ((bf16[4,256,512]{2,1,0:T(8,128)(2,1)}), bf16[4,256,512]{2,1,0:T(8,128)(2,1)S(1)}, u32[]{:S(2)}, u32[]{:S(2)}) async-start(bf16[4,256,512]{2,1,0:T(8,128)(2,1)} %bitcast.40), calls=%async_computation.4 | async-start | bytes 2097152 | tf_op jit(solution)/shard_map/all_to_all | solution.py:754
  202.9 15.0 %collective-permute-start.26 = (bf16[2,256,512]{2,1,0:T(8,128)(2,1)S(1)}, bf16[2,256,512]{2,1,0:T(8,128)(2,1)S(1)}, u32[]{:S(2)}, u32[]{:S(2)}) collective-permute-start(bf16[2,256,512]{2,1,0:T(8,128)(2,1)S(1)} %get-tuple-element.491), channel_id=1, source_target_pairs={{0,4},{4,0},{1,5},{5,1},{2,6},{6,2},{3,7},{7,3},{8,12},{12,8},{9,1... | collective-permute-start | bytes 1572872 | tf_op jit(solution)/shard_map/ppermute | solution.py:62
  214.0 17.7 %collective-permute-start.23 = (bf16[384,512]{1,0:T(8,128)(2,1)S(1)}, bf16[384,512]{1,0:T(8,128)(2,1)S(1)}, u32[]{:S(2)}, u32[]{:S(2)}) collective-permute-start(bf16[384,512]{1,0:T(8,128)(2,1)S(1)} %fusion.22.refs_0_), channel_id=1, source_target_pairs={{0,8},{8,16},{16,24},{24,0},{1,9},{9,17},{17,25},{25,1},{2,10},{10... | collective-permute-start | bytes 1179656 | tf_op jit(solution)/shard_map/ppermute | solution.py:66
  215.8 16.0 %collective-permute-start.24 = (bf16[384,512]{1,0:T(8,128)(2,1)S(1)}, bf16[384,512]{1,0:T(8,128)(2,1)}, u32[]{:S(2)}, u32[]{:S(2)}) collective-permute-start(bf16[384,512]{1,0:T(8,128)(2,1)S(1)} %fusion.22.refs_0_), channel_id=1, source_target_pairs={{0,2},{2,0},{1,3},{3,1},{4,6},{6,4},{5,7},{7,5},{8,10},{10,8},{9,1... | collective-permute-start | bytes 1179656 | tf_op jit(solution)/shard_map/ppermute | solution.py:62
  216.3 15.5 %collective-permute-start.25 = (bf16[384,512]{1,0:T(8,128)(2,1)S(1)}, bf16[384,512]{1,0:T(8,128)(2,1)S(1)}, u32[]{:S(2)}, u32[]{:S(2)}) collective-permute-start(bf16[384,512]{1,0:T(8,128)(2,1)S(1)} %fusion.22.refs_0_), channel_id=1, source_target_pairs={{0,1},{1,0},{2,3},{3,2},{4,5},{5,4},{6,7},{7,6},{8,9},{9,8},{10,11... | collective-permute-start | bytes 1179656 | tf_op jit(solution)/shard_map/ppermute | solution.py:62
  216.3 21.4 %collective-permute-start.31 = (bf16[2,256,512]{2,1,0:T(8,128)(2,1)S(1)}, bf16[2,256,512]{2,1,0:T(8,128)(2,1)S(1)}, u32[]{:S(2)}, u32[]{:S(2)}) collective-permute-start(bf16[2,256,512]{2,1,0:T(8,128)(2,1)S(1)} %get-tuple-element.490), channel_id=1, source_target_pairs={{0,4},{4,0},{1,5},{5,1},{2,6},{6,2},{3,7},{7,3},{8,12},{12,8},{9,1... | collective-permute-start | bytes 1572872 | tf_op jit(solution)/shard_map/ppermute | solution.py:62
  231.7 14.9 %collective-permute-start.27 = (bf16[384,512]{1,0:T(8,128)(2,1)S(1)}, bf16[384,512]{1,0:T(8,128)(2,1)S(1)}, u32[]{:S(2)}, u32[]{:S(2)}) collective-permute-start(bf16[384,512]{1,0:T(8,128)(2,1)S(1)} %collective-permute-done.23.refs_4_), channel_id=1, source_target_pairs={{0,8},{8,16},{16,24},{24,0},{1,9},{9,17},{17,25},{25,1},{2,10},{10... | collective-permute-start | bytes 1179656 | tf_op jit(solution)/shard_map/ppermute | solution.py:66
  247.4 15.4 %collective-permute-start.36 = (bf16[2,256,512]{2,1,0:T(8,128)(2,1)S(1)}, bf16[2,256,512]{2,1,0:T(8,128)(2,1)}, u32[]{:S(2)}, u32[]{:S(2)}) collective-permute-start(bf16[2,256,512]{2,1,0:T(8,128)(2,1)S(1)} %get-tuple-element.489), channel_id=1, source_target_pairs={{0,4},{4,0},{1,5},{5,1},{2,6},{6,2},{3,7},{7,3},{8,12},{12,8},{9,1... | collective-permute-start | bytes 1572872 | tf_op jit(solution)/shard_map/ppermute | solution.py:62
  310.7 20.2 %collective-permute-start.43 = (bf16[784,512]{1,0:T(8,128)(2,1)}, bf16[784,512]{1,0:T(8,128)(2,1)S(1)}, u32[]{:S(2)}, u32[]{:S(2)}) collective-permute-start(bf16[784,512]{1,0:T(8,128)(2,1)} %fusion.3), channel_id=1, source_target_pairs={{0,2},{2,0},{1,3},{3,1},{4,6},{6,4},{5,7},{7,5},{8,10},{10,8},{9,1... | collective-permute-start | bytes 2408456 | tf_op jit(solution)/shard_map/ppermute | solution.py:62
  312.1 18.9 %collective-permute-start.44 = (bf16[2,784,512]{2,1,0:T(8,128)(2,1)}, bf16[2,784,512]{2,1,0:T(8,128)(2,1)}, u32[]{:S(2)}, u32[]{:S(2)}) collective-permute-start(bf16[2,784,512]{2,1,0:T(8,128)(2,1)} %get-tuple-element.347), channel_id=1, source_target_pairs={{0,1},{1,0},{2,3},{3,2},{4,5},{5,4},{6,7},{7,6},{8,9},{9,8},{10,11... | collective-permute-start | bytes 4816904 | tf_op jit(solution)/shard_map/ppermute | solution.py:62
  331.3 21.0 %collective-permute-start.45 = (bf16[784,512]{1,0:T(8,128)(2,1)S(1)}, bf16[784,512]{1,0:T(8,128)(2,1)S(1)}, u32[]{:S(2)}, u32[]{:S(2)}) collective-permute-start(bf16[784,512]{1,0:T(8,128)(2,1)S(1)} %add_convert_fusion.2), channel_id=1, source_target_pairs={{0,8},{8,16},{16,24},{24,0},{1,9},{9,17},{17,25},{25,1},{2,10},{10... | collective-permute-start | bytes 2408456 | tf_op jit(solution)/shard_map/ppermute | solution.py:66
  331.6 22.4 %collective-permute-start.47 = (bf16[2,784,512]{2,1,0:T(8,128)(2,1)S(1)}, bf16[2,784,512]{2,1,0:T(8,128)(2,1)S(1)}, u32[]{:S(2)}, u32[]{:S(2)}) collective-permute-start(bf16[2,784,512]{2,1,0:T(8,128)(2,1)S(1)} %copy-done.58), channel_id=1, source_target_pairs={{0,1},{1,0},{2,3},{3,2},{4,5},{5,4},{6,7},{7,6},{8,9},{9,8},{10,11... | collective-permute-start | bytes 4816904 | tf_op jit(solution)/shard_map/ppermute | solution.py:62
  333.8 20.2 %collective-permute-start.46 = (bf16[784,512]{1,0:T(8,128)(2,1)S(1)}, bf16[784,512]{1,0:T(8,128)(2,1)S(1)}, u32[]{:S(2)}, u32[]{:S(2)}) collective-permute-start(bf16[784,512]{1,0:T(8,128)(2,1)S(1)} %fusion.4), channel_id=1, source_target_pairs={{0,2},{2,0},{1,3},{3,1},{4,6},{6,4},{5,7},{7,5},{8,10},{10,8},{9,1... | collective-permute-start | bytes 2408456 | tf_op jit(solution)/shard_map/ppermute | solution.py:62
  342.0 20.6 %collective-permute-start.50 = (bf16[2,784,512]{2,1,0:T(8,128)(2,1)S(1)}, bf16[2,784,512]{2,1,0:T(8,128)(2,1)S(1)}, u32[]{:S(2)}, u32[]{:S(2)}) collective-permute-start(bf16[2,784,512]{2,1,0:T(8,128)(2,1)S(1)} %copy-done.57), channel_id=1, source_target_pairs={{0,1},{1,0},{2,3},{3,2},{4,5},{5,4},{6,7},{7,6},{8,9},{9,8},{10,11... | collective-permute-start | bytes 4816904 | tf_op jit(solution)/shard_map/ppermute | solution.py:62
  354.4 21.4 %collective-permute-start.48 = (bf16[784,512]{1,0:T(8,128)(2,1)S(1)}, bf16[784,512]{1,0:T(8,128)(2,1)S(1)}, u32[]{:S(2)}, u32[]{:S(2)}) collective-permute-start(bf16[784,512]{1,0:T(8,128)(2,1)S(1)} %add_convert_fusion.1), channel_id=1, source_target_pairs={{0,8},{8,16},{16,24},{24,0},{1,9},{9,17},{17,25},{25,1},{2,10},{10... | collective-permute-start | bytes 2408456 | tf_op jit(solution)/shard_map/ppermute | solution.py:66
  355.5 20.3 %collective-permute-start.49 = (bf16[784,512]{1,0:T(8,128)(2,1)S(1)}, bf16[784,512]{1,0:T(8,128)(2,1)S(1)}, u32[]{:S(2)}, u32[]{:S(2)}) collective-permute-start(bf16[784,512]{1,0:T(8,128)(2,1)S(1)} %fusion.5), channel_id=1, source_target_pairs={{0,2},{2,0},{1,3},{3,1},{4,6},{6,4},{5,7},{7,5},{8,10},{10,8},{9,1... | collective-permute-start | bytes 2408456 | tf_op jit(solution)/shard_map/ppermute | solution.py:62
  357.0 24.3 %collective-permute-start.51 = (bf16[1024,512]{1,0:T(8,128)(2,1)S(1)}, bf16[1024,512]{1,0:T(8,128)(2,1)S(1)}, u32[]{:S(2)}, u32[]{:S(2)}) collective-permute-start(bf16[1024,512]{1,0:T(8,128)(2,1)S(1)} %dynamic-slice_bitcast_fusion.2), channel_id=1, source_target_pairs={{0,4},{4,0},{1,5},{5,1},{2,6},{6,2},{3,7},{7,3},{8,12},{12,8},{9,1... | collective-permute-start | bytes 3145736 | tf_op jit(solution)/shard_map/ppermute | solution.py:62
  383.3 23.0 %collective-permute-start.52 = (bf16[784,512]{1,0:T(8,128)(2,1)}, bf16[784,512]{1,0:T(8,128)(2,1)S(1)}, u32[]{:S(2)}, u32[]{:S(2)}) collective-permute-start(bf16[784,512]{1,0:T(8,128)(2,1)} %add_convert_fusion), channel_id=1, source_target_pairs={{0,8},{8,16},{16,24},{24,0},{1,9},{9,17},{17,25},{25,1},{2,10},{10... | collective-permute-start | bytes 2408456 | tf_op jit(solution)/shard_map/ppermute | solution.py:66
  385.1 22.1 %collective-permute-start.53 = (bf16[784,512]{1,0:T(8,128)(2,1)S(1)}, bf16[784,512]{1,0:T(8,128)(2,1)}, u32[]{:S(2)}, u32[]{:S(2)}) collective-permute-start(bf16[784,512]{1,0:T(8,128)(2,1)S(1)} %fusion.6), channel_id=1, source_target_pairs={{0,2},{2,0},{1,3},{3,1},{4,6},{6,4},{5,7},{7,5},{8,10},{10,8},{9,1... | collective-permute-start | bytes 2408456 | tf_op jit(solution)/shard_map/ppermute | solution.py:62
  386.8 30.4 %collective-permute-start.57 = (bf16[1024,512]{1,0:T(8,128)(2,1)}, bf16[1024,512]{1,0:T(8,128)(2,1)}, u32[]{:S(2)}, u32[]{:S(2)}) collective-permute-start(bf16[1024,512]{1,0:T(8,128)(2,1)} %dynamic-slice_bitcast_fusion.1), channel_id=1, source_target_pairs={{0,4},{4,0},{1,5},{5,1},{2,6},{6,2},{3,7},{7,3},{8,12},{12,8},{9,1... | collective-permute-start | bytes 3145736 | tf_op jit(solution)/shard_map/ppermute | solution.py:62
  389.3 37.0 %all-to-all-start.5 = ((bf16[4,256,512]{2,1,0:T(8,128)(2,1)}), bf16[4,256,512]{2,1,0:T(8,128)(2,1)}, u32[]{:S(2)}, u32[]{:S(2)}) async-start(bf16[4,256,512]{2,1,0:T(8,128)(2,1)} %bitcast.62), calls=%async_computation.5 | async-start | bytes 2097152 | tf_op jit(solution)/shard_map/all_to_all | solution.py:754
  426.3 17.9 %all-to-all-start.6 = ((bf16[8,64,384]{2,1,0:T(8,128)(2,1)}), bf16[8,64,384]{2,1,0:T(8,128)(2,1)S(1)}, u32[]{:S(2)}, u32[]{:S(2)}) async-start(bf16[8,64,384]{2,1,0:T(8,128)(2,1)} %bitcast.184), calls=%async_computation.6 | async-start | bytes 786432 | tf_op jit(solution)/shard_map/all_to_all | solution.py:1119
  433.6 36.9 %collective-permute-start.58 = (bf16[1024,512]{1,0:T(8,128)(2,1)S(1)}, bf16[1024,512]{1,0:T(8,128)(2,1)}, u32[]{:S(2)}, u32[]{:S(2)}) collective-permute-start(bf16[1024,512]{1,0:T(8,128)(2,1)S(1)} %dynamic-slice_bitcast_fusion), channel_id=1, source_target_pairs={{0,4},{4,0},{1,5},{5,1},{2,6},{6,2},{3,7},{7,3},{8,12},{12,8},{9,1... | collective-permute-start | bytes 3145736 | tf_op jit(solution)/shard_map/ppermute | solution.py:62
  444.2 38.2 %all-to-all-start.7 = ((bf16[4,256,512]{2,1,0:T(8,128)(2,1)}), bf16[4,256,512]{2,1,0:T(8,128)(2,1)}, u32[]{:S(2)}, u32[]{:S(2)}) async-start(bf16[4,256,512]{2,1,0:T(8,128)(2,1)} %bitcast.65), calls=%async_computation.7 | async-start | bytes 2097152 | tf_op jit(solution)/shard_map/all_to_all | solution.py:754
  448.5 123.0 %reduce-scatter.2.cloned.1.call-start = ((), (), s32[]{:S(2)}) async-start(), calls=%async_computation.11 | async-start | bytes 2359296 | tf_op jit(solution)/shard_map/reduce_scatter | solution.py:1220
  471.7 17.3 %collective-permute-start.59 = (bf16[4,192,384]{2,1,0:T(8,128)(2,1)S(1)}, bf16[4,192,384]{2,1,0:T(8,128)(2,1)}, u32[]{:S(2)}, u32[]{:S(2)}) collective-permute-start(bf16[4,192,384]{2,1,0:T(8,128)(2,1)S(1)} %slice.181), channel_id=1, source_target_pairs={{0,4},{4,0},{1,5},{5,1},{2,6},{6,2},{3,7},{7,3},{8,12},{12,8},{9,1... | collective-permute-start | bytes 1769480 | tf_op jit(solution)/shard_map/ppermute | solution.py:62
  482.4 43.5 %all-to-all-start.8 = ((bf16[4,256,512]{2,1,0:T(8,128)(2,1)}), bf16[4,256,512]{2,1,0:T(8,128)(2,1)S(1)}, u32[]{:S(2)}, u32[]{:S(2)}) async-start(bf16[4,256,512]{2,1,0:T(8,128)(2,1)} %bitcast.70), calls=%async_computation.8 | async-start | bytes 2097152 | tf_op jit(solution)/shard_map/all_to_all | solution.py:754
  494.2 31.7 %collective-permute-start.60 = (bf16[2,400,512]{2,1,0:T(8,128)(2,1)}, bf16[2,400,512]{2,1,0:T(8,128)(2,1)S(1)}, u32[]{:S(2)}, u32[]{:S(2)}) collective-permute-start(bf16[2,400,512]{2,1,0:T(8,128)(2,1)} %get-tuple-element.411), channel_id=1, source_target_pairs={{0,1},{1,0},{2,3},{3,2},{4,5},{5,4},{6,7},{7,6},{8,9},{9,8},{10,11... | collective-permute-start | bytes 2457608 | tf_op jit(solution)/shard_map/ppermute | solution.py:62
  530.1 23.3 %collective-permute-start.62 = (bf16[2,400,512]{2,1,0:T(8,128)(2,1)}, bf16[2,400,512]{2,1,0:T(8,128)(2,1)}, u32[]{:S(2)}, u32[]{:S(2)}) collective-permute-start(bf16[2,400,512]{2,1,0:T(8,128)(2,1)} %get-tuple-element.421), channel_id=1, source_target_pairs={{0,1},{1,0},{2,3},{3,2},{4,5},{5,4},{6,7},{7,6},{8,9},{9,8},{10,11... | collective-permute-start | bytes 2457608 | tf_op jit(solution)/shard_map/ppermute | solution.py:62
  530.1 23.3 %collective-permute-start.63 = (bf16[4,384,256]{2,1,0:T(8,128)(2,1)}, bf16[4,384,256]{2,1,0:T(8,128)(2,1)}, u32[]{:S(2)}, u32[]{:S(2)}) collective-permute-start(bf16[4,384,256]{2,1,0:T(8,128)(2,1)} %get-tuple-element.427), channel_id=1, source_target_pairs={{0,4},{4,0},{1,5},{5,1},{2,6},{6,2},{3,7},{7,3},{8,12},{12,8},{9,1... | collective-permute-start | bytes 2359304 | tf_op jit(solution)/shard_map/ppermute | solution.py:62
  554.3 19.0 %collective-permute-start.64 = (bf16[400,512]{1,0:T(8,128)(2,1)}, bf16[400,512]{1,0:T(8,128)(2,1)}, u32[]{:S(2)}, u32[]{:S(2)}) collective-permute-start(bf16[400,512]{1,0:T(8,128)(2,1)} %add_convert_fusion.6), channel_id=1, source_target_pairs={{0,8},{8,16},{16,24},{24,0},{1,9},{9,17},{17,25},{25,1},{2,10},{10... | collective-permute-start | bytes 1228808 | tf_op jit(solution)/shard_map/ppermute | solution.py:66
  556.6 16.7 %collective-permute-start.65 = (bf16[400,512]{1,0:T(8,128)(2,1)}, bf16[400,512]{1,0:T(8,128)(2,1)}, u32[]{:S(2)}, u32[]{:S(2)}) collective-permute-start(bf16[400,512]{1,0:T(8,128)(2,1)} %fusion.18), channel_id=1, source_target_pairs={{0,2},{2,0},{1,3},{3,1},{4,6},{6,4},{5,7},{7,5},{8,10},{10,8},{9,1... | collective-permute-start | bytes 1228808 | tf_op jit(solution)/shard_map/ppermute | solution.py:62
  558.0 15.3 %collective-permute-start.66 = (bf16[2,400,512]{2,1,0:T(8,128)(2,1)}, bf16[2,400,512]{2,1,0:T(8,128)(2,1)}, u32[]{:S(2)}, u32[]{:S(2)}) collective-permute-start(bf16[2,400,512]{2,1,0:T(8,128)(2,1)} %get-tuple-element.432), channel_id=1, source_target_pairs={{0,1},{1,0},{2,3},{3,2},{4,5},{5,4},{6,7},{7,6},{8,9},{9,8},{10,11... | collective-permute-start | bytes 2457608 | tf_op jit(solution)/shard_map/ppermute | solution.py:62
  560.2 34.7 %all-to-all-start.9 = ((bf16[4,384,256]{2,1,0:T(8,128)(2,1)}), bf16[4,384,256]{2,1,0:T(8,128)(2,1)}, u32[]{:S(2)}, u32[]{:S(2)}) async-start(bf16[4,384,256]{2,1,0:T(8,128)(2,1)} %add_convert_fusion.3), calls=%async_computation.9 | async-start | bytes 1572864 | tf_op jit(solution)/shard_map/all_to_all | solution.py:754
  575.6 19.4 %collective-permute-start.67 = (bf16[400,512]{1,0:T(8,128)(2,1)}, bf16[400,512]{1,0:T(8,128)(2,1)}, u32[]{:S(2)}, u32[]{:S(2)}) collective-permute-start(bf16[400,512]{1,0:T(8,128)(2,1)} %add_convert_fusion.5), channel_id=1, source_target_pairs={{0,8},{8,16},{16,24},{24,0},{1,9},{9,17},{17,25},{25,1},{2,10},{10... | collective-permute-start | bytes 1228808 | tf_op jit(solution)/shard_map/ppermute | solution.py:66
  577.6 17.3 %collective-permute-start.69 = (bf16[2,400,512]{2,1,0:T(8,128)(2,1)}, bf16[2,400,512]{2,1,0:T(8,128)(2,1)S(1)}, u32[]{:S(2)}, u32[]{:S(2)}) collective-permute-start(bf16[2,400,512]{2,1,0:T(8,128)(2,1)} %get-tuple-element.442), channel_id=1, source_target_pairs={{0,1},{1,0},{2,3},{3,2},{4,5},{5,4},{6,7},{7,6},{8,9},{9,8},{10,11... | collective-permute-start | bytes 2457608 | tf_op jit(solution)/shard_map/ppermute | solution.py:62
  (131 other events, 1394.9 us)
Sparse Core Ops, SparseCore 0:
  71.7 63.1 all-gather.4
  137.2 79.4 all-gather.6
  475.9 86.0 reduce-scatter.1

commit v6 on v5

--- a/solution.py
+++ b/solution.py
@@ -1144,7 +1144,8 @@
 
     other_back, place, gate = together(swap(back[nz:], "y"), where[1], gate)
     part1, place = together(qkv_back(1, place), where[2])
-    got1, part2, qkv_grads, up, place = together(
+    up = spread_z(up)
+    got1, part2, qkv_grads, place = together(
         swap(part1[1], "c"),
         qkv_back(2, place),
         small_call(
@@ -1155,11 +1156,10 @@
             (normed1, back, other_back),
             [shape((nz, ny * head, half), BF16)] * 2,
         ),
-        spread_z(up),
         where[3],
     )
     own1, send1 = first_sum(part1[0], got1)
-    own1, got1, got2, part3, qkv_own, qkv_got, place = together(
+    own1, got1, got2, part3, qkv_own, qkv_got, place, up = together(
         own1,
         swap(send1, "x"),
         swap(part2[1], "c"),
@@ -1167,6 +1167,7 @@
         qkv_grads[0],
         exchange_lanes(qkv_grads[1]),
         where[0],
+        up,
     )
     own2, send2 = first_sum(part2[0], got2)
     sum1 = (own1 + got1.astype(F32)).astype(BF16)

time: 633 us -> 628 us (level)
  waiting for transfers between devices: 206 us -> 196 us
  starting transfers between devices: 105 us -> 113 us
    all_to_all x8, waiting for transfers between devices: 59.2 us -> 46.9 us  [spread_z(): return lax.all_to_all(parts, 'z', split_axis=0, concat_axis=0, tiled=True)]
    reduce_scatter x1, waiting for transfers between devices: 0.02 us -> 8.37 us  [on_device(): lax.psum_scatter(wo_back, WIDE, scatter_dimension=0, tiled=False)]
    unnamed x184 -> x180, local copies, waits for them, and re-layouts: 13.2 us -> 12 us
  transfers between devices with their start and end apart: 89 -> 89, of which waited for: 33 -> 33; matrix products, arithmetic and copies ran while one was open for 13% -> 12% of each run, Pallas kernels for 24% -> 24%
where the time goes in v6:
time: 628 us; the launch traced here: 621 us
  waiting for transfers between devices  196 us (31%)
  Pallas kernels  175 us (28%)
  starting transfers between devices  113 us (18%)
  other arithmetic  46.2 us (7%)
  local copies, waits for them, and re-layouts  32.5 us (5%)
  blocking collectives  25.1 us (4%)
  matrix products  18.5 us (3%)
  between operations  15.5 us (2%)
    ppermute x63, waiting for transfers between devices, swap(): return lax.ppermute(array, axis, [(0, 1), (1, 0)])  75.4 us
    pallas_call x8, Pallas kernels, chunk_call(): pl.pallas_call(kernel, grid_spec=pltpu.PrefetchScalarGridSpec(num_scalar_...  72.2 us
    ppermute x12, waiting for transfers between devices, ring(): return lax.ppermute(array, 'z', [(i, (i + 1) % size) for i in range(size)])  56.3 us
    all_to_all x8, waiting for transfers between devices, spread_z(): return lax.all_to_all(parts, 'z', split_axis=0, concat_axis=0, tiled=True)  46.9 us
    ppermute x63, starting transfers between devices, swap(): return lax.ppermute(array, axis, [(0, 1), (1, 0)])  45.3 us
    pallas_call x8, Pallas kernels, small_call(): pl.pallas_call(kernel, grid_spec=pltpu.PrefetchScalarGridSpec(num_scalar_...  43.7 us
    all_to_all x8, starting transfers between devices, spread_z(): return lax.all_to_all(parts, 'z', split_axis=0, concat_axis=0, tiled=True)  32.8 us
    all_to_all x1, blocking collectives, on_device(): lax.all_to_all(att_low, ('z', 'y'), split_axis=0, concat_axis=0, tiled=True)  25.1 us
  transfers between devices with their start and end apart: 89, of which 33 were waited for; matrix products, arithmetic and copies ran while one was open for 12% of the time, Pallas kernels for 24%

profile of v6, /device:TPU:0, one launch (start us, length us, event | category | flops | bytes accessed | tf_op | source)
XLA Modules:
  0.0 621.1 jit_solution(4033597162541944523)
XLA Ops:
  24.9 4.0 all-to-all-start
  34.9 16.5 %all-to-all-done.refs_5_.w_first = bf16[4,400,256]{2,1,0:T(8,128)(2,1)S(1)} async-done(((bf16[4,400,256]{2,1,0:T(8,128)(2,1)}), bf16[4,400,256]{2,1,0:T(8,128)(2,1)S(1)}, u32[]{:S(2)}, u32[]{:S(2)}) %all-to-all-start) | async-done | bytes 819232 | tf_op jit(solution)/shard_map/all_to_all | solution.py:754
  54.6 10.8 %collective-permute-done.7.refs_0_ = bf16[384,512]{1,0:T(8,128)(2,1)S(1)} collective-permute-done((bf16[384,512]{1,0:T(8,128)(2,1)}, bf16[384,512]{1,0:T(8,128)(2,1)S(1)}, u32[]{:S(2)}, u32[]{:S(2)}) %collective-permute-start.7) | collective-permute-done | bytes 393248 | tf_op jit(solution)/shard_map/ppermute | solution.py:66
  81.9 5.7 qkv.4
  89.1 5.7 qkv.5
  96.1 5.7 qkv.6
  104.2 5.9 qkv.7
  111.3 8.5 %collective-permute-done.19.refs_7_ = bf16[192,384]{1,0:T(8,128)(2,1)S(1)} collective-permute-done((bf16[192,384]{1,0:T(8,128)(2,1)}, bf16[192,384]{1,0:T(8,128)(2,1)S(1)}, u32[]{:S(2)}, u32[]{:S(2)}) %collective-permute-start.19) | collective-permute-done | bytes 147488 | tf_op jit(solution)/shard_map/ppermute | solution.py:62
  129.2 18.6 %attend.1 = (bf16[8,64,384]{2,1,0:T(8,128)(2,1)}, f32[8,64,384]{2,1,0:T(8,128)}, f32[8,1,384]{2,1,0:T(1,128)}, f32[8,1,384]{2,1,0:T(1,128)}) custom-call(s32[64]{0:T(128)} %reshape.313.visible, s32[8]{0:T(128)} %get-tuple-element.249.counts, s32[17]{0:T(128)} %concatenate.20.q_pos, s32[8]{0:T(128)} %copy-done.53, ...), custom_call_target="tpu_custom_call" | custom-call | flops 17999998976 | bytes 1000 | tf_op jit(solution)/shard_map/attend/pallas_call | solution.py:166
  147.8 4.8 collective-permute-done.20
  152.6 13.6 %all-to-all-done.2 = bf16[4,256,512]{2,1,0:T(8,128)(2,1)S(1)} async-done(((bf16[4,256,512]{2,1,0:T(8,128)(2,1)}), bf16[4,256,512]{2,1,0:T(8,128)(2,1)S(1)}, u32[]{:S(2)}, u32[]{:S(2)}) %all-to-all-start.2) | async-done | bytes 1048608 | tf_op jit(solution)/shard_map/all_to_all | solution.py:754
  166.2 25.1 %all_to_all.50 = bf16[8,64,384]{2,1,0:T(8,128)(2,1)} all-to-all(bf16[8,64,384]{2,1,0:T(8,128)(2,1)} %get-tuple-element.295), channel_id=1, replica_groups=mesh['z'=4,'q'=1,'y'=2,'x'=2,'c'=2] {'z','y'}, dimensions={0} | all-to-all | bytes 786432 | tf_op jit(solution)/shard_map/all_to_all | solution.py:938
  191.3 4.5 project.1
  204.8 9.0 %collective-permute-done.22 = bf16[384,512]{1,0:T(8,128)(2,1)S(1)} collective-permute-done((bf16[384,512]{1,0:T(8,128)(2,1)S(1)}, bf16[384,512]{1,0:T(8,128)(2,1)S(1)}, u32[]{:S(2)}, u32[]{:S(2)}) %collective-permute-start.22) | collective-permute-done | bytes 393248 | tf_op jit(solution)/shard_map/ppermute | solution.py:62
  217.8 13.8 %collective-permute-done.23.refs_4_ = bf16[384,512]{1,0:T(8,128)(2,1)S(1)} collective-permute-done((bf16[384,512]{1,0:T(8,128)(2,1)S(1)}, bf16[384,512]{1,0:T(8,128)(2,1)S(1)}, u32[]{:S(2)}, u32[]{:S(2)}) %collective-permute-start.23) | collective-permute-done | bytes 393248 | tf_op jit(solution)/shard_map/ppermute | solution.py:66
  231.7 4.8 collective-permute-start.27
  237.6 8.9 %all-to-all-done.4 = bf16[4,256,512]{2,1,0:T(8,128)(2,1)S(1)} async-done(((bf16[4,256,512]{2,1,0:T(8,128)(2,1)}), bf16[4,256,512]{2,1,0:T(8,128)(2,1)S(1)}, u32[]{:S(2)}, u32[]{:S(2)}) %all-to-all-start.4) | async-done | bytes 1048608 | tf_op jit(solution)/shard_map/all_to_all | solution.py:754
  253.9 7.0 %arrange.1.refs_12_ = bf16[1536,2048]{1,0:T(8,128)(2,1)} custom-call(s32[4]{0:T(128)} %add_add_fusion.1.zs, bf16[16,384,512]{2,1,0:T(8,128)(2,1)} %bitcast.192), custom_call_target="tpu_custom_call" | custom-call | flops 5000000000 | bytes 1000 | tf_op jit(solution)/shard_map/arrange/pallas_call | solution.py:482
  263.9 11.0 %feed_forward.2 = (bf16[1536,2048]{1,0:T(8,128)(2,1)}, bf16[1536,512]{1,0:T(8,128)(2,1)}, f32[384,512]{1,0:T(8,128)}, f32[384,512]{1,0:T(8,128)}, f32[384,512]{1...) custom-call(s32[4]{0:T(128)} %get-tuple-element.433.where, bf16[384,512]{1,0:T(8,128)(2,1)} %copy-done.6, ...), custom_call_target="tpu_custom_call" | custom-call | flops 8999999488 | bytes 1000 | tf_op jit(solution)/shard_map/feed_forward/pallas_call | solution.py:370
  277.5 10.9 %feed_forward.3 = (bf16[1536,2048]{1,0:T(8,128)(2,1)}, bf16[1536,512]{1,0:T(8,128)(2,1)}, f32[384,512]{1,0:T(8,128)}, f32[384,512]{1,0:T(8,128)}, f32[384,512]{1...) custom-call(s32[4]{0:T(128)} %get-tuple-element.433.where, ...), custom_call_target="tpu_custom_call", output_to_operand_aliasing={{0}: (15, {}), {1}: (16, {})} | custom-call | flops 8999999488 | bytes 1000 | tf_op jit(solution)/shard_map/feed_forward/pallas_call | solution.py:370
  288.4 13.9 %feed_forward_back.2 = (bf16[1536,512]{1,0:T(8,128)(2,1)}, bf16[1536,512]{1,0:T(8,128)(2,1)}, bf16[2,784,512]{2,1,0:T(8,128)(2,1)}, bf16[2,784,512]{2,1,0:T(8,12...) custom-call(s32[4]{0:T(128)} %get-tuple-element.433.where, ...), custom_call_target="tpu_custom_call" | custom-call | flops 15000000512 | bytes 1000 | tf_op jit(solution)/shard_map/feed_forward_back/pallas_call | solution.py:370
  312.0 13.4 %feed_forward_back.3 = (bf16[1536,512]{1,0:T(8,128)(2,1)}, bf16[1536,512]{1,0:T(8,128)(2,1)}, bf16[2,784,512]{2,1,0:T(8,128)(2,1)}, bf16[2,784,512]{2,1,0:T(8,12...) custom-call(s32[4]{0:T(128)} %get-tuple-element.433.where, ...), custom_call_target="tpu_custom_call", output_to_operand_aliasing={{0}: (16, {}), {1}: (17, {})} | custom-call | flops 15000000512 | bytes 1000 | tf_op jit(solution)/shard_map/feed_forward_back/pallas_call | solution.py:370
  325.6 5.2 collective-permute-done.43
  335.1 6.8 %convolution_convert_fusion.2 = bf16[2048,512]{1,0:T(8,128)(2,1)S(1)} fusion(bf16[1536,2048]{1,0:T(8,128)(2,1)} %arrange.1.refs_12_, bf16[1536,512]{1,0:T(8,128)(2,1)S(1)} %copy-done.85), kind=kOutput, calls=%fused_computation.6 | convolution fusion | flops 3222274048 | bytes 9961472 | tf_op jit(solution)/shard_map/dot_general | solution.py:52
  342.3 9.9 %collective-permute-done.45 = bf16[784,512]{1,0:T(8,128)(2,1)S(1)} collective-permute-done((bf16[784,512]{1,0:T(8,128)(2,1)S(1)}, bf16[784,512]{1,0:T(8,128)(2,1)S(1)}, u32[]{:S(2)}, u32[]{:S(2)}) %collective-permute-start.45) | collective-permute-done | bytes 802848 | tf_op jit(solution)/shard_map/ppermute | solution.py:66
  362.5 13.2 %collective-permute-done.48 = bf16[784,512]{1,0:T(8,128)(2,1)S(1)} collective-permute-done((bf16[784,512]{1,0:T(8,128)(2,1)S(1)}, bf16[784,512]{1,0:T(8,128)(2,1)S(1)}, u32[]{:S(2)}, u32[]{:S(2)}) %collective-permute-start.48) | collective-permute-done | bytes 802848 | tf_op jit(solution)/shard_map/ppermute | solution.py:66
  375.6 5.4 collective-permute-done.51
  389.1 4.5 all-to-all-start.5
  393.6 8.0 %convolution_convert_fusion = bf16[2048,512]{1,0:T(8,128)(2,1)} fusion(bf16[1536,2048]{1,0:T(8,128)(2,1)} %get-tuple-element.340.refs_14_, bf16[1536,512]{1,0:T(8,128)(2,1)} %get-tuple-element.380), kind=kOutput, calls=%fused_computation.4 | convolution fusion | flops 3222274048 | bytes 9961472 | tf_op jit(solution)/shard_map/dot_general | solution.py:52
  401.6 4.5 collective-permute-done.52
  409.9 7.1 %collective-permute-done.54.p2 = bf16[384,512]{1,0:T(8,128)(2,1)S(1)} collective-permute-done((bf16[384,512]{1,0:T(8,128)(2,1)S(1)}, bf16[384,512]{1,0:T(8,128)(2,1)S(1)}, u32[]{:S(2)}, u32[]{:S(2)}) %collective-permute-start.54) | collective-permute-done | bytes 393248 | tf_op jit(solution)/shard_map/ppermute | solution.py:62
  419.5 6.6 %project_back.1 = (bf16[512,384]{1,0:T(8,128)(2,1)}, bf16[8,512,256]{2,1,0:T(8,128)(2,1)}) custom-call(s32[4]{0:T(128)} %get-tuple-element.433.where, bf16[384,512]{1,0:T(8,128)(2,1)} %copy-done.37, bf16[384,512]{1,0:T(8,128)(2,1)} %copy-done.77, bf16[384,512]{1,0:T(8,128)(2,1)} %copy-done.76, bf16[384,512]{1,0:T(8,128)(2,1)} %copy-done.79, ...), custom_call_target="tpu_custom_call" | custom-call | flops 6000000000 | bytes 1000 | tf_op jit(solution)/shard_map/project_back/pallas_call | solution.py:697
  426.1 6.0 all-to-all-start.6
  438.1 5.9 all-to-all-done.6.refs_10_
  444.0 4.3 all-to-all-start.7
  448.4 22.0 %attend_back.1.mine.refs_0_ = bf16[8,192,384]{2,1,0:T(8,128)(2,1)} custom-call(s32[64]{0:T(128)} %reshape.313.visible, s32[8]{0:T(128)} %get-tuple-element.249.counts, s32[17]{0:T(128)} %concatenate.20.q_pos, s32[8]{0:T(128)} %copy-done.53, bf16[192,384]{1,0:T(8,128)(2,1)} %get-tuple-element.278.refs_0_, bf16[192,384]{1,0:T(8,128)(2,1)} %get-tuple-element.279.refs_1_, ...), custom_call_target="tpu_custom_call" | custom-call | flops 22000001024 | bytes 1000 | tf_op jit(solution)/shard_map/attend_back/pallas_call | solution.py:256
  482.2 5.0 all-to-all-start.8
  488.9 5.2 qkv_back.4
  494.1 8.3 %qkv_weights.1 = (bf16[4,384,256]{2,1,0:T(8,128)(2,1)}, bf16[4,384,256]{2,1,0:T(8,128)(2,1)}) custom-call(s32[4]{0:T(128)} %get-tuple-element.412.where, bf16[1536,2048]{1,0:T(8,128)(2,1)} %get-tuple-element.405.normed, bf16[8,192,384]{2,1,0:T(8,128)(2,1)} %attend_back.1.mine.refs_0_, bf16[4,192,384]{2,1,0:T(8,128)(2,1)} %collective-permute-done.59.other.refs_1_), custom_call_target="tpu_custom_call" | custom-call | flops 8000000000 | bytes 1000 | tf_op jit(solution)/shard_map/qkv_weights/pallas_call | solution.py:697
  502.4 5.3 qkv_back.5
  515.8 5.2 qkv_back.6
  521.1 4.6 all-to-all-done.8.parts
  527.3 10.1 %collective-permute-done.63 = bf16[4,384,256]{2,1,0:T(8,128)(2,1)} collective-permute-done((bf16[4,384,256]{2,1,0:T(8,128)(2,1)}, bf16[4,384,256]{2,1,0:T(8,128)(2,1)}, u32[]{:S(2)}, u32[]{:S(2)}) %collective-permute-start.63) | collective-permute-done | bytes 786464 | tf_op jit(solution)/shard_map/ppermute | solution.py:62
  545.5 4.2 all-to-all-start.9
  550.6 5.3 qkv_back.7
  559.5 8.4 %reduce-scatter.2.cloned.1.call-done = bf16[1,512,256]{2,1,0:T(8,128)(2,1)} async-done(((bf16[8,512,256]{2,1,0:T(8,128)(2,1)}), bf16[1,512,256]{2,1,0:T(8,128)(2,1)}) %reduce-scatter.2.cloned.1.call-update) | async-done | bytes 262160 | tf_op jit(solution)/shard_map/reduce_scatter | solution.py:1221
  577.8 9.6 %collective-permute-done.71 = f32[2,2048]{1,0:T(2,128)S(1)} collective-permute-done((f32[2,2048]{1,0:T(2,128)S(1)}, f32[2,2048]{1,0:T(2,128)S(1)}, u32[]{:S(2)}, u32[]{:S(2)}) %collective-permute-start.71) | collective-permute-done | bytes 16416 | tf_op jit(solution)/shard_map/ppermute | solution.py:62
  598.7 5.3 collective-permute-start.75
  (468 shorter events, 197.5 us)
Async XLA Ops:
  24.9 26.4 %all-to-all-start = ((bf16[4,400,256]{2,1,0:T(8,128)(2,1)}), bf16[4,400,256]{2,1,0:T(8,128)(2,1)S(1)}, u32[]{:S(2)}, u32[]{:S(2)}) async-start(bf16[4,400,256]{2,1,0:T(8,128)(2,1)} %pad_maximum_fusion), calls=%async_computation | async-start | bytes 1638400 | tf_op jit(solution)/shard_map/all_to_all | solution.py:754
  29.0 162.3 %all-gather.5.cloned.1.call-start = ((), (), s32[]{:S(2)}) async-start(), calls=%async_computation.12 | async-start | bytes 2359296 | tf_op jit(solution)/shard_map/all_gather | solution.py:905
  51.3 20.2 %collective-permute-start.11 = (bf16[4,400,256]{2,1,0:T(8,128)(2,1)S(1)}, bf16[4,400,256]{2,1,0:T(8,128)(2,1)S(1)}, u32[]{:S(2)}, u32[]{:S(2)}) collective-permute-start(bf16[4,400,256]{2,1,0:T(8,128)(2,1)S(1)} %all-to-all-done.refs_5_.w_first), channel_id=1, source_target_pairs={{0,4},{4,0},{1,5},{5,1},{2,6},{6,2},{3,7},{7,3},{8,12},{12,8},{9,1... | collective-permute-start | bytes 2457608 | tf_op jit(solution)/shard_map/ppermute | solution.py:62
  71.5 182.4 %all-gather.7.cloned.1.call-start = ((), (), s32[]{:S(2)}) async-start(), calls=%async_computation.13 | async-start | bytes 6684672 | tf_op jit(solution)/shard_map/all_gather | solution.py:910
  74.4 29.1 %collective-permute-start.13 = (bf16[384,512]{1,0:T(8,128)(2,1)}, bf16[384,512]{1,0:T(8,128)(2,1)}, u32[]{:S(2)}, u32[]{:S(2)}) collective-permute-start(bf16[384,512]{1,0:T(8,128)(2,1)} %copy-done.64), channel_id=1, source_target_pairs={{0,1},{1,0},{2,3},{3,2},{4,5},{5,4},{6,7},{7,6},{8,9},{9,8},{10,11... | collective-permute-start | bytes 1179656 | tf_op jit(solution)/shard_map/ppermute | solution.py:62
  74.4 21.0 %collective-permute-start.14 = (bf16[384,512]{1,0:T(8,128)(2,1)}, bf16[384,512]{1,0:T(8,128)(2,1)}, u32[]{:S(2)}, u32[]{:S(2)}) collective-permute-start(bf16[384,512]{1,0:T(8,128)(2,1)} %copy-done.64), channel_id=1, source_target_pairs={{0,2},{2,0},{1,3},{3,1},{4,6},{6,4},{5,7},{7,5},{8,10},{10,8},{9,1... | collective-permute-start | bytes 1179656 | tf_op jit(solution)/shard_map/ppermute | solution.py:62
  76.9 18.5 %collective-permute-start.12 = (bf16[384,512]{1,0:T(8,128)(2,1)}, bf16[384,512]{1,0:T(8,128)(2,1)S(1)}, u32[]{:S(2)}, u32[]{:S(2)}) collective-permute-start(bf16[384,512]{1,0:T(8,128)(2,1)} %copy-done.66), channel_id=1, source_target_pairs={{0,1},{1,0},{2,3},{3,2},{4,5},{5,4},{6,7},{7,6},{8,9},{9,8},{10,11... | collective-permute-start | bytes 1179656 | tf_op jit(solution)/shard_map/ppermute | solution.py:62
  78.2 44.9 %all-to-all-start.1 = ((bf16[4,256,512]{2,1,0:T(8,128)(2,1)}), bf16[4,256,512]{2,1,0:T(8,128)(2,1)S(1)}, u32[]{:S(2)}, u32[]{:S(2)}) async-start(bf16[4,256,512]{2,1,0:T(8,128)(2,1)} %bitcast.158), calls=%async_computation.1 | async-start | bytes 2097152 | tf_op jit(solution)/shard_map/all_to_all | solution.py:754
  87.6 23.1 %collective-permute-start.16 = (bf16[192,384]{1,0:T(8,128)(2,1)}, bf16[192,384]{1,0:T(8,128)(2,1)S(1)}, u32[]{:S(2)}, u32[]{:S(2)}) collective-permute-start(bf16[192,384]{1,0:T(8,128)(2,1)} %get-tuple-element.273), channel_id=1, source_target_pairs={{0,4},{4,0},{1,5},{5,1},{2,6},{6,2},{3,7},{7,3},{8,12},{12,8},{9,1... | collective-permute-start | bytes 442376 | tf_op jit(solution)/shard_map/ppermute | solution.py:62
  94.9 15.8 %collective-permute-start.17 = (bf16[192,384]{1,0:T(8,128)(2,1)}, bf16[192,384]{1,0:T(8,128)(2,1)S(1)}, u32[]{:S(2)}, u32[]{:S(2)}) collective-permute-start(bf16[192,384]{1,0:T(8,128)(2,1)} %get-tuple-element.274), channel_id=1, source_target_pairs={{0,4},{4,0},{1,5},{5,1},{2,6},{6,2},{3,7},{7,3},{8,12},{12,8},{9,1... | collective-permute-start | bytes 442376 | tf_op jit(solution)/shard_map/ppermute | solution.py:62
  124.3 41.9 %all-to-all-start.2 = ((bf16[4,256,512]{2,1,0:T(8,128)(2,1)}), bf16[4,256,512]{2,1,0:T(8,128)(2,1)S(1)}, u32[]{:S(2)}, u32[]{:S(2)}) async-start(bf16[4,256,512]{2,1,0:T(8,128)(2,1)} %bitcast.156), calls=%async_computation.2 | async-start | bytes 2097152 | tf_op jit(solution)/shard_map/all_to_all | solution.py:754
  127.8 24.8 %collective-permute-start.20 = (bf16[4,256,512]{2,1,0:T(8,128)(2,1)S(1)}, bf16[4,256,512]{2,1,0:T(8,128)(2,1)S(1)}, u32[]{:S(2)}, u32[]{:S(2)}) collective-permute-start(bf16[4,256,512]{2,1,0:T(8,128)(2,1)S(1)} %all-to-all-done.1), channel_id=1, source_target_pairs={{0,4},{4,0},{1,5},{5,1},{2,6},{6,2},{3,7},{7,3},{8,12},{12,8},{9,1... | collective-permute-start | bytes 3145736 | tf_op jit(solution)/shard_map/ppermute | solution.py:62
  197.2 49.4 %all-to-all-start.4 = ((bf16[4,256,512]{2,1,0:T(8,128)(2,1)}), bf16[4,256,512]{2,1,0:T(8,128)(2,1)S(1)}, u32[]{:S(2)}, u32[]{:S(2)}) async-start(bf16[4,256,512]{2,1,0:T(8,128)(2,1)} %bitcast.40), calls=%async_computation.4 | async-start | bytes 2097152 | tf_op jit(solution)/shard_map/all_to_all | solution.py:754
  202.8 15.0 %collective-permute-start.26 = (bf16[2,256,512]{2,1,0:T(8,128)(2,1)S(1)}, bf16[2,256,512]{2,1,0:T(8,128)(2,1)S(1)}, u32[]{:S(2)}, u32[]{:S(2)}) collective-permute-start(bf16[2,256,512]{2,1,0:T(8,128)(2,1)S(1)} %get-tuple-element.491), channel_id=1, source_target_pairs={{0,4},{4,0},{1,5},{5,1},{2,6},{6,2},{3,7},{7,3},{8,12},{12,8},{9,1... | collective-permute-start | bytes 1572872 | tf_op jit(solution)/shard_map/ppermute | solution.py:62
  213.9 17.7 %collective-permute-start.23 = (bf16[384,512]{1,0:T(8,128)(2,1)S(1)}, bf16[384,512]{1,0:T(8,128)(2,1)S(1)}, u32[]{:S(2)}, u32[]{:S(2)}) collective-permute-start(bf16[384,512]{1,0:T(8,128)(2,1)S(1)} %fusion.22.refs_0_), channel_id=1, source_target_pairs={{0,8},{8,16},{16,24},{24,0},{1,9},{9,17},{17,25},{25,1},{2,10},{10... | collective-permute-start | bytes 1179656 | tf_op jit(solution)/shard_map/ppermute | solution.py:66
  215.7 16.0 %collective-permute-start.24 = (bf16[384,512]{1,0:T(8,128)(2,1)S(1)}, bf16[384,512]{1,0:T(8,128)(2,1)}, u32[]{:S(2)}, u32[]{:S(2)}) collective-permute-start(bf16[384,512]{1,0:T(8,128)(2,1)S(1)} %fusion.22.refs_0_), channel_id=1, source_target_pairs={{0,2},{2,0},{1,3},{3,1},{4,6},{6,4},{5,7},{7,5},{8,10},{10,8},{9,1... | collective-permute-start | bytes 1179656 | tf_op jit(solution)/shard_map/ppermute | solution.py:62
  216.2 15.4 %collective-permute-start.25 = (bf16[384,512]{1,0:T(8,128)(2,1)S(1)}, bf16[384,512]{1,0:T(8,128)(2,1)S(1)}, u32[]{:S(2)}, u32[]{:S(2)}) collective-permute-start(bf16[384,512]{1,0:T(8,128)(2,1)S(1)} %fusion.22.refs_0_), channel_id=1, source_target_pairs={{0,1},{1,0},{2,3},{3,2},{4,5},{5,4},{6,7},{7,6},{8,9},{9,8},{10,11... | collective-permute-start | bytes 1179656 | tf_op jit(solution)/shard_map/ppermute | solution.py:62
  216.2 21.4 %collective-permute-start.31 = (bf16[2,256,512]{2,1,0:T(8,128)(2,1)S(1)}, bf16[2,256,512]{2,1,0:T(8,128)(2,1)S(1)}, u32[]{:S(2)}, u32[]{:S(2)}) collective-permute-start(bf16[2,256,512]{2,1,0:T(8,128)(2,1)S(1)} %get-tuple-element.490), channel_id=1, source_target_pairs={{0,4},{4,0},{1,5},{5,1},{2,6},{6,2},{3,7},{7,3},{8,12},{12,8},{9,1... | collective-permute-start | bytes 1572872 | tf_op jit(solution)/shard_map/ppermute | solution.py:62
  231.7 14.9 %collective-permute-start.27 = (bf16[384,512]{1,0:T(8,128)(2,1)S(1)}, bf16[384,512]{1,0:T(8,128)(2,1)S(1)}, u32[]{:S(2)}, u32[]{:S(2)}) collective-permute-start(bf16[384,512]{1,0:T(8,128)(2,1)S(1)} %collective-permute-done.23.refs_4_), channel_id=1, source_target_pairs={{0,8},{8,16},{16,24},{24,0},{1,9},{9,17},{17,25},{25,1},{2,10},{10... | collective-permute-start | bytes 1179656 | tf_op jit(solution)/shard_map/ppermute | solution.py:66
  247.3 15.4 %collective-permute-start.36 = (bf16[2,256,512]{2,1,0:T(8,128)(2,1)S(1)}, bf16[2,256,512]{2,1,0:T(8,128)(2,1)}, u32[]{:S(2)}, u32[]{:S(2)}) collective-permute-start(bf16[2,256,512]{2,1,0:T(8,128)(2,1)S(1)} %get-tuple-element.489), channel_id=1, source_target_pairs={{0,4},{4,0},{1,5},{5,1},{2,6},{6,2},{3,7},{7,3},{8,12},{12,8},{9,1... | collective-permute-start | bytes 1572872 | tf_op jit(solution)/shard_map/ppermute | solution.py:62
  310.6 20.2 %collective-permute-start.43 = (bf16[784,512]{1,0:T(8,128)(2,1)}, bf16[784,512]{1,0:T(8,128)(2,1)S(1)}, u32[]{:S(2)}, u32[]{:S(2)}) collective-permute-start(bf16[784,512]{1,0:T(8,128)(2,1)} %fusion.3), channel_id=1, source_target_pairs={{0,2},{2,0},{1,3},{3,1},{4,6},{6,4},{5,7},{7,5},{8,10},{10,8},{9,1... | collective-permute-start | bytes 2408456 | tf_op jit(solution)/shard_map/ppermute | solution.py:62
  312.0 18.8 %collective-permute-start.44 = (bf16[2,784,512]{2,1,0:T(8,128)(2,1)}, bf16[2,784,512]{2,1,0:T(8,128)(2,1)}, u32[]{:S(2)}, u32[]{:S(2)}) collective-permute-start(bf16[2,784,512]{2,1,0:T(8,128)(2,1)} %get-tuple-element.347), channel_id=1, source_target_pairs={{0,1},{1,0},{2,3},{3,2},{4,5},{5,4},{6,7},{7,6},{8,9},{9,8},{10,11... | collective-permute-start | bytes 4816904 | tf_op jit(solution)/shard_map/ppermute | solution.py:62
  331.2 21.0 %collective-permute-start.45 = (bf16[784,512]{1,0:T(8,128)(2,1)S(1)}, bf16[784,512]{1,0:T(8,128)(2,1)S(1)}, u32[]{:S(2)}, u32[]{:S(2)}) collective-permute-start(bf16[784,512]{1,0:T(8,128)(2,1)S(1)} %add_convert_fusion.2), channel_id=1, source_target_pairs={{0,8},{8,16},{16,24},{24,0},{1,9},{9,17},{17,25},{25,1},{2,10},{10... | collective-permute-start | bytes 2408456 | tf_op jit(solution)/shard_map/ppermute | solution.py:66
  331.6 22.4 %collective-permute-start.47 = (bf16[2,784,512]{2,1,0:T(8,128)(2,1)S(1)}, bf16[2,784,512]{2,1,0:T(8,128)(2,1)S(1)}, u32[]{:S(2)}, u32[]{:S(2)}) collective-permute-start(bf16[2,784,512]{2,1,0:T(8,128)(2,1)S(1)} %copy-done.57), channel_id=1, source_target_pairs={{0,1},{1,0},{2,3},{3,2},{4,5},{5,4},{6,7},{7,6},{8,9},{9,8},{10,11... | collective-permute-start | bytes 4816904 | tf_op jit(solution)/shard_map/ppermute | solution.py:62
  333.7 20.3 %collective-permute-start.46 = (bf16[784,512]{1,0:T(8,128)(2,1)S(1)}, bf16[784,512]{1,0:T(8,128)(2,1)S(1)}, u32[]{:S(2)}, u32[]{:S(2)}) collective-permute-start(bf16[784,512]{1,0:T(8,128)(2,1)S(1)} %fusion.4), channel_id=1, source_target_pairs={{0,2},{2,0},{1,3},{3,1},{4,6},{6,4},{5,7},{7,5},{8,10},{10,8},{9,1... | collective-permute-start | bytes 2408456 | tf_op jit(solution)/shard_map/ppermute | solution.py:62
  341.9 20.5 %collective-permute-start.50 = (bf16[2,784,512]{2,1,0:T(8,128)(2,1)S(1)}, bf16[2,784,512]{2,1,0:T(8,128)(2,1)S(1)}, u32[]{:S(2)}, u32[]{:S(2)}) collective-permute-start(bf16[2,784,512]{2,1,0:T(8,128)(2,1)S(1)} %copy-done.56), channel_id=1, source_target_pairs={{0,1},{1,0},{2,3},{3,2},{4,5},{5,4},{6,7},{7,6},{8,9},{9,8},{10,11... | collective-permute-start | bytes 4816904 | tf_op jit(solution)/shard_map/ppermute | solution.py:62
  354.3 21.3 %collective-permute-start.48 = (bf16[784,512]{1,0:T(8,128)(2,1)S(1)}, bf16[784,512]{1,0:T(8,128)(2,1)S(1)}, u32[]{:S(2)}, u32[]{:S(2)}) collective-permute-start(bf16[784,512]{1,0:T(8,128)(2,1)S(1)} %add_convert_fusion.1), channel_id=1, source_target_pairs={{0,8},{8,16},{16,24},{24,0},{1,9},{9,17},{17,25},{25,1},{2,10},{10... | collective-permute-start | bytes 2408456 | tf_op jit(solution)/shard_map/ppermute | solution.py:66
  355.4 20.3 %collective-permute-start.49 = (bf16[784,512]{1,0:T(8,128)(2,1)S(1)}, bf16[784,512]{1,0:T(8,128)(2,1)S(1)}, u32[]{:S(2)}, u32[]{:S(2)}) collective-permute-start(bf16[784,512]{1,0:T(8,128)(2,1)S(1)} %fusion.5), channel_id=1, source_target_pairs={{0,2},{2,0},{1,3},{3,1},{4,6},{6,4},{5,7},{7,5},{8,10},{10,8},{9,1... | collective-permute-start | bytes 2408456 | tf_op jit(solution)/shard_map/ppermute | solution.py:62
  356.8 24.2 %collective-permute-start.51 = (bf16[1024,512]{1,0:T(8,128)(2,1)S(1)}, bf16[1024,512]{1,0:T(8,128)(2,1)S(1)}, u32[]{:S(2)}, u32[]{:S(2)}) collective-permute-start(bf16[1024,512]{1,0:T(8,128)(2,1)S(1)} %dynamic-slice_bitcast_fusion.2), channel_id=1, source_target_pairs={{0,4},{4,0},{1,5},{5,1},{2,6},{6,2},{3,7},{7,3},{8,12},{12,8},{9,1... | collective-permute-start | bytes 3145736 | tf_op jit(solution)/shard_map/ppermute | solution.py:62
  383.2 23.0 %collective-permute-start.52 = (bf16[784,512]{1,0:T(8,128)(2,1)}, bf16[784,512]{1,0:T(8,128)(2,1)S(1)}, u32[]{:S(2)}, u32[]{:S(2)}) collective-permute-start(bf16[784,512]{1,0:T(8,128)(2,1)} %add_convert_fusion), channel_id=1, source_target_pairs={{0,8},{8,16},{16,24},{24,0},{1,9},{9,17},{17,25},{25,1},{2,10},{10... | collective-permute-start | bytes 2408456 | tf_op jit(solution)/shard_map/ppermute | solution.py:66
  385.0 22.1 %collective-permute-start.53 = (bf16[784,512]{1,0:T(8,128)(2,1)S(1)}, bf16[784,512]{1,0:T(8,128)(2,1)}, u32[]{:S(2)}, u32[]{:S(2)}) collective-permute-start(bf16[784,512]{1,0:T(8,128)(2,1)S(1)} %fusion.6), channel_id=1, source_target_pairs={{0,2},{2,0},{1,3},{3,1},{4,6},{6,4},{5,7},{7,5},{8,10},{10,8},{9,1... | collective-permute-start | bytes 2408456 | tf_op jit(solution)/shard_map/ppermute | solution.py:62
  386.6 30.3 %collective-permute-start.57 = (bf16[1024,512]{1,0:T(8,128)(2,1)}, bf16[1024,512]{1,0:T(8,128)(2,1)}, u32[]{:S(2)}, u32[]{:S(2)}) collective-permute-start(bf16[1024,512]{1,0:T(8,128)(2,1)} %dynamic-slice_bitcast_fusion.1), channel_id=1, source_target_pairs={{0,4},{4,0},{1,5},{5,1},{2,6},{6,2},{3,7},{7,3},{8,12},{12,8},{9,1... | collective-permute-start | bytes 3145736 | tf_op jit(solution)/shard_map/ppermute | solution.py:62
  389.1 37.0 %all-to-all-start.5 = ((bf16[4,256,512]{2,1,0:T(8,128)(2,1)}), bf16[4,256,512]{2,1,0:T(8,128)(2,1)}, u32[]{:S(2)}, u32[]{:S(2)}) async-start(bf16[4,256,512]{2,1,0:T(8,128)(2,1)} %bitcast.62), calls=%async_computation.5 | async-start | bytes 2097152 | tf_op jit(solution)/shard_map/all_to_all | solution.py:754
  426.1 17.9 %all-to-all-start.6 = ((bf16[8,64,384]{2,1,0:T(8,128)(2,1)}), bf16[8,64,384]{2,1,0:T(8,128)(2,1)S(1)}, u32[]{:S(2)}, u32[]{:S(2)}) async-start(bf16[8,64,384]{2,1,0:T(8,128)(2,1)} %bitcast.184), calls=%async_computation.6 | async-start | bytes 786432 | tf_op jit(solution)/shard_map/all_to_all | solution.py:1119
  433.5 36.9 %collective-permute-start.58 = (bf16[1024,512]{1,0:T(8,128)(2,1)S(1)}, bf16[1024,512]{1,0:T(8,128)(2,1)}, u32[]{:S(2)}, u32[]{:S(2)}) collective-permute-start(bf16[1024,512]{1,0:T(8,128)(2,1)S(1)} %dynamic-slice_bitcast_fusion), channel_id=1, source_target_pairs={{0,4},{4,0},{1,5},{5,1},{2,6},{6,2},{3,7},{7,3},{8,12},{12,8},{9,1... | collective-permute-start | bytes 3145736 | tf_op jit(solution)/shard_map/ppermute | solution.py:62
  444.0 38.2 %all-to-all-start.7 = ((bf16[4,256,512]{2,1,0:T(8,128)(2,1)}), bf16[4,256,512]{2,1,0:T(8,128)(2,1)}, u32[]{:S(2)}, u32[]{:S(2)}) async-start(bf16[4,256,512]{2,1,0:T(8,128)(2,1)} %bitcast.65), calls=%async_computation.7 | async-start | bytes 2097152 | tf_op jit(solution)/shard_map/all_to_all | solution.py:754
  448.3 119.6 %reduce-scatter.2.cloned.1.call-start = ((), (), s32[]{:S(2)}) async-start(), calls=%async_computation.11 | async-start | bytes 2359296 | tf_op jit(solution)/shard_map/reduce_scatter | solution.py:1221
  471.6 17.3 %collective-permute-start.59 = (bf16[4,192,384]{2,1,0:T(8,128)(2,1)S(1)}, bf16[4,192,384]{2,1,0:T(8,128)(2,1)}, u32[]{:S(2)}, u32[]{:S(2)}) collective-permute-start(bf16[4,192,384]{2,1,0:T(8,128)(2,1)S(1)} %slice.181), channel_id=1, source_target_pairs={{0,4},{4,0},{1,5},{5,1},{2,6},{6,2},{3,7},{7,3},{8,12},{12,8},{9,1... | collective-permute-start | bytes 1769480 | tf_op jit(solution)/shard_map/ppermute | solution.py:62
  482.2 43.5 %all-to-all-start.8 = ((bf16[4,256,512]{2,1,0:T(8,128)(2,1)}), bf16[4,256,512]{2,1,0:T(8,128)(2,1)S(1)}, u32[]{:S(2)}, u32[]{:S(2)}) async-start(bf16[4,256,512]{2,1,0:T(8,128)(2,1)} %bitcast.72), calls=%async_computation.8 | async-start | bytes 2097152 | tf_op jit(solution)/shard_map/all_to_all | solution.py:754
  494.1 17.3 %collective-permute-start.60 = (bf16[2,400,512]{2,1,0:T(8,128)(2,1)}, bf16[2,400,512]{2,1,0:T(8,128)(2,1)}, u32[]{:S(2)}, u32[]{:S(2)}) collective-permute-start(bf16[2,400,512]{2,1,0:T(8,128)(2,1)} %get-tuple-element.411), channel_id=1, source_target_pairs={{0,1},{1,0},{2,3},{3,2},{4,5},{5,4},{6,7},{7,6},{8,9},{9,8},{10,11... | collective-permute-start | bytes 2457608 | tf_op jit(solution)/shard_map/ppermute | solution.py:62
  511.4 25.9 %collective-permute-start.62 = (bf16[2,400,512]{2,1,0:T(8,128)(2,1)}, bf16[2,400,512]{2,1,0:T(8,128)(2,1)}, u32[]{:S(2)}, u32[]{:S(2)}) collective-permute-start(bf16[2,400,512]{2,1,0:T(8,128)(2,1)} %get-tuple-element.419), channel_id=1, source_target_pairs={{0,1},{1,0},{2,3},{3,2},{4,5},{5,4},{6,7},{7,6},{8,9},{9,8},{10,11... | collective-permute-start | bytes 2457608 | tf_op jit(solution)/shard_map/ppermute | solution.py:62
  511.9 25.4 %collective-permute-start.63 = (bf16[4,384,256]{2,1,0:T(8,128)(2,1)}, bf16[4,384,256]{2,1,0:T(8,128)(2,1)}, u32[]{:S(2)}, u32[]{:S(2)}) collective-permute-start(bf16[4,384,256]{2,1,0:T(8,128)(2,1)} %get-tuple-element.425), channel_id=1, source_target_pairs={{0,4},{4,0},{1,5},{5,1},{2,6},{6,2},{3,7},{7,3},{8,12},{12,8},{9,1... | collective-permute-start | bytes 2359304 | tf_op jit(solution)/shard_map/ppermute | solution.py:62
  539.2 30.5 %collective-permute-start.64 = (bf16[400,512]{1,0:T(8,128)(2,1)}, bf16[400,512]{1,0:T(8,128)(2,1)}, u32[]{:S(2)}, u32[]{:S(2)}) collective-permute-start(bf16[400,512]{1,0:T(8,128)(2,1)} %add_convert_fusion.6), channel_id=1, source_target_pairs={{0,8},{8,16},{16,24},{24,0},{1,9},{9,17},{17,25},{25,1},{2,10},{10... | collective-permute-start | bytes 1228808 | tf_op jit(solution)/shard_map/ppermute | solution.py:66
  543.2 26.5 %collective-permute-start.65 = (bf16[400,512]{1,0:T(8,128)(2,1)}, bf16[400,512]{1,0:T(8,128)(2,1)}, u32[]{:S(2)}, u32[]{:S(2)}) collective-permute-start(bf16[400,512]{1,0:T(8,128)(2,1)} %fusion.18), channel_id=1, source_target_pairs={{0,2},{2,0},{1,3},{3,1},{4,6},{6,4},{5,7},{7,5},{8,10},{10,8},{9,1... | collective-permute-start | bytes 1228808 | tf_op jit(solution)/shard_map/ppermute | solution.py:62
  543.2 26.5 %collective-permute-start.66 = (bf16[2,400,512]{2,1,0:T(8,128)(2,1)}, bf16[2,400,512]{2,1,0:T(8,128)(2,1)}, u32[]{:S(2)}, u32[]{:S(2)}) collective-permute-start(bf16[2,400,512]{2,1,0:T(8,128)(2,1)} %get-tuple-element.432), channel_id=1, source_target_pairs={{0,1},{1,0},{2,3},{3,2},{4,5},{5,4},{6,7},{7,6},{8,9},{9,8},{10,11... | collective-permute-start | bytes 2457608 | tf_op jit(solution)/shard_map/ppermute | solution.py:62
  545.5 41.9 %all-to-all-start.9 = ((bf16[4,384,256]{2,1,0:T(8,128)(2,1)}), bf16[4,384,256]{2,1,0:T(8,128)(2,1)}, u32[]{:S(2)}, u32[]{:S(2)}) async-start(bf16[4,384,256]{2,1,0:T(8,128)(2,1)} %add_convert_fusion.3), calls=%async_computation.9 | async-start | bytes 1572864 | tf_op jit(solution)/shard_map/all_to_all | solution.py:754
  571.8 15.6 %collective-permute-start.67 = (bf16[400,512]{1,0:T(8,128)(2,1)}, bf16[400,512]{1,0:T(8,128)(2,1)}, u32[]{:S(2)}, u32[]{:S(2)}) collective-permute-start(bf16[400,512]{1,0:T(8,128)(2,1)} %add_convert_fusion.5), channel_id=1, source_target_pairs={{0,8},{8,16},{16,24},{24,0},{1,9},{9,17},{17,25},{25,1},{2,10},{10... | collective-permute-start | bytes 1228808 | tf_op jit(solution)/shard_map/ppermute | solution.py:66
  589.3 16.7 %collective-permute-start.72 = (bf16[400,512]{1,0:T(8,128)(2,1)}, bf16[400,512]{1,0:T(8,128)(2,1)S(1)}, u32[]{:S(2)}, u32[]{:S(2)}) collective-permute-start(bf16[400,512]{1,0:T(8,128)(2,1)} %add_convert_fusion.4), channel_id=1, source_target_pairs={{0,8},{8,16},{16,24},{24,0},{1,9},{9,17},{17,25},{25,1},{2,10},{10... | collective-permute-start | bytes 1228808 | tf_op jit(solution)/shard_map/ppermute | solution.py:66
  (129 other events, 1405.3 us)
Sparse Core Ops, SparseCore 0:
  71.7 63.1 all-gather.4
  137.1 79.4 all-gather.6
  475.7 92.1 reduce-scatter.1
